TPU v7x, 32 devices: a whole 2x2x4 slice. The times are simulated.
32 devices in a mesh: batch: 8 (over y, x, core), slab: 4 (over z).
Axes of the slice: x: 2, y: 2, z: 4, core: 2. Of those that a mesh axis runs over, the one named last changes fastest.
Arguments:
- images: bfloat16 [256, 384, 384], P(('batch', 'slab')), may hold values from -6 to 6
- classes: int32 [256], P(('batch', 'slab')), may hold values from 0 to 767
- shifts: int32 [256, 2], P(('batch', 'slab')), may hold values from -16 to 16
- defocus_class: int32 [256], P(('batch', 'slab')), may hold values from 0 to 15
- defocus: float32 [16], replicated, may hold values from 150 to 600
- run_counts: int32 [256, 4], P(('batch', 'slab')), may hold values from 1 to 192, 384 in all within a row
- dest_map: int32 [768, 384], replicated, may hold values from 0 to 15
- ref: bfloat16 [384, 64, 768], P('batch', 'slab'), may hold values from -6 to 6
Outputs:
- updated: bfloat16 [384, 64, 768], P('batch', 'slab')
Inputs may be any that keep to these rules, and one draw needn't show every extreme that they name: `run_counts`: each particle's counts sum to 384; in every particle's row the largest count is exactly 192.
All inputs are finite; a program needn't handle non-finite values.
Results may differ from a plain program's by a relative error of at most 0.0065.
Values may be sent and summed in bfloat16 or wider, within the bound.
No kernel may reach another device: no remote copies, remote signals or barrier semaphores. Data moves between devices by JAX's collectives and lax.ppermute only.
A program may use at most 128 MiB of HBM per device.

v0:
```python
import math

import jax
import jax.numpy as jnp
from jax import lax
from jax.sharding import PartitionSpec as P

TAU_PRIOR = 4.0
PHASE_OFFSET = 0.1


def dft_tables(length):
    index = jnp.arange(length, dtype=jnp.int32)
    turns = index[:, None] * index[None, :] % length
    angle = 2.0 * math.pi / length * turns.astype(jnp.float32)
    factor = 1.0 / math.sqrt(length)
    cosine = jnp.cos(angle) * factor
    sine = jnp.sin(angle) * factor
    table_left = jnp.concatenate([cosine, -sine], axis=0).astype(jnp.bfloat16)
    upper_rows = jnp.concatenate([cosine, -sine], axis=1)
    lower_rows = jnp.concatenate([sine, cosine], axis=1)
    table_right = jnp.concatenate([upper_rows, lower_rows], axis=0).astype(jnp.bfloat16)
    return (table_left, table_right)


def contrast(focus_value, freq_row, freq_col, length):
    half_length = length // 2
    spatial_row = ((freq_row + half_length) % length - half_length).astype(jnp.float32) / length
    spatial_col = ((freq_col + half_length) % length - half_length).astype(jnp.float32) / length
    return -jnp.sin(
        focus_value * (spatial_row * spatial_row + spatial_col * spatial_col) + PHASE_OFFSET
    )


def shifted_parts(real_part, imag_part, shift_x, shift_y, freq_row, freq_col, length):
    turns = (freq_col * shift_x + freq_row * shift_y) % length
    angle = 2.0 * math.pi / length * turns.astype(jnp.float32)
    cosine = jnp.cos(angle)
    sine = jnp.sin(angle)
    return (real_part * cosine + imag_part * sine, imag_part * cosine - real_part * sine)


def lookup(values, indices):
    matches = indices[:, None] == jnp.arange(values.shape[0], dtype=jnp.int32)[None, :]
    return jnp.sum(jnp.where(matches, values[None, :], 0.0), axis=1)


def insert_window(
    flat_rows,
    row_index,
    plane_index,
    focus_in,
    is_valid,
    rows_window,
    planes_window,
    row_start,
    defocus,
    length,
):
    bin_count = rows_window * planes_window + 1
    segment_ids = jnp.where(
        is_valid, row_index * planes_window + plane_index, rows_window * planes_window
    )
    numerator = jax.ops.segment_sum(flat_rows.astype(jnp.float32), segment_ids, bin_count)[
        :-1
    ].reshape(rows_window, planes_window, 2 * length)
    focus_rows = lookup(defocus, focus_in)
    global_rows = row_start + row_index
    transfer_in = contrast(
        focus_rows[:, None],
        global_rows[:, None],
        jnp.arange(length, dtype=jnp.int32)[None, :],
        length,
    )
    second = jax.ops.segment_sum(transfer_in * transfer_in, segment_ids, bin_count)[:-1].reshape(
        rows_window, planes_window, length
    )
    return (numerator, second)


def per_device(images, classes, shifts, defocus_class, defocus, run_counts, dest_map, ref):
    particle_count = images.shape[0]
    length = images.shape[1]
    slab_count = lax.axis_size("slab")
    capacity = 2 * length // slab_count
    plane_count = ref.shape[1]
    table_left, table_right = dft_tables(length)
    section = jnp.einsum(
        "ay,pyx->pax", table_left, images, preferred_element_type=jnp.float32
    ).astype(jnp.bfloat16)
    joined = jnp.concatenate([section[:, :length], section[:, length:]], axis=2)
    spectrum = jnp.einsum("pyc,cd->pyd", joined, table_right, preferred_element_type=jnp.float32)
    freq_row = jnp.arange(length, dtype=jnp.int32)[None, :, None]
    freq_col = jnp.arange(length, dtype=jnp.int32)[None, None, :]
    real_part, imag_part = shifted_parts(
        spectrum[..., :length],
        spectrum[..., length:],
        shifts[:, 0][:, None, None],
        shifts[:, 1][:, None, None],
        freq_row,
        freq_col,
        length,
    )
    focus_values = lookup(defocus, defocus_class)
    transfer = contrast(focus_values[:, None, None], freq_row, freq_col, length)
    weighted = jnp.concatenate([transfer * real_part, transfer * imag_part], axis=2).astype(
        jnp.bfloat16
    )
    run_ends = jnp.cumsum(run_counts, axis=1)
    run_starts = run_ends - run_counts
    dest_rows = dest_map[classes]
    padded = jnp.concatenate(
        [weighted, jnp.zeros((particle_count, capacity, 2 * length), jnp.bfloat16)], axis=1
    )

    def take_run(block, begin):
        return lax.dynamic_slice_in_dim(block, begin, capacity, 0)

    def take_owner(begin_cols):
        return jax.vmap(take_run)(padded, begin_cols)

    run_slots = jax.vmap(take_owner, in_axes=1)(run_starts)
    offsets = jnp.arange(capacity, dtype=jnp.int32)
    slot_rows = run_starts.T[:, :, None] + offsets[None, None, :]
    is_valid = offsets[None, None, :] < run_counts.T[:, :, None]
    safe_rows = jnp.minimum(slot_rows, length - 1)
    slot_planes = jnp.take_along_axis(
        jnp.broadcast_to(dest_rows[None], (slab_count, particle_count, length)), safe_rows, axis=2
    )
    slot_codes = jnp.where(
        is_valid,
        (defocus_class[None, :, None] * plane_count + slot_planes) * length + safe_rows,
        -1,
    )
    received, codes_in = (
        lax.all_to_all(run_slots, "slab", split_axis=0, concat_axis=0, tiled=True),
        lax.all_to_all(slot_codes, "slab", split_axis=0, concat_axis=0, tiled=True),
    )
    flat_rows = received.reshape(-1, 2 * length)
    flat_codes = codes_in.reshape(-1)
    is_valid_in = flat_codes >= 0
    safe_codes = jnp.maximum(flat_codes, 0)
    row_index = safe_codes % length
    rest_code = safe_codes // length
    plane_index = rest_code % plane_count
    focus_in = rest_code // plane_count
    numerator, second = insert_window(
        flat_rows,
        row_index,
        plane_index,
        focus_in,
        is_valid_in,
        length,
        plane_count,
        0,
        defocus,
        length,
    )
    own_sums, own_second = (
        lax.psum_scatter(
            numerator.astype(jnp.bfloat16), "batch", scatter_dimension=0, tiled=True
        ).astype(jnp.float32),
        lax.psum_scatter(
            second.astype(jnp.bfloat16), "batch", scatter_dimension=0, tiled=True
        ).astype(jnp.float32),
    )
    prior = ref.astype(jnp.float32)
    denom = own_second + TAU_PRIOR
    real_new = (TAU_PRIOR * prior[..., :length] + own_sums[..., :length]) / denom
    imag_new = (TAU_PRIOR * prior[..., length:] + own_sums[..., length:]) / denom
    return jnp.concatenate([real_new, imag_new], axis=2).astype(jnp.bfloat16)


def solution(mesh):
    placed = (
        P(("batch", "slab"), None, None),
        P(("batch", "slab")),
        P(("batch", "slab"), None),
        P(("batch", "slab")),
        P(),
        P(("batch", "slab"), None),
        P(),
        P("batch", "slab", None),
    )
    return jax.shard_map(
        per_device, mesh=mesh, in_specs=placed, out_specs=P("batch", "slab", None), check_vma=False
    )
```

profile of v0, /device:TPU:0, one launch (start us, length us, event | category | flops | bytes accessed | tf_op | source)
XLA Modules:
  0.0 663.7 jit_solution(3716863432095399917)
XLA Ops:
  10.8 47.6 %gather_fusion.1 = s32[6144]{0:T(1024)S(1)} fusion(s32[4,8,384]{2,1,0:T(8,128)S(1)} %broadcast_in_dim.44, s32[6144]{0:T(1024)S(1)} %reshape.393), kind=kCustom, calls=%fused_computation.1 | custom fusion | bytes 122880 | tf_op jit(solution)/shard_map/jit(take_along_axis)/gather | solution.py:127
  59.2 6.3 all-to-all-start
  76.7 5.8 fusion.15
  82.5 37.8 %multiply_convert_fusion.1 = (bf16[8,384,384]{2,1,0:T(8,128)(2,1)S(1)}, bf16[8,384,384]{2,1,0:T(8,128)(2,1)S(1)}) fusion(f32[8,384,768]{2,1,0:T(8,128)S(1)} %fusion.15, s32[8,384]{1,0:T(8,128)S(1)} %get-tuple-element.39, s32[8,384]{1,0:T(8,128)S(1)} %get-tuple-element.40, f32[384,384]{1,0:T(8,128)S(1)} %broadcast_add_fusion, f32[8]{0:T(128)S(1)} %select_reduce_fusion.1), kind=kLoop, calls=%fused_computation.34 | loop fusion | flops 25952256 | bytes 14770208 | tf_op jit(solution)/shard_map/convert.5
  120.3 3.3 fusion.11
  123.6 118.6 %while.1 = (s32[]{:T(128)}, bf16[8,576,768]{2,1,0:T(8,128)(2,1)}, s32[32,3]{0,1:T(4,128)S(1)}, bf16[32,192,768]{2,1,0:T(8,128)(2,1)}, s32[]{:T(128)}) while((s32[]{:T(128)}, bf16[8,576,768]{2,1,0:T(8,128)(2,1)}, s32[32,3]{0,1:T(4,128)S(1)}, bf16[32,192,768]{2,1,0:T(8,128)(2,1)}, s32[]{:T(128)}) %tuple.28), condition=%wide.while_cond, body=%wide.while_body.sunk | while | flops 2 | bytes 591465 | solution.py:117
  157.6 3.1 dynamic-slice_dynamic-update-slice_fusion.2
  161.3 3.1 dynamic-slice_dynamic-update-slice_fusion.2
  179.8 3.1 dynamic-slice_dynamic-update-slice_fusion.2
  190.9 3.1 dynamic-slice_dynamic-update-slice_fusion.2
  194.6 3.1 dynamic-slice_dynamic-update-slice_fusion.2
  205.8 3.1 dynamic-slice_dynamic-update-slice_fusion.2
  224.3 3.1 dynamic-slice_dynamic-update-slice_fusion.2
  228.0 3.1 dynamic-slice_dynamic-update-slice_fusion.2
  231.7 3.1 dynamic-slice_dynamic-update-slice_fusion.2
  235.5 3.1 dynamic-slice_dynamic-update-slice_fusion.2
  242.2 5.8 all-to-all-start.1
  248.7 204.9 %all-to-all-done.1 = bf16[4,8,192,768]{3,2,1,0:T(8,128)(2,1)} async-done(((bf16[4,8,192,768]{3,2,1,0:T(8,128)(2,1)}), bf16[4,8,192,768]{3,2,1,0:T(8,128)(2,1)}, u32[]{:S(2)}, u32[]{:S(2)}) %all-to-all-start.1) | async-done | bytes 9437216 | tf_op jit(solution)/shard_map/all_to_all | solution.py:136
  453.7 50.4 %scatter_custom_fusion = f32[6145,768]{1,0:T(8,128)} fusion(s32[6144]{0:T(1024)S(1)} %bitcast.41, bf16[6144,768]{1,0:T(8,128)(2,1)} %bitcast.17, f32[]{:T(128)} %constant.88.clone.1), kind=kCustom, calls=%fused_computation.7 | custom fusion | flops 9437184 | bytes 28314628 | tf_op jit(solution)/shard_map/scatter-add | solution.py:64
  504.0 11.1 %slice.106 = bf16[6144,768]{1,0:T(8,128)(2,1)} slice(f32[6145,768]{1,0:T(8,128)} %scatter_custom_fusion), slice={[0:6144], [0:768]} | slice | bytes 18874368 | tf_op jit(solution)/shard_map/slice | solution.py:64
  516.0 76.8 %scatter_custom_fusion.1 = f32[6145,384]{1,0:T(8,128)} fusion(s32[6144]{0:T(1024)S(1)} %bitcast.42, f32[]{:T(128)} %constant.88.clone.1, f32[]{:T(128)} %constant.137.clone.1, f32[384]{0:T(512)S(1)} %fusion.67, f32[6144]{0:T(1024)S(1)} %fusion.60, f32[6144]{0:T(1024)S(1)} %select_reduce_fusion), kind=kCustom, calls=%fused_computation.14 | custom fusion | flops 11796480 | bytes 9489928 | tf_op jit(solution)/shard_map/scatter-add | solution.py:75
  592.8 6.4 slice.107
  602.2 3.1 convert_element_type.88
  605.3 47.6 %reduce-scatter.5.cloned.1.call-done = bf16[48,16,384]{2,1,0:T(8,128)(2,1)} async-done(((bf16[384,16,384]{2,1,0:T(8,128)(2,1)}), bf16[48,16,384]{2,1,0:T(8,128)(2,1)}) %reduce-scatter.5.cloned.1.call-update) | async-done | bytes 589840 | tf_op jit(solution)/shard_map/reduce_scatter | solution.py:163
  (148 shorter events, 112.5 us)
Async XLA Ops:
  6.5 64.6 %copy-start = (bf16[8,384,384]{2,1,0:T(8,128)(2,1)S(1)}, bf16[8,384,384]{2,1,0:T(8,128)(2,1)}, u32[]{:S(2)}) copy-start(bf16[8,384,384]{2,1,0:T(8,128)(2,1)} %param.8) | copy-start | bytes 7077892
  10.8 47.7 %copy-start.7 = (s32[8]{0:T(128)S(1)}, s32[8]{0:T(128)}, u32[]{:S(2)}) copy-start(s32[8]{0:T(128)} %param.11) | copy-start | bytes 100
  10.8 47.7 %copy-start.4 = (s32[8,4]{0,1:T(4,128)S(1)}, s32[8,4]{0,1:T(4,128)}, u32[]{:S(2)}) copy-start(s32[8,4]{0,1:T(4,128)} %param.13) | copy-start | bytes 388
  59.2 183.1 %all-to-all-start = ((s32[4,8,192]{2,1,0:T(8,128)}), s32[4,8,192]{2,1,0:T(8,128)S(1)}, u32[]{:S(2)}, u32[]{:S(2)}) async-start(s32[4,8,192]{2,1,0:T(8,128)} %add_select_fusion.6), calls=%async_computation | async-start | bytes 65536 | tf_op jit(solution)/shard_map/all_to_all | solution.py:137
  68.1 8.1 %copy-start.3 = (bf16[384,384]{1,0:T(8,128)(2,1)}, bf16[384,384]{1,0:T(8,128)(2,1)S(1)}, u32[]{:S(2)}) copy-start(bf16[384,384]{1,0:T(8,128)(2,1)S(1)} %get-tuple-element.38) | copy-start | bytes 884740
  74.0 2.2 copy-start.5
  74.0 2.3 copy-start.6
  242.2 211.4 %all-to-all-start.1 = ((bf16[4,8,192,768]{3,2,1,0:T(8,128)(2,1)}), bf16[4,8,192,768]{3,2,1,0:T(8,128)(2,1)}, u32[]{:S(2)}, u32[]{:S(2)}) async-start(bf16[4,8,192,768]{3,2,1,0:T(8,128)(2,1)} %bitcast.40), calls=%async_computation.1 | async-start | bytes 18874368 | tf_op jit(solution)/shard_map/all_to_all | solution.py:136
  248.0 354.2 %reduce-scatter.3.cloned.1.call-start = ((), (), s32[]{:S(2)}) async-start(), calls=%async_computation.4 | async-start | bytes 10616832 | tf_op jit(solution)/shard_map/reduce_scatter | solution.py:160
  515.2 137.7 %reduce-scatter.5.cloned.1.call-start = ((), (), s32[]{:S(2)}) async-start(), calls=%async_computation.5 | async-start | bytes 5308416 | tf_op jit(solution)/shard_map/reduce_scatter | solution.py:163
  599.2 1.3 copy-start.2
  602.2 54.7 %copy-start.1 = (bf16[8,384,384]{2,1,0:T(8,128)(2,1)S(1)}, bf16[8,384,384]{2,1,0:T(8,128)(2,1)}, u32[]{:S(2)}) copy-start(bf16[8,384,384]{2,1,0:T(8,128)(2,1)} %param.8) | copy-start | bytes 7077892
Sparse Core Ops, SparseCore 0:
  515.3 75.8 reduce-scatter.2
  599.4 53.4 reduce-scatter.4
where the time goes:
time: 669 us; the launch traced here: 664 us
  waiting for transfers between devices  253 us (38%)
  local copies, waits for them, and re-layouts  190 us (28%)
  other arithmetic  187 us (28%)
  between operations  13.6 us (2%)
  starting transfers between devices  12.4 us (2%)
  matrix products  8.7 us (1%)
    all_to_all x1, waiting for transfers between devices, per_device(): lax.all_to_all(run_slots, 'slab', split_axis=0, concat_axis=0, tiled=True)  205 us
    gather x96, local copies, waits for them, and re-layouts  119 us
    scatter-add x1, other arithmetic, insert_window(): jax.ops.segment_sum(transfer_in * transfer_in, segment_ids, bin_count)[:-1]  76.8 us
    scatter-add x1, other arithmetic, insert_window(): jax.ops.segment_sum(flat_rows.astype(jnp.float32), segment_ids, bin_count)  50.4 us
    gather x3, local copies, waits for them, and re-layouts, per_device(): jnp.take_along_axis(jnp.broadcast_to(dest_rows[None], (slab_count, partic...  47.7 us
    reduce_scatter x1, waiting for transfers between devices, per_device(): lax.psum_scatter(second.astype(jnp.bfloat16), 'batch', scatter_dimension=...  47.6 us
    another operation x4, other arithmetic  46.2 us
  transfers between devices with their start and end apart: 4, of which 2 were waited for; matrix products, arithmetic and copies ran while one was open for 40% of the time, Pallas kernels for 0%

commit v1 on v0

v1 whole, which is shorter than its diff:
```python
import math

import jax
import jax.numpy as jnp
import numpy as np
from jax import lax
from jax.experimental import pallas as pl
from jax.experimental.pallas import tpu as pltpu
from jax.sharding import PartitionSpec as P

TAU_PRIOR = 4.0
PHASE_OFFSET = 0.1
CHUNKS = 3
VMEM_LIMIT = 48 * 1024 * 1024


def dft_tables(length):
    index = np.arange(length, dtype=np.int32)
    turns = index[:, None] * index[None, :] % length
    angle = np.float32(2.0 * math.pi / length) * turns.astype(np.float32)
    factor = np.float32(1.0 / math.sqrt(length))
    cosine = np.cos(angle) * factor
    sine = np.sin(angle) * factor
    upper_rows = np.concatenate([cosine, -sine], axis=1)
    lower_rows = np.concatenate([sine, cosine], axis=1)
    table_right = np.concatenate([upper_rows, lower_rows], axis=0)
    return cosine, -sine, table_right


def spectrum_kernel(images, left, right, row_factors, col_factors, out, joined):
    particles, length = images.shape[0], images.shape[1]
    owners, _, rows_each, _ = out.shape
    rows = owners * rows_each
    table = left[...]
    for p in range(particles):
        section = jnp.dot(table, images[p], preferred_element_type=jnp.float32)
        section = section.astype(jnp.bfloat16)
        joined[p * rows : (p + 1) * rows, :length] = section[:rows]
        joined[p * rows : (p + 1) * rows, length:] = section[rows:]
    factors = row_factors[...]
    for first in range(0, particles, 2):
        spectrum = jnp.dot(
            joined[first * rows : (first + 2) * rows, :],
            right[...],
            preferred_element_type=jnp.float32,
        )
        for p in range(first, first + 2):
            part = spectrum[(p - first) * rows : (p - first + 1) * rows]
            real_part, imag_part = part[:, :length], part[:, length:]

            def row(q):
                at = q * particles + p
                return factors[:, at : at + 1]

            def col(q):
                at = q * particles + p
                return col_factors[at : at + 1, :]

            transfer = -(row(2) * col(3) + row(3) * col(2))
            cosine = transfer * (row(1) * col(1) - row(0) * col(0))
            sine = transfer * (row(0) * col(1) + row(1) * col(0))
            real_new = real_part * cosine + imag_part * sine
            imag_new = imag_part * cosine - real_part * sine
            weighted = jnp.concatenate([real_new, imag_new], axis=1).astype(jnp.bfloat16)
            out[:, p] = weighted.reshape(owners, rows_each, 2 * length)


def insert_kernel(received, codes, *outs):
    bins = outs[0].shape[0]
    rows = received[...]
    codes_all = codes[...]
    for k, out in enumerate(outs):
        bin_index = lax.broadcasted_iota(jnp.int32, (bins, 1), 0) + k * bins
        hot = jnp.where(codes_all == bin_index, 1.0, 0.0).astype(jnp.bfloat16)
        out[...] = jnp.dot(hot, rows, preferred_element_type=jnp.float32).astype(out.dtype)


def whole_vmem(count):
    return [pl.BlockSpec(memory_space=pltpu.VMEM)] * count


def lookup(values, indices):
    matches = indices[:, None] == jnp.arange(values.shape[0], dtype=jnp.int32)[None, :]
    return jnp.sum(jnp.where(matches, values[None, :], 0.0), axis=1)


def centred_square(freq, length):
    half_length = length // 2
    value = ((freq + half_length) % length - half_length).astype(jnp.float32) / length
    return value * value


def trig_factors(shift, focus, freq, offset, length, axis):
    if axis == 0:
        freq, shift, focus = freq[:, None], shift[None, :], focus[None, :]
    else:
        freq, shift, focus = freq[None, :], shift[:, None], focus[:, None]
    turns = (freq * shift) % length
    phase = 2.0 * math.pi / length * turns.astype(jnp.float32)
    angle = focus * centred_square(freq, length) + offset
    return jnp.concatenate(
        [jnp.sin(phase), jnp.cos(phase), jnp.sin(angle), jnp.cos(angle)], axis=1 - axis
    )


def slab_sums(parts, slab, slab_count):
    if slab_count != 4:
        merged = jnp.stack(parts)
        order = (jnp.arange(slab_count) - slab) % slab_count
        return lax.psum_scatter(
            jnp.take(merged, order, axis=0), "slab", scatter_dimension=0, tiled=False
        ).astype(jnp.float32)
    edge = jnp.where(slab == 0, parts[3], parts[1])
    edge_in = lax.ppermute(edge, "slab", [(0, 1), (3, 2)])
    right_in = lax.ppermute(parts[1], "slab", [(0, 1), (1, 2), (2, 3)])
    left_in = lax.ppermute(parts[3], "slab", [(1, 0), (2, 1), (3, 2)])
    far = (parts[2].astype(jnp.float32) + edge_in.astype(jnp.float32)).astype(jnp.bfloat16)
    far_in = lax.ppermute(far, "slab", [(0, 2), (1, 3), (2, 0), (3, 1)])
    total = parts[0].astype(jnp.float32) + right_in.astype(jnp.float32)
    return total + left_in.astype(jnp.float32) + far_in.astype(jnp.float32)


def per_device(images, classes, shifts, defocus_class, defocus, run_counts, dest_map, ref):
    particles, length, _ = images.shape
    batch_count = lax.axis_size("batch")
    slab_count = lax.axis_size("slab")
    batch = lax.axis_index("batch")
    slab = lax.axis_index("slab")
    rows, planes, _ = ref.shape
    each = rows // CHUNKS
    chunk_rows = batch_count * each
    freq = jnp.arange(length, dtype=jnp.int32)

    ends = jnp.cumsum(run_counts, axis=1)
    meta = jnp.concatenate([classes[:, None], defocus_class[:, None], ends], axis=1)
    meta_all = lax.all_gather(meta, ("batch", "slab"), axis=0, tiled=True)

    cosine, minus_sine, table_right = dft_tables(length)
    order = np.arange(length).reshape(batch_count, CHUNKS, each).transpose(1, 0, 2)
    order = order.reshape(CHUNKS, chunk_rows)
    table_right = jnp.asarray(table_right.astype(jnp.bfloat16))
    focus = lookup(defocus, defocus_class)
    row_factors = trig_factors(shifts[:, 1], focus, freq, PHASE_OFFSET, length, 0)
    col_factors = trig_factors(shifts[:, 0], focus, freq, 0.0, length, 1)
    row_factors = row_factors.reshape(batch_count, CHUNKS, each, 4 * particles)
    row_factors = row_factors.transpose(1, 0, 2, 3).reshape(CHUNKS, chunk_rows, 4 * particles)
    received = []
    for c in range(CHUNKS):
        left = np.concatenate([cosine[order[c]], minus_sine[order[c]]], axis=0)
        weighted = pl.pallas_call(
            spectrum_kernel,
            out_shape=jax.ShapeDtypeStruct(
                (batch_count, particles, each, 2 * length), jnp.bfloat16
            ),
            in_specs=whole_vmem(5),
            out_specs=pl.BlockSpec(memory_space=pltpu.VMEM),
            scratch_shapes=[pltpu.VMEM((particles * chunk_rows, 2 * length), jnp.bfloat16)],
            compiler_params=pltpu.CompilerParams(vmem_limit_bytes=VMEM_LIMIT),
            cost_estimate=pl.CostEstimate(
                flops=2 * particles * chunk_rows * 2 * length * 3 * length,
                bytes_accessed=6 * 1024 * 1024,
                transcendentals=0,
            ),
            name="spectrum",
        )(
            images,
            jnp.asarray(left.astype(jnp.bfloat16)),
            table_right,
            row_factors[c],
            col_factors,
        )
        received.append(lax.all_to_all(weighted, "batch", 0, 0, tiled=True))

    class_count = dest_map.shape[0]
    own_dest = lax.dynamic_slice_in_dim(dest_map, batch * rows, rows, 1).astype(jnp.bfloat16)
    class_hot = (meta_all[:, :1] == jnp.arange(class_count)[None, :]).astype(jnp.bfloat16)
    local_plane = jnp.dot(class_hot, own_dest, preferred_element_type=jnp.float32)
    local_plane = local_plane.astype(jnp.int32)
    own_freq = batch * rows + jnp.arange(rows, dtype=jnp.int32)
    owner = jnp.sum(
        (own_freq[None, :, None] >= meta_all[:, None, 2:]).astype(jnp.int32), axis=2
    )

    grouped = (batch_count, slab_count, particles, rows)
    relative = (owner - slab) % slab_count
    local_bin = relative * (each * planes) + (jnp.arange(rows) % each)[None, :] * planes
    codes = lax.dynamic_index_in_dim(
        (local_bin + local_plane).reshape(grouped), slab, 1, keepdims=False
    )
    codes = codes.reshape(batch_count * particles, CHUNKS, each).transpose(1, 0, 2)
    codes = codes.reshape(CHUNKS, 1, batch_count * particles * each)

    focus_count = defocus.shape[0]
    focus_hot = (meta_all[:, 1:2] == jnp.arange(focus_count)[None, :]).astype(jnp.bfloat16)
    own_plane = jnp.where(owner == slab, local_plane, -1)
    bin_hot = (own_plane.T[:, None, :] == jnp.arange(planes)[None, :, None]).astype(jnp.bfloat16)
    counts = jnp.einsum("kzp,pd->kzd", bin_hot, focus_hot, preferred_element_type=jnp.float32)
    row_angle = 2.0 * (
        defocus[None, :] * centred_square(own_freq, length)[:, None] + PHASE_OFFSET
    )
    col_angle = 2.0 * (defocus[:, None] * centred_square(freq, length)[None, :])
    row_side = jnp.concatenate(
        [counts * jnp.cos(row_angle)[:, None, :], counts * jnp.sin(row_angle)[:, None, :]], axis=2
    )
    col_side = jnp.concatenate([jnp.cos(col_angle), -jnp.sin(col_angle)], axis=0)
    double = jnp.einsum("kzd,dx->kzx", row_side, col_side, precision=lax.Precision.HIGHEST)
    weights = 0.5 * (jnp.sum(counts, axis=2, keepdims=True) - double)
    denom = weights + TAU_PRIOR

    bins = each * planes
    updated = []
    for c in range(CHUNKS):
        rows_in = received[c].reshape(batch_count * particles * each, 2 * length)
        parts = pl.pallas_call(
            insert_kernel,
            out_shape=[jax.ShapeDtypeStruct((bins, 2 * length), jnp.bfloat16)] * slab_count,
            in_specs=whole_vmem(2),
            out_specs=whole_vmem(slab_count),
            compiler_params=pltpu.CompilerParams(vmem_limit_bytes=VMEM_LIMIT),
            cost_estimate=pl.CostEstimate(
                flops=2 * bins * slab_count * rows_in.shape[0] * 2 * length,
                bytes_accessed=4 * 1024 * 1024,
                transcendentals=0,
            ),
            name="insert",
        )(rows_in, codes[c])
        sums = slab_sums(parts, slab, slab_count).reshape(each, planes, 2 * length)
        here = slice(c * each, (c + 1) * each)
        prior = ref[here].astype(jnp.float32)
        under = denom[here]
        updated.append(
            (
                (TAU_PRIOR * prior + sums) / jnp.concatenate([under, under], axis=2)
            ).astype(jnp.bfloat16)
        )
    return jnp.concatenate(updated, axis=0)


def solution(mesh):
    placed = (
        P(("batch", "slab"), None, None),
        P(("batch", "slab")),
        P(("batch", "slab"), None),
        P(("batch", "slab")),
        P(),
        P(("batch", "slab"), None),
        P(),
        P("batch", "slab", None),
    )
    return jax.shard_map(
        per_device, mesh=mesh, in_specs=placed, out_specs=P("batch", "slab", None), check_vma=False
    )
```

time: 669 us -> 243 us (0.36)
  other arithmetic: 187 us -> 11.5 us
  waiting for transfers between devices: 253 us -> 79 us
  local copies, waits for them, and re-layouts: 190 us -> 21.8 us
  blocking collectives: 0 us -> 70.3 us
  starting transfers between devices: 12.4 us -> 36.2 us
  Pallas kernels: 0 us -> 16.7 us
  between operations: 13.6 us -> 0.43 us
    all_to_all x2 -> x3, waiting for transfers between devices: 205 us -> 4.83 us  [per_device(): received.append(lax.all_to_all(weighted, 'batch', 0, 0, tiled=True))]
    gather x101 -> x0, local copies, waits for them, and re-layouts: 168 us -> none
    scatter-add x2 -> x0, other arithmetic: 127 us -> none  [the longest x1 76.8 us: insert_window(): jax.ops.segment_sum(transfer_in * transfer_in, segment_ids, bin_count)[:-1]]
    ppermute x0 -> x12, waiting for transfers between devices: none -> 74.2 us  [the longest x3 54.6 us: slab_sums(): far_in = lax.ppermute(far, 'slab', [(0, 2), (1, 3), (2, 0), (3, 1)])]
    all_gather x0 -> x1, blocking collectives: none -> 70.3 us  [per_device(): meta_all = lax.all_gather(meta, ('batch', 'slab'), axis=0, tiled=True)]
    reduce_scatter x2 -> x0, waiting for transfers between devices: 47.6 us -> none  [the longest x1 47.6 us: per_device(): lax.psum_scatter(second.astype(jnp.bfloat16), 'batch', scatter_dimension=...]
    another operation x5 -> x1, other arithmetic: 47.1 us -> 0.16 us  [per_device(): ends = jnp.cumsum(run_counts, axis=1)]
    ppermute x0 -> x12, starting transfers between devices: none -> 22.7 us  [the longest x3 11 us: slab_sums(): edge_in = lax.ppermute(edge, 'slab', [(0, 1), (3, 2)])]
  transfers between devices with their start and end apart: 4 -> 15, of which waited for: 2 -> 7; matrix products, arithmetic and copies ran while one was open for 40% -> 10% of each run, Pallas kernels for 0% -> 5%
where the time goes in v1:
time: 243 us; the launch traced here: 242 us
  waiting for transfers between devices  79 us (33%)
  blocking collectives  70.3 us (29%)
  starting transfers between devices  36.2 us (15%)
  local copies, waits for them, and re-layouts  21.8 us (9%)
  Pallas kernels  16.7 us (7%)
  other arithmetic  11.5 us (5%)
  matrix products  6.04 us (2%)
    all_gather x1, blocking collectives, per_device(): meta_all = lax.all_gather(meta, ('batch', 'slab'), axis=0, tiled=True)  70.3 us
    ppermute x3, waiting for transfers between devices, slab_sums(): far_in = lax.ppermute(far, 'slab', [(0, 2), (1, 3), (2, 0), (3, 1)])  54.6 us
    ppermute x3, waiting for transfers between devices, slab_sums(): edge_in = lax.ppermute(edge, 'slab', [(0, 1), (3, 2)])  19.5 us
    all_to_all x3, starting transfers between devices, per_device(): received.append(lax.all_to_all(weighted, 'batch', 0, 0, tiled=True))  13.5 us
    ppermute x3, starting transfers between devices, slab_sums(): edge_in = lax.ppermute(edge, 'slab', [(0, 1), (3, 2)])  11 us
    unnamed x55, local copies, waits for them, and re-layouts  10.7 us
    pallas_call x3, Pallas kernels, per_device(): pl.pallas_call(spectrum_kernel, out_shape=jax.ShapeDtypeStruct((batch_cou...  9.12 us
    ppermute x3, starting transfers between devices, slab_sums(): right_in = lax.ppermute(parts[1], 'slab', [(0, 1), (1, 2), (2, 3)])  7.77 us
  transfers between devices with their start and end apart: 15, of which 7 were waited for; matrix products, arithmetic and copies ran while one was open for 10% of the time, Pallas kernels for 5%

profile of v1, /device:TPU:0, one launch (start us, length us, event | category | flops | bytes accessed | tf_op | source)
XLA Modules:
  0.0 242.0 jit_solution(12462933287074362342)
XLA Ops:
  6.2 3.8 %spectrum.4 = bf16[8,8,16,768]{3,2,1,0:T(8,128)(2,1)} custom-call(bf16[8,384,384]{2,1,0:T(8,128)(2,1)S(1)} %copy-done.4, bf16[256,384]{1,0:T(8,128)(2,1)S(1)} %copy-done.12, bf16[768,768]{1,0:T(8,128)(2,1)S(1)} %copy-done.7, f32[128,32]{1,0:T(8,128)S(1)} %bitcast.35, f32[32,384]{1,0:T(8,128)S(1)} %pad_maximum_fusion.1.col_factors), custom_call_target="tpu_custom_call" | custom-call | flops 1811939328 | bytes 6291456 | tf_op jit(solution)/shard_map/spectrum/pallas_call | solution.py:150
  10.1 5.3 %all-to-all-start.1 = ((bf16[8,8,16,768]{3,2,1,0:T(8,128)(2,1)}), bf16[8,8,16,768]{3,2,1,0:T(8,128)(2,1)S(1)}, u32[]{:S(2)}, u32[]{:S(2)}) async-start(bf16[8,8,16,768]{3,2,1,0:T(8,128)(2,1)} %spectrum.4), calls=%async_computation.1 | async-start | bytes 3145728 | tf_op jit(solution)/shard_map/all_to_all | solution.py:172
  15.9 70.3 %all_gather.3 = s32[256,6]{1,0:T(8,128)S(1)} all-gather(s32[8,6]{1,0:T(8,128)S(1)} %pad_add_fusion), channel_id=1, replica_groups=mesh['batch'=8,'slab'=4] {'batch','slab'}, dimensions={0}, use_global_device_ids=true | all-gather | bytes 6336 | tf_op jit(solution)/shard_map/all_gather | solution.py:136
  89.0 2.6 %spectrum.5 = bf16[8,8,16,768]{3,2,1,0:T(8,128)(2,1)S(1)} custom-call(bf16[8,384,384]{2,1,0:T(8,128)(2,1)S(1)} %copy-done.5, bf16[256,384]{1,0:T(8,128)(2,1)S(1)} %copy-done.11, bf16[768,768]{1,0:T(8,128)(2,1)S(1)} %copy-done.8, f32[128,32]{1,0:T(8,128)S(1)} %bitcast.34, f32[32,384]{1,0:T(8,128)S(1)} %pad_maximum_fusion.1.col_factors), custom_call_target="tpu_custom_call" | custom-call | flops 1811939328 | bytes 6291456 | tf_op jit(solution)/shard_map/spectrum/pallas_call | solution.py:150
  92.8 3.9 %all-to-all-start.2 = ((bf16[8,8,16,768]{3,2,1,0:T(8,128)(2,1)}), bf16[8,8,16,768]{3,2,1,0:T(8,128)(2,1)S(1)}, u32[]{:S(2)}, u32[]{:S(2)}) async-start(bf16[8,8,16,768]{3,2,1,0:T(8,128)(2,1)} %copy-done.1), calls=%async_computation.2 | async-start | bytes 3145728 | tf_op jit(solution)/shard_map/all_to_all | solution.py:172
  96.7 2.3 fusion.23
  106.4 2.6 %spectrum.3 = bf16[8,8,16,768]{3,2,1,0:T(8,128)(2,1)S(1)} custom-call(bf16[8,384,384]{2,1,0:T(8,128)(2,1)S(1)} %copy-done.6, bf16[256,384]{1,0:T(8,128)(2,1)S(1)} %copy-done.10, bf16[768,768]{1,0:T(8,128)(2,1)S(1)} %copy-done.9, f32[128,32]{1,0:T(8,128)S(1)} %bitcast.33, f32[32,384]{1,0:T(8,128)S(1)} %pad_maximum_fusion.1.col_factors), custom_call_target="tpu_custom_call" | custom-call | flops 1811939328 | bytes 6291456 | tf_op jit(solution)/shard_map/spectrum/pallas_call | solution.py:150
  112.6 4.8 %all-to-all-done.2 = bf16[8,8,16,768]{3,2,1,0:T(8,128)(2,1)S(1)} async-done(((bf16[8,8,16,768]{3,2,1,0:T(8,128)(2,1)}), bf16[8,8,16,768]{3,2,1,0:T(8,128)(2,1)S(1)}, u32[]{:S(2)}, u32[]{:S(2)}) %all-to-all-start.2) | async-done | bytes 1572896 | tf_op jit(solution)/shard_map/all_to_all | solution.py:172
  117.4 4.3 %all-to-all-start = ((bf16[8,8,16,768]{3,2,1,0:T(8,128)(2,1)}), bf16[8,8,16,768]{3,2,1,0:T(8,128)(2,1)}, u32[]{:S(2)}, u32[]{:S(2)}) async-start(bf16[8,8,16,768]{3,2,1,0:T(8,128)(2,1)} %copy-done), calls=%async_computation | async-start | bytes 3145728 | tf_op jit(solution)/shard_map/all_to_all | solution.py:172
  121.8 2.0 slice_reduce_fusion.4
  126.3 2.2 fusion.1
  129.5 2.6 %insert.4 = (bf16[256,768]{1,0:T(8,128)(2,1)S(1)}, bf16[256,768]{1,0:T(8,128)(2,1)}, bf16[256,768]{1,0:T(8,128)(2,1)S(1)}, bf16[256,768]{1,0:T(8,128)(2,1)}) custom-call(bf16[1024,768]{1,0:T(8,128)(2,1)S(1)} %bitcast.31, s32[1,1024]{1,0:T(1,128)S(1)} %squeeze.23.codes), custom_call_target="tpu_custom_call" | custom-call | flops 1610612736 | bytes 4194304 | tf_op jit(solution)/shard_map/insert/pallas_call | solution.py:214
  132.0 2.0 collective-permute-start.4
  135.4 1.8 broadcast_select_fusion.1
  137.2 5.3 %collective-permute-start.6 = (bf16[256,768]{1,0:T(8,128)(2,1)}, bf16[256,768]{1,0:T(8,128)(2,1)}, u32[]{:S(2)}, u32[]{:S(2)}) collective-permute-start(bf16[256,768]{1,0:T(8,128)(2,1)} %broadcast_select_fusion.1), channel_id=1, source_target_pairs={{0,1},{3,2},{4,5},{7,6},{8,9},{11,10},{12,13},{15,14},{16,17},{19,... | collective-permute-start | bytes 1179656 | tf_op jit(solution)/shard_map/ppermute | solution.py:114
  142.5 1.8 insert.5
  147.0 3.2 %insert.3 = (bf16[256,768]{1,0:T(8,128)(2,1)S(1)}, bf16[256,768]{1,0:T(8,128)(2,1)S(1)}, bf16[256,768]{1,0:T(8,128)(2,1)S(1)}, bf16[256,768]{1,0:T(8,128)(2,1)S(1)}) custom-call(bf16[1024,768]{1,0:T(8,128)(2,1)} %bitcast.4.received, s32[1,1024]{1,0:T(1,128)S(1)} %squeeze.21.codes), custom_call_target="tpu_custom_call" | custom-call | flops 1610612736 | bytes 4194304 | tf_op jit(solution)/shard_map/insert/pallas_call | solution.py:214
  151.5 4.4 %collective-permute-start.2 = (bf16[256,768]{1,0:T(8,128)(2,1)S(1)}, bf16[256,768]{1,0:T(8,128)(2,1)S(1)}, u32[]{:S(2)}, u32[]{:S(2)}) collective-permute-start(bf16[256,768]{1,0:T(8,128)(2,1)S(1)} %broadcast_select_fusion.2), channel_id=1, source_target_pairs={{0,1},{3,2},{4,5},{7,6},{8,9},{11,10},{12,13},{15,14},{16,17},{19,... | collective-permute-start | bytes 1179656 | tf_op jit(solution)/shard_map/ppermute | solution.py:114
  157.0 11.2 %collective-permute-done.10 = bf16[256,768]{1,0:T(8,128)(2,1)S(1)} collective-permute-done((bf16[256,768]{1,0:T(8,128)(2,1)S(1)}, bf16[256,768]{1,0:T(8,128)(2,1)S(1)}, u32[]{:S(2)}, u32[]{:S(2)}) %collective-permute-start.10) | collective-permute-done | bytes 393248 | tf_op jit(solution)/shard_map/ppermute | solution.py:114
  169.7 7.0 %collective-permute-done.2 = bf16[256,768]{1,0:T(8,128)(2,1)S(1)} collective-permute-done((bf16[256,768]{1,0:T(8,128)(2,1)S(1)}, bf16[256,768]{1,0:T(8,128)(2,1)S(1)}, u32[]{:S(2)}, u32[]{:S(2)}) %collective-permute-start.2) | collective-permute-done | bytes 393248 | tf_op jit(solution)/shard_map/ppermute | solution.py:114
  176.8 4.4 %collective-permute-start = (bf16[256,768]{1,0:T(8,128)(2,1)S(1)}, bf16[256,768]{1,0:T(8,128)(2,1)S(1)}, u32[]{:S(2)}, u32[]{:S(2)}) collective-permute-start(bf16[256,768]{1,0:T(8,128)(2,1)S(1)} %get-tuple-element.18), channel_id=1, source_target_pairs={{0,1},{1,2},{2,3},{4,5},{5,6},{6,7},{8,9},{9,10},{10,11},{12,13},{... | collective-permute-start | bytes 1179656 | tf_op jit(solution)/shard_map/ppermute | solution.py:115
  182.6 8.2 %collective-permute-done.7 = bf16[256,768]{1,0:T(8,128)(2,1)S(1)} collective-permute-done((bf16[256,768]{1,0:T(8,128)(2,1)S(1)}, bf16[256,768]{1,0:T(8,128)(2,1)S(1)}, u32[]{:S(2)}, u32[]{:S(2)}) %collective-permute-start.7) | collective-permute-done | bytes 393248 | tf_op jit(solution)/shard_map/ppermute | solution.py:118
  192.1 31.3 %collective-permute-done.11 = bf16[256,768]{1,0:T(8,128)(2,1)S(1)} collective-permute-done((bf16[256,768]{1,0:T(8,128)(2,1)S(1)}, bf16[256,768]{1,0:T(8,128)(2,1)S(1)}, u32[]{:S(2)}, u32[]{:S(2)}) %collective-permute-start.11) | collective-permute-done | bytes 393248 | tf_op jit(solution)/shard_map/ppermute | solution.py:118
  223.6 15.1 %collective-permute-done.3 = bf16[256,768]{1,0:T(8,128)(2,1)S(1)} collective-permute-done((bf16[256,768]{1,0:T(8,128)(2,1)S(1)}, bf16[256,768]{1,0:T(8,128)(2,1)S(1)}, u32[]{:S(2)}, u32[]{:S(2)}) %collective-permute-start.3) | collective-permute-done | bytes 393248 | tf_op jit(solution)/shard_map/ppermute | solution.py:118
  (117 shorter events, 38.9 us)
Async XLA Ops:
  10.0 5.3 %copy-start.24 = (s32[8,4]{0,1:T(4,128)S(1)}, s32[8,4]{0,1:T(4,128)}, u32[]{:S(2)}) copy-start(s32[8,4]{0,1:T(4,128)} %param.17) | copy-start | bytes 388
  10.0 5.6 %copy-start.25 = (s32[8]{0:T(128)S(1)}, s32[8]{0:T(128)}, u32[]{:S(2)}) copy-start(s32[8]{0:T(128)} %param.13) | copy-start | bytes 100
  10.0 5.7 %copy-start.26 = (s32[8]{0:T(128)S(1)}, s32[8]{0:T(128)}, u32[]{:S(2)}) copy-start(s32[8]{0:T(128)} %param.15) | copy-start | bytes 100
  10.0 77.2 %copy-start.8 = (bf16[768,768]{1,0:T(8,128)(2,1)S(1)}, bf16[768,768]{1,0:T(8,128)(2,1)}, u32[]{:S(2)}) copy-start(bf16[768,768]{1,0:T(8,128)(2,1)} %constant.141.clone.right) | copy-start | bytes 3538948
  10.1 77.2 %copy-start.11 = (bf16[256,384]{1,0:T(8,128)(2,1)S(1)}, bf16[256,384]{1,0:T(8,128)(2,1)}, u32[]{:S(2)}) copy-start(bf16[256,384]{1,0:T(8,128)(2,1)} %constant.144.clone.left) | copy-start | bytes 589828
  10.1 82.7 %all-to-all-start.1 = ((bf16[8,8,16,768]{3,2,1,0:T(8,128)(2,1)}), bf16[8,8,16,768]{3,2,1,0:T(8,128)(2,1)S(1)}, u32[]{:S(2)}, u32[]{:S(2)}) async-start(bf16[8,8,16,768]{3,2,1,0:T(8,128)(2,1)} %spectrum.4), calls=%async_computation.1 | async-start | bytes 3145728 | tf_op jit(solution)/shard_map/all_to_all | solution.py:172
  92.8 10.6 %copy-start.10 = (bf16[256,384]{1,0:T(8,128)(2,1)S(1)}, bf16[256,384]{1,0:T(8,128)(2,1)}, u32[]{:S(2)}) copy-start(bf16[256,384]{1,0:T(8,128)(2,1)} %constant.142.clone.left) | copy-start | bytes 589828
  92.8 24.7 %all-to-all-start.2 = ((bf16[8,8,16,768]{3,2,1,0:T(8,128)(2,1)}), bf16[8,8,16,768]{3,2,1,0:T(8,128)(2,1)S(1)}, u32[]{:S(2)}, u32[]{:S(2)}) async-start(bf16[8,8,16,768]{3,2,1,0:T(8,128)(2,1)} %copy-done.1), calls=%async_computation.2 | async-start | bytes 3145728 | tf_op jit(solution)/shard_map/all_to_all | solution.py:172
  106.3 4.7 %copy-start.18 = (f32[48,16]{1,0:T(8,128)S(1)}, f32[48,16]{1,0:T(8,128)}, u32[]{:S(2)}) copy-start(f32[48,16]{1,0:T(8,128)} %copy.35) | copy-start | bytes 9220
  117.4 29.6 %all-to-all-start = ((bf16[8,8,16,768]{3,2,1,0:T(8,128)(2,1)}), bf16[8,8,16,768]{3,2,1,0:T(8,128)(2,1)}, u32[]{:S(2)}, u32[]{:S(2)}) async-start(bf16[8,8,16,768]{3,2,1,0:T(8,128)(2,1)} %copy-done), calls=%async_computation | async-start | bytes 3145728 | tf_op jit(solution)/shard_map/all_to_all | solution.py:172
  132.0 12.3 %copy-start.2 = (bf16[256,768]{1,0:T(8,128)(2,1)}, bf16[256,768]{1,0:T(8,128)(2,1)S(1)}, u32[]{:S(2)}) copy-start(bf16[256,768]{1,0:T(8,128)(2,1)S(1)} %get-tuple-element.24) | copy-start | bytes 1179652
  132.0 36.4 %collective-permute-start.4 = (bf16[256,768]{1,0:T(8,128)(2,1)}, bf16[256,768]{1,0:T(8,128)(2,1)}, u32[]{:S(2)}, u32[]{:S(2)}) collective-permute-start(bf16[256,768]{1,0:T(8,128)(2,1)} %get-tuple-element.22), channel_id=1, source_target_pairs={{0,1},{1,2},{2,3},{4,5},{5,6},{6,7},{8,9},{9,10},{10,11},{12,13},{... | collective-permute-start | bytes 1179656 | tf_op jit(solution)/shard_map/ppermute | solution.py:115
  134.1 42.7 %collective-permute-start.5 = (bf16[256,768]{1,0:T(8,128)(2,1)}, bf16[256,768]{1,0:T(8,128)(2,1)}, u32[]{:S(2)}, u32[]{:S(2)}) collective-permute-start(bf16[256,768]{1,0:T(8,128)(2,1)} %get-tuple-element.23), channel_id=1, source_target_pairs={{1,0},{2,1},{3,2},{5,4},{6,5},{7,6},{9,8},{10,9},{11,10},{13,12},{... | collective-permute-start | bytes 1179656 | tf_op jit(solution)/shard_map/ppermute | solution.py:116
  137.2 14.4 %collective-permute-start.6 = (bf16[256,768]{1,0:T(8,128)(2,1)}, bf16[256,768]{1,0:T(8,128)(2,1)}, u32[]{:S(2)}, u32[]{:S(2)}) collective-permute-start(bf16[256,768]{1,0:T(8,128)(2,1)} %broadcast_select_fusion.1), channel_id=1, source_target_pairs={{0,1},{3,2},{4,5},{7,6},{8,9},{11,10},{12,13},{15,14},{16,17},{19,... | collective-permute-start | bytes 1179656 | tf_op jit(solution)/shard_map/ppermute | solution.py:114
  144.3 36.9 %collective-permute-start.8 = (bf16[256,768]{1,0:T(8,128)(2,1)S(1)}, bf16[256,768]{1,0:T(8,128)(2,1)S(1)}, u32[]{:S(2)}, u32[]{:S(2)}) collective-permute-start(bf16[256,768]{1,0:T(8,128)(2,1)S(1)} %get-tuple-element.26), channel_id=1, source_target_pairs={{0,1},{1,2},{2,3},{4,5},{5,6},{6,7},{8,9},{9,10},{10,11},{12,13},{... | collective-permute-start | bytes 1179656 | tf_op jit(solution)/shard_map/ppermute | solution.py:115
  145.7 22.6 %collective-permute-start.10 = (bf16[256,768]{1,0:T(8,128)(2,1)S(1)}, bf16[256,768]{1,0:T(8,128)(2,1)S(1)}, u32[]{:S(2)}, u32[]{:S(2)}) collective-permute-start(bf16[256,768]{1,0:T(8,128)(2,1)S(1)} %broadcast_select_fusion), channel_id=1, source_target_pairs={{0,1},{3,2},{4,5},{7,6},{8,9},{11,10},{12,13},{15,14},{16,17},{19,... | collective-permute-start | bytes 1179656 | tf_op jit(solution)/shard_map/ppermute | solution.py:114
  150.2 5.7 %copy-start.3 = (bf16[256,768]{1,0:T(8,128)(2,1)S(1)}, bf16[256,768]{1,0:T(8,128)(2,1)}, u32[]{:S(2)}) copy-start(bf16[256,768]{1,0:T(8,128)(2,1)} %copy-done.2) | copy-start | bytes 1179652
  151.5 25.2 %collective-permute-start.2 = (bf16[256,768]{1,0:T(8,128)(2,1)S(1)}, bf16[256,768]{1,0:T(8,128)(2,1)S(1)}, u32[]{:S(2)}, u32[]{:S(2)}) collective-permute-start(bf16[256,768]{1,0:T(8,128)(2,1)S(1)} %broadcast_select_fusion.2), channel_id=1, source_target_pairs={{0,1},{3,2},{4,5},{7,6},{8,9},{11,10},{12,13},{15,14},{16,17},{19,... | collective-permute-start | bytes 1179656 | tf_op jit(solution)/shard_map/ppermute | solution.py:114
  168.3 22.5 %collective-permute-start.7 = (bf16[256,768]{1,0:T(8,128)(2,1)S(1)}, bf16[256,768]{1,0:T(8,128)(2,1)S(1)}, u32[]{:S(2)}, u32[]{:S(2)}) collective-permute-start(bf16[256,768]{1,0:T(8,128)(2,1)S(1)} %add_convert_fusion.1), channel_id=1, source_target_pairs={{0,2},{1,3},{2,0},{3,1},{4,6},{5,7},{6,4},{7,5},{8,10},{9,11},{10,... | collective-permute-start | bytes 1179656 | tf_op jit(solution)/shard_map/ppermute | solution.py:118
  168.4 23.7 %collective-permute-start.9 = (bf16[256,768]{1,0:T(8,128)(2,1)S(1)}, bf16[256,768]{1,0:T(8,128)(2,1)S(1)}, u32[]{:S(2)}, u32[]{:S(2)}) collective-permute-start(bf16[256,768]{1,0:T(8,128)(2,1)S(1)} %get-tuple-element.27), channel_id=1, source_target_pairs={{1,0},{2,1},{3,2},{5,4},{6,5},{7,6},{9,8},{10,9},{11,10},{13,12},{... | collective-permute-start | bytes 1179656 | tf_op jit(solution)/shard_map/ppermute | solution.py:116
  176.7 46.7 %collective-permute-start.11 = (bf16[256,768]{1,0:T(8,128)(2,1)S(1)}, bf16[256,768]{1,0:T(8,128)(2,1)S(1)}, u32[]{:S(2)}, u32[]{:S(2)}) collective-permute-start(bf16[256,768]{1,0:T(8,128)(2,1)S(1)} %add_convert_fusion), channel_id=1, source_target_pairs={{0,2},{1,3},{2,0},{3,1},{4,6},{5,7},{6,4},{7,5},{8,10},{9,11},{10,... | collective-permute-start | bytes 1179656 | tf_op jit(solution)/shard_map/ppermute | solution.py:118
  176.8 46.7 %collective-permute-start = (bf16[256,768]{1,0:T(8,128)(2,1)S(1)}, bf16[256,768]{1,0:T(8,128)(2,1)S(1)}, u32[]{:S(2)}, u32[]{:S(2)}) collective-permute-start(bf16[256,768]{1,0:T(8,128)(2,1)S(1)} %get-tuple-element.18), channel_id=1, source_target_pairs={{0,1},{1,2},{2,3},{4,5},{5,6},{6,7},{8,9},{9,10},{10,11},{12,13},{... | collective-permute-start | bytes 1179656 | tf_op jit(solution)/shard_map/ppermute | solution.py:115
  181.3 42.3 %collective-permute-start.1 = (bf16[256,768]{1,0:T(8,128)(2,1)S(1)}, bf16[256,768]{1,0:T(8,128)(2,1)S(1)}, u32[]{:S(2)}, u32[]{:S(2)}) collective-permute-start(bf16[256,768]{1,0:T(8,128)(2,1)S(1)} %get-tuple-element.19), channel_id=1, source_target_pairs={{1,0},{2,1},{3,2},{5,4},{6,5},{7,6},{9,8},{10,9},{11,10},{13,12},{... | collective-permute-start | bytes 1179656 | tf_op jit(solution)/shard_map/ppermute | solution.py:116
  190.8 47.9 %collective-permute-start.3 = (bf16[256,768]{1,0:T(8,128)(2,1)S(1)}, bf16[256,768]{1,0:T(8,128)(2,1)S(1)}, u32[]{:S(2)}, u32[]{:S(2)}) collective-permute-start(bf16[256,768]{1,0:T(8,128)(2,1)S(1)} %add_convert_fusion.2), channel_id=1, source_target_pairs={{0,2},{1,3},{2,0},{3,1},{4,6},{5,7},{6,4},{7,5},{8,10},{9,11},{10,... | collective-permute-start | bytes 1179656 | tf_op jit(solution)/shard_map/ppermute | solution.py:118
  (18 other events, 42.9 us)

commit v2 on v1

--- a/solution.py
+++ b/solution.py
@@ -103,21 +103,31 @@
     )
 
 
-def slab_sums(parts, slab, slab_count):
-    if slab_count != 4:
-        merged = jnp.stack(parts)
-        order = (jnp.arange(slab_count) - slab) % slab_count
-        return lax.psum_scatter(
-            jnp.take(merged, order, axis=0), "slab", scatter_dimension=0, tiled=False
-        ).astype(jnp.float32)
-    edge = jnp.where(slab == 0, parts[3], parts[1])
-    edge_in = lax.ppermute(edge, "slab", [(0, 1), (3, 2)])
-    right_in = lax.ppermute(parts[1], "slab", [(0, 1), (1, 2), (2, 3)])
-    left_in = lax.ppermute(parts[3], "slab", [(1, 0), (2, 1), (3, 2)])
-    far = (parts[2].astype(jnp.float32) + edge_in.astype(jnp.float32)).astype(jnp.bfloat16)
-    far_in = lax.ppermute(far, "slab", [(0, 2), (1, 3), (2, 0), (3, 1)])
-    total = parts[0].astype(jnp.float32) + right_in.astype(jnp.float32)
-    return total + left_in.astype(jnp.float32) + far_in.astype(jnp.float32)
+def slab_sums(parts, place, slab_count, mirror_count):
+    def permute(block, pairs):
+        perm = []
+        for b in range(2 * mirror_count):
+            for source, target in pairs:
+                if b >= mirror_count:
+                    source, target = slab_count - 1 - source, slab_count - 1 - target
+                perm.append((b * slab_count + source, b * slab_count + target))
+        return lax.ppermute(block, ("batch", "slab"), perm)
+
+    near_in = permute(jnp.where(place == 2, parts[1], parts[0]), [(3, 2), (2, 1), (1, 0)])
+    out_in = permute(jnp.where(place == 0, parts[1], parts[2]), [(0, 1), (1, 2)])
+    last_in = permute(parts[2], [(3, 2)])
+    merged = (parts[0].astype(jnp.float32) + near_in.astype(jnp.float32)).astype(jnp.bfloat16)
+    far = jnp.where(place == 0, parts[2], jnp.where(place == 3, parts[1], merged))
+
+    def finish(far):
+        far_in = permute(far, [(3, 1), (2, 0), (0, 2)])
+        own = jnp.where(place == 0, parts[0], jnp.where(place == 1, parts[1], parts[2]))
+        total = jnp.where(place == 3, 0.0, own.astype(jnp.float32))
+        total = total + jnp.where(place == 2, 0.0, near_in.astype(jnp.float32))
+        total = total + out_in.astype(jnp.float32) + last_in.astype(jnp.float32)
+        return total + far_in.astype(jnp.float32)
+
+    return far, finish
 
 
 def per_device(images, classes, shifts, defocus_class, defocus, run_counts, dest_map, ref):
@@ -133,7 +143,6 @@
 
     ends = jnp.cumsum(run_counts, axis=1)
     meta = jnp.concatenate([classes[:, None], defocus_class[:, None], ends], axis=1)
-    meta_all = lax.all_gather(meta, ("batch", "slab"), axis=0, tiled=True)
 
     cosine, minus_sine, table_right = dft_tables(length)
     order = np.arange(length).reshape(batch_count, CHUNKS, each).transpose(1, 0, 2)
@@ -170,26 +179,43 @@
             col_factors,
         )
         received.append(lax.all_to_all(weighted, "batch", 0, 0, tiled=True))
+        if c == 0:
+            meta_layer = lax.all_to_all(
+                jnp.broadcast_to(meta[None], (batch_count, *meta.shape)), "batch", 0, 0, tiled=True
+            )
+            meta_all = lax.all_to_all(
+                jnp.broadcast_to(meta_layer[None], (slab_count, *meta_layer.shape)),
+                "slab",
+                0,
+                0,
+                tiled=True,
+            )
+            meta_layer = meta_layer.reshape(-1, meta.shape[1])
+            meta_all = meta_all.reshape(-1, meta.shape[1])
 
     class_count = dest_map.shape[0]
     own_dest = lax.dynamic_slice_in_dim(dest_map, batch * rows, rows, 1).astype(jnp.bfloat16)
-    class_hot = (meta_all[:, :1] == jnp.arange(class_count)[None, :]).astype(jnp.bfloat16)
-    local_plane = jnp.dot(class_hot, own_dest, preferred_element_type=jnp.float32)
-    local_plane = local_plane.astype(jnp.int32)
     own_freq = batch * rows + jnp.arange(rows, dtype=jnp.int32)
-    owner = jnp.sum(
-        (own_freq[None, :, None] >= meta_all[:, None, 2:]).astype(jnp.int32), axis=2
-    )
-
-    grouped = (batch_count, slab_count, particles, rows)
-    relative = (owner - slab) % slab_count
-    local_bin = relative * (each * planes) + (jnp.arange(rows) % each)[None, :] * planes
-    codes = lax.dynamic_index_in_dim(
-        (local_bin + local_plane).reshape(grouped), slab, 1, keepdims=False
-    )
+
+    def find_planes(table):
+        class_hot = (table[:, :1] == jnp.arange(class_count)[None, :]).astype(jnp.bfloat16)
+        local_plane = jnp.dot(class_hot, own_dest, preferred_element_type=jnp.float32)
+        past = own_freq[None, :, None] >= table[:, None, 2:]
+        return jnp.sum(past.astype(jnp.int32), axis=2), local_plane.astype(jnp.int32)
+
+    mirrored = slab_count == 4 and batch_count % 2 == 0
+    window_slabs = 3 if mirrored else slab_count
+    owner, local_plane = find_planes(meta_layer)
+    place = slab
+    if mirrored:
+        upper = batch >= batch_count // 2
+        owner = jnp.where(upper, slab_count - 1 - owner, owner)
+        place = jnp.where(upper, slab_count - 1 - slab, slab)
+    codes = owner * (each * planes) + (jnp.arange(rows) % each)[None, :] * planes + local_plane
     codes = codes.reshape(batch_count * particles, CHUNKS, each).transpose(1, 0, 2)
     codes = codes.reshape(CHUNKS, 1, batch_count * particles * each)
 
+    owner, local_plane = find_planes(meta_all)
     focus_count = defocus.shape[0]
     focus_hot = (meta_all[:, 1:2] == jnp.arange(focus_count)[None, :]).astype(jnp.bfloat16)
     own_plane = jnp.where(owner == slab, local_plane, -1)
@@ -208,29 +234,43 @@
     denom = weights + TAU_PRIOR
 
     bins = each * planes
-    updated = []
+    sums = []
+    far = None
     for c in range(CHUNKS):
         rows_in = received[c].reshape(batch_count * particles * each, 2 * length)
+        codes_in = codes[c]
+        if far is not None:
+            codes_in, far = lax.optimization_barrier((codes_in, far))
+            sums.append(finish(far))
         parts = pl.pallas_call(
             insert_kernel,
-            out_shape=[jax.ShapeDtypeStruct((bins, 2 * length), jnp.bfloat16)] * slab_count,
+            out_shape=[jax.ShapeDtypeStruct((bins, 2 * length), jnp.bfloat16)] * window_slabs,
             in_specs=whole_vmem(2),
-            out_specs=whole_vmem(slab_count),
+            out_specs=whole_vmem(window_slabs),
             compiler_params=pltpu.CompilerParams(vmem_limit_bytes=VMEM_LIMIT),
             cost_estimate=pl.CostEstimate(
-                flops=2 * bins * slab_count * rows_in.shape[0] * 2 * length,
+                flops=2 * bins * window_slabs * rows_in.shape[0] * 2 * length,
                 bytes_accessed=4 * 1024 * 1024,
                 transcendentals=0,
             ),
             name="insert",
-        )(rows_in, codes[c])
-        sums = slab_sums(parts, slab, slab_count).reshape(each, planes, 2 * length)
+        )(rows_in, codes_in)
+        if mirrored:
+            far, finish = slab_sums(parts, place, slab_count, batch_count // 2)
+        else:
+            windows = jnp.stack(parts)
+            sums.append(lax.psum_scatter(windows, "slab", scatter_dimension=0, tiled=False))
+    if far is not None:
+        sums.append(finish(far))
+    updated = []
+    for c in range(CHUNKS):
         here = slice(c * each, (c + 1) * each)
         prior = ref[here].astype(jnp.float32)
         under = denom[here]
+        total = sums[c].astype(jnp.float32).reshape(each, planes, 2 * length)
         updated.append(
             (
-                (TAU_PRIOR * prior + sums) / jnp.concatenate([under, under], axis=2)
+                (TAU_PRIOR * prior + total) / jnp.concatenate([under, under], axis=2)
             ).astype(jnp.bfloat16)
         )
     return jnp.concatenate(updated, axis=0)

time: 243 us -> 168 us (0.69)
  blocking collectives: 70.3 us -> 0 us
  starting transfers between devices: 36.2 us -> 46.4 us
  waiting for transfers between devices: 79 us -> 69.7 us
  local copies, waits for them, and re-layouts: 21.8 us -> 13.2 us
  other arithmetic: 11.5 us -> 14.7 us
    all_gather x1 -> x0, blocking collectives: 70.3 us -> none  [per_device(): meta_all = lax.all_gather(meta, ('batch', 'slab'), axis=0, tiled=True)]
    ppermute x12, waiting for transfers between devices: 74.2 us -> 45.4 us  [permute(): return lax.ppermute(block, ('batch', 'slab'), perm)]
    all_to_all x3, waiting for transfers between devices: 4.83 us -> 23.8 us  [per_device(): received.append(lax.all_to_all(weighted, 'batch', 0, 0, tiled=True))]
    all_to_all x0 -> x2, starting transfers between devices: none -> 10 us  [the longest x1 5.17 us: per_device(): lax.all_to_all(jnp.broadcast_to(meta[None], (batch_count, *meta.shape)),...]
    unnamed x55 -> x77, local copies, waits for them, and re-layouts: 10.7 us -> 8.63 us
  transfers between devices with their start and end apart: 15 -> 17, of which waited for: 7 -> 9; matrix products, arithmetic and copies ran while one was open for 10% -> 13% of each run, Pallas kernels for 5% -> 10%
where the time goes in v2:
time: 168 us; the launch traced here: 167 us
  waiting for transfers between devices  69.7 us (41%)
  starting transfers between devices  46.4 us (28%)
  Pallas kernels  15.8 us (9%)
  other arithmetic  14.7 us (9%)
  local copies, waits for them, and re-layouts  13.2 us (8%)
  matrix products  6.02 us (4%)
    ppermute x12, waiting for transfers between devices, permute(): return lax.ppermute(block, ('batch', 'slab'), perm)  45.4 us
    ppermute x12, starting transfers between devices, permute(): return lax.ppermute(block, ('batch', 'slab'), perm)  24.6 us
    all_to_all x3, waiting for transfers between devices, per_device(): received.append(lax.all_to_all(weighted, 'batch', 0, 0, tiled=True))  23.8 us
    all_to_all x3, starting transfers between devices, per_device(): received.append(lax.all_to_all(weighted, 'batch', 0, 0, tiled=True))  11.7 us
    pallas_call x3, Pallas kernels, per_device(): pl.pallas_call(spectrum_kernel, out_shape=jax.ShapeDtypeStruct((batch_cou...  10.3 us
    unnamed x77, local copies, waits for them, and re-layouts  8.63 us
    pallas_call x3, Pallas kernels, per_device(): pl.pallas_call(insert_kernel, out_shape=[jax.ShapeDtypeStruct((bins, 2 *...  5.56 us
    all_to_all x1, starting transfers between devices, per_device(): lax.all_to_all(jnp.broadcast_to(meta[None], (batch_count, *meta.shape)),...  5.17 us
  transfers between devices with their start and end apart: 17, of which 9 were waited for; matrix products, arithmetic and copies ran while one was open for 13% of the time, Pallas kernels for 10%

profile of v2, /device:TPU:0, one launch (start us, length us, event | category | flops | bytes accessed | tf_op | source)
XLA Modules:
  0.0 166.5 jit_solution(15492965211528173955)
XLA Ops:
  2.0 5.2 %all-to-all-start.1 = ((s32[8,8,6]{1,2,0:T(8,128)}), s32[8,8,6]{1,2,0:T(8,128)S(1)}, u32[]{:S(2)}, u32[]{:S(2)}) async-start(s32[8,8,6]{1,2,0:T(8,128)} %broadcast_in_dim.37), calls=%async_computation.1 | async-start | bytes 65536 | tf_op jit(solution)/shard_map/all_to_all | solution.py:183
  12.8 4.9 %all-to-all-start.2 = ((s32[4,1,384]{2,1,0:T(1,128)}), s32[4,1,384]{2,1,0:T(1,128)S(1)}, u32[]{:S(2)}, u32[]{:S(2)}) async-start(s32[4,1,384]{2,1,0:T(1,128)} %reshape.240), calls=%async_computation.2 | async-start | bytes 12288 | tf_op jit(solution)/shard_map/all_to_all | solution.py:186
  17.6 1.7 copy-done.8
  19.3 3.8 %spectrum.3 = bf16[8,8,16,768]{3,2,1,0:T(8,128)(2,1)} custom-call(bf16[8,384,384]{2,1,0:T(8,128)(2,1)S(1)} %copy-done.8, bf16[256,384]{1,0:T(8,128)(2,1)S(1)} %copy-done.15, bf16[768,768]{1,0:T(8,128)(2,1)S(1)} %copy-done.11, f32[128,32]{1,0:T(8,128)S(1)} %bitcast.46, f32[32,384]{1,0:T(8,128)S(1)} %pad_maximum_fusion.1.col_factors), custom_call_target="tpu_custom_call" | custom-call | flops 1811939328 | bytes 6291456 | tf_op jit(solution)/shard_map/spectrum/pallas_call | solution.py:159
  23.8 3.8 %all-to-all-start = ((bf16[8,8,16,768]{3,2,1,0:T(8,128)(2,1)}), bf16[8,8,16,768]{3,2,1,0:T(8,128)(2,1)S(1)}, u32[]{:S(2)}, u32[]{:S(2)}) async-start(bf16[8,8,16,768]{3,2,1,0:T(8,128)(2,1)} %spectrum.3), calls=%async_computation | async-start | bytes 3145728 | tf_op jit(solution)/shard_map/all_to_all | solution.py:181
  27.7 1.7 copy-done.9
  29.4 3.8 %spectrum.4 = bf16[8,8,16,768]{3,2,1,0:T(8,128)(2,1)} custom-call(bf16[8,384,384]{2,1,0:T(8,128)(2,1)S(1)} %copy-done.9, bf16[256,384]{1,0:T(8,128)(2,1)S(1)} %copy-done.14, bf16[768,768]{1,0:T(8,128)(2,1)S(1)} %copy-done.11, f32[128,32]{1,0:T(8,128)S(1)} %bitcast.45, f32[32,384]{1,0:T(8,128)S(1)} %pad_maximum_fusion.1.col_factors), custom_call_target="tpu_custom_call" | custom-call | flops 1811939328 | bytes 6291456 | tf_op jit(solution)/shard_map/spectrum/pallas_call | solution.py:159
  34.2 14.5 %all-to-all-done = bf16[8,8,16,768]{3,2,1,0:T(8,128)(2,1)S(1)} async-done(((bf16[8,8,16,768]{3,2,1,0:T(8,128)(2,1)}), bf16[8,8,16,768]{3,2,1,0:T(8,128)(2,1)S(1)}, u32[]{:S(2)}, u32[]{:S(2)}) %all-to-all-start) | async-done | bytes 1572896 | tf_op jit(solution)/shard_map/all_to_all | solution.py:181
  49.9 3.6 %all-to-all-start.3 = ((bf16[8,8,16,768]{3,2,1,0:T(8,128)(2,1)}), bf16[8,8,16,768]{3,2,1,0:T(8,128)(2,1)S(1)}, u32[]{:S(2)}, u32[]{:S(2)}) async-start(bf16[8,8,16,768]{3,2,1,0:T(8,128)(2,1)} %spectrum.4), calls=%async_computation.3 | async-start | bytes 3145728 | tf_op jit(solution)/shard_map/all_to_all | solution.py:181
  60.4 2.6 %spectrum.5 = bf16[8,8,16,768]{3,2,1,0:T(8,128)(2,1)S(1)} custom-call(bf16[8,384,384]{2,1,0:T(8,128)(2,1)S(1)} %copy-done.10, bf16[256,384]{1,0:T(8,128)(2,1)S(1)} %copy-done.13, bf16[768,768]{1,0:T(8,128)(2,1)S(1)} %copy-done.12, f32[128,32]{1,0:T(8,128)S(1)} %bitcast.44, f32[32,384]{1,0:T(8,128)S(1)} %copy-done.7), custom_call_target="tpu_custom_call" | custom-call | flops 1811939328 | bytes 6291456 | tf_op jit(solution)/shard_map/spectrum/pallas_call | solution.py:159
  68.7 5.7 %all-to-all-done.3 = bf16[8,8,16,768]{3,2,1,0:T(8,128)(2,1)S(1)} async-done(((bf16[8,8,16,768]{3,2,1,0:T(8,128)(2,1)}), bf16[8,8,16,768]{3,2,1,0:T(8,128)(2,1)S(1)}, u32[]{:S(2)}, u32[]{:S(2)}) %all-to-all-start.3) | async-done | bytes 1572896 | tf_op jit(solution)/shard_map/all_to_all | solution.py:181
  74.4 4.3 %all-to-all-start.4 = ((bf16[8,8,16,768]{3,2,1,0:T(8,128)(2,1)}), bf16[8,8,16,768]{3,2,1,0:T(8,128)(2,1)}, u32[]{:S(2)}, u32[]{:S(2)}) async-start(bf16[8,8,16,768]{3,2,1,0:T(8,128)(2,1)} %copy-done), calls=%async_computation.4 | async-start | bytes 3145728 | tf_op jit(solution)/shard_map/all_to_all | solution.py:181
  82.8 1.6 fusion.2
  84.4 1.8 %broadcast_multiply_fusion.1 = (f32[48,16,16]{2,1,0:T(8,128)}, f32[48,16,16]{2,1,0:T(8,128)}, f32[48,16]{1,0:T(8,128)}) fusion(f32[48,16]{1,0:T(8,128)S(1)} %copy-done.31, f32[48,16]{1,0:T(8,128)S(1)} %copy-done.32, s32[256]{0:T(256)S(1)} %bitcast.54, s32[48,256]{1,0:T(8,128)S(1)} %fusion.2), kind=kOutput, calls=%fused_computation.61 | convolution fusion | flops 6528256 | bytes 157696 | tf_op jit(solution)/shard_map/kzp,pd->kzd/dot_general | solution.py:223
  87.6 7.4 %collective-permute-done.4 = bf16[256,768]{1,0:T(8,128)(2,1)S(1)} collective-permute-done((bf16[256,768]{1,0:T(8,128)(2,1)S(1)}, bf16[256,768]{1,0:T(8,128)(2,1)S(1)}, u32[]{:S(2)}, u32[]{:S(2)}) %collective-permute-start.4) | collective-permute-done | bytes 393248 | tf_op jit(solution)/shard_map/ppermute | solution.py:114
  96.1 3.6 %all-to-all-done.4 = bf16[8,8,16,768]{3,2,1,0:T(8,128)(2,1)} async-done(((bf16[8,8,16,768]{3,2,1,0:T(8,128)(2,1)}), bf16[8,8,16,768]{3,2,1,0:T(8,128)(2,1)}, u32[]{:S(2)}, u32[]{:S(2)}) %all-to-all-start.4) | async-done | bytes 1572896 | tf_op jit(solution)/shard_map/all_to_all | solution.py:181
  99.7 2.8 %insert.5 = (bf16[256,768]{1,0:T(8,128)(2,1)S(1)}, bf16[256,768]{1,0:T(8,128)(2,1)S(1)}, bf16[256,768]{1,0:T(8,128)(2,1)S(1)}) custom-call(bf16[1024,768]{1,0:T(8,128)(2,1)} %bitcast.20.received, s32[1,1024]{1,0:T(1,128)S(1)} %squeeze.22.codes), custom_call_target="tpu_custom_call" | custom-call | flops 1207959552 | bytes 4194304 | tf_op jit(solution)/shard_map/insert/pallas_call | solution.py:245
  106.0 6.5 %collective-permute-start.3 = (bf16[256,768]{1,0:T(8,128)(2,1)S(1)}, bf16[256,768]{1,0:T(8,128)(2,1)S(1)}, u32[]{:S(2)}, u32[]{:S(2)}) collective-permute-start(bf16[256,768]{1,0:T(8,128)(2,1)S(1)} %copy-done.24), channel_id=1, source_target_pairs={{3,1},{2,0},{0,2},{7,5},{6,4},{4,6},{11,9},{10,8},{8,10},{15,13},{... | collective-permute-start | bytes 1179656 | tf_op jit(solution)/shard_map/ppermute | solution.py:114
  114.2 1.9 %collective-permute-start.7 = (bf16[256,768]{1,0:T(8,128)(2,1)S(1)}, bf16[256,768]{1,0:T(8,128)(2,1)S(1)}, u32[]{:S(2)}, u32[]{:S(2)}) collective-permute-start(bf16[256,768]{1,0:T(8,128)(2,1)S(1)} %copy-done.26), channel_id=1, source_target_pairs={{3,1},{2,0},{0,2},{7,5},{6,4},{4,6},{11,9},{10,8},{8,10},{15,13},{... | collective-permute-start | bytes 1179656 | tf_op jit(solution)/shard_map/ppermute | solution.py:114
  116.1 4.3 %collective-permute-start.5 = (bf16[256,768]{1,0:T(8,128)(2,1)S(1)}, bf16[256,768]{1,0:T(8,128)(2,1)S(1)}, u32[]{:S(2)}, u32[]{:S(2)}) collective-permute-start(bf16[256,768]{1,0:T(8,128)(2,1)S(1)} %copy-done.25), channel_id=1, source_target_pairs={{0,1},{1,2},{4,5},{5,6},{8,9},{9,10},{12,13},{13,14},{19,18},{18,1... | collective-permute-start | bytes 1179656 | tf_op jit(solution)/shard_map/ppermute | solution.py:114
  121.3 20.7 %collective-permute-done.3 = bf16[256,768]{1,0:T(8,128)(2,1)S(1)} collective-permute-done((bf16[256,768]{1,0:T(8,128)(2,1)S(1)}, bf16[256,768]{1,0:T(8,128)(2,1)S(1)}, u32[]{:S(2)}, u32[]{:S(2)}) %collective-permute-start.3) | collective-permute-done | bytes 393248 | tf_op jit(solution)/shard_map/ppermute | solution.py:114
  142.0 1.9 %collective-permute-start.11 = (bf16[256,768]{1,0:T(8,128)(2,1)S(1)}, bf16[256,768]{1,0:T(8,128)(2,1)S(1)}, u32[]{:S(2)}, u32[]{:S(2)}) collective-permute-start(bf16[256,768]{1,0:T(8,128)(2,1)S(1)} %get-tuple-element.42), channel_id=1, source_target_pairs={{3,1},{2,0},{0,2},{7,5},{6,4},{4,6},{11,9},{10,8},{8,10},{15,13},{... | collective-permute-start | bytes 1179656 | tf_op jit(solution)/shard_map/ppermute | solution.py:114
  146.8 13.2 %collective-permute-done.7 = bf16[256,768]{1,0:T(8,128)(2,1)S(1)} collective-permute-done((bf16[256,768]{1,0:T(8,128)(2,1)S(1)}, bf16[256,768]{1,0:T(8,128)(2,1)S(1)}, u32[]{:S(2)}, u32[]{:S(2)}) %collective-permute-start.7) | collective-permute-done | bytes 393248 | tf_op jit(solution)/shard_map/ppermute | solution.py:114
  160.5 4.1 %collective-permute-done.11 = bf16[256,768]{1,0:T(8,128)(2,1)S(1)} collective-permute-done((bf16[256,768]{1,0:T(8,128)(2,1)S(1)}, bf16[256,768]{1,0:T(8,128)(2,1)S(1)}, u32[]{:S(2)}, u32[]{:S(2)}) %collective-permute-start.11) | collective-permute-done | bytes 393248 | tf_op jit(solution)/shard_map/ppermute | solution.py:114
  (148 shorter events, 40.5 us)
Async XLA Ops:
  2.0 10.0 %all-to-all-start.1 = ((s32[8,8,6]{1,2,0:T(8,128)}), s32[8,8,6]{1,2,0:T(8,128)S(1)}, u32[]{:S(2)}, u32[]{:S(2)}) async-start(s32[8,8,6]{1,2,0:T(8,128)} %broadcast_in_dim.37), calls=%async_computation.1 | async-start | bytes 65536 | tf_op jit(solution)/shard_map/all_to_all | solution.py:183
  9.9 7.7 %copy-start.11 = (bf16[768,768]{1,0:T(8,128)(2,1)S(1)}, bf16[768,768]{1,0:T(8,128)(2,1)}, u32[]{:S(2)}) copy-start(bf16[768,768]{1,0:T(8,128)(2,1)} %constant.132.clone.right) | copy-start | bytes 3538948
  11.7 16.0 %copy-start.6 = (f32[32,384]{1,0:T(8,128)}, f32[32,384]{1,0:T(8,128)S(1)}, u32[]{:S(2)}) copy-start(f32[32,384]{1,0:T(8,128)S(1)} %pad_maximum_fusion.1.col_factors) | copy-start | bytes 147460
  12.8 10.5 %all-to-all-start.2 = ((s32[4,1,384]{2,1,0:T(1,128)}), s32[4,1,384]{2,1,0:T(1,128)S(1)}, u32[]{:S(2)}, u32[]{:S(2)}) async-start(s32[4,1,384]{2,1,0:T(1,128)} %reshape.240), calls=%async_computation.2 | async-start | bytes 12288 | tf_op jit(solution)/shard_map/all_to_all | solution.py:186
  23.8 24.9 %all-to-all-start = ((bf16[8,8,16,768]{3,2,1,0:T(8,128)(2,1)}), bf16[8,8,16,768]{3,2,1,0:T(8,128)(2,1)S(1)}, u32[]{:S(2)}, u32[]{:S(2)}) async-start(bf16[8,8,16,768]{3,2,1,0:T(8,128)(2,1)} %spectrum.3), calls=%async_computation | async-start | bytes 3145728 | tf_op jit(solution)/shard_map/all_to_all | solution.py:181
  27.6 25.8 %copy-start.36 = (s32[48]{0:T(128)}, s32[48]{0:T(128)S(1)}, u32[]{:S(2)}) copy-start(s32[48]{0:T(128)S(1)} %iota_add_fusion) | copy-start | bytes 580
  49.9 24.5 %all-to-all-start.3 = ((bf16[8,8,16,768]{3,2,1,0:T(8,128)(2,1)}), bf16[8,8,16,768]{3,2,1,0:T(8,128)(2,1)S(1)}, u32[]{:S(2)}, u32[]{:S(2)}) async-start(bf16[8,8,16,768]{3,2,1,0:T(8,128)(2,1)} %spectrum.4), calls=%async_computation.3 | async-start | bytes 3145728 | tf_op jit(solution)/shard_map/all_to_all | solution.py:181
  58.9 19.8 %collective-permute-start = (bf16[256,768]{1,0:T(8,128)(2,1)}, bf16[256,768]{1,0:T(8,128)(2,1)S(1)}, u32[]{:S(2)}, u32[]{:S(2)}) collective-permute-start(bf16[256,768]{1,0:T(8,128)(2,1)} %broadcast_select_fusion.2), channel_id=1, source_target_pairs={{3,2},{2,1},{1,0},{7,6},{6,5},{5,4},{11,10},{10,9},{9,8},{15,14},{... | collective-permute-start | bytes 1179656 | tf_op jit(solution)/shard_map/ppermute | solution.py:114
  74.4 25.3 %all-to-all-start.4 = ((bf16[8,8,16,768]{3,2,1,0:T(8,128)(2,1)}), bf16[8,8,16,768]{3,2,1,0:T(8,128)(2,1)}, u32[]{:S(2)}, u32[]{:S(2)}) async-start(bf16[8,8,16,768]{3,2,1,0:T(8,128)(2,1)} %copy-done), calls=%async_computation.4 | async-start | bytes 3145728 | tf_op jit(solution)/shard_map/all_to_all | solution.py:181
  81.2 13.7 %copy-start.3 = (bf16[256,768]{1,0:T(8,128)(2,1)}, bf16[256,768]{1,0:T(8,128)(2,1)S(1)}, u32[]{:S(2)}) copy-start(bf16[256,768]{1,0:T(8,128)(2,1)S(1)} %get-tuple-element.25) | copy-start | bytes 1179652
  81.3 13.6 %collective-permute-start.4 = (bf16[256,768]{1,0:T(8,128)(2,1)S(1)}, bf16[256,768]{1,0:T(8,128)(2,1)S(1)}, u32[]{:S(2)}, u32[]{:S(2)}) collective-permute-start(bf16[256,768]{1,0:T(8,128)(2,1)S(1)} %broadcast_select_fusion.1), channel_id=1, source_target_pairs={{3,2},{2,1},{1,0},{7,6},{6,5},{5,4},{11,10},{10,9},{9,8},{15,14},{... | collective-permute-start | bytes 1179656 | tf_op jit(solution)/shard_map/ppermute | solution.py:114
  86.1 28.0 %collective-permute-start.2 = (bf16[256,768]{1,0:T(8,128)(2,1)S(1)}, bf16[256,768]{1,0:T(8,128)(2,1)}, u32[]{:S(2)}, u32[]{:S(2)}) collective-permute-start(bf16[256,768]{1,0:T(8,128)(2,1)S(1)} %get-tuple-element.20), channel_id=1, source_target_pairs={{3,2},{7,6},{11,10},{15,14},{16,17},{20,21},{24,25},{28,29}} | collective-permute-start | bytes 1179656 | tf_op jit(solution)/shard_map/ppermute | solution.py:114
  102.7 9.9 %copy-start.23 = (bf16[256,768]{1,0:T(8,128)(2,1)S(1)}, bf16[256,768]{1,0:T(8,128)(2,1)}, u32[]{:S(2)}) copy-start(bf16[256,768]{1,0:T(8,128)(2,1)} %get-tuple-element.37) | copy-start | bytes 1179652
  102.7 13.4 %collective-permute-start.8 = (bf16[256,768]{1,0:T(8,128)(2,1)S(1)}, bf16[256,768]{1,0:T(8,128)(2,1)S(1)}, u32[]{:S(2)}, u32[]{:S(2)}) collective-permute-start(bf16[256,768]{1,0:T(8,128)(2,1)S(1)} %broadcast_select_fusion), channel_id=1, source_target_pairs={{3,2},{2,1},{1,0},{7,6},{6,5},{5,4},{11,10},{10,9},{9,8},{15,14},{... | collective-permute-start | bytes 1179656 | tf_op jit(solution)/shard_map/ppermute | solution.py:114
  105.3 15.3 %collective-permute-start.6 = (bf16[256,768]{1,0:T(8,128)(2,1)S(1)}, bf16[256,768]{1,0:T(8,128)(2,1)S(1)}, u32[]{:S(2)}, u32[]{:S(2)}) collective-permute-start(bf16[256,768]{1,0:T(8,128)(2,1)S(1)} %copy-done.4), channel_id=1, source_target_pairs={{3,2},{7,6},{11,10},{15,14},{16,17},{20,21},{24,25},{28,29}} | collective-permute-start | bytes 1179656 | tf_op jit(solution)/shard_map/ppermute | solution.py:114
  106.0 36.0 %collective-permute-start.3 = (bf16[256,768]{1,0:T(8,128)(2,1)S(1)}, bf16[256,768]{1,0:T(8,128)(2,1)S(1)}, u32[]{:S(2)}, u32[]{:S(2)}) collective-permute-start(bf16[256,768]{1,0:T(8,128)(2,1)S(1)} %copy-done.24), channel_id=1, source_target_pairs={{3,1},{2,0},{0,2},{7,5},{6,4},{4,6},{11,9},{10,8},{8,10},{15,13},{... | collective-permute-start | bytes 1179656 | tf_op jit(solution)/shard_map/ppermute | solution.py:114
  112.6 31.3 %collective-permute-start.1 = (bf16[256,768]{1,0:T(8,128)(2,1)S(1)}, bf16[256,768]{1,0:T(8,128)(2,1)S(1)}, u32[]{:S(2)}, u32[]{:S(2)}) collective-permute-start(bf16[256,768]{1,0:T(8,128)(2,1)S(1)} %copy-done.23), channel_id=1, source_target_pairs={{0,1},{1,2},{4,5},{5,6},{8,9},{9,10},{12,13},{13,14},{19,18},{18,1... | collective-permute-start | bytes 1179656 | tf_op jit(solution)/shard_map/ppermute | solution.py:114
  114.2 45.9 %collective-permute-start.7 = (bf16[256,768]{1,0:T(8,128)(2,1)S(1)}, bf16[256,768]{1,0:T(8,128)(2,1)S(1)}, u32[]{:S(2)}, u32[]{:S(2)}) collective-permute-start(bf16[256,768]{1,0:T(8,128)(2,1)S(1)} %copy-done.26), channel_id=1, source_target_pairs={{3,1},{2,0},{0,2},{7,5},{6,4},{4,6},{11,9},{10,8},{8,10},{15,13},{... | collective-permute-start | bytes 1179656 | tf_op jit(solution)/shard_map/ppermute | solution.py:114
  116.1 43.9 %collective-permute-start.5 = (bf16[256,768]{1,0:T(8,128)(2,1)S(1)}, bf16[256,768]{1,0:T(8,128)(2,1)S(1)}, u32[]{:S(2)}, u32[]{:S(2)}) collective-permute-start(bf16[256,768]{1,0:T(8,128)(2,1)S(1)} %copy-done.25), channel_id=1, source_target_pairs={{0,1},{1,2},{4,5},{5,6},{8,9},{9,10},{12,13},{13,14},{19,18},{18,1... | collective-permute-start | bytes 1179656 | tf_op jit(solution)/shard_map/ppermute | solution.py:114
  120.4 25.0 %copy-start.17 = (bf16[256,768]{1,0:T(8,128)(2,1)S(1)}, bf16[256,768]{1,0:T(8,128)(2,1)}, u32[]{:S(2)}) copy-start(bf16[256,768]{1,0:T(8,128)(2,1)} %copy-done.16) | copy-start | bytes 1179652
  120.7 39.8 %collective-permute-start.10 = (bf16[256,768]{1,0:T(8,128)(2,1)S(1)}, bf16[256,768]{1,0:T(8,128)(2,1)S(1)}, u32[]{:S(2)}, u32[]{:S(2)}) collective-permute-start(bf16[256,768]{1,0:T(8,128)(2,1)S(1)} %get-tuple-element.30), channel_id=1, source_target_pairs={{3,2},{7,6},{11,10},{15,14},{16,17},{20,21},{24,25},{28,29}} | collective-permute-start | bytes 1179656 | tf_op jit(solution)/shard_map/ppermute | solution.py:114
  142.0 22.5 %collective-permute-start.11 = (bf16[256,768]{1,0:T(8,128)(2,1)S(1)}, bf16[256,768]{1,0:T(8,128)(2,1)S(1)}, u32[]{:S(2)}, u32[]{:S(2)}) collective-permute-start(bf16[256,768]{1,0:T(8,128)(2,1)S(1)} %get-tuple-element.42), channel_id=1, source_target_pairs={{3,1},{2,0},{0,2},{7,5},{6,4},{4,6},{11,9},{10,8},{8,10},{15,13},{... | collective-permute-start | bytes 1179656 | tf_op jit(solution)/shard_map/ppermute | solution.py:114
  143.9 16.1 %copy-start.19 = (bf16[256,768]{1,0:T(8,128)(2,1)S(1)}, bf16[256,768]{1,0:T(8,128)(2,1)}, u32[]{:S(2)}) copy-start(bf16[256,768]{1,0:T(8,128)(2,1)} %copy-done.18) | copy-start | bytes 1179652
  143.9 20.6 %collective-permute-start.9 = (bf16[256,768]{1,0:T(8,128)(2,1)S(1)}, bf16[256,768]{1,0:T(8,128)(2,1)S(1)}, u32[]{:S(2)}, u32[]{:S(2)}) collective-permute-start(bf16[256,768]{1,0:T(8,128)(2,1)S(1)} %get-tuple-element.41), channel_id=1, source_target_pairs={{0,1},{1,2},{4,5},{5,6},{8,9},{9,10},{12,13},{13,14},{19,18},{18,1... | collective-permute-start | bytes 1179656 | tf_op jit(solution)/shard_map/ppermute | solution.py:114
  (30 other events, 77.6 us)

commit v3 on v2

--- a/solution.py
+++ b/solution.py
@@ -11,6 +11,8 @@
 TAU_PRIOR = 4.0
 PHASE_OFFSET = 0.1
 CHUNKS = 3
+META_BASE = 32
+META_ROWS = 16
 VMEM_LIMIT = 48 * 1024 * 1024
 
 
@@ -27,10 +29,15 @@
     return cosine, -sine, table_right
 
 
-def spectrum_kernel(images, left, right, row_factors, col_factors, out, joined):
+def spectrum_kernel(images, left, right, row_factors, col_factors, *rest):
+    *meta, out, joined = rest
     particles, length = images.shape[0], images.shape[1]
-    owners, _, rows_each, _ = out.shape
-    rows = owners * rows_each
+    owners = out.shape[0]
+    rows = row_factors.shape[0]
+    rows_each = rows // owners
+    for block in meta:
+        for d in range(owners):
+            out[d, particles * rows_each :, :] = block[...]
     table = left[...]
     for p in range(particles):
         section = jnp.dot(table, images[p], preferred_element_type=jnp.float32)
@@ -62,7 +69,9 @@
             real_new = real_part * cosine + imag_part * sine
             imag_new = imag_part * cosine - real_part * sine
             weighted = jnp.concatenate([real_new, imag_new], axis=1).astype(jnp.bfloat16)
-            out[:, p] = weighted.reshape(owners, rows_each, 2 * length)
+            out[:, p * rows_each : (p + 1) * rows_each, :] = weighted.reshape(
+                owners, rows_each, 2 * length
+            )
 
 
 def insert_kernel(received, codes, *outs):
@@ -115,19 +124,16 @@
 
     near_in = permute(jnp.where(place == 2, parts[1], parts[0]), [(3, 2), (2, 1), (1, 0)])
     out_in = permute(jnp.where(place == 0, parts[1], parts[2]), [(0, 1), (1, 2)])
-    last_in = permute(parts[2], [(3, 2)])
     merged = (parts[0].astype(jnp.float32) + near_in.astype(jnp.float32)).astype(jnp.bfloat16)
     far = jnp.where(place == 0, parts[2], jnp.where(place == 3, parts[1], merged))
-
-    def finish(far):
-        far_in = permute(far, [(3, 1), (2, 0), (0, 2)])
-        own = jnp.where(place == 0, parts[0], jnp.where(place == 1, parts[1], parts[2]))
-        total = jnp.where(place == 3, 0.0, own.astype(jnp.float32))
-        total = total + jnp.where(place == 2, 0.0, near_in.astype(jnp.float32))
-        total = total + out_in.astype(jnp.float32) + last_in.astype(jnp.float32)
-        return total + far_in.astype(jnp.float32)
-
-    return far, finish
+    far, last = lax.optimization_barrier((far, parts[2]))
+    far_in = permute(far, [(3, 1), (2, 0), (0, 2)])
+    last_in = permute(last, [(3, 2)])
+    own = jnp.where(place == 0, parts[0], jnp.where(place == 1, parts[1], parts[2]))
+    total = jnp.where(place == 3, 0.0, own.astype(jnp.float32))
+    total = total + jnp.where(place == 2, 0.0, near_in.astype(jnp.float32))
+    total = total + out_in.astype(jnp.float32) + last_in.astype(jnp.float32)
+    return total + far_in.astype(jnp.float32)
 
 
 def per_device(images, classes, shifts, defocus_class, defocus, run_counts, dest_map, ref):
@@ -141,8 +147,11 @@
     chunk_rows = batch_count * each
     freq = jnp.arange(length, dtype=jnp.int32)
 
-    ends = jnp.cumsum(run_counts, axis=1)
+    ends = jnp.cumsum(run_counts, axis=1)[:, : slab_count - 1]
     meta = jnp.concatenate([classes[:, None], defocus_class[:, None], ends], axis=1)
+    fields = meta.shape[1]
+    digits = jnp.concatenate([meta // META_BASE, meta % META_BASE], axis=1).astype(jnp.bfloat16)
+    digits = jnp.pad(digits, ((0, META_ROWS - particles), (0, 2 * length - 2 * fields)))
 
     cosine, minus_sine, table_right = dft_tables(length)
     order = np.arange(length).reshape(batch_count, CHUNKS, each).transpose(1, 0, 2)
@@ -156,12 +165,12 @@
     received = []
     for c in range(CHUNKS):
         left = np.concatenate([cosine[order[c]], minus_sine[order[c]]], axis=0)
+        extra = (digits,) if c == 0 else ()
+        block_rows = particles * each + META_ROWS * len(extra)
         weighted = pl.pallas_call(
             spectrum_kernel,
-            out_shape=jax.ShapeDtypeStruct(
-                (batch_count, particles, each, 2 * length), jnp.bfloat16
-            ),
-            in_specs=whole_vmem(5),
+            out_shape=jax.ShapeDtypeStruct((batch_count, block_rows, 2 * length), jnp.bfloat16),
+            in_specs=whole_vmem(5 + len(extra)),
             out_specs=pl.BlockSpec(memory_space=pltpu.VMEM),
             scratch_shapes=[pltpu.VMEM((particles * chunk_rows, 2 * length), jnp.bfloat16)],
             compiler_params=pltpu.CompilerParams(vmem_limit_bytes=VMEM_LIMIT),
@@ -177,21 +186,17 @@
             table_right,
             row_factors[c],
             col_factors,
+            *extra,
         )
         received.append(lax.all_to_all(weighted, "batch", 0, 0, tiled=True))
-        if c == 0:
-            meta_layer = lax.all_to_all(
-                jnp.broadcast_to(meta[None], (batch_count, *meta.shape)), "batch", 0, 0, tiled=True
-            )
-            meta_all = lax.all_to_all(
-                jnp.broadcast_to(meta_layer[None], (slab_count, *meta_layer.shape)),
-                "slab",
-                0,
-                0,
-                tiled=True,
-            )
-            meta_layer = meta_layer.reshape(-1, meta.shape[1])
-            meta_all = meta_all.reshape(-1, meta.shape[1])
+
+    digits_in = received[0][:, particles * each : particles * (each + 1), : 2 * fields]
+    digits_in = digits_in.astype(jnp.int32).reshape(-1, 2 * fields)
+    meta_layer = digits_in[:, :fields] * META_BASE + digits_in[:, fields:]
+    meta_send, _ = lax.optimization_barrier((meta_layer, received[1]))
+    meta_all = lax.all_to_all(
+        jnp.broadcast_to(meta_send[None], (slab_count, *meta_send.shape)), "slab", 0, 0, tiled=True
+    ).reshape(-1, fields)
 
     class_count = dest_map.shape[0]
     own_dest = lax.dynamic_slice_in_dim(dest_map, batch * rows, rows, 1).astype(jnp.bfloat16)
@@ -213,7 +218,7 @@
         place = jnp.where(upper, slab_count - 1 - slab, slab)
     codes = owner * (each * planes) + (jnp.arange(rows) % each)[None, :] * planes + local_plane
     codes = codes.reshape(batch_count * particles, CHUNKS, each).transpose(1, 0, 2)
-    codes = codes.reshape(CHUNKS, 1, batch_count * particles * each)
+    codes = codes.reshape(CHUNKS, batch_count, particles * each)
 
     owner, local_plane = find_planes(meta_all)
     focus_count = defocus.shape[0]
@@ -235,13 +240,14 @@
 
     bins = each * planes
     sums = []
-    far = None
     for c in range(CHUNKS):
-        rows_in = received[c].reshape(batch_count * particles * each, 2 * length)
+        rows_in = received[c].reshape(-1, 2 * length)
         codes_in = codes[c]
-        if far is not None:
-            codes_in, far = lax.optimization_barrier((codes_in, far))
-            sums.append(finish(far))
+        if c == 0:
+            codes_in = jnp.pad(codes_in, ((0, 0), (0, META_ROWS)), constant_values=-1)
+        codes_in = codes_in.reshape(1, -1)
+        if c > 0 and mirrored:
+            codes_in, sums[-1] = lax.optimization_barrier((codes_in, sums[-1]))
         parts = pl.pallas_call(
             insert_kernel,
             out_shape=[jax.ShapeDtypeStruct((bins, 2 * length), jnp.bfloat16)] * window_slabs,
@@ -256,12 +262,10 @@
             name="insert",
         )(rows_in, codes_in)
         if mirrored:
-            far, finish = slab_sums(parts, place, slab_count, batch_count // 2)
+            sums.append(slab_sums(parts, place, slab_count, batch_count // 2))
         else:
             windows = jnp.stack(parts)
             sums.append(lax.psum_scatter(windows, "slab", scatter_dimension=0, tiled=False))
-    if far is not None:
-        sums.append(finish(far))
     updated = []
     for c in range(CHUNKS):
         here = slice(c * each, (c + 1) * each)

time: 168 us -> 177 us (1.054)
  waiting for transfers between devices: 69.7 us -> 77.7 us
  starting transfers between devices: 46.4 us -> 42.2 us
  local copies, waits for them, and re-layouts: 13.2 us -> 16.9 us
    ppermute x12, waiting for transfers between devices: 45.4 us -> 54.8 us  [permute(): return lax.ppermute(block, ('batch', 'slab'), perm)]
    all_to_all x3, waiting for transfers between devices: 23.8 us -> 16.4 us  [per_device(): received.append(lax.all_to_all(weighted, 'batch', 0, 0, tiled=True))]
    all_to_all x2 -> x1, waiting for transfers between devices: 0.45 us -> 6.51 us  [per_device(): lax.all_to_all(jnp.broadcast_to(meta_send[None], (slab_count, *meta_send....]
    all_to_all x2 -> x1, starting transfers between devices: 10 us -> 5.99 us  [per_device(): lax.all_to_all(jnp.broadcast_to(meta_send[None], (slab_count, *meta_send....]
    add x3 -> x4, other arithmetic: 2.16 us -> 4.51 us  [the longest x3 4.5 us: slab_sums(): return total + far_in.astype(jnp.float32)]
    unnamed x77 -> x60, local copies, waits for them, and re-layouts: 8.63 us -> 9.24 us
  transfers between devices with their start and end apart: 17 -> 16, of which waited for: 9 -> 7; matrix products, arithmetic and copies ran while one was open for 13% -> 12% of each run, Pallas kernels for 10% -> 5%
where the time goes in v3:
time: 177 us; the launch traced here: 176 us
  waiting for transfers between devices  77.7 us (44%)
  starting transfers between devices  42.2 us (24%)
  Pallas kernels  17.4 us (10%)
  local copies, waits for them, and re-layouts  16.9 us (10%)
  other arithmetic  16.2 us (9%)
  matrix products  4.6 us (3%)
    ppermute x12, waiting for transfers between devices, permute(): return lax.ppermute(block, ('batch', 'slab'), perm)  54.8 us
    ppermute x12, starting transfers between devices, permute(): return lax.ppermute(block, ('batch', 'slab'), perm)  23 us
    all_to_all x3, waiting for transfers between devices, per_device(): received.append(lax.all_to_all(weighted, 'batch', 0, 0, tiled=True))  16.4 us
    all_to_all x3, starting transfers between devices, per_device(): received.append(lax.all_to_all(weighted, 'batch', 0, 0, tiled=True))  13.2 us
    pallas_call x3, Pallas kernels, per_device(): pl.pallas_call(spectrum_kernel, out_shape=jax.ShapeDtypeStruct((batch_cou...  11.5 us
    unnamed x60, local copies, waits for them, and re-layouts  9.24 us
    all_to_all x1, waiting for transfers between devices, per_device(): lax.all_to_all(jnp.broadcast_to(meta_send[None], (slab_count, *meta_send....  6.51 us
    all_to_all x1, starting transfers between devices, per_device(): lax.all_to_all(jnp.broadcast_to(meta_send[None], (slab_count, *meta_send....  5.99 us
  transfers between devices with their start and end apart: 16, of which 7 were waited for; matrix products, arithmetic and copies ran while one was open for 12% of the time, Pallas kernels for 5%

profile of v3, /device:TPU:0, one launch (start us, length us, event | category | flops | bytes accessed | tf_op | source)
XLA Modules:
  0.0 175.5 jit_solution(18059751815370549739)
XLA Ops:
  6.0 3.9 %spectrum.3 = bf16[8,144,768]{2,1,0:T(8,128)(2,1)} custom-call(bf16[8,384,384]{2,1,0:T(8,128)(2,1)S(1)} %copy-done, bf16[256,384]{1,0:T(8,128)(2,1)S(1)} %copy-done.8, bf16[768,768]{1,0:T(8,128)(2,1)S(1)} %copy-done.3, f32[128,32]{1,0:T(8,128)S(1)} %bitcast.48, f32[32,384]{1,0:T(8,128)S(1)} %pad_maximum_fusion.1.col_factors, bf16[16,768]{1,0:T(8,128)(2,1)S(1)} %fusion.53.rest_0_), custom_call_target="tpu_custom_call" | custom-call | flops 1811939328 | bytes 6291456 | tf_op jit(solution)/shard_map/spectrum/pallas_call | solution.py:170
  9.9 5.3 %all-to-all-start = ((bf16[8,144,768]{2,1,0:T(8,128)(2,1)}), bf16[8,144,768]{2,1,0:T(8,128)(2,1)S(1)}, u32[]{:S(2)}, u32[]{:S(2)}) async-start(bf16[8,144,768]{2,1,0:T(8,128)(2,1)} %spectrum.3), calls=%async_computation | async-start | bytes 3538944 | tf_op jit(solution)/shard_map/all_to_all | solution.py:191
  18.2 3.8 %spectrum.4 = bf16[8,128,768]{2,1,0:T(8,128)(2,1)} custom-call(bf16[8,384,384]{2,1,0:T(8,128)(2,1)S(1)} %copy-done.1, bf16[256,384]{1,0:T(8,128)(2,1)S(1)} %copy-done.7, bf16[768,768]{1,0:T(8,128)(2,1)S(1)} %copy-done.4, f32[128,32]{1,0:T(8,128)S(1)} %bitcast.47, f32[32,384]{1,0:T(8,128)S(1)} %pad_maximum_fusion.1.col_factors), custom_call_target="tpu_custom_call" | custom-call | flops 1811939328 | bytes 6291456 | tf_op jit(solution)/shard_map/spectrum/pallas_call | solution.py:170
  22.0 16.4 %all-to-all-done = bf16[8,144,768]{2,1,0:T(8,128)(2,1)S(1)} async-done(((bf16[8,144,768]{2,1,0:T(8,128)(2,1)}), bf16[8,144,768]{2,1,0:T(8,128)(2,1)S(1)}, u32[]{:S(2)}, u32[]{:S(2)}) %all-to-all-start) | async-done | bytes 1769504 | tf_op jit(solution)/shard_map/all_to_all | solution.py:191
  38.4 4.3 %all-to-all-start.1 = ((bf16[8,128,768]{2,1,0:T(8,128)(2,1)}), bf16[8,128,768]{2,1,0:T(8,128)(2,1)}, u32[]{:S(2)}, u32[]{:S(2)}) async-start(bf16[8,128,768]{2,1,0:T(8,128)(2,1)} %spectrum.4), calls=%async_computation.1 | async-start | bytes 3145728 | tf_op jit(solution)/shard_map/all_to_all | solution.py:191
  45.5 1.7 insert.3
  48.5 12.0 %collective-permute-done = bf16[256,768]{1,0:T(8,128)(2,1)S(1)} collective-permute-done((bf16[256,768]{1,0:T(8,128)(2,1)S(1)}, bf16[256,768]{1,0:T(8,128)(2,1)S(1)}, u32[]{:S(2)}, u32[]{:S(2)}) %collective-permute-start) | collective-permute-done | bytes 393248 | tf_op jit(solution)/shard_map/ppermute | solution.py:123
  62.3 5.1 %collective-permute-start.3 = (bf16[256,768]{1,0:T(8,128)(2,1)}, bf16[256,768]{1,0:T(8,128)(2,1)}, u32[]{:S(2)}, u32[]{:S(2)}) collective-permute-start(bf16[256,768]{1,0:T(8,128)(2,1)} %get-tuple-element.29), channel_id=1, source_target_pairs={{3,1},{2,0},{0,2},{7,5},{6,4},{4,6},{11,9},{10,8},{8,10},{15,13},{... | collective-permute-start | bytes 1179656 | tf_op jit(solution)/shard_map/ppermute | solution.py:123
  67.5 2.1 %collective-permute-start.1 = (bf16[256,768]{1,0:T(8,128)(2,1)}, bf16[256,768]{1,0:T(8,128)(2,1)}, u32[]{:S(2)}, u32[]{:S(2)}) collective-permute-start(bf16[256,768]{1,0:T(8,128)(2,1)} %get-tuple-element.55), channel_id=1, source_target_pairs={{0,1},{1,2},{4,5},{5,6},{8,9},{9,10},{12,13},{13,14},{19,18},{18,1... | collective-permute-start | bytes 1179656 | tf_op jit(solution)/shard_map/ppermute | solution.py:123
  69.5 1.7 copy-done.2
  71.2 3.8 %spectrum.5 = bf16[8,128,768]{2,1,0:T(8,128)(2,1)} custom-call(bf16[8,384,384]{2,1,0:T(8,128)(2,1)S(1)} %copy-done.2, bf16[256,384]{1,0:T(8,128)(2,1)S(1)} %copy-done.6, bf16[768,768]{1,0:T(8,128)(2,1)S(1)} %copy-done.5, f32[128,32]{1,0:T(8,128)S(1)} %bitcast.46, f32[32,384]{1,0:T(8,128)S(1)} %pad_maximum_fusion.1.col_factors), custom_call_target="tpu_custom_call" | custom-call | flops 1811939328 | bytes 6291456 | tf_op jit(solution)/shard_map/spectrum/pallas_call | solution.py:170
  75.1 10.0 %collective-permute-done.3 = bf16[256,768]{1,0:T(8,128)(2,1)} collective-permute-done((bf16[256,768]{1,0:T(8,128)(2,1)}, bf16[256,768]{1,0:T(8,128)(2,1)}, u32[]{:S(2)}, u32[]{:S(2)}) %collective-permute-start.3) | collective-permute-done | bytes 393248 | tf_op jit(solution)/shard_map/ppermute | solution.py:123
  85.1 2.4 %fusion.7 = f32[256,768]{1,0:T(8,128)} fusion(bf16[256,768]{1,0:T(8,128)(2,1)S(1)} %collective-permute-done, bf16[256,768]{1,0:T(8,128)(2,1)} %collective-permute-done.3, bf16[256,768]{1,0:T(8,128)(2,1)S(1)} %collective-permute-done.2, bf16[256,768]{1,0:T(8,128)(2,1)} %collective-permute-done.1, bf16[256,768]{1,0:T(8,128)(2,1)S(1)} %get-tuple-element.25, ...), kind=kLoop, calls=%fused_computation.17 | loop fusion | flops 2555904 | bytes 3538948 | tf_op jit(solution)/shard_map/add | solution.py:136
  87.5 2.8 %insert.4 = (bf16[256,768]{1,0:T(8,128)(2,1)S(1)}, bf16[256,768]{1,0:T(8,128)(2,1)S(1)}, bf16[256,768]{1,0:T(8,128)(2,1)S(1)}) custom-call(bf16[1024,768]{1,0:T(8,128)(2,1)} %bitcast.19.received, s32[1,1024]{1,0:T(1,128)S(1)} %reshape_squeeze.6.codes), custom_call_target="tpu_custom_call" | custom-call | flops 1207959552 | bytes 4194304 | tf_op jit(solution)/shard_map/insert/pallas_call | solution.py:251
  92.3 6.0 %all-to-all-start.2 = ((s32[4,1,320]{2,1,0:T(1,128)}), s32[4,1,320]{2,1,0:T(1,128)S(1)}, u32[]{:S(2)}, u32[]{:S(2)}) async-start(s32[4,1,320]{2,1,0:T(1,128)} %reshape.249), calls=%async_computation.2 | async-start | bytes 12288 | tf_op jit(solution)/shard_map/all_to_all | solution.py:197
  98.9 6.5 %all-to-all-done.2 = s32[4,1,320]{2,1,0:T(1,128)S(1)} async-done(((s32[4,1,320]{2,1,0:T(1,128)}), s32[4,1,320]{2,1,0:T(1,128)S(1)}, u32[]{:S(2)}, u32[]{:S(2)}) %all-to-all-start.2) | async-done | bytes 5152 | tf_op jit(solution)/shard_map/all_to_all | solution.py:197
  106.0 3.6 %all-to-all-start.3 = ((bf16[8,128,768]{2,1,0:T(8,128)(2,1)}), bf16[8,128,768]{2,1,0:T(8,128)(2,1)S(1)}, u32[]{:S(2)}, u32[]{:S(2)}) async-start(bf16[8,128,768]{2,1,0:T(8,128)(2,1)} %spectrum.5), calls=%async_computation.3 | async-start | bytes 3145728 | tf_op jit(solution)/shard_map/all_to_all | solution.py:191
  112.2 3.1 %collective-permute-start.7 = (bf16[256,768]{1,0:T(8,128)(2,1)}, bf16[256,768]{1,0:T(8,128)(2,1)S(1)}, u32[]{:S(2)}, u32[]{:S(2)}) collective-permute-start(bf16[256,768]{1,0:T(8,128)(2,1)} %get-tuple-element.37), channel_id=1, source_target_pairs={{3,1},{2,0},{0,2},{7,5},{6,4},{4,6},{11,9},{10,8},{8,10},{15,13},{... | collective-permute-start | bytes 1179656 | tf_op jit(solution)/shard_map/ppermute | solution.py:123
  115.3 2.1 %collective-permute-start.5 = (bf16[256,768]{1,0:T(8,128)(2,1)}, bf16[256,768]{1,0:T(8,128)(2,1)}, u32[]{:S(2)}, u32[]{:S(2)}) collective-permute-start(bf16[256,768]{1,0:T(8,128)(2,1)} %get-tuple-element.53), channel_id=1, source_target_pairs={{0,1},{1,2},{4,5},{5,6},{8,9},{9,10},{12,13},{13,14},{19,18},{18,1... | collective-permute-start | bytes 1179656 | tf_op jit(solution)/shard_map/ppermute | solution.py:123
  126.4 8.7 %collective-permute-done.7 = bf16[256,768]{1,0:T(8,128)(2,1)S(1)} collective-permute-done((bf16[256,768]{1,0:T(8,128)(2,1)}, bf16[256,768]{1,0:T(8,128)(2,1)S(1)}, u32[]{:S(2)}, u32[]{:S(2)}) %collective-permute-start.7) | collective-permute-done | bytes 393248 | tf_op jit(solution)/shard_map/ppermute | solution.py:123
  135.8 1.7 fusion.12
  142.3 9.3 %collective-permute-done.8 = bf16[256,768]{1,0:T(8,128)(2,1)S(1)} collective-permute-done((bf16[256,768]{1,0:T(8,128)(2,1)S(1)}, bf16[256,768]{1,0:T(8,128)(2,1)S(1)}, u32[]{:S(2)}, u32[]{:S(2)}) %collective-permute-start.8) | collective-permute-done | bytes 393248 | tf_op jit(solution)/shard_map/ppermute | solution.py:123
  152.5 3.5 %collective-permute-start.11 = (bf16[256,768]{1,0:T(8,128)(2,1)S(1)}, bf16[256,768]{1,0:T(8,128)(2,1)S(1)}, u32[]{:S(2)}, u32[]{:S(2)}) collective-permute-start(bf16[256,768]{1,0:T(8,128)(2,1)S(1)} %get-tuple-element.44), channel_id=1, source_target_pairs={{3,1},{2,0},{0,2},{7,5},{6,4},{4,6},{11,9},{10,8},{8,10},{15,13},{... | collective-permute-start | bytes 1179656 | tf_op jit(solution)/shard_map/ppermute | solution.py:123
  158.7 14.8 %collective-permute-done.11 = bf16[256,768]{1,0:T(8,128)(2,1)S(1)} collective-permute-done((bf16[256,768]{1,0:T(8,128)(2,1)S(1)}, bf16[256,768]{1,0:T(8,128)(2,1)S(1)}, u32[]{:S(2)}, u32[]{:S(2)}) %collective-permute-start.11) | collective-permute-done | bytes 393248 | tf_op jit(solution)/shard_map/ppermute | solution.py:123
  (133 shorter events, 40.6 us)
Async XLA Ops:
  9.9 28.4 %all-to-all-start = ((bf16[8,144,768]{2,1,0:T(8,128)(2,1)}), bf16[8,144,768]{2,1,0:T(8,128)(2,1)S(1)}, u32[]{:S(2)}, u32[]{:S(2)}) async-start(bf16[8,144,768]{2,1,0:T(8,128)(2,1)} %spectrum.3), calls=%async_computation | async-start | bytes 3538944 | tf_op jit(solution)/shard_map/all_to_all | solution.py:191
  15.3 27.7 %copy-start.22 = (s32[48]{0:T(128)}, s32[48]{0:T(128)S(1)}, u32[]{:S(2)}) copy-start(s32[48]{0:T(128)S(1)} %iota_add_fusion) | copy-start | bytes 580
  38.4 36.7 %all-to-all-start.1 = ((bf16[8,128,768]{2,1,0:T(8,128)(2,1)}), bf16[8,128,768]{2,1,0:T(8,128)(2,1)}, u32[]{:S(2)}, u32[]{:S(2)}) async-start(bf16[8,128,768]{2,1,0:T(8,128)(2,1)} %spectrum.4), calls=%async_computation.1 | async-start | bytes 3145728 | tf_op jit(solution)/shard_map/all_to_all | solution.py:191
  47.2 13.3 %collective-permute-start = (bf16[256,768]{1,0:T(8,128)(2,1)S(1)}, bf16[256,768]{1,0:T(8,128)(2,1)S(1)}, u32[]{:S(2)}, u32[]{:S(2)}) collective-permute-start(bf16[256,768]{1,0:T(8,128)(2,1)S(1)} %broadcast_select_fusion.2), channel_id=1, source_target_pairs={{3,2},{2,1},{1,0},{7,6},{6,5},{5,4},{11,10},{10,9},{9,8},{15,14},{... | collective-permute-start | bytes 1179656 | tf_op jit(solution)/shard_map/ppermute | solution.py:123
  60.5 9.0 %copy-start.5 = (bf16[768,768]{1,0:T(8,128)(2,1)S(1)}, bf16[768,768]{1,0:T(8,128)(2,1)}, u32[]{:S(2)}) copy-start(bf16[768,768]{1,0:T(8,128)(2,1)} %constant.160.clone.right) | copy-start | bytes 3538948
  60.5 9.0 %copy-start.6 = (bf16[256,384]{1,0:T(8,128)(2,1)S(1)}, bf16[256,384]{1,0:T(8,128)(2,1)}, u32[]{:S(2)}) copy-start(bf16[256,384]{1,0:T(8,128)(2,1)} %constant.163.clone.left) | copy-start | bytes 589828
  61.7 13.5 %collective-permute-start.2 = (bf16[256,768]{1,0:T(8,128)(2,1)S(1)}, bf16[256,768]{1,0:T(8,128)(2,1)S(1)}, u32[]{:S(2)}, u32[]{:S(2)}) collective-permute-start(bf16[256,768]{1,0:T(8,128)(2,1)S(1)} %get-tuple-element.28), channel_id=1, source_target_pairs={{3,2},{7,6},{11,10},{15,14},{16,17},{20,21},{24,25},{28,29}} | collective-permute-start | bytes 1179656 | tf_op jit(solution)/shard_map/ppermute | solution.py:123
  62.3 22.8 %collective-permute-start.3 = (bf16[256,768]{1,0:T(8,128)(2,1)}, bf16[256,768]{1,0:T(8,128)(2,1)}, u32[]{:S(2)}, u32[]{:S(2)}) collective-permute-start(bf16[256,768]{1,0:T(8,128)(2,1)} %get-tuple-element.29), channel_id=1, source_target_pairs={{3,1},{2,0},{0,2},{7,5},{6,4},{4,6},{11,9},{10,8},{8,10},{15,13},{... | collective-permute-start | bytes 1179656 | tf_op jit(solution)/shard_map/ppermute | solution.py:123
  67.5 17.7 %collective-permute-start.1 = (bf16[256,768]{1,0:T(8,128)(2,1)}, bf16[256,768]{1,0:T(8,128)(2,1)}, u32[]{:S(2)}, u32[]{:S(2)}) collective-permute-start(bf16[256,768]{1,0:T(8,128)(2,1)} %get-tuple-element.55), channel_id=1, source_target_pairs={{0,1},{1,2},{4,5},{5,6},{8,9},{9,10},{12,13},{13,14},{19,18},{18,1... | collective-permute-start | bytes 1179656 | tf_op jit(solution)/shard_map/ppermute | solution.py:123
  90.4 20.0 %collective-permute-start.4 = (bf16[256,768]{1,0:T(8,128)(2,1)S(1)}, bf16[256,768]{1,0:T(8,128)(2,1)S(1)}, u32[]{:S(2)}, u32[]{:S(2)}) collective-permute-start(bf16[256,768]{1,0:T(8,128)(2,1)S(1)} %broadcast_select_fusion.1), channel_id=1, source_target_pairs={{3,2},{2,1},{1,0},{7,6},{6,5},{5,4},{11,10},{10,9},{9,8},{15,14},{... | collective-permute-start | bytes 1179656 | tf_op jit(solution)/shard_map/ppermute | solution.py:123
  92.3 13.1 %all-to-all-start.2 = ((s32[4,1,320]{2,1,0:T(1,128)}), s32[4,1,320]{2,1,0:T(1,128)S(1)}, u32[]{:S(2)}, u32[]{:S(2)}) async-start(s32[4,1,320]{2,1,0:T(1,128)} %reshape.249), calls=%async_computation.2 | async-start | bytes 12288 | tf_op jit(solution)/shard_map/all_to_all | solution.py:197
  98.9 10.7 %copy-start.20 = (f32[16]{0:T(128)S(1)}, f32[16]{0:T(128)}, u32[]{:S(2)}) copy-start(f32[16]{0:T(128)} %param.16) | copy-start | bytes 196
  106.0 31.5 %all-to-all-start.3 = ((bf16[8,128,768]{2,1,0:T(8,128)(2,1)}), bf16[8,128,768]{2,1,0:T(8,128)(2,1)S(1)}, u32[]{:S(2)}, u32[]{:S(2)}) async-start(bf16[8,128,768]{2,1,0:T(8,128)(2,1)} %spectrum.5), calls=%async_computation.3 | async-start | bytes 3145728 | tf_op jit(solution)/shard_map/all_to_all | solution.py:191
  110.4 7.0 %copy-start.26 = (f32[48]{0:T(128)S(1)}, f32[48]{0:T(128)}, u32[]{:S(2)}) copy-start(f32[48]{0:T(128)} %fusion.87) | copy-start | bytes 580
  111.5 14.9 %collective-permute-start.6 = (bf16[256,768]{1,0:T(8,128)(2,1)S(1)}, bf16[256,768]{1,0:T(8,128)(2,1)S(1)}, u32[]{:S(2)}, u32[]{:S(2)}) collective-permute-start(bf16[256,768]{1,0:T(8,128)(2,1)S(1)} %get-tuple-element.36), channel_id=1, source_target_pairs={{3,2},{7,6},{11,10},{15,14},{16,17},{20,21},{24,25},{28,29}} | collective-permute-start | bytes 1179656 | tf_op jit(solution)/shard_map/ppermute | solution.py:123
  112.2 22.9 %collective-permute-start.7 = (bf16[256,768]{1,0:T(8,128)(2,1)}, bf16[256,768]{1,0:T(8,128)(2,1)S(1)}, u32[]{:S(2)}, u32[]{:S(2)}) collective-permute-start(bf16[256,768]{1,0:T(8,128)(2,1)} %get-tuple-element.37), channel_id=1, source_target_pairs={{3,1},{2,0},{0,2},{7,5},{6,4},{4,6},{11,9},{10,8},{8,10},{15,13},{... | collective-permute-start | bytes 1179656 | tf_op jit(solution)/shard_map/ppermute | solution.py:123
  115.3 20.5 %collective-permute-start.5 = (bf16[256,768]{1,0:T(8,128)(2,1)}, bf16[256,768]{1,0:T(8,128)(2,1)}, u32[]{:S(2)}, u32[]{:S(2)}) collective-permute-start(bf16[256,768]{1,0:T(8,128)(2,1)} %get-tuple-element.53), channel_id=1, source_target_pairs={{0,1},{1,2},{4,5},{5,6},{8,9},{9,10},{12,13},{13,14},{19,18},{18,1... | collective-permute-start | bytes 1179656 | tf_op jit(solution)/shard_map/ppermute | solution.py:123
  126.4 8.7 %copy-start.12 = (bf16[256,768]{1,0:T(8,128)(2,1)}, bf16[256,768]{1,0:T(8,128)(2,1)S(1)}, u32[]{:S(2)}) copy-start(bf16[256,768]{1,0:T(8,128)(2,1)S(1)} %collective-permute-done.6) | copy-start | bytes 1179652
  139.0 12.6 %collective-permute-start.8 = (bf16[256,768]{1,0:T(8,128)(2,1)S(1)}, bf16[256,768]{1,0:T(8,128)(2,1)S(1)}, u32[]{:S(2)}, u32[]{:S(2)}) collective-permute-start(bf16[256,768]{1,0:T(8,128)(2,1)S(1)} %broadcast_select_fusion), channel_id=1, source_target_pairs={{3,2},{2,1},{1,0},{7,6},{6,5},{5,4},{11,10},{10,9},{9,8},{15,14},{... | collective-permute-start | bytes 1179656 | tf_op jit(solution)/shard_map/ppermute | solution.py:123
  151.8 6.8 %collective-permute-start.10 = (bf16[256,768]{1,0:T(8,128)(2,1)S(1)}, bf16[256,768]{1,0:T(8,128)(2,1)S(1)}, u32[]{:S(2)}, u32[]{:S(2)}) collective-permute-start(bf16[256,768]{1,0:T(8,128)(2,1)S(1)} %get-tuple-element.43), channel_id=1, source_target_pairs={{3,2},{7,6},{11,10},{15,14},{16,17},{20,21},{24,25},{28,29}} | collective-permute-start | bytes 1179656 | tf_op jit(solution)/shard_map/ppermute | solution.py:123
  152.5 21.0 %collective-permute-start.11 = (bf16[256,768]{1,0:T(8,128)(2,1)S(1)}, bf16[256,768]{1,0:T(8,128)(2,1)S(1)}, u32[]{:S(2)}, u32[]{:S(2)}) collective-permute-start(bf16[256,768]{1,0:T(8,128)(2,1)S(1)} %get-tuple-element.44), channel_id=1, source_target_pairs={{3,1},{2,0},{0,2},{7,5},{6,4},{4,6},{11,9},{10,8},{8,10},{15,13},{... | collective-permute-start | bytes 1179656 | tf_op jit(solution)/shard_map/ppermute | solution.py:123
  156.0 17.5 %collective-permute-start.9 = (bf16[256,768]{1,0:T(8,128)(2,1)S(1)}, bf16[256,768]{1,0:T(8,128)(2,1)S(1)}, u32[]{:S(2)}, u32[]{:S(2)}) collective-permute-start(bf16[256,768]{1,0:T(8,128)(2,1)S(1)} %get-tuple-element.51), channel_id=1, source_target_pairs={{0,1},{1,2},{4,5},{5,6},{8,9},{9,10},{12,13},{13,14},{19,18},{18,1... | collective-permute-start | bytes 1179656 | tf_op jit(solution)/shard_map/ppermute | solution.py:123
  158.6 15.3 %copy-start.9 = (f32[256,768]{1,0:T(8,128)S(1)}, f32[256,768]{1,0:T(8,128)}, u32[]{:S(2)}) copy-start(f32[256,768]{1,0:T(8,128)} %fusion.7) | copy-start | bytes 2359300
  158.6 15.3 %copy-start.11 = (bf16[48,16,768]{2,1,0:T(8,128)(2,1)S(1)}, bf16[48,16,768]{2,1,0:T(8,128)(2,1)}, u32[]{:S(2)}) copy-start(bf16[48,16,768]{2,1,0:T(8,128)(2,1)} %param.19) | copy-start | bytes 3538948
  (19 other events, 56.2 us)

commit v4 on v3

--- a/solution.py
+++ b/solution.py
@@ -74,14 +74,14 @@
             )
 
 
-def insert_kernel(received, codes, *outs):
-    bins = outs[0].shape[0]
+def insert_kernel(received, codes, out):
+    windows, bins, _ = out.shape
     rows = received[...]
     codes_all = codes[...]
-    for k, out in enumerate(outs):
+    for k in range(windows):
         bin_index = lax.broadcasted_iota(jnp.int32, (bins, 1), 0) + k * bins
         hot = jnp.where(codes_all == bin_index, 1.0, 0.0).astype(jnp.bfloat16)
-        out[...] = jnp.dot(hot, rows, preferred_element_type=jnp.float32).astype(out.dtype)
+        out[k] = jnp.dot(hot, rows, preferred_element_type=jnp.float32).astype(out.dtype)
 
 
 def whole_vmem(count):
@@ -175,8 +175,8 @@
             scratch_shapes=[pltpu.VMEM((particles * chunk_rows, 2 * length), jnp.bfloat16)],
             compiler_params=pltpu.CompilerParams(vmem_limit_bytes=VMEM_LIMIT),
             cost_estimate=pl.CostEstimate(
-                flops=2 * particles * chunk_rows * 2 * length * 3 * length,
-                bytes_accessed=6 * 1024 * 1024,
+                flops=0,
+                bytes_accessed=0,
                 transcendentals=0,
             ),
             name="spectrum",
@@ -193,10 +193,11 @@
     digits_in = received[0][:, particles * each : particles * (each + 1), : 2 * fields]
     digits_in = digits_in.astype(jnp.int32).reshape(-1, 2 * fields)
     meta_layer = digits_in[:, :fields] * META_BASE + digits_in[:, fields:]
-    meta_send, _ = lax.optimization_barrier((meta_layer, received[1]))
-    meta_all = lax.all_to_all(
-        jnp.broadcast_to(meta_send[None], (slab_count, *meta_send.shape)), "slab", 0, 0, tiled=True
-    ).reshape(-1, fields)
+    meta_all = [meta_layer]
+    for step in range(1, slab_count):
+        ring = [(s, (s + step) % slab_count) for s in range(slab_count)]
+        meta_all.append(lax.ppermute(meta_layer, "slab", ring))
+    meta_all = jnp.concatenate(meta_all, axis=0)
 
     class_count = dest_map.shape[0]
     own_dest = lax.dynamic_slice_in_dim(dest_map, batch * rows, rows, 1).astype(jnp.bfloat16)
@@ -208,7 +209,7 @@
         past = own_freq[None, :, None] >= table[:, None, 2:]
         return jnp.sum(past.astype(jnp.int32), axis=2), local_plane.astype(jnp.int32)
 
-    mirrored = slab_count == 4 and batch_count % 2 == 0
+    mirrored = False
     window_slabs = 3 if mirrored else slab_count
     owner, local_plane = find_planes(meta_layer)
     place = slab
@@ -250,13 +251,13 @@
             codes_in, sums[-1] = lax.optimization_barrier((codes_in, sums[-1]))
         parts = pl.pallas_call(
             insert_kernel,
-            out_shape=[jax.ShapeDtypeStruct((bins, 2 * length), jnp.bfloat16)] * window_slabs,
+            out_shape=jax.ShapeDtypeStruct((window_slabs, bins, 2 * length), jnp.bfloat16),
             in_specs=whole_vmem(2),
-            out_specs=whole_vmem(window_slabs),
+            out_specs=pl.BlockSpec(memory_space=pltpu.VMEM),
             compiler_params=pltpu.CompilerParams(vmem_limit_bytes=VMEM_LIMIT),
             cost_estimate=pl.CostEstimate(
-                flops=2 * bins * window_slabs * rows_in.shape[0] * 2 * length,
-                bytes_accessed=4 * 1024 * 1024,
+                flops=0,
+                bytes_accessed=0,
                 transcendentals=0,
             ),
             name="insert",
@@ -264,8 +265,7 @@
         if mirrored:
             sums.append(slab_sums(parts, place, slab_count, batch_count // 2))
         else:
-            windows = jnp.stack(parts)
-            sums.append(lax.psum_scatter(windows, "slab", scatter_dimension=0, tiled=False))
+            sums.append(lax.psum_scatter(parts, "slab", scatter_dimension=0, tiled=False))
     updated = []
     for c in range(CHUNKS):
         here = slice(c * each, (c + 1) * each)

time: 177 us -> 175 us (0.989)
  starting transfers between devices: 42.2 us -> 18.7 us
  waiting for transfers between devices: 77.7 us -> 92.1 us
  between operations: 0.55 us -> 13.4 us
  other arithmetic: 16.2 us -> 7.49 us
  local copies, waits for them, and re-layouts: 16.9 us -> 20.8 us
    ppermute x12 -> x3, waiting for transfers between devices: 54.8 us -> 4.09 us  [per_device(): meta_all.append(lax.ppermute(meta_layer, 'slab', ring))]
    all_to_all x3, waiting for transfers between devices: 16.4 us -> 63.9 us  [per_device(): received.append(lax.all_to_all(weighted, 'batch', 0, 0, tiled=True))]
    reduce_scatter x0 -> x3, waiting for transfers between devices: none -> 24 us  [per_device(): lax.psum_scatter(parts, 'slab', scatter_dimension=0, tiled=False)]
    ppermute x12 -> x3, starting transfers between devices: 23 us -> 5.2 us  [per_device(): meta_all.append(lax.ppermute(meta_layer, 'slab', ring))]
    unnamed x60 -> x49, local copies, waits for them, and re-layouts: 9.24 us -> 17.1 us
    all_to_all x1 -> x0, waiting for transfers between devices: 6.51 us -> none  [per_device(): lax.all_to_all(jnp.broadcast_to(meta_send[None], (slab_count, *meta_send....]
    all_to_all x1 -> x0, starting transfers between devices: 5.99 us -> none  [per_device(): lax.all_to_all(jnp.broadcast_to(meta_send[None], (slab_count, *meta_send....]
    add x3 -> x0, other arithmetic: 4.5 us -> none  [slab_sums(): return total + far_in.astype(jnp.float32)]
  transfers between devices with their start and end apart: 16 -> 9, of which waited for: 7 -> 6; matrix products, arithmetic and copies ran while one was open for 12% -> 3% of each run, Pallas kernels for 5% -> 6%
where the time goes in v4:
time: 175 us; the launch traced here: 174 us
  waiting for transfers between devices  92.1 us (53%)
  local copies, waits for them, and re-layouts  20.8 us (12%)
  starting transfers between devices  18.7 us (11%)
  Pallas kernels  16.6 us (9%)
  between operations  13.4 us (8%)
  other arithmetic  7.49 us (4%)
  matrix products  4.61 us (3%)
    all_to_all x3, waiting for transfers between devices, per_device(): received.append(lax.all_to_all(weighted, 'batch', 0, 0, tiled=True))  63.9 us
    reduce_scatter x3, waiting for transfers between devices, per_device(): lax.psum_scatter(parts, 'slab', scatter_dimension=0, tiled=False)  24 us
    unnamed x49, local copies, waits for them, and re-layouts  17.1 us
    all_to_all x3, starting transfers between devices, per_device(): received.append(lax.all_to_all(weighted, 'batch', 0, 0, tiled=True))  13.2 us
    pallas_call x3, Pallas kernels, per_device(): pl.pallas_call(insert_kernel, out_shape=jax.ShapeDtypeStruct((window_slab...  8.66 us
    pallas_call x3, Pallas kernels, per_device(): pl.pallas_call(spectrum_kernel, out_shape=jax.ShapeDtypeStruct((batch_cou...  7.95 us
    ppermute x3, starting transfers between devices, per_device(): meta_all.append(lax.ppermute(meta_layer, 'slab', ring))  5.2 us
    ppermute x3, waiting for transfers between devices, per_device(): meta_all.append(lax.ppermute(meta_layer, 'slab', ring))  4.09 us
  transfers between devices with their start and end apart: 9, of which 6 were waited for; matrix products, arithmetic and copies ran while one was open for 3% of the time, Pallas kernels for 6%

profile of v4, /device:TPU:0, one launch (start us, length us, event | category | flops | bytes accessed | tf_op | source)
XLA Modules:
  0.0 173.8 jit_solution(10488701203846078929)
XLA Ops:
  11.5 1.3 copy-done.1
  13.7 2.7 %spectrum.3 = bf16[8,144,768]{2,1,0:T(8,128)(2,1)S(1)} custom-call(bf16[8,384,384]{2,1,0:T(8,128)(2,1)S(1)} %copy-done, bf16[256,384]{1,0:T(8,128)(2,1)S(1)} %copy-done.14, bf16[768,768]{1,0:T(8,128)(2,1)S(1)} %copy-done.1, f32[128,32]{1,0:T(8,128)S(1)} %bitcast.45, f32[32,384]{1,0:T(8,128)S(1)} %pad_maximum_fusion.1.col_factors, ...), custom_call_target="tpu_custom_call" | custom-call | tf_op jit(solution)/shard_map/spectrum/pallas_call | solution.py:170
  16.4 1.2 copy-done.3
  18.2 5.2 %all-to-all-start = ((bf16[8,144,768]{2,1,0:T(8,128)(2,1)}), bf16[8,144,768]{2,1,0:T(8,128)(2,1)}, u32[]{:S(2)}, u32[]{:S(2)}) async-start(bf16[8,144,768]{2,1,0:T(8,128)(2,1)} %copy-done.3), calls=%async_computation | async-start | bytes 3538944 | tf_op jit(solution)/shard_map/all_to_all | solution.py:191
  23.4 23.2 %all-to-all-done = bf16[8,144,768]{2,1,0:T(8,128)(2,1)} async-done(((bf16[8,144,768]{2,1,0:T(8,128)(2,1)}), bf16[8,144,768]{2,1,0:T(8,128)(2,1)}, u32[]{:S(2)}, u32[]{:S(2)}) %all-to-all-start) | async-done | bytes 1769504 | tf_op jit(solution)/shard_map/all_to_all | solution.py:191
  47.7 1.5 fusion.3
  50.1 3.7 %insert.3 = bf16[4,256,768]{2,1,0:T(8,128)(2,1)S(1)} custom-call(bf16[1152,768]{1,0:T(8,128)(2,1)} %bitcast.6.received, s32[1,1152]{1,0:T(1,128)S(1)} %reshape.237.codes), custom_call_target="tpu_custom_call" | custom-call | tf_op jit(solution)/shard_map/insert/pallas_call | solution.py:252
  53.8 1.2 copy-done.4
  55.0 1.2 copy-done.2
  58.8 2.6 %spectrum.5 = bf16[8,128,768]{2,1,0:T(8,128)(2,1)S(1)} custom-call(bf16[8,384,384]{2,1,0:T(8,128)(2,1)S(1)} %copy-done, bf16[256,384]{1,0:T(8,128)(2,1)S(1)} %copy-done.16, bf16[768,768]{1,0:T(8,128)(2,1)S(1)} %copy-done.2, f32[128,32]{1,0:T(8,128)S(1)} %bitcast.44, f32[32,384]{1,0:T(8,128)S(1)} %copy-done.10), custom_call_target="tpu_custom_call" | custom-call | tf_op jit(solution)/shard_map/spectrum/pallas_call | solution.py:170
  61.5 1.2 copy-done.8
  62.7 4.3 %all-to-all-start.2 = ((bf16[8,128,768]{2,1,0:T(8,128)(2,1)}), bf16[8,128,768]{2,1,0:T(8,128)(2,1)}, u32[]{:S(2)}, u32[]{:S(2)}) async-start(bf16[8,128,768]{2,1,0:T(8,128)(2,1)} %copy-done.8), calls=%async_computation.4 | async-start | bytes 3145728 | tf_op jit(solution)/shard_map/all_to_all | solution.py:191
  68.1 20.0 %all-to-all-done.2 = bf16[8,128,768]{2,1,0:T(8,128)(2,1)} async-done(((bf16[8,128,768]{2,1,0:T(8,128)(2,1)}), bf16[8,128,768]{2,1,0:T(8,128)(2,1)}, u32[]{:S(2)}, u32[]{:S(2)}) %all-to-all-start.2) | async-done | bytes 1572896 | tf_op jit(solution)/shard_map/all_to_all | solution.py:191
  88.0 3.2 %insert.5 = bf16[4,256,768]{2,1,0:T(8,128)(2,1)S(1)} custom-call(bf16[1024,768]{1,0:T(8,128)(2,1)} %bitcast.22.received, s32[1,1024]{1,0:T(1,128)S(1)} %reshape_squeeze.7.codes), custom_call_target="tpu_custom_call" | custom-call | tf_op jit(solution)/shard_map/insert/pallas_call | solution.py:252
  95.0 2.6 %spectrum.4 = bf16[8,128,768]{2,1,0:T(8,128)(2,1)S(1)} custom-call(bf16[8,384,384]{2,1,0:T(8,128)(2,1)S(1)} %copy-done, bf16[256,384]{1,0:T(8,128)(2,1)S(1)} %copy-done.15, bf16[768,768]{1,0:T(8,128)(2,1)S(1)} %copy-done.2, f32[128,32]{1,0:T(8,128)S(1)} %bitcast.43, f32[32,384]{1,0:T(8,128)S(1)} %copy-done.11), custom_call_target="tpu_custom_call" | custom-call | tf_op jit(solution)/shard_map/spectrum/pallas_call | solution.py:170
  98.8 3.7 %all-to-all-start.1 = ((bf16[8,128,768]{2,1,0:T(8,128)(2,1)}), bf16[8,128,768]{2,1,0:T(8,128)(2,1)S(1)}, u32[]{:S(2)}, u32[]{:S(2)}) async-start(bf16[8,128,768]{2,1,0:T(8,128)(2,1)} %copy-done.7), calls=%async_computation.2 | async-start | bytes 3145728 | tf_op jit(solution)/shard_map/all_to_all | solution.py:191
  102.7 20.8 %all-to-all-done.1 = bf16[8,128,768]{2,1,0:T(8,128)(2,1)S(1)} async-done(((bf16[8,128,768]{2,1,0:T(8,128)(2,1)}), bf16[8,128,768]{2,1,0:T(8,128)(2,1)S(1)}, u32[]{:S(2)}, u32[]{:S(2)}) %all-to-all-start.1) | async-done | bytes 1572896 | tf_op jit(solution)/shard_map/all_to_all | solution.py:191
  123.5 1.8 %insert.4 = bf16[4,256,768]{2,1,0:T(8,128)(2,1)S(1)} custom-call(bf16[1024,768]{1,0:T(8,128)(2,1)S(1)} %bitcast.42, s32[1,1024]{1,0:T(1,128)S(1)} %reshape_squeeze.6.codes), custom_call_target="tpu_custom_call" | custom-call | tf_op jit(solution)/shard_map/insert/pallas_call | solution.py:252
  127.3 4.2 %collective-permute-start.2 = (s32[64,5]{0,1:T(8,128)S(1)}, s32[64,5]{0,1:T(8,128)S(1)}, u32[]{:S(2)}, u32[]{:S(2)}) collective-permute-start(s32[64,5]{0,1:T(8,128)S(1)} %multiply_add_fusion.2), channel_id=1, source_target_pairs={{0,3},{1,0},{2,1},{3,2},{4,7},{5,4},{6,5},{7,6},{8,11},{9,8},{10,9... | collective-permute-start | bytes 3848 | tf_op jit(solution)/shard_map/ppermute | solution.py:199
  132.8 3.2 %collective-permute-done.1 = s32[64,5]{0,1:T(8,128)S(1)} collective-permute-done((s32[64,5]{0,1:T(8,128)S(1)}, s32[64,5]{0,1:T(8,128)S(1)}, u32[]{:S(2)}, u32[]{:S(2)}) %collective-permute-start.1) | collective-permute-done | bytes 1312 | tf_op jit(solution)/shard_map/ppermute | solution.py:199
  137.1 1.6 fusion.2
  139.0 1.2 fusion.1
  140.4 24.0 %reduce-scatter.6.cloned.1.call-done = bf16[1,256,768]{2,1,0:T(8,128)(2,1)} async-done(((bf16[4,256,768]{2,1,0:T(8,128)(2,1)}), bf16[1,256,768]{2,1,0:T(8,128)(2,1)}) %reduce-scatter.6.cloned.1.call-update) | async-done | bytes 393232 | tf_op jit(solution)/shard_map/reduce_scatter | solution.py:268
  164.4 1.7 fusion.4
  (99 shorter events, 23.2 us)
Async XLA Ops:
  6.5 4.3 %copy-start.21 = (s32[8]{0:T(128)S(1)}, s32[8]{0:T(128)}, u32[]{:S(2)}) copy-start(s32[8]{0:T(128)} %param.15) | copy-start | bytes 100
  6.5 4.2 %copy-start.20 = (s32[8,4]{0,1:T(4,128)S(1)}, s32[8,4]{0,1:T(4,128)}, u32[]{:S(2)}) copy-start(s32[8,4]{0,1:T(4,128)} %param.17) | copy-start | bytes 388
  6.5 4.4 %copy-start.22 = (s32[8]{0:T(128)S(1)}, s32[8]{0:T(128)}, u32[]{:S(2)}) copy-start(s32[8]{0:T(128)} %param.13) | copy-start | bytes 100
  8.2 3.3 %copy-start = (bf16[8,384,384]{2,1,0:T(8,128)(2,1)S(1)}, bf16[8,384,384]{2,1,0:T(8,128)(2,1)}, u32[]{:S(2)}) copy-start(bf16[8,384,384]{2,1,0:T(8,128)(2,1)} %images.5) | copy-start | bytes 7077892
  11.5 1.3 copy-start.1
  12.8 0.9 copy-start.14
  16.4 1.2 copy-start.3
  18.2 28.4 %all-to-all-start = ((bf16[8,144,768]{2,1,0:T(8,128)(2,1)}), bf16[8,144,768]{2,1,0:T(8,128)(2,1)}, u32[]{:S(2)}, u32[]{:S(2)}) async-start(bf16[8,144,768]{2,1,0:T(8,128)(2,1)} %copy-done.3), calls=%async_computation | async-start | bytes 3538944 | tf_op jit(solution)/shard_map/all_to_all | solution.py:191
  23.4 117.0 %reduce-scatter.4.cloned.1.call-start = ((), (), s32[]{:S(2)}) async-start(), calls=%async_computation.6 | async-start | bytes 1966080 | tf_op jit(solution)/shard_map/reduce_scatter | solution.py:268
  53.8 1.2 copy-start.4
  55.0 1.3 copy-start.2
  61.5 1.2 copy-start.8
  62.7 25.4 %all-to-all-start.2 = ((bf16[8,128,768]{2,1,0:T(8,128)(2,1)}), bf16[8,128,768]{2,1,0:T(8,128)(2,1)}, u32[]{:S(2)}, u32[]{:S(2)}) async-start(bf16[8,128,768]{2,1,0:T(8,128)(2,1)} %copy-done.8), calls=%async_computation.4 | async-start | bytes 3145728 | tf_op jit(solution)/shard_map/all_to_all | solution.py:191
  67.0 73.4 %reduce-scatter.8.cloned.1.call-start = ((), (), s32[]{:S(2)}) async-start(), calls=%async_computation.8 | async-start | bytes 1966080 | tf_op jit(solution)/shard_map/reduce_scatter | solution.py:268
  91.2 1.2 copy-start.5
  97.6 1.2 copy-start.7
  98.8 3.8 %copy-start.18 = (s32[1,64,16]{2,1,0:T(8,128)S(1)}, s32[1,64,16]{2,1,0:T(8,128)}, u32[]{:S(2)}) copy-start(s32[1,64,16]{2,1,0:T(8,128)} %get-tuple-element.19) | copy-start | bytes 12292
  98.8 24.7 %all-to-all-start.1 = ((bf16[8,128,768]{2,1,0:T(8,128)(2,1)}), bf16[8,128,768]{2,1,0:T(8,128)(2,1)S(1)}, u32[]{:S(2)}, u32[]{:S(2)}) async-start(bf16[8,128,768]{2,1,0:T(8,128)(2,1)} %copy-done.7), calls=%async_computation.2 | async-start | bytes 3145728 | tf_op jit(solution)/shard_map/all_to_all | solution.py:191
  102.5 61.9 %reduce-scatter.6.cloned.1.call-start = ((), (), s32[]{:S(2)}) async-start(), calls=%async_computation.7 | async-start | bytes 1966080 | tf_op jit(solution)/shard_map/reduce_scatter | solution.py:268
  125.3 1.2 copy-start.6
  127.3 5.5 %collective-permute-start.2 = (s32[64,5]{0,1:T(8,128)S(1)}, s32[64,5]{0,1:T(8,128)S(1)}, u32[]{:S(2)}, u32[]{:S(2)}) collective-permute-start(s32[64,5]{0,1:T(8,128)S(1)} %multiply_add_fusion.2), channel_id=1, source_target_pairs={{0,3},{1,0},{2,1},{3,2},{4,7},{5,4},{6,5},{7,6},{8,11},{9,8},{10,9... | collective-permute-start | bytes 3848 | tf_op jit(solution)/shard_map/ppermute | solution.py:199
  131.4 4.5 %collective-permute-start.1 = (s32[64,5]{0,1:T(8,128)S(1)}, s32[64,5]{0,1:T(8,128)S(1)}, u32[]{:S(2)}, u32[]{:S(2)}) collective-permute-start(s32[64,5]{0,1:T(8,128)S(1)} %multiply_add_fusion.2), channel_id=1, source_target_pairs={{0,2},{1,3},{2,0},{3,1},{4,6},{5,7},{6,4},{7,5},{8,10},{9,11},{10,... | collective-permute-start | bytes 3848 | tf_op jit(solution)/shard_map/ppermute | solution.py:199
  131.5 5.4 %collective-permute-start = (s32[64,5]{0,1:T(8,128)S(1)}, s32[64,5]{0,1:T(8,128)S(1)}, u32[]{:S(2)}, u32[]{:S(2)}) collective-permute-start(s32[64,5]{0,1:T(8,128)S(1)} %multiply_add_fusion.2), channel_id=1, source_target_pairs={{0,1},{1,2},{2,3},{3,0},{4,5},{5,6},{6,7},{7,4},{8,9},{9,10},{10,1... | collective-permute-start | bytes 3848 | tf_op jit(solution)/shard_map/ppermute | solution.py:199
  140.2 24.2 %copy-start.17 = (bf16[48,16,768]{2,1,0:T(8,128)(2,1)S(1)}, bf16[48,16,768]{2,1,0:T(8,128)(2,1)}, u32[]{:S(2)}) copy-start(bf16[48,16,768]{2,1,0:T(8,128)(2,1)} %param.19) | copy-start | bytes 3538948
  (8 other events, 6.4 us)
Sparse Core Ops, SparseCore 0:
  55.1 35.1 reduce-scatter.3
  92.7 35.0 reduce-scatter.7
  130.1 34.2 reduce-scatter.5

commit v5 on v4

--- a/solution.py
+++ b/solution.py
@@ -10,7 +10,8 @@
 
 TAU_PRIOR = 4.0
 PHASE_OFFSET = 0.1
-CHUNKS = 3
+CHUNKS = ((2, False), (2, True), (2, False))
+SHARES = 6
 META_BASE = 32
 META_ROWS = 16
 VMEM_LIMIT = 48 * 1024 * 1024
@@ -112,28 +113,28 @@
     )
 
 
-def slab_sums(parts, place, slab_count, mirror_count):
-    def permute(block, pairs):
+def slab_sums(parts, place, slab_count, batch_count, swapped):
+    total = jnp.where(place == 3, 0.0, choose(parts, place).astype(jnp.float32))
+    for shift in range(1, slab_count):
         perm = []
-        for b in range(2 * mirror_count):
-            for source, target in pairs:
-                if b >= mirror_count:
-                    source, target = slab_count - 1 - source, slab_count - 1 - target
-                perm.append((b * slab_count + source, b * slab_count + target))
-        return lax.ppermute(block, ("batch", "slab"), perm)
-
-    near_in = permute(jnp.where(place == 2, parts[1], parts[0]), [(3, 2), (2, 1), (1, 0)])
-    out_in = permute(jnp.where(place == 0, parts[1], parts[2]), [(0, 1), (1, 2)])
-    merged = (parts[0].astype(jnp.float32) + near_in.astype(jnp.float32)).astype(jnp.bfloat16)
-    far = jnp.where(place == 0, parts[2], jnp.where(place == 3, parts[1], merged))
-    far, last = lax.optimization_barrier((far, parts[2]))
-    far_in = permute(far, [(3, 1), (2, 0), (0, 2)])
-    last_in = permute(last, [(3, 2)])
-    own = jnp.where(place == 0, parts[0], jnp.where(place == 1, parts[1], parts[2]))
-    total = jnp.where(place == 3, 0.0, own.astype(jnp.float32))
-    total = total + jnp.where(place == 2, 0.0, near_in.astype(jnp.float32))
-    total = total + out_in.astype(jnp.float32) + last_in.astype(jnp.float32)
-    return total + far_in.astype(jnp.float32)
+        for b in range(batch_count):
+            upper = (b >= batch_count // 2) != swapped
+            for source in range(slab_count):
+                target = (source + shift) % slab_count
+                if target < slab_count - 1:
+                    ends = (slab_count - 1 - source, slab_count - 1 - target)
+                    ends = ends if upper else (source, target)
+                    perm.append((b * slab_count + ends[0], b * slab_count + ends[1]))
+        block = choose(parts, (place + shift) % slab_count)
+        total = total + lax.ppermute(block, ("batch", "slab"), perm).astype(jnp.float32)
+    return total
+
+
+def choose(parts, index):
+    chosen = parts[-1]
+    for d in range(parts.shape[0] - 1):
+        chosen = jnp.where(index == d, parts[d], chosen)
+    return chosen
 
 
 def per_device(images, classes, shifts, defocus_class, defocus, run_counts, dest_map, ref):
@@ -143,8 +144,11 @@
     batch = lax.axis_index("batch")
     slab = lax.axis_index("slab")
     rows, planes, _ = ref.shape
-    each = rows // CHUNKS
-    chunk_rows = batch_count * each
+    mirrored = slab_count == 4 and batch_count % 2 == 0
+    half_batch = batch_count // 2
+    sizes = [rows * share // SHARES for share, _ in CHUNKS]
+    starts = [sum(sizes[:c]) for c in range(len(CHUNKS))]
+    swaps = [mirrored and swapped for _, swapped in CHUNKS]
     freq = jnp.arange(length, dtype=jnp.int32)
 
     ends = jnp.cumsum(run_counts, axis=1)[:, : slab_count - 1]
@@ -154,20 +158,25 @@
     digits = jnp.pad(digits, ((0, META_ROWS - particles), (0, 2 * length - 2 * fields)))
 
     cosine, minus_sine, table_right = dft_tables(length)
-    order = np.arange(length).reshape(batch_count, CHUNKS, each).transpose(1, 0, 2)
-    order = order.reshape(CHUNKS, chunk_rows)
     table_right = jnp.asarray(table_right.astype(jnp.bfloat16))
     focus = lookup(defocus, defocus_class)
     row_factors = trig_factors(shifts[:, 1], focus, freq, PHASE_OFFSET, length, 0)
     col_factors = trig_factors(shifts[:, 0], focus, freq, 0.0, length, 1)
-    row_factors = row_factors.reshape(batch_count, CHUNKS, each, 4 * particles)
-    row_factors = row_factors.transpose(1, 0, 2, 3).reshape(CHUNKS, chunk_rows, 4 * particles)
+    row_factors = row_factors.reshape(batch_count, rows, 4 * particles)
     received = []
-    for c in range(CHUNKS):
-        left = np.concatenate([cosine[order[c]], minus_sine[order[c]]], axis=0)
+    weighted = []
+    for c, each in enumerate(sizes):
+        chunk_rows = batch_count * each
+        block = np.roll(np.arange(batch_count), -half_batch if swaps[c] else 0)
+        order = (block[:, None] * rows + starts[c] + np.arange(each)[None, :]).reshape(-1)
+        left = np.concatenate([cosine[order], minus_sine[order]], axis=0)
+        factors = row_factors[:, starts[c] : starts[c] + each]
+        if swaps[c]:
+            factors = jnp.concatenate([factors[half_batch:], factors[:half_batch]], axis=0)
+        factors = factors.reshape(chunk_rows, 4 * particles)
         extra = (digits,) if c == 0 else ()
         block_rows = particles * each + META_ROWS * len(extra)
-        weighted = pl.pallas_call(
+        send = pl.pallas_call(
             spectrum_kernel,
             out_shape=jax.ShapeDtypeStruct((batch_count, block_rows, 2 * length), jnp.bfloat16),
             in_specs=whole_vmem(5 + len(extra)),
@@ -175,8 +184,8 @@
             scratch_shapes=[pltpu.VMEM((particles * chunk_rows, 2 * length), jnp.bfloat16)],
             compiler_params=pltpu.CompilerParams(vmem_limit_bytes=VMEM_LIMIT),
             cost_estimate=pl.CostEstimate(
-                flops=0,
-                bytes_accessed=0,
+                flops=2 * particles * chunk_rows * 2 * length * 3 * length,
+                bytes_accessed=6 * 1024 * 1024,
                 transcendentals=0,
             ),
             name="spectrum",
@@ -184,13 +193,14 @@
             images,
             jnp.asarray(left.astype(jnp.bfloat16)),
             table_right,
-            row_factors[c],
+            factors,
             col_factors,
             *extra,
         )
-        received.append(lax.all_to_all(weighted, "batch", 0, 0, tiled=True))
-
-    digits_in = received[0][:, particles * each : particles * (each + 1), : 2 * fields]
+        weighted.append(send)
+        received.append(lax.all_to_all(send, "batch", 0, 0, tiled=True))
+
+    digits_in = received[0][:, particles * sizes[0] : particles * (sizes[0] + 1), : 2 * fields]
     digits_in = digits_in.astype(jnp.int32).reshape(-1, 2 * fields)
     meta_layer = digits_in[:, :fields] * META_BASE + digits_in[:, fields:]
     meta_all = [meta_layer]
@@ -200,28 +210,43 @@
     meta_all = jnp.concatenate(meta_all, axis=0)
 
     class_count = dest_map.shape[0]
-    own_dest = lax.dynamic_slice_in_dim(dest_map, batch * rows, rows, 1).astype(jnp.bfloat16)
+
+    def find_planes(table, dest, freq_in):
+        class_hot = (table[:, :1] == jnp.arange(class_count)[None, :]).astype(jnp.bfloat16)
+        local_plane = jnp.dot(
+            class_hot, dest.astype(jnp.bfloat16), preferred_element_type=jnp.float32
+        )
+        past = freq_in[None, :, None] >= table[:, None, 2:]
+        return jnp.sum(past.astype(jnp.int32), axis=2), local_plane.astype(jnp.int32)
+
+    window_slabs = 3 if mirrored else slab_count
+    blocks = [(batch + half_batch) % batch_count if swap else batch for swap in swaps]
+    begins = [block * rows + start for block, start in zip(blocks, starts)]
+    dest_in = jnp.concatenate(
+        [lax.dynamic_slice_in_dim(dest_map, at, n, 1) for at, n in zip(begins, sizes)], axis=1
+    )
+    freq_in = jnp.concatenate(
+        [at + jnp.arange(n, dtype=jnp.int32) for at, n in zip(begins, sizes)]
+    )
+    owner, local_plane = find_planes(meta_layer, dest_in, freq_in)
+    places, codes = [], []
+    for c, each in enumerate(sizes):
+        here = slice(starts[c], starts[c] + each)
+        place, owner_place = slab, owner[:, here]
+        if mirrored:
+            upper = blocks[c] >= half_batch
+            owner_place = jnp.where(upper, slab_count - 1 - owner_place, owner_place)
+            place = jnp.where(upper, slab_count - 1 - slab, slab)
+        places.append(place)
+        code = owner_place * (each * planes) + jnp.arange(each)[None, :] * planes
+        code = (code + local_plane[:, here]).reshape(batch_count, particles * each)
+        if c == 0:
+            code = jnp.pad(code, ((0, 0), (0, META_ROWS)), constant_values=-1)
+        codes.append(code.reshape(1, -1))
+
     own_freq = batch * rows + jnp.arange(rows, dtype=jnp.int32)
-
-    def find_planes(table):
-        class_hot = (table[:, :1] == jnp.arange(class_count)[None, :]).astype(jnp.bfloat16)
-        local_plane = jnp.dot(class_hot, own_dest, preferred_element_type=jnp.float32)
-        past = own_freq[None, :, None] >= table[:, None, 2:]
-        return jnp.sum(past.astype(jnp.int32), axis=2), local_plane.astype(jnp.int32)
-
-    mirrored = False
-    window_slabs = 3 if mirrored else slab_count
-    owner, local_plane = find_planes(meta_layer)
-    place = slab
-    if mirrored:
-        upper = batch >= batch_count // 2
-        owner = jnp.where(upper, slab_count - 1 - owner, owner)
-        place = jnp.where(upper, slab_count - 1 - slab, slab)
-    codes = owner * (each * planes) + (jnp.arange(rows) % each)[None, :] * planes + local_plane
-    codes = codes.reshape(batch_count * particles, CHUNKS, each).transpose(1, 0, 2)
-    codes = codes.reshape(CHUNKS, batch_count, particles * each)
-
-    owner, local_plane = find_planes(meta_all)
+    own_dest = lax.dynamic_slice_in_dim(dest_map, batch * rows, rows, 1)
+    owner, local_plane = find_planes(meta_all, own_dest, own_freq)
     focus_count = defocus.shape[0]
     focus_hot = (meta_all[:, 1:2] == jnp.arange(focus_count)[None, :]).astype(jnp.bfloat16)
     own_plane = jnp.where(owner == slab, local_plane, -1)
@@ -239,16 +264,15 @@
     weights = 0.5 * (jnp.sum(counts, axis=2, keepdims=True) - double)
     denom = weights + TAU_PRIOR
 
-    bins = each * planes
     sums = []
-    for c in range(CHUNKS):
+    for c, each in enumerate(sizes):
+        bins = each * planes
         rows_in = received[c].reshape(-1, 2 * length)
         codes_in = codes[c]
-        if c == 0:
-            codes_in = jnp.pad(codes_in, ((0, 0), (0, META_ROWS)), constant_values=-1)
-        codes_in = codes_in.reshape(1, -1)
-        if c > 0 and mirrored:
-            codes_in, sums[-1] = lax.optimization_barrier((codes_in, sums[-1]))
+        if c + 1 < len(sizes):
+            codes_in, _ = lax.optimization_barrier((codes_in, weighted[c + 1]))
+        if c > 1:
+            codes_in, sums[c - 2] = lax.optimization_barrier((codes_in, sums[c - 2]))
         parts = pl.pallas_call(
             insert_kernel,
             out_shape=jax.ShapeDtypeStruct((window_slabs, bins, 2 * length), jnp.bfloat16),
@@ -256,19 +280,23 @@
             out_specs=pl.BlockSpec(memory_space=pltpu.VMEM),
             compiler_params=pltpu.CompilerParams(vmem_limit_bytes=VMEM_LIMIT),
             cost_estimate=pl.CostEstimate(
-                flops=0,
-                bytes_accessed=0,
+                flops=2 * bins * window_slabs * rows_in.shape[0] * 2 * length,
+                bytes_accessed=4 * 1024 * 1024,
                 transcendentals=0,
             ),
             name="insert",
         )(rows_in, codes_in)
         if mirrored:
-            sums.append(slab_sums(parts, place, slab_count, batch_count // 2))
+            total = slab_sums(parts, places[c], slab_count, batch_count, swaps[c])
+            if swaps[c]:
+                over = [(b, (b + half_batch) % batch_count) for b in range(batch_count)]
+                total = lax.ppermute(total.astype(jnp.bfloat16), "batch", over)
+            sums.append(total)
         else:
             sums.append(lax.psum_scatter(parts, "slab", scatter_dimension=0, tiled=False))
     updated = []
-    for c in range(CHUNKS):
-        here = slice(c * each, (c + 1) * each)
+    for c, each in enumerate(sizes):
+        here = slice(starts[c], starts[c] + each)
         prior = ref[here].astype(jnp.float32)
         under = denom[here]
         total = sums[c].astype(jnp.float32).reshape(each, planes, 2 * length)

time: 175 us -> 168 us (0.960)
  the two profiles are of different devices: /device:TPU:0 before, /device:TPU:11 now
where the time goes in v5:
time: 168 us; the launch traced here: 167 us
  waiting for transfers between devices  71.4 us (43%)
  starting transfers between devices  45.8 us (27%)
  Pallas kernels  17.4 us (10%)
  local copies, waits for them, and re-layouts  16 us (10%)
  other arithmetic  11.6 us (7%)
  matrix products  4.09 us (2%)
    ppermute x9, waiting for transfers between devices, slab_sums(): lax.ppermute(block, ('batch', 'slab'), perm).astype(jnp.float32)  53.7 us
    ppermute x9, starting transfers between devices, slab_sums(): lax.ppermute(block, ('batch', 'slab'), perm).astype(jnp.float32)  25.1 us
    all_to_all x3, waiting for transfers between devices, per_device(): received.append(lax.all_to_all(send, 'batch', 0, 0, tiled=True))  17.6 us
    all_to_all x3, starting transfers between devices, per_device(): received.append(lax.all_to_all(send, 'batch', 0, 0, tiled=True))  15.4 us
    pallas_call x3, Pallas kernels, per_device(): pl.pallas_call(spectrum_kernel, out_shape=jax.ShapeDtypeStruct((batch_cou...  11.5 us
    unnamed x34, local copies, waits for them, and re-layouts  9.17 us
    pallas_call x3, Pallas kernels, per_device(): pl.pallas_call(insert_kernel, out_shape=jax.ShapeDtypeStruct((window_slab...  5.87 us
    ppermute x3, starting transfers between devices, per_device(): meta_all.append(lax.ppermute(meta_layer, 'slab', ring))  3.83 us
  transfers between devices with their start and end apart: 16, of which 7 were waited for; matrix products, arithmetic and copies ran while one was open for 12% of the time, Pallas kernels for 8%

profile of v5, /device:TPU:11, one launch (start us, length us, event | category | flops | bytes accessed | tf_op | source)
XLA Modules:
  0.0 166.6 jit_solution(920394781409510284)
XLA Ops:
  6.7 3.9 %spectrum.3 = bf16[8,144,768]{2,1,0:T(8,128)(2,1)} custom-call(bf16[8,384,384]{2,1,0:T(8,128)(2,1)S(1)} %copy-done.2, bf16[256,384]{1,0:T(8,128)(2,1)S(1)} %copy-done.7, bf16[768,768]{1,0:T(8,128)(2,1)S(1)} %copy-done.4, f32[128,32]{1,0:T(8,128)S(1)} %bitcast.77, f32[32,384]{1,0:T(8,128)S(1)} %pad_maximum_fusion.3.col_factors, ...), custom_call_target="tpu_custom_call" | custom-call | flops 1811939328 | bytes 6291456 | tf_op jit(solution)/shard_map/spectrum/pallas_call | solution.py:179
  10.6 4.6 %all-to-all-start = ((bf16[8,144,768]{2,1,0:T(8,128)(2,1)}), bf16[8,144,768]{2,1,0:T(8,128)(2,1)S(1)}, u32[]{:S(2)}, u32[]{:S(2)}) async-start(bf16[8,144,768]{2,1,0:T(8,128)(2,1)} %spectrum.3), calls=%async_computation | async-start | bytes 3538944 | tf_op jit(solution)/shard_map/all_to_all | solution.py:201
  15.9 2.6 %constant_dynamic-slice_fusion.2 = (s32[768,16]{1,0:T(8,128)}, s32[768,16]{1,0:T(8,128)}, s32[768,16]{1,0:T(8,128)}) fusion(s32[768,384]{1,0:T(8,128)} %param.18, s32[]{:T(128)S(6)} %select_n.354, s32[]{:T(128)S(6)} %select_n.355, s32[]{:T(128)S(6)} %select_n.356), kind=kLoop, calls=%fused_computation.150 | loop fusion | bytes 294924 | tf_op jit(solution)/shard_map/dynamic_slice | solution.py:226
  23.8 1.7 copy-done.3
  25.5 3.8 %spectrum.5 = bf16[8,128,768]{2,1,0:T(8,128)(2,1)} custom-call(bf16[8,384,384]{2,1,0:T(8,128)(2,1)S(1)} %copy-done.3, bf16[256,384]{1,0:T(8,128)(2,1)S(1)} %copy-done.6, bf16[768,768]{1,0:T(8,128)(2,1)S(1)} %copy-done.4, f32[128,32]{1,0:T(8,128)S(1)} %bitcast.76, f32[32,384]{1,0:T(8,128)S(1)} %pad_maximum_fusion.3.col_factors), custom_call_target="tpu_custom_call" | custom-call | flops 1811939328 | bytes 6291456 | tf_op jit(solution)/shard_map/spectrum/pallas_call | solution.py:179
  29.3 3.8 %spectrum.4 = bf16[8,128,768]{2,1,0:T(8,128)(2,1)} custom-call(bf16[8,384,384]{2,1,0:T(8,128)(2,1)S(1)} %copy-done.3, bf16[256,384]{1,0:T(8,128)(2,1)S(1)} %copy-done.5, bf16[768,768]{1,0:T(8,128)(2,1)S(1)} %copy-done.4, f32[128,32]{1,0:T(8,128)S(1)} %bitcast.78, f32[32,384]{1,0:T(8,128)S(1)} %pad_maximum_fusion.3.col_factors), custom_call_target="tpu_custom_call" | custom-call | flops 1811939328 | bytes 6291456 | tf_op jit(solution)/shard_map/spectrum/pallas_call | solution.py:179
  33.8 2.9 %all-to-all-done = bf16[8,144,768]{2,1,0:T(8,128)(2,1)S(1)} async-done(((bf16[8,144,768]{2,1,0:T(8,128)(2,1)}), bf16[8,144,768]{2,1,0:T(8,128)(2,1)S(1)}, u32[]{:S(2)}, u32[]{:S(2)}) %all-to-all-start) | async-done | bytes 1769504 | tf_op jit(solution)/shard_map/all_to_all | solution.py:201
  36.7 5.1 %all-to-all-start.1 = ((bf16[8,128,768]{2,1,0:T(8,128)(2,1)}), bf16[8,128,768]{2,1,0:T(8,128)(2,1)S(1)}, u32[]{:S(2)}, u32[]{:S(2)}) async-start(bf16[8,128,768]{2,1,0:T(8,128)(2,1)} %spectrum.4), calls=%async_computation.1 | async-start | bytes 3145728 | tf_op jit(solution)/shard_map/all_to_all | solution.py:201
  46.5 14.8 %all-to-all-done.1 = bf16[8,128,768]{2,1,0:T(8,128)(2,1)S(1)} async-done(((bf16[8,128,768]{2,1,0:T(8,128)(2,1)}), bf16[8,128,768]{2,1,0:T(8,128)(2,1)S(1)}, u32[]{:S(2)}, u32[]{:S(2)}) %all-to-all-start.1) | async-done | bytes 1572896 | tf_op jit(solution)/shard_map/all_to_all | solution.py:201
  61.2 5.8 %all-to-all-start.2 = ((bf16[8,128,768]{2,1,0:T(8,128)(2,1)}), bf16[8,128,768]{2,1,0:T(8,128)(2,1)}, u32[]{:S(2)}, u32[]{:S(2)}) async-start(bf16[8,128,768]{2,1,0:T(8,128)(2,1)} %spectrum.5), calls=%async_computation.2 | async-start | bytes 3145728 | tf_op jit(solution)/shard_map/all_to_all | solution.py:201
  70.9 5.0 %collective-permute-start.7 = (bf16[256,768]{1,0:T(8,128)(2,1)}, bf16[256,768]{1,0:T(8,128)(2,1)}, u32[]{:S(2)}, u32[]{:S(2)}) collective-permute-start(bf16[256,768]{1,0:T(8,128)(2,1)} %get-tuple-element.21), channel_id=1, source_target_pairs={{3,1},{1,3},{0,2},{7,5},{5,7},{4,6},{11,9},{9,11},{8,10},{15,13},{... | collective-permute-start | bytes 1179656 | tf_op jit(solution)/shard_map/ppermute | solution.py:129
  77.7 1.7 %insert.3 = bf16[3,256,768]{2,1,0:T(8,128)(2,1)S(1)} custom-call(bf16[1152,768]{1,0:T(8,128)(2,1)S(1)} %bitcast.74, s32[1,1152]{1,0:T(1,128)S(1)} %reshape.284.codes), custom_call_target="tpu_custom_call" | custom-call | flops 1358954496 | bytes 4194304 | tf_op jit(solution)/shard_map/insert/pallas_call | solution.py:276
  80.7 1.9 %collective-permute-start = (bf16[256,768]{1,0:T(8,128)(2,1)}, bf16[256,768]{1,0:T(8,128)(2,1)S(1)}, u32[]{:S(2)}, u32[]{:S(2)}) collective-permute-start(bf16[256,768]{1,0:T(8,128)(2,1)} %get-tuple-element.25), channel_id=1, source_target_pairs={{0,1},{1,2},{3,0},{4,5},{5,6},{7,4},{8,9},{9,10},{11,8},{12,13},{1... | collective-permute-start | bytes 1179656 | tf_op jit(solution)/shard_map/ppermute | solution.py:129
  83.9 4.4 %collective-permute-start.2 = (bf16[256,768]{1,0:T(8,128)(2,1)}, bf16[256,768]{1,0:T(8,128)(2,1)S(1)}, u32[]{:S(2)}, u32[]{:S(2)}) collective-permute-start(bf16[256,768]{1,0:T(8,128)(2,1)} %get-tuple-element.26), channel_id=1, source_target_pairs={{1,0},{2,1},{3,2},{5,4},{6,5},{7,6},{9,8},{10,9},{11,10},{13,12},{... | collective-permute-start | bytes 1179656 | tf_op jit(solution)/shard_map/ppermute | solution.py:129
  90.6 1.9 %fusion.1 = f32[48,16,384]{2,1,0:T(8,128)S(1)} fusion(f32[48,16]{1,0:T(8,128)S(1)} %get-tuple-element.33, f32[48,16,16]{2,1,0:T(8,128)S(1)} %get-tuple-element.32, f32[48,16,16]{2,1,0:T(8,128)S(1)} %get-tuple-element.31, f32[16,384]{1,0:T(8,128)} %get-tuple-element.52, f32[16,384]{1,0:T(8,128)} %get-tuple-element.51), kind=kOutput, calls=%fused_computation.2 | convolution fusion | flops 114167808 | bytes 1330176 | tf_op jit(solution)/shard_map/kzd,dx->kzx/dot_general | solution.py:263
  92.5 25.0 %collective-permute-done = bf16[256,768]{1,0:T(8,128)(2,1)S(1)} collective-permute-done((bf16[256,768]{1,0:T(8,128)(2,1)}, bf16[256,768]{1,0:T(8,128)(2,1)S(1)}, u32[]{:S(2)}, u32[]{:S(2)}) %collective-permute-start) | collective-permute-done | bytes 393248 | tf_op jit(solution)/shard_map/ppermute | solution.py:129
  117.6 4.0 %collective-permute-start.8 = (bf16[256,768]{1,0:T(8,128)(2,1)}, bf16[256,768]{1,0:T(8,128)(2,1)}, u32[]{:S(2)}, u32[]{:S(2)}) collective-permute-start(bf16[256,768]{1,0:T(8,128)(2,1)} %get-tuple-element.20), channel_id=1, source_target_pairs={{2,3},{1,2},{0,1},{6,7},{5,6},{4,5},{10,11},{9,10},{8,9},{14,15},{... | collective-permute-start | bytes 1179656 | tf_op jit(solution)/shard_map/ppermute | solution.py:129
  121.6 4.5 %collective-permute-done.2 = bf16[256,768]{1,0:T(8,128)(2,1)S(1)} collective-permute-done((bf16[256,768]{1,0:T(8,128)(2,1)}, bf16[256,768]{1,0:T(8,128)(2,1)S(1)}, u32[]{:S(2)}, u32[]{:S(2)}) %collective-permute-start.2) | collective-permute-done | bytes 393248 | tf_op jit(solution)/shard_map/ppermute | solution.py:129
  127.2 2.8 %insert.5 = bf16[3,256,768]{2,1,0:T(8,128)(2,1)S(1)} custom-call(bf16[1024,768]{1,0:T(8,128)(2,1)} %bitcast.27.received, s32[1,1024]{1,0:T(1,128)S(1)} %reshape_reshape.6.codes), custom_call_target="tpu_custom_call" | custom-call | flops 1207959552 | bytes 4194304 | tf_op jit(solution)/shard_map/insert/pallas_call | solution.py:276
  130.1 1.9 %collective-permute-start.10 = (bf16[256,768]{1,0:T(8,128)(2,1)S(1)}, bf16[256,768]{1,0:T(8,128)(2,1)S(1)}, u32[]{:S(2)}, u32[]{:S(2)}) collective-permute-start(bf16[256,768]{1,0:T(8,128)(2,1)S(1)} %get-tuple-element.22), channel_id=1, source_target_pairs={{0,1},{1,2},{3,0},{4,5},{5,6},{7,4},{8,9},{9,10},{11,8},{12,13},{1... | collective-permute-start | bytes 1179656 | tf_op jit(solution)/shard_map/ppermute | solution.py:129
  133.4 4.0 %collective-permute-start.12 = (bf16[256,768]{1,0:T(8,128)(2,1)S(1)}, bf16[256,768]{1,0:T(8,128)(2,1)S(1)}, u32[]{:S(2)}, u32[]{:S(2)}) collective-permute-start(bf16[256,768]{1,0:T(8,128)(2,1)S(1)} %get-tuple-element.23), channel_id=1, source_target_pairs={{1,0},{2,1},{3,2},{5,4},{6,5},{7,6},{9,8},{10,9},{11,10},{13,12},{... | collective-permute-start | bytes 1179656 | tf_op jit(solution)/shard_map/ppermute | solution.py:129
  140.4 1.9 %collective-permute-done.10 = bf16[256,768]{1,0:T(8,128)(2,1)S(1)} collective-permute-done((bf16[256,768]{1,0:T(8,128)(2,1)S(1)}, bf16[256,768]{1,0:T(8,128)(2,1)S(1)}, u32[]{:S(2)}, u32[]{:S(2)}) %collective-permute-start.10) | collective-permute-done | bytes 393248 | tf_op jit(solution)/shard_map/ppermute | solution.py:129
  142.4 4.3 %collective-permute-done.11 = bf16[256,768]{1,0:T(8,128)(2,1)S(1)} collective-permute-done((bf16[256,768]{1,0:T(8,128)(2,1)S(1)}, bf16[256,768]{1,0:T(8,128)(2,1)S(1)}, u32[]{:S(2)}, u32[]{:S(2)}) %collective-permute-start.11) | collective-permute-done | bytes 393248 | tf_op jit(solution)/shard_map/ppermute | solution.py:129
  146.6 18.0 %collective-permute-done.12 = bf16[256,768]{1,0:T(8,128)(2,1)S(1)} collective-permute-done((bf16[256,768]{1,0:T(8,128)(2,1)S(1)}, bf16[256,768]{1,0:T(8,128)(2,1)S(1)}, u32[]{:S(2)}, u32[]{:S(2)}) %collective-permute-start.12) | collective-permute-done | bytes 393248 | tf_op jit(solution)/shard_map/ppermute | solution.py:129
  (114 shorter events, 35.9 us)
Async XLA Ops:
  0.0 5.0 %copy-start.4 = (bf16[768,768]{1,0:T(8,128)(2,1)S(1)}, bf16[768,768]{1,0:T(8,128)(2,1)}, u32[]{:S(2)}) copy-start(bf16[768,768]{1,0:T(8,128)(2,1)} %constant.196.clone.right) | copy-start | bytes 3538948
  0.0 5.0 %copy-start.7 = (bf16[256,384]{1,0:T(8,128)(2,1)S(1)}, bf16[256,384]{1,0:T(8,128)(2,1)}, u32[]{:S(2)}) copy-start(bf16[256,384]{1,0:T(8,128)(2,1)} %constant.197.clone.left) | copy-start | bytes 589828
  10.6 26.1 %all-to-all-start = ((bf16[8,144,768]{2,1,0:T(8,128)(2,1)}), bf16[8,144,768]{2,1,0:T(8,128)(2,1)S(1)}, u32[]{:S(2)}, u32[]{:S(2)}) async-start(bf16[8,144,768]{2,1,0:T(8,128)(2,1)} %spectrum.3), calls=%async_computation | async-start | bytes 3538944 | tf_op jit(solution)/shard_map/all_to_all | solution.py:201
  18.5 5.3 %copy-start.6 = (bf16[256,384]{1,0:T(8,128)(2,1)S(1)}, bf16[256,384]{1,0:T(8,128)(2,1)}, u32[]{:S(2)}) copy-start(bf16[256,384]{1,0:T(8,128)(2,1)} %constant.199.clone.left) | copy-start | bytes 589828
  33.8 12.1 %copy-start.11 = (bf16[768,16]{0,1:T(8,128)(2,1)S(1)}, bf16[768,16]{0,1:T(8,128)(2,1)}, u32[]{:S(2)}) copy-start(bf16[768,16]{0,1:T(8,128)(2,1)} %convert.20) | copy-start | bytes 73732
  33.8 12.1 %copy-start.12 = (bf16[768,16]{0,1:T(8,128)(2,1)S(1)}, bf16[768,16]{0,1:T(8,128)(2,1)}, u32[]{:S(2)}) copy-start(bf16[768,16]{0,1:T(8,128)(2,1)} %convert.21) | copy-start | bytes 73732
  36.7 5.1 %copy-start = (bf16[8,144,768]{2,1,0:T(8,128)(2,1)}, bf16[8,144,768]{2,1,0:T(8,128)(2,1)S(1)}, u32[]{:S(2)}) copy-start(bf16[8,144,768]{2,1,0:T(8,128)(2,1)S(1)} %all-to-all-done) | copy-start | bytes 5308420
  36.7 24.5 %all-to-all-start.1 = ((bf16[8,128,768]{2,1,0:T(8,128)(2,1)}), bf16[8,128,768]{2,1,0:T(8,128)(2,1)S(1)}, u32[]{:S(2)}, u32[]{:S(2)}) async-start(bf16[8,128,768]{2,1,0:T(8,128)(2,1)} %spectrum.4), calls=%async_computation.1 | async-start | bytes 3145728 | tf_op jit(solution)/shard_map/all_to_all | solution.py:201
  42.0 38.6 %collective-permute-start.3 = (s32[64,5]{0,1:T(8,128)S(1)}, s32[64,5]{0,1:T(8,128)S(1)}, u32[]{:S(2)}, u32[]{:S(2)}) collective-permute-start(s32[64,5]{0,1:T(8,128)S(1)} %multiply_add_fusion.1), channel_id=1, source_target_pairs={{0,1},{1,2},{2,3},{3,0},{4,5},{5,6},{6,7},{7,4},{8,9},{9,10},{10,1... | collective-permute-start | bytes 3848 | tf_op jit(solution)/shard_map/ppermute | solution.py:209
  43.4 39.2 %collective-permute-start.4 = (s32[64,5]{0,1:T(8,128)S(1)}, s32[64,5]{0,1:T(8,128)S(1)}, u32[]{:S(2)}, u32[]{:S(2)}) collective-permute-start(s32[64,5]{0,1:T(8,128)S(1)} %multiply_add_fusion.1), channel_id=1, source_target_pairs={{0,2},{1,3},{2,0},{3,1},{4,6},{5,7},{6,4},{7,5},{8,10},{9,11},{10,... | collective-permute-start | bytes 3848 | tf_op jit(solution)/shard_map/ppermute | solution.py:209
  44.5 39.4 %collective-permute-start.5 = (s32[64,5]{0,1:T(8,128)S(1)}, s32[64,5]{0,1:T(8,128)S(1)}, u32[]{:S(2)}, u32[]{:S(2)}) collective-permute-start(s32[64,5]{0,1:T(8,128)S(1)} %multiply_add_fusion.1), channel_id=1, source_target_pairs={{0,3},{1,0},{2,1},{3,2},{4,7},{5,4},{6,5},{7,6},{8,11},{9,8},{10,9... | collective-permute-start | bytes 3848 | tf_op jit(solution)/shard_map/ppermute | solution.py:209
  61.2 66.0 %all-to-all-start.2 = ((bf16[8,128,768]{2,1,0:T(8,128)(2,1)}), bf16[8,128,768]{2,1,0:T(8,128)(2,1)}, u32[]{:S(2)}, u32[]{:S(2)}) async-start(bf16[8,128,768]{2,1,0:T(8,128)(2,1)} %spectrum.5), calls=%async_computation.2 | async-start | bytes 3145728 | tf_op jit(solution)/shard_map/all_to_all | solution.py:201
  69.6 63.8 %collective-permute-start.6 = (bf16[256,768]{1,0:T(8,128)(2,1)}, bf16[256,768]{1,0:T(8,128)(2,1)}, u32[]{:S(2)}, u32[]{:S(2)}) collective-permute-start(bf16[256,768]{1,0:T(8,128)(2,1)} %get-tuple-element.19), channel_id=1, source_target_pairs={{3,2},{2,1},{0,3},{7,6},{6,5},{4,7},{11,10},{10,9},{8,11},{15,14},... | collective-permute-start | bytes 1179656 | tf_op jit(solution)/shard_map/ppermute | solution.py:129
  70.9 66.5 %collective-permute-start.7 = (bf16[256,768]{1,0:T(8,128)(2,1)}, bf16[256,768]{1,0:T(8,128)(2,1)}, u32[]{:S(2)}, u32[]{:S(2)}) collective-permute-start(bf16[256,768]{1,0:T(8,128)(2,1)} %get-tuple-element.21), channel_id=1, source_target_pairs={{3,1},{1,3},{0,2},{7,5},{5,7},{4,6},{11,9},{9,11},{8,10},{15,13},{... | collective-permute-start | bytes 1179656 | tf_op jit(solution)/shard_map/ppermute | solution.py:129
  80.7 36.9 %collective-permute-start = (bf16[256,768]{1,0:T(8,128)(2,1)}, bf16[256,768]{1,0:T(8,128)(2,1)S(1)}, u32[]{:S(2)}, u32[]{:S(2)}) collective-permute-start(bf16[256,768]{1,0:T(8,128)(2,1)} %get-tuple-element.25), channel_id=1, source_target_pairs={{0,1},{1,2},{3,0},{4,5},{5,6},{7,4},{8,9},{9,10},{11,8},{12,13},{1... | collective-permute-start | bytes 1179656 | tf_op jit(solution)/shard_map/ppermute | solution.py:129
  82.6 38.9 %collective-permute-start.1 = (bf16[256,768]{1,0:T(8,128)(2,1)}, bf16[256,768]{1,0:T(8,128)(2,1)S(1)}, u32[]{:S(2)}, u32[]{:S(2)}) collective-permute-start(bf16[256,768]{1,0:T(8,128)(2,1)} %get-tuple-element.27), channel_id=1, source_target_pairs={{0,2},{2,0},{3,1},{4,6},{6,4},{7,5},{8,10},{10,8},{11,9},{12,14},{... | collective-permute-start | bytes 1179656 | tf_op jit(solution)/shard_map/ppermute | solution.py:129
  83.9 42.1 %collective-permute-start.2 = (bf16[256,768]{1,0:T(8,128)(2,1)}, bf16[256,768]{1,0:T(8,128)(2,1)S(1)}, u32[]{:S(2)}, u32[]{:S(2)}) collective-permute-start(bf16[256,768]{1,0:T(8,128)(2,1)} %get-tuple-element.26), channel_id=1, source_target_pairs={{1,0},{2,1},{3,2},{5,4},{6,5},{7,6},{9,8},{10,9},{11,10},{13,12},{... | collective-permute-start | bytes 1179656 | tf_op jit(solution)/shard_map/ppermute | solution.py:129
  117.6 19.8 %collective-permute-start.8 = (bf16[256,768]{1,0:T(8,128)(2,1)}, bf16[256,768]{1,0:T(8,128)(2,1)}, u32[]{:S(2)}, u32[]{:S(2)}) collective-permute-start(bf16[256,768]{1,0:T(8,128)(2,1)} %get-tuple-element.20), channel_id=1, source_target_pairs={{2,3},{1,2},{0,1},{6,7},{5,6},{4,5},{10,11},{9,10},{8,9},{14,15},{... | collective-permute-start | bytes 1179656 | tf_op jit(solution)/shard_map/ppermute | solution.py:129
  130.1 12.2 %collective-permute-start.10 = (bf16[256,768]{1,0:T(8,128)(2,1)S(1)}, bf16[256,768]{1,0:T(8,128)(2,1)S(1)}, u32[]{:S(2)}, u32[]{:S(2)}) collective-permute-start(bf16[256,768]{1,0:T(8,128)(2,1)S(1)} %get-tuple-element.22), channel_id=1, source_target_pairs={{0,1},{1,2},{3,0},{4,5},{5,6},{7,4},{8,9},{9,10},{11,8},{12,13},{1... | collective-permute-start | bytes 1179656 | tf_op jit(solution)/shard_map/ppermute | solution.py:129
  132.1 14.6 %collective-permute-start.11 = (bf16[256,768]{1,0:T(8,128)(2,1)S(1)}, bf16[256,768]{1,0:T(8,128)(2,1)S(1)}, u32[]{:S(2)}, u32[]{:S(2)}) collective-permute-start(bf16[256,768]{1,0:T(8,128)(2,1)S(1)} %get-tuple-element.24), channel_id=1, source_target_pairs={{0,2},{2,0},{3,1},{4,6},{6,4},{7,5},{8,10},{10,8},{11,9},{12,14},{... | collective-permute-start | bytes 1179656 | tf_op jit(solution)/shard_map/ppermute | solution.py:129
  133.4 31.3 %collective-permute-start.12 = (bf16[256,768]{1,0:T(8,128)(2,1)S(1)}, bf16[256,768]{1,0:T(8,128)(2,1)S(1)}, u32[]{:S(2)}, u32[]{:S(2)}) collective-permute-start(bf16[256,768]{1,0:T(8,128)(2,1)S(1)} %get-tuple-element.23), channel_id=1, source_target_pairs={{1,0},{2,1},{3,2},{5,4},{6,5},{7,6},{9,8},{10,9},{11,10},{13,12},{... | collective-permute-start | bytes 1179656 | tf_op jit(solution)/shard_map/ppermute | solution.py:129
  139.0 26.0 %collective-permute-start.9 = (bf16[256,768]{1,0:T(8,128)(2,1)S(1)}, bf16[256,768]{1,0:T(8,128)(2,1)S(1)}, u32[]{:S(2)}, u32[]{:S(2)}) collective-permute-start(bf16[256,768]{1,0:T(8,128)(2,1)S(1)} %fusion.10), channel_id=1, source_target_pairs={{0,16},{4,20},{8,24},{12,28},{16,0},{20,4},{24,8},{28,12},{1,17},{... | collective-permute-start | bytes 1179656 | tf_op jit(solution)/shard_map/ppermute | solution.py:293
  140.4 24.6 %copy-start.8 = (f32[256,768]{1,0:T(8,128)S(1)}, f32[256,768]{1,0:T(8,128)}, u32[]{:S(2)}) copy-start(f32[256,768]{1,0:T(8,128)} %fusion.12) | copy-start | bytes 2359300
  140.4 24.6 %copy-start.9 = (bf16[48,16,768]{2,1,0:T(8,128)(2,1)S(1)}, bf16[48,16,768]{2,1,0:T(8,128)(2,1)}, u32[]{:S(2)}) copy-start(bf16[48,16,768]{2,1,0:T(8,128)(2,1)} %param.19) | copy-start | bytes 3538948
  (6 other events, 18.3 us)

commit v6 on v5

--- a/solution.py
+++ b/solution.py
@@ -1,3 +1,4 @@
+import functools
 import math
 
 import jax
@@ -14,6 +15,7 @@
 SHARES = 6
 META_BASE = 32
 META_ROWS = 16
+LANES = 128
 VMEM_LIMIT = 48 * 1024 * 1024
 
 
@@ -30,12 +32,12 @@
     return cosine, -sine, table_right
 
 
-def spectrum_kernel(images, left, right, row_factors, col_factors, *rest):
+def spectrum_kernel(runs, images, left, right, row_factors, col_factors, *rest):
     *meta, out, joined = rest
     particles, length = images.shape[0], images.shape[1]
     owners = out.shape[0]
-    rows = row_factors.shape[0]
-    rows_each = rows // owners
+    rows_each = runs[0][1] - runs[0][0]
+    rows = owners * rows_each
     for block in meta:
         for d in range(owners):
             out[d, particles * rows_each :, :] = block[...]
@@ -45,7 +47,7 @@
         section = section.astype(jnp.bfloat16)
         joined[p * rows : (p + 1) * rows, :length] = section[:rows]
         joined[p * rows : (p + 1) * rows, length:] = section[rows:]
-    factors = row_factors[...]
+    factors = jnp.concatenate([row_factors[begin:end, :] for begin, end in runs], axis=0)
     for first in range(0, particles, 2):
         spectrum = jnp.dot(
             joined[first * rows : (first + 2) * rows, :],
@@ -75,14 +77,26 @@
             )
 
 
-def insert_kernel(received, codes, out):
-    windows, bins, _ = out.shape
-    rows = received[...]
+def insert_kernel(bins, meta_at, received, codes, out):
+    sources = received.shape[0]
+    rows = received[...].reshape(-1, received.shape[2])
     codes_all = codes[...]
-    for k in range(windows):
+    for k in range(out.shape[0]):
         bin_index = lax.broadcasted_iota(jnp.int32, (bins, 1), 0) + k * bins
         hot = jnp.where(codes_all == bin_index, 1.0, 0.0).astype(jnp.bfloat16)
-        out[k] = jnp.dot(hot, rows, preferred_element_type=jnp.float32).astype(out.dtype)
+        total = jnp.dot(hot, rows, preferred_element_type=jnp.float32)
+        out[k, :bins, :] = total.astype(out.dtype)
+        if out.shape[1] > bins:
+            tiles = out.shape[2] // LANES
+            first_half = lax.broadcasted_iota(jnp.int32, (META_ROWS, LANES), 0) < META_ROWS // 2
+            for i in range(min(sources, tiles)):
+                low = received[i, meta_at : meta_at + META_ROWS, :LANES]
+                if i + tiles < sources:
+                    high = received[i + tiles, meta_at : meta_at + META_ROWS, :LANES]
+                    low = jnp.where(
+                        first_half, low.astype(jnp.float32), high.astype(jnp.float32)
+                    ).astype(low.dtype)
+                out[k, bins:, i * LANES : (i + 1) * LANES] = low
 
 
 def whole_vmem(count):
@@ -113,8 +127,8 @@
     )
 
 
-def slab_sums(parts, place, slab_count, batch_count, swapped):
-    total = jnp.where(place == 3, 0.0, choose(parts, place).astype(jnp.float32))
+def slab_exchange(parts, place, slab_count, batch_count, swapped):
+    arrived = []
     for shift in range(1, slab_count):
         perm = []
         for b in range(batch_count):
@@ -126,8 +140,8 @@
                     ends = ends if upper else (source, target)
                     perm.append((b * slab_count + ends[0], b * slab_count + ends[1]))
         block = choose(parts, (place + shift) % slab_count)
-        total = total + lax.ppermute(block, ("batch", "slab"), perm).astype(jnp.float32)
-    return total
+        arrived.append(lax.ppermute(block, ("batch", "slab"), perm))
+    return arrived
 
 
 def choose(parts, index):
@@ -144,7 +158,8 @@
     batch = lax.axis_index("batch")
     slab = lax.axis_index("slab")
     rows, planes, _ = ref.shape
-    mirrored = slab_count == 4 and batch_count % 2 == 0
+    mirrored = slab_count == 4 and batch_count % 2 == 0 and 2 * particles <= META_ROWS
+    mirrored = mirrored and batch_count * LANES <= 4 * length
     half_batch = batch_count // 2
     sizes = [rows * share // SHARES for share, _ in CHUNKS]
     starts = [sum(sizes[:c]) for c in range(len(CHUNKS))]
@@ -155,14 +170,14 @@
     meta = jnp.concatenate([classes[:, None], defocus_class[:, None], ends], axis=1)
     fields = meta.shape[1]
     digits = jnp.concatenate([meta // META_BASE, meta % META_BASE], axis=1).astype(jnp.bfloat16)
-    digits = jnp.pad(digits, ((0, META_ROWS - particles), (0, 2 * length - 2 * fields)))
+    digits = jnp.concatenate([digits] * (META_ROWS // particles), axis=0)
+    digits = jnp.pad(digits, ((0, META_ROWS - len(digits)), (0, 2 * length - 2 * fields)))
 
     cosine, minus_sine, table_right = dft_tables(length)
     table_right = jnp.asarray(table_right.astype(jnp.bfloat16))
     focus = lookup(defocus, defocus_class)
     row_factors = trig_factors(shifts[:, 1], focus, freq, PHASE_OFFSET, length, 0)
     col_factors = trig_factors(shifts[:, 0], focus, freq, 0.0, length, 1)
-    row_factors = row_factors.reshape(batch_count, rows, 4 * particles)
     received = []
     weighted = []
     for c, each in enumerate(sizes):
@@ -170,22 +185,19 @@
         block = np.roll(np.arange(batch_count), -half_batch if swaps[c] else 0)
         order = (block[:, None] * rows + starts[c] + np.arange(each)[None, :]).reshape(-1)
         left = np.concatenate([cosine[order], minus_sine[order]], axis=0)
-        factors = row_factors[:, starts[c] : starts[c] + each]
-        if swaps[c]:
-            factors = jnp.concatenate([factors[half_batch:], factors[:half_batch]], axis=0)
-        factors = factors.reshape(chunk_rows, 4 * particles)
+        runs = [(k * rows + starts[c], k * rows + starts[c] + each) for k in block.tolist()]
         extra = (digits,) if c == 0 else ()
         block_rows = particles * each + META_ROWS * len(extra)
         send = pl.pallas_call(
-            spectrum_kernel,
+            functools.partial(spectrum_kernel, runs),
             out_shape=jax.ShapeDtypeStruct((batch_count, block_rows, 2 * length), jnp.bfloat16),
             in_specs=whole_vmem(5 + len(extra)),
             out_specs=pl.BlockSpec(memory_space=pltpu.VMEM),
             scratch_shapes=[pltpu.VMEM((particles * chunk_rows, 2 * length), jnp.bfloat16)],
             compiler_params=pltpu.CompilerParams(vmem_limit_bytes=VMEM_LIMIT),
             cost_estimate=pl.CostEstimate(
-                flops=2 * particles * chunk_rows * 2 * length * 3 * length,
-                bytes_accessed=6 * 1024 * 1024,
+                flops=0,
+                bytes_accessed=0,
                 transcendentals=0,
             ),
             name="spectrum",
@@ -193,21 +205,19 @@
             images,
             jnp.asarray(left.astype(jnp.bfloat16)),
             table_right,
-            factors,
+            row_factors,
             col_factors,
             *extra,
         )
         weighted.append(send)
         received.append(lax.all_to_all(send, "batch", 0, 0, tiled=True))
 
-    digits_in = received[0][:, particles * sizes[0] : particles * (sizes[0] + 1), : 2 * fields]
-    digits_in = digits_in.astype(jnp.int32).reshape(-1, 2 * fields)
-    meta_layer = digits_in[:, :fields] * META_BASE + digits_in[:, fields:]
-    meta_all = [meta_layer]
-    for step in range(1, slab_count):
-        ring = [(s, (s + step) % slab_count) for s in range(slab_count)]
-        meta_all.append(lax.ppermute(meta_layer, "slab", ring))
-    meta_all = jnp.concatenate(meta_all, axis=0)
+    def read_digits(rows_in):
+        whole = rows_in.astype(jnp.int32).reshape(-1, 2 * fields)
+        return whole[:, :fields] * META_BASE + whole[:, fields:]
+
+    meta_at = particles * sizes[0]
+    meta_layer = read_digits(received[0][:, meta_at : meta_at + particles, : 2 * fields])
 
     class_count = dest_map.shape[0]
 
@@ -244,12 +254,65 @@
             code = jnp.pad(code, ((0, 0), (0, META_ROWS)), constant_values=-1)
         codes.append(code.reshape(1, -1))
 
+    sums = []
+    for c, each in enumerate(sizes):
+        bins = each * planes
+        extra_rows = META_ROWS if c == 0 and mirrored else 0
+        codes_in = codes[c]
+        if c + 1 < len(sizes):
+            codes_in, _ = lax.optimization_barrier((codes_in, weighted[c + 1]))
+        if c > 0:
+            codes_in, parts = lax.optimization_barrier((codes_in, parts))
+        parts = pl.pallas_call(
+            functools.partial(insert_kernel, bins, meta_at),
+            out_shape=jax.ShapeDtypeStruct(
+                (window_slabs, bins + extra_rows, 2 * length), jnp.bfloat16
+            ),
+            in_specs=whole_vmem(2),
+            out_specs=pl.BlockSpec(memory_space=pltpu.VMEM),
+            compiler_params=pltpu.CompilerParams(vmem_limit_bytes=VMEM_LIMIT),
+            cost_estimate=pl.CostEstimate(
+                flops=0,
+                bytes_accessed=0,
+                transcendentals=0,
+            ),
+            name="insert",
+        )(received[c], codes_in)
+        if not mirrored:
+            sums.append(lax.psum_scatter(parts, "slab", scatter_dimension=0, tiled=False))
+            continue
+        arrived = slab_exchange(parts, places[c], slab_count, batch_count, swaps[c])
+        total = choose(parts[:, :bins], places[c]).astype(jnp.float32)
+        total = jnp.where(places[c] == slab_count - 1, 0.0, total)
+        for block in arrived:
+            total = total + block[:bins].astype(jnp.float32)
+        if swaps[c]:
+            over = [(b, (b + half_batch) % batch_count) for b in range(batch_count)]
+            total = lax.ppermute(total.astype(jnp.bfloat16), "batch", over)
+        sums.append(total)
+        if c == 0:
+            meta_in = [block[bins:].reshape(META_ROWS, -1, LANES) for block in arrived]
+
+    meta_all = [meta_layer]
+    if mirrored:
+        for block in meta_in:
+            halves = (block[:particles], block[particles : 2 * particles])
+            low = jnp.concatenate(halves, axis=1)[:, :batch_count, : 2 * fields]
+            meta_all.append(read_digits(low.transpose(1, 0, 2)))
+    else:
+        for step in range(1, slab_count):
+            ring = [(s, (s + step) % slab_count) for s in range(slab_count)]
+            meta_all.append(lax.ppermute(meta_layer, "slab", ring))
+    meta_all = jnp.concatenate(meta_all, axis=0)
+
     own_freq = batch * rows + jnp.arange(rows, dtype=jnp.int32)
     own_dest = lax.dynamic_slice_in_dim(dest_map, batch * rows, rows, 1)
     owner, local_plane = find_planes(meta_all, own_dest, own_freq)
     focus_count = defocus.shape[0]
     focus_hot = (meta_all[:, 1:2] == jnp.arange(focus_count)[None, :]).astype(jnp.bfloat16)
     own_plane = jnp.where(owner == slab, local_plane, -1)
+    if mirrored:
+        own_plane = jnp.where(places[0] == slab_count - 1, -1, own_plane)
     bin_hot = (own_plane.T[:, None, :] == jnp.arange(planes)[None, :, None]).astype(jnp.bfloat16)
     counts = jnp.einsum("kzp,pd->kzd", bin_hot, focus_hot, preferred_element_type=jnp.float32)
     row_angle = 2.0 * (
@@ -264,36 +327,6 @@
     weights = 0.5 * (jnp.sum(counts, axis=2, keepdims=True) - double)
     denom = weights + TAU_PRIOR
 
-    sums = []
-    for c, each in enumerate(sizes):
-        bins = each * planes
-        rows_in = received[c].reshape(-1, 2 * length)
-        codes_in = codes[c]
-        if c + 1 < len(sizes):
-            codes_in, _ = lax.optimization_barrier((codes_in, weighted[c + 1]))
-        if c > 1:
-            codes_in, sums[c - 2] = lax.optimization_barrier((codes_in, sums[c - 2]))
-        parts = pl.pallas_call(
-            insert_kernel,
-            out_shape=jax.ShapeDtypeStruct((window_slabs, bins, 2 * length), jnp.bfloat16),
-            in_specs=whole_vmem(2),
-            out_specs=pl.BlockSpec(memory_space=pltpu.VMEM),
-            compiler_params=pltpu.CompilerParams(vmem_limit_bytes=VMEM_LIMIT),
-            cost_estimate=pl.CostEstimate(
-                flops=2 * bins * window_slabs * rows_in.shape[0] * 2 * length,
-                bytes_accessed=4 * 1024 * 1024,
-                transcendentals=0,
-            ),
-            name="insert",
-        )(rows_in, codes_in)
-        if mirrored:
-            total = slab_sums(parts, places[c], slab_count, batch_count, swaps[c])
-            if swaps[c]:
-                over = [(b, (b + half_batch) % batch_count) for b in range(batch_count)]
-                total = lax.ppermute(total.astype(jnp.bfloat16), "batch", over)
-            sums.append(total)
-        else:
-            sums.append(lax.psum_scatter(parts, "slab", scatter_dimension=0, tiled=False))
     updated = []
     for c, each in enumerate(sizes):
         here = slice(starts[c], starts[c] + each)

time: 168 us -> 180 us (1.071)
  local copies, waits for them, and re-layouts: 16 us -> 26.8 us
  starting transfers between devices: 45.8 us -> 38.4 us
  waiting for transfers between devices: 71.4 us -> 78 us
  other arithmetic: 11.6 us -> 14.9 us
    unnamed x34 -> x54, local copies, waits for them, and re-layouts: 9.17 us -> 19.9 us
    ppermute x12 -> x9, starting transfers between devices: 29 us -> 20.9 us  [slab_exchange(): arrived.append(lax.ppermute(block, ('batch', 'slab'), perm))]
    ppermute x12 -> x9, waiting for transfers between devices: 53.8 us -> 60.1 us  [slab_exchange(): arrived.append(lax.ppermute(block, ('batch', 'slab'), perm))]
    another operation x4, other arithmetic: 1.34 us -> 4.3 us
  transfers between devices with their start and end apart: 16 -> 13, of which waited for: 7 -> 8; matrix products, arithmetic and copies ran while one was open for 12% -> 14% of each run, Pallas kernels for 8% -> 8%
where the time goes in v6:
time: 180 us; the launch traced here: 179 us
  waiting for transfers between devices  78 us (43%)
  starting transfers between devices  38.4 us (21%)
  local copies, waits for them, and re-layouts  26.8 us (15%)
  Pallas kernels  17 us (9%)
  other arithmetic  14.9 us (8%)
  matrix products  3.32 us (2%)
    ppermute x9, waiting for transfers between devices, slab_exchange(): arrived.append(lax.ppermute(block, ('batch', 'slab'), perm))  60.1 us
    ppermute x9, starting transfers between devices, slab_exchange(): arrived.append(lax.ppermute(block, ('batch', 'slab'), perm))  20.9 us
    unnamed x54, local copies, waits for them, and re-layouts  19.9 us
    all_to_all x3, waiting for transfers between devices, per_device(): received.append(lax.all_to_all(send, 'batch', 0, 0, tiled=True))  18 us
    all_to_all x3, starting transfers between devices, per_device(): received.append(lax.all_to_all(send, 'batch', 0, 0, tiled=True))  16.9 us
    pallas_call x3, Pallas kernels, per_device(): pl.pallas_call(functools.partial(insert_kernel, bins, meta_at), out_shape...  8.77 us
    pallas_call x3, Pallas kernels, per_device(): pl.pallas_call(functools.partial(spectrum_kernel, runs), out_shape=jax.Sh...  8.19 us
    another operation x4, other arithmetic  4.3 us
  transfers between devices with their start and end apart: 13, of which 8 were waited for; matrix products, arithmetic and copies ran while one was open for 14% of the time, Pallas kernels for 8%

profile of v6, /device:TPU:11, one launch (start us, length us, event | category | flops | bytes accessed | tf_op | source)
XLA Modules:
  0.0 178.9 jit_solution(12873282352106495384)
XLA Ops:
  8.6 2.9 %spectrum.3 = bf16[8,144,768]{2,1,0:T(8,128)(2,1)S(1)} custom-call(bf16[8,384,384]{2,1,0:T(8,128)(2,1)S(1)} %copy-done, bf16[256,384]{1,0:T(8,128)(2,1)S(1)} %copy-done.15, bf16[768,768]{1,0:T(8,128)(2,1)S(1)} %copy-done.2, f32[384,32]{1,0:T(8,128)S(1)} %copy.80.row_factors, f32[32,384]{1,0:T(8,128)S(1)} %pad_maximum_fusion.2.col_factors, ...), custom_call_target="tpu_custom_call" | custom-call | tf_op jit(solution)/shard_map/spectrum/pallas_call | solution.py:191
  13.3 5.3 %all-to-all-start = ((bf16[8,144,768]{2,1,0:T(8,128)(2,1)}), bf16[8,144,768]{2,1,0:T(8,128)(2,1)}, u32[]{:S(2)}, u32[]{:S(2)}) async-start(bf16[8,144,768]{2,1,0:T(8,128)(2,1)} %copy-done.4), calls=%async_computation | async-start | bytes 3538944 | tf_op jit(solution)/shard_map/all_to_all | solution.py:213
  21.3 2.6 %spectrum.4 = bf16[8,128,768]{2,1,0:T(8,128)(2,1)S(1)} custom-call(bf16[8,384,384]{2,1,0:T(8,128)(2,1)S(1)} %copy-done.1, bf16[256,384]{1,0:T(8,128)(2,1)S(1)} %copy-done.14, bf16[768,768]{1,0:T(8,128)(2,1)S(1)} %copy-done.3, f32[384,32]{1,0:T(8,128)S(1)} %copy-done.8, f32[32,384]{1,0:T(8,128)S(1)} %copy-done.11), custom_call_target="tpu_custom_call" | custom-call | tf_op jit(solution)/shard_map/spectrum/pallas_call | solution.py:191
  25.1 2.6 %constant_dynamic-slice_fusion.2 = (s32[768,16]{1,0:T(8,128)}, s32[768,16]{1,0:T(8,128)}, s32[768,16]{1,0:T(8,128)}) fusion(s32[768,384]{1,0:T(8,128)} %param.18, s32[]{:T(128)S(6)} %select_n.377, s32[]{:T(128)S(6)} %select_n.378, s32[]{:T(128)S(6)} %select_n.379), kind=kLoop, calls=%fused_computation.160 | loop fusion | bytes 294924 | tf_op jit(solution)/shard_map/dynamic_slice | solution.py:236
  27.7 12.6 %all-to-all-done.received = bf16[8,144,768]{2,1,0:T(8,128)(2,1)} async-done(((bf16[8,144,768]{2,1,0:T(8,128)(2,1)}), bf16[8,144,768]{2,1,0:T(8,128)(2,1)}, u32[]{:S(2)}, u32[]{:S(2)}) %all-to-all-start) | async-done | bytes 1769504 | tf_op jit(solution)/shard_map/all_to_all | solution.py:213
  40.3 5.8 %all-to-all-start.1 = ((bf16[8,128,768]{2,1,0:T(8,128)(2,1)}), bf16[8,128,768]{2,1,0:T(8,128)(2,1)}, u32[]{:S(2)}, u32[]{:S(2)}) async-start(bf16[8,128,768]{2,1,0:T(8,128)(2,1)} %copy-done.6), calls=%async_computation.1 | async-start | bytes 3145728 | tf_op jit(solution)/shard_map/all_to_all | solution.py:213
  58.2 2.6 %spectrum.5 = bf16[8,128,768]{2,1,0:T(8,128)(2,1)S(1)} custom-call(bf16[8,384,384]{2,1,0:T(8,128)(2,1)S(1)} %copy-done.1, bf16[256,384]{1,0:T(8,128)(2,1)S(1)} %copy-done.13, bf16[768,768]{1,0:T(8,128)(2,1)S(1)} %copy-done.3, f32[384,32]{1,0:T(8,128)S(1)} %copy-done.9, f32[32,384]{1,0:T(8,128)S(1)} %copy-done.12), custom_call_target="tpu_custom_call" | custom-call | tf_op jit(solution)/shard_map/spectrum/pallas_call | solution.py:191
  63.3 2.3 %all-to-all-done.1.received = bf16[8,128,768]{2,1,0:T(8,128)(2,1)} async-done(((bf16[8,128,768]{2,1,0:T(8,128)(2,1)}), bf16[8,128,768]{2,1,0:T(8,128)(2,1)}, u32[]{:S(2)}, u32[]{:S(2)}) %all-to-all-start.1) | async-done | bytes 1572896 | tf_op jit(solution)/shard_map/all_to_all | solution.py:213
  65.6 5.8 %all-to-all-start.2 = ((bf16[8,128,768]{2,1,0:T(8,128)(2,1)}), bf16[8,128,768]{2,1,0:T(8,128)(2,1)}, u32[]{:S(2)}, u32[]{:S(2)}) async-start(bf16[8,128,768]{2,1,0:T(8,128)(2,1)} %copy-done.5), calls=%async_computation.2 | async-start | bytes 3145728 | tf_op jit(solution)/shard_map/all_to_all | solution.py:213
  72.3 3.2 %insert.3 = bf16[3,272,768]{2,1,0:T(8,128)(2,1)S(1)} custom-call(bf16[8,144,768]{2,1,0:T(8,128)(2,1)} %all-to-all-done.received, s32[1,1152]{1,0:T(1,128)S(1)} %reshape.245.codes), custom_call_target="tpu_custom_call" | custom-call | tf_op jit(solution)/shard_map/insert/pallas_call | solution.py:266
  75.5 2.8 %insert.4 = bf16[3,256,768]{2,1,0:T(8,128)(2,1)S(1)} custom-call(bf16[8,128,768]{2,1,0:T(8,128)(2,1)} %all-to-all-done.1.received, s32[1,1024]{1,0:T(1,128)S(1)} %reshape_reshape.6.codes), custom_call_target="tpu_custom_call" | custom-call | tf_op jit(solution)/shard_map/insert/pallas_call | solution.py:266
  80.7 5.0 %collective-permute-start.4 = (bf16[256,768]{1,0:T(8,128)(2,1)S(1)}, bf16[256,768]{1,0:T(8,128)(2,1)}, u32[]{:S(2)}, u32[]{:S(2)}) collective-permute-start(bf16[256,768]{1,0:T(8,128)(2,1)S(1)} %get-tuple-element.24), channel_id=1, source_target_pairs={{3,1},{1,3},{0,2},{7,5},{5,7},{4,6},{11,9},{9,11},{8,10},{15,13},{... | collective-permute-start | bytes 1179656 | tf_op jit(solution)/shard_map/ppermute | solution.py:143
  85.7 1.9 %collective-permute-start.5 = (bf16[256,768]{1,0:T(8,128)(2,1)S(1)}, bf16[256,768]{1,0:T(8,128)(2,1)}, u32[]{:S(2)}, u32[]{:S(2)}) collective-permute-start(bf16[256,768]{1,0:T(8,128)(2,1)S(1)} %get-tuple-element.23), channel_id=1, source_target_pairs={{2,3},{1,2},{0,1},{6,7},{5,6},{4,5},{10,11},{9,10},{8,9},{14,15},{... | collective-permute-start | bytes 1179656 | tf_op jit(solution)/shard_map/ppermute | solution.py:143
  87.8 3.1 %all-to-all-done.2.received = bf16[8,128,768]{2,1,0:T(8,128)(2,1)} async-done(((bf16[8,128,768]{2,1,0:T(8,128)(2,1)}), bf16[8,128,768]{2,1,0:T(8,128)(2,1)}, u32[]{:S(2)}, u32[]{:S(2)}) %all-to-all-start.2) | async-done | bytes 1572896 | tf_op jit(solution)/shard_map/all_to_all | solution.py:213
  90.9 2.8 %insert.5 = bf16[3,256,768]{2,1,0:T(8,128)(2,1)S(1)} custom-call(bf16[8,128,768]{2,1,0:T(8,128)(2,1)} %all-to-all-done.2.received, s32[1,1024]{1,0:T(1,128)S(1)} %reshape_reshape.7.codes), custom_call_target="tpu_custom_call" | custom-call | tf_op jit(solution)/shard_map/insert/pallas_call | solution.py:266
  93.9 3.2 %collective-permute-start.7 = (bf16[256,768]{1,0:T(8,128)(2,1)S(1)}, bf16[256,768]{1,0:T(8,128)(2,1)S(1)}, u32[]{:S(2)}, u32[]{:S(2)}) collective-permute-start(bf16[256,768]{1,0:T(8,128)(2,1)S(1)} %get-tuple-element.25), channel_id=1, source_target_pairs={{0,1},{1,2},{3,0},{4,5},{5,6},{7,4},{8,9},{9,10},{11,8},{12,13},{1... | collective-permute-start | bytes 1179656 | tf_op jit(solution)/shard_map/ppermute | solution.py:143
  98.4 3.1 %collective-permute-start.9 = (bf16[256,768]{1,0:T(8,128)(2,1)S(1)}, bf16[256,768]{1,0:T(8,128)(2,1)S(1)}, u32[]{:S(2)}, u32[]{:S(2)}) collective-permute-start(bf16[256,768]{1,0:T(8,128)(2,1)S(1)} %get-tuple-element.26), channel_id=1, source_target_pairs={{1,0},{2,1},{3,2},{5,4},{6,5},{7,6},{9,8},{10,9},{11,10},{13,12},{... | collective-permute-start | bytes 1179656 | tf_op jit(solution)/shard_map/ppermute | solution.py:143
  102.3 7.8 %collective-permute-done.4 = bf16[256,768]{1,0:T(8,128)(2,1)} collective-permute-done((bf16[256,768]{1,0:T(8,128)(2,1)S(1)}, bf16[256,768]{1,0:T(8,128)(2,1)}, u32[]{:S(2)}, u32[]{:S(2)}) %collective-permute-start.4) | collective-permute-done | bytes 393248 | tf_op jit(solution)/shard_map/ppermute | solution.py:143
  112.1 6.7 %collective-permute-done.5 = bf16[256,768]{1,0:T(8,128)(2,1)} collective-permute-done((bf16[256,768]{1,0:T(8,128)(2,1)S(1)}, bf16[256,768]{1,0:T(8,128)(2,1)}, u32[]{:S(2)}, u32[]{:S(2)}) %collective-permute-start.5) | collective-permute-done | bytes 393248 | tf_op jit(solution)/shard_map/ppermute | solution.py:143
  120.0 2.4 %fusion.11 = bf16[256,768]{1,0:T(8,128)(2,1)} fusion(bf16[256,768]{1,0:T(8,128)(2,1)} %collective-permute-done.5, bf16[256,768]{1,0:T(8,128)(2,1)} %collective-permute-done.4, bf16[256,768]{1,0:T(8,128)(2,1)} %collective-permute-done.3, pred[]{:T(512)S(6)} %eq.202, pred[]{:T(512)S(6)} %eq.201, pred[]{:T(512)S(6)} %eq.200, bf16[3,256,768]{2,1,0:T(8,128)(2,1)S(1)} %insert.4), kind=kLoop, calls=%fused_computation.21 | loop fusion | flops 2162688 | bytes 2752515 | tf_op jit(solution)/shard_map/convert_element_type | solution.py:291
  122.4 13.1 %collective-permute-done.7 = bf16[256,768]{1,0:T(8,128)(2,1)S(1)} collective-permute-done((bf16[256,768]{1,0:T(8,128)(2,1)S(1)}, bf16[256,768]{1,0:T(8,128)(2,1)S(1)}, u32[]{:S(2)}, u32[]{:S(2)}) %collective-permute-start.7) | collective-permute-done | bytes 393248 | tf_op jit(solution)/shard_map/ppermute | solution.py:143
  135.4 1.9 %collective-permute-start.2 = (bf16[272,768]{1,0:T(8,128)(2,1)}, bf16[272,768]{1,0:T(8,128)(2,1)}, u32[]{:S(2)}, u32[]{:S(2)}) collective-permute-start(bf16[272,768]{1,0:T(8,128)(2,1)} %get-tuple-element.15), channel_id=1, source_target_pairs={{1,0},{2,1},{3,2},{5,4},{6,5},{7,6},{9,8},{10,9},{11,10},{13,12},{... | collective-permute-start | bytes 1253384 | tf_op jit(solution)/shard_map/ppermute | solution.py:143
  138.0 15.3 %collective-permute-done.9 = bf16[256,768]{1,0:T(8,128)(2,1)S(1)} collective-permute-done((bf16[256,768]{1,0:T(8,128)(2,1)S(1)}, bf16[256,768]{1,0:T(8,128)(2,1)S(1)}, u32[]{:S(2)}, u32[]{:S(2)}) %collective-permute-start.9) | collective-permute-done | bytes 393248 | tf_op jit(solution)/shard_map/ppermute | solution.py:143
  154.2 17.2 %collective-permute-done.2 = bf16[272,768]{1,0:T(8,128)(2,1)} collective-permute-done((bf16[272,768]{1,0:T(8,128)(2,1)}, bf16[272,768]{1,0:T(8,128)(2,1)}, u32[]{:S(2)}, u32[]{:S(2)}) %collective-permute-start.2) | collective-permute-done | bytes 417824 | tf_op jit(solution)/shard_map/ppermute | solution.py:143
  (133 shorter events, 46.4 us)
Async XLA Ops:
  2.0 2.7 %copy-start.7 = (f32[384,32]{1,0:T(8,128)}, f32[384,32]{1,0:T(8,128)S(1)}, u32[]{:S(2)}) copy-start(f32[384,32]{1,0:T(8,128)S(1)} %copy.80.row_factors) | copy-start | bytes 147460
  4.7 1.7 copy-start
  6.4 1.3 copy-start.2
  11.5 1.2 copy-start.4
  13.3 5.3 %copy-start.1 = (bf16[8,384,384]{2,1,0:T(8,128)(2,1)S(1)}, bf16[8,384,384]{2,1,0:T(8,128)(2,1)}, u32[]{:S(2)}) copy-start(bf16[8,384,384]{2,1,0:T(8,128)(2,1)} %images.5) | copy-start | bytes 7077892
  13.3 5.3 %copy-start.3 = (bf16[768,768]{1,0:T(8,128)(2,1)S(1)}, bf16[768,768]{1,0:T(8,128)(2,1)}, u32[]{:S(2)}) copy-start(bf16[768,768]{1,0:T(8,128)(2,1)} %constant.193.clone.right) | copy-start | bytes 3538948
  13.3 27.0 %all-to-all-start = ((bf16[8,144,768]{2,1,0:T(8,128)(2,1)}), bf16[8,144,768]{2,1,0:T(8,128)(2,1)}, u32[]{:S(2)}, u32[]{:S(2)}) async-start(bf16[8,144,768]{2,1,0:T(8,128)(2,1)} %copy-done.4), calls=%async_computation | async-start | bytes 3538944 | tf_op jit(solution)/shard_map/all_to_all | solution.py:213
  40.3 25.3 %all-to-all-start.1 = ((bf16[8,128,768]{2,1,0:T(8,128)(2,1)}), bf16[8,128,768]{2,1,0:T(8,128)(2,1)}, u32[]{:S(2)}, u32[]{:S(2)}) async-start(bf16[8,128,768]{2,1,0:T(8,128)(2,1)} %copy-done.6), calls=%async_computation.1 | async-start | bytes 3145728 | tf_op jit(solution)/shard_map/all_to_all | solution.py:213
  58.2 3.9 %copy-start.20 = (f32[16]{0:T(128)S(1)}, f32[16]{0:T(128)}, u32[]{:S(2)}) copy-start(f32[16]{0:T(128)} %param.16) | copy-start | bytes 196
  63.3 8.2 %copy-start.17 = (bf16[768,16]{0,1:T(8,128)(2,1)S(1)}, bf16[768,16]{0,1:T(8,128)(2,1)}, u32[]{:S(2)}) copy-start(bf16[768,16]{0,1:T(8,128)(2,1)} %convert.25) | copy-start | bytes 73732
  63.3 8.2 %copy-start.18 = (bf16[768,16]{0,1:T(8,128)(2,1)S(1)}, bf16[768,16]{0,1:T(8,128)(2,1)}, u32[]{:S(2)}) copy-start(bf16[768,16]{0,1:T(8,128)(2,1)} %convert.26) | copy-start | bytes 73732
  63.3 8.2 %copy-start.19 = (bf16[768,16]{0,1:T(8,128)(2,1)S(1)}, bf16[768,16]{0,1:T(8,128)(2,1)}, u32[]{:S(2)}) copy-start(bf16[768,16]{0,1:T(8,128)(2,1)} %convert.27) | copy-start | bytes 73732
  65.6 25.3 %all-to-all-start.2 = ((bf16[8,128,768]{2,1,0:T(8,128)(2,1)}), bf16[8,128,768]{2,1,0:T(8,128)(2,1)}, u32[]{:S(2)}, u32[]{:S(2)}) async-start(bf16[8,128,768]{2,1,0:T(8,128)(2,1)} %copy-done.5), calls=%async_computation.2 | async-start | bytes 3145728 | tf_op jit(solution)/shard_map/all_to_all | solution.py:213
  79.1 19.3 %collective-permute-start.3 = (bf16[256,768]{1,0:T(8,128)(2,1)}, bf16[256,768]{1,0:T(8,128)(2,1)}, u32[]{:S(2)}, u32[]{:S(2)}) collective-permute-start(bf16[256,768]{1,0:T(8,128)(2,1)} %get-tuple-element.22), channel_id=1, source_target_pairs={{3,2},{2,1},{0,3},{7,6},{6,5},{4,7},{11,10},{10,9},{8,11},{15,14},... | collective-permute-start | bytes 1179656 | tf_op jit(solution)/shard_map/ppermute | solution.py:143
  80.7 29.4 %collective-permute-start.4 = (bf16[256,768]{1,0:T(8,128)(2,1)S(1)}, bf16[256,768]{1,0:T(8,128)(2,1)}, u32[]{:S(2)}, u32[]{:S(2)}) collective-permute-start(bf16[256,768]{1,0:T(8,128)(2,1)S(1)} %get-tuple-element.24), channel_id=1, source_target_pairs={{3,1},{1,3},{0,2},{7,5},{5,7},{4,6},{11,9},{9,11},{8,10},{15,13},{... | collective-permute-start | bytes 1179656 | tf_op jit(solution)/shard_map/ppermute | solution.py:143
  85.7 33.0 %collective-permute-start.5 = (bf16[256,768]{1,0:T(8,128)(2,1)S(1)}, bf16[256,768]{1,0:T(8,128)(2,1)}, u32[]{:S(2)}, u32[]{:S(2)}) collective-permute-start(bf16[256,768]{1,0:T(8,128)(2,1)S(1)} %get-tuple-element.23), channel_id=1, source_target_pairs={{2,3},{1,2},{0,1},{6,7},{5,6},{4,5},{10,11},{9,10},{8,9},{14,15},{... | collective-permute-start | bytes 1179656 | tf_op jit(solution)/shard_map/ppermute | solution.py:143
  93.9 41.6 %collective-permute-start.7 = (bf16[256,768]{1,0:T(8,128)(2,1)S(1)}, bf16[256,768]{1,0:T(8,128)(2,1)S(1)}, u32[]{:S(2)}, u32[]{:S(2)}) collective-permute-start(bf16[256,768]{1,0:T(8,128)(2,1)S(1)} %get-tuple-element.25), channel_id=1, source_target_pairs={{0,1},{1,2},{3,0},{4,5},{5,6},{7,4},{8,9},{9,10},{11,8},{12,13},{1... | collective-permute-start | bytes 1179656 | tf_op jit(solution)/shard_map/ppermute | solution.py:143
  97.1 40.3 %collective-permute-start.8 = (bf16[256,768]{1,0:T(8,128)(2,1)S(1)}, bf16[256,768]{1,0:T(8,128)(2,1)S(1)}, u32[]{:S(2)}, u32[]{:S(2)}) collective-permute-start(bf16[256,768]{1,0:T(8,128)(2,1)S(1)} %get-tuple-element.27), channel_id=1, source_target_pairs={{0,2},{2,0},{3,1},{4,6},{6,4},{7,5},{8,10},{10,8},{11,9},{12,14},{... | collective-permute-start | bytes 1179656 | tf_op jit(solution)/shard_map/ppermute | solution.py:143
  98.4 55.0 %collective-permute-start.9 = (bf16[256,768]{1,0:T(8,128)(2,1)S(1)}, bf16[256,768]{1,0:T(8,128)(2,1)S(1)}, u32[]{:S(2)}, u32[]{:S(2)}) collective-permute-start(bf16[256,768]{1,0:T(8,128)(2,1)S(1)} %get-tuple-element.26), channel_id=1, source_target_pairs={{1,0},{2,1},{3,2},{5,4},{6,5},{7,6},{9,8},{10,9},{11,10},{13,12},{... | collective-permute-start | bytes 1179656 | tf_op jit(solution)/shard_map/ppermute | solution.py:143
  110.1 43.5 %collective-permute-start = (bf16[272,768]{1,0:T(8,128)(2,1)S(1)}, bf16[272,768]{1,0:T(8,128)(2,1)S(1)}, u32[]{:S(2)}, u32[]{:S(2)}) collective-permute-start(bf16[272,768]{1,0:T(8,128)(2,1)S(1)} %get-tuple-element.13), channel_id=1, source_target_pairs={{0,1},{1,2},{3,0},{4,5},{5,6},{7,4},{8,9},{9,10},{11,8},{12,13},{1... | collective-permute-start | bytes 1253384 | tf_op jit(solution)/shard_map/ppermute | solution.py:143
  118.7 35.0 %collective-permute-start.1 = (bf16[272,768]{1,0:T(8,128)(2,1)S(1)}, bf16[272,768]{1,0:T(8,128)(2,1)S(1)}, u32[]{:S(2)}, u32[]{:S(2)}) collective-permute-start(bf16[272,768]{1,0:T(8,128)(2,1)S(1)} %get-tuple-element.14), channel_id=1, source_target_pairs={{0,2},{2,0},{3,1},{4,6},{6,4},{7,5},{8,10},{10,8},{11,9},{12,14},{... | collective-permute-start | bytes 1253384 | tf_op jit(solution)/shard_map/ppermute | solution.py:143
  135.4 35.9 %collective-permute-start.2 = (bf16[272,768]{1,0:T(8,128)(2,1)}, bf16[272,768]{1,0:T(8,128)(2,1)}, u32[]{:S(2)}, u32[]{:S(2)}) collective-permute-start(bf16[272,768]{1,0:T(8,128)(2,1)} %get-tuple-element.15), channel_id=1, source_target_pairs={{1,0},{2,1},{3,2},{5,4},{6,5},{7,6},{9,8},{10,9},{11,10},{13,12},{... | collective-permute-start | bytes 1253384 | tf_op jit(solution)/shard_map/ppermute | solution.py:143
  137.3 39.9 %collective-permute-start.6 = (bf16[256,768]{1,0:T(8,128)(2,1)}, bf16[256,768]{1,0:T(8,128)(2,1)S(1)}, u32[]{:S(2)}, u32[]{:S(2)}) collective-permute-start(bf16[256,768]{1,0:T(8,128)(2,1)} %fusion.11), channel_id=1, source_target_pairs={{0,16},{4,20},{8,24},{12,28},{16,0},{20,4},{24,8},{28,12},{1,17},{... | collective-permute-start | bytes 1179656 | tf_op jit(solution)/shard_map/ppermute | solution.py:291
  175.8 1.4 copy-start.16
  (10 other events, 9.2 us)

commit v7 on v6

--- a/solution.py
+++ b/solution.py
@@ -221,48 +221,51 @@
 
     class_count = dest_map.shape[0]
 
-    def find_planes(table, dest, freq_in):
+    dest_wide = dest_map.astype(jnp.bfloat16)
+
+    def find_planes(table):
         class_hot = (table[:, :1] == jnp.arange(class_count)[None, :]).astype(jnp.bfloat16)
-        local_plane = jnp.dot(
-            class_hot, dest.astype(jnp.bfloat16), preferred_element_type=jnp.float32
+        local_plane = jnp.dot(class_hot, dest_wide, preferred_element_type=jnp.float32)
+        past = freq[None, :, None] >= table[:, None, 2:]
+        owner = jnp.sum(past.astype(jnp.int32), axis=2)
+        return owner * planes + local_plane.astype(jnp.int32)
+
+    def pick_block(table, block):
+        return sum(
+            jnp.where(block == k, table[:, k * rows : (k + 1) * rows], 0)
+            for k in range(batch_count)
         )
-        past = freq_in[None, :, None] >= table[:, None, 2:]
-        return jnp.sum(past.astype(jnp.int32), axis=2), local_plane.astype(jnp.int32)
 
     window_slabs = 3 if mirrored else slab_count
     blocks = [(batch + half_batch) % batch_count if swap else batch for swap in swaps]
-    begins = [block * rows + start for block, start in zip(blocks, starts)]
-    dest_in = jnp.concatenate(
-        [lax.dynamic_slice_in_dim(dest_map, at, n, 1) for at, n in zip(begins, sizes)], axis=1
-    )
-    freq_in = jnp.concatenate(
-        [at + jnp.arange(n, dtype=jnp.int32) for at, n in zip(begins, sizes)]
-    )
-    owner, local_plane = find_planes(meta_layer, dest_in, freq_in)
+    layer_planes = find_planes(meta_layer)
     places, codes = [], []
     for c, each in enumerate(sizes):
         here = slice(starts[c], starts[c] + each)
-        place, owner_place = slab, owner[:, here]
+        plane = pick_block(layer_planes, blocks[c])[:, here]
+        place, owner_place = slab, plane // planes
         if mirrored:
             upper = blocks[c] >= half_batch
             owner_place = jnp.where(upper, slab_count - 1 - owner_place, owner_place)
             place = jnp.where(upper, slab_count - 1 - slab, slab)
         places.append(place)
         code = owner_place * (each * planes) + jnp.arange(each)[None, :] * planes
-        code = (code + local_plane[:, here]).reshape(batch_count, particles * each)
+        code = (code + plane % planes).reshape(batch_count, particles * each)
         if c == 0:
             code = jnp.pad(code, ((0, 0), (0, META_ROWS)), constant_values=-1)
         codes.append(code.reshape(1, -1))
 
-    sums = []
+    sums, arrived = [], []
     for c, each in enumerate(sizes):
         bins = each * planes
         extra_rows = META_ROWS if c == 0 and mirrored else 0
         codes_in = codes[c]
         if c + 1 < len(sizes):
             codes_in, _ = lax.optimization_barrier((codes_in, weighted[c + 1]))
-        if c > 0:
-            codes_in, parts = lax.optimization_barrier((codes_in, parts))
+        if c > 0 and mirrored:
+            near = [arrived[c - 1][0], arrived[c - 1][2]]
+            codes_in, *near = lax.optimization_barrier((codes_in, *near))
+            arrived[c - 1][0], arrived[c - 1][2] = near[:2]
         parts = pl.pallas_call(
             functools.partial(insert_kernel, bins, meta_at),
             out_shape=jax.ShapeDtypeStruct(
@@ -281,21 +284,24 @@
         if not mirrored:
             sums.append(lax.psum_scatter(parts, "slab", scatter_dimension=0, tiled=False))
             continue
-        arrived = slab_exchange(parts, places[c], slab_count, batch_count, swaps[c])
-        total = choose(parts[:, :bins], places[c]).astype(jnp.float32)
-        total = jnp.where(places[c] == slab_count - 1, 0.0, total)
-        for block in arrived:
-            total = total + block[:bins].astype(jnp.float32)
+        for before in arrived:
+            before[1], _ = lax.optimization_barrier((before[1], parts))
+        arrived.append(slab_exchange(parts, places[c], slab_count, batch_count, swaps[c]))
+        own = choose(parts[:, :bins], places[c]).astype(jnp.float32)
+        sums.append(jnp.where(places[c] == slab_count - 1, 0.0, own))
+    for c, each in enumerate(sizes):
+        if not mirrored:
+            break
+        for block in arrived[c]:
+            sums[c] = sums[c] + block[: each * planes].astype(jnp.float32)
         if swaps[c]:
             over = [(b, (b + half_batch) % batch_count) for b in range(batch_count)]
-            total = lax.ppermute(total.astype(jnp.bfloat16), "batch", over)
-        sums.append(total)
-        if c == 0:
-            meta_in = [block[bins:].reshape(META_ROWS, -1, LANES) for block in arrived]
+            sums[c] = lax.ppermute(sums[c].astype(jnp.bfloat16), "batch", over)
 
     meta_all = [meta_layer]
     if mirrored:
-        for block in meta_in:
+        for block in [block[sizes[0] * planes :] for block in arrived[0]]:
+            block = block.reshape(META_ROWS, -1, LANES)
             halves = (block[:particles], block[particles : 2 * particles])
             low = jnp.concatenate(halves, axis=1)[:, :batch_count, : 2 * fields]
             meta_all.append(read_digits(low.transpose(1, 0, 2)))
@@ -306,11 +312,9 @@
     meta_all = jnp.concatenate(meta_all, axis=0)
 
     own_freq = batch * rows + jnp.arange(rows, dtype=jnp.int32)
-    own_dest = lax.dynamic_slice_in_dim(dest_map, batch * rows, rows, 1)
-    owner, local_plane = find_planes(meta_all, own_dest, own_freq)
+    own_plane = pick_block(find_planes(meta_all), batch) - slab * planes
     focus_count = defocus.shape[0]
     focus_hot = (meta_all[:, 1:2] == jnp.arange(focus_count)[None, :]).astype(jnp.bfloat16)
-    own_plane = jnp.where(owner == slab, local_plane, -1)
     if mirrored:
         own_plane = jnp.where(places[0] == slab_count - 1, -1, own_plane)
     bin_hot = (own_plane.T[:, None, :] == jnp.arange(planes)[None, :, None]).astype(jnp.bfloat16)

time: 180 us -> 171 us (0.950)
  the two profiles are of different devices: /device:TPU:11 before, /device:TPU:9 now
where the time goes in v7:
time: 171 us; the launch traced here: 170 us
  waiting for transfers between devices  78.2 us (46%)
  starting transfers between devices  41.2 us (24%)
  local copies, waits for them, and re-layouts  17.3 us (10%)
  Pallas kernels  16.7 us (10%)
  other arithmetic  13.9 us (8%)
  matrix products  2.19 us (1%)
    ppermute x9, waiting for transfers between devices, slab_exchange(): arrived.append(lax.ppermute(block, ('batch', 'slab'), perm))  69 us
    ppermute x9, starting transfers between devices, slab_exchange(): arrived.append(lax.ppermute(block, ('batch', 'slab'), perm))  22.4 us
    all_to_all x3, starting transfers between devices, per_device(): received.append(lax.all_to_all(send, 'batch', 0, 0, tiled=True))  18.8 us
    unnamed x51, local copies, waits for them, and re-layouts  12.5 us
    pallas_call x3, Pallas kernels, per_device(): pl.pallas_call(functools.partial(spectrum_kernel, runs), out_shape=jax.Sh...  9.37 us
    all_to_all x3, waiting for transfers between devices, per_device(): received.append(lax.all_to_all(send, 'batch', 0, 0, tiled=True))  9.27 us
    pallas_call x3, Pallas kernels, per_device(): pl.pallas_call(functools.partial(insert_kernel, bins, meta_at), out_shape...  7.36 us
  transfers between devices with their start and end apart: 13, of which 8 were waited for; matrix products, arithmetic and copies ran while one was open for 7% of the time, Pallas kernels for 8%

profile of v7, /device:TPU:9, one launch (start us, length us, event | category | flops | bytes accessed | tf_op | source)
XLA Modules:
  0.0 170.1 jit_solution(8212286891962843609)
XLA Ops:
  4.7 1.7 copy-done
  8.6 2.9 %spectrum.3 = bf16[8,144,768]{2,1,0:T(8,128)(2,1)S(1)} custom-call(bf16[8,384,384]{2,1,0:T(8,128)(2,1)S(1)} %copy-done, bf16[256,384]{1,0:T(8,128)(2,1)S(1)} %copy-done.14, bf16[768,768]{1,0:T(8,128)(2,1)S(1)} %copy-done.4, f32[384,32]{1,0:T(8,128)S(1)} %copy.67.row_factors, f32[32,384]{1,0:T(8,128)S(1)} %pad_maximum_fusion.2.col_factors, ...), custom_call_target="tpu_custom_call" | custom-call | tf_op jit(solution)/shard_map/spectrum/pallas_call | solution.py:191
  13.3 5.1 %all-to-all-start = ((bf16[8,144,768]{2,1,0:T(8,128)(2,1)}), bf16[8,144,768]{2,1,0:T(8,128)(2,1)}, u32[]{:S(2)}, u32[]{:S(2)}) async-start(bf16[8,144,768]{2,1,0:T(8,128)(2,1)} %copy-done.6), calls=%async_computation | async-start | bytes 3538944 | tf_op jit(solution)/shard_map/all_to_all | solution.py:213
  21.1 2.6 %spectrum.4 = bf16[8,128,768]{2,1,0:T(8,128)(2,1)S(1)} custom-call(bf16[8,384,384]{2,1,0:T(8,128)(2,1)S(1)} %copy-done.1, bf16[256,384]{1,0:T(8,128)(2,1)S(1)} %copy-done.13, bf16[768,768]{1,0:T(8,128)(2,1)S(1)} %copy-done.5, f32[384,32]{1,0:T(8,128)S(1)} %copy-done.9, f32[32,384]{1,0:T(8,128)S(1)} %copy-done.11), custom_call_target="tpu_custom_call" | custom-call | tf_op jit(solution)/shard_map/spectrum/pallas_call | solution.py:191
  25.0 3.8 %spectrum.5 = bf16[8,128,768]{2,1,0:T(8,128)(2,1)} custom-call(bf16[8,384,384]{2,1,0:T(8,128)(2,1)S(1)} %copy-done.1, bf16[256,384]{1,0:T(8,128)(2,1)S(1)} %copy-done.12, bf16[768,768]{1,0:T(8,128)(2,1)S(1)} %copy-done.5, f32[384,32]{1,0:T(8,128)S(1)} %copy-done.9, f32[32,384]{1,0:T(8,128)S(1)} %copy-done.11), custom_call_target="tpu_custom_call" | custom-call | tf_op jit(solution)/shard_map/spectrum/pallas_call | solution.py:191
  28.8 9.3 %all-to-all-done.received = bf16[8,144,768]{2,1,0:T(8,128)(2,1)} async-done(((bf16[8,144,768]{2,1,0:T(8,128)(2,1)}), bf16[8,144,768]{2,1,0:T(8,128)(2,1)}, u32[]{:S(2)}, u32[]{:S(2)}) %all-to-all-start) | async-done | bytes 1769504 | tf_op jit(solution)/shard_map/all_to_all | solution.py:213
  38.1 7.1 %all-to-all-start.1 = ((bf16[8,128,768]{2,1,0:T(8,128)(2,1)}), bf16[8,128,768]{2,1,0:T(8,128)(2,1)S(1)}, u32[]{:S(2)}, u32[]{:S(2)}) async-start(bf16[8,128,768]{2,1,0:T(8,128)(2,1)} %copy-done.7), calls=%async_computation.1 | async-start | bytes 3145728 | tf_op jit(solution)/shard_map/all_to_all | solution.py:213
  47.2 3.2 %insert.3 = bf16[3,272,768]{2,1,0:T(8,128)(2,1)S(1)} custom-call(bf16[8,144,768]{2,1,0:T(8,128)(2,1)} %all-to-all-done.received, s32[1,1152]{1,0:T(1,128)S(1)} %reshape.240.codes), custom_call_target="tpu_custom_call" | custom-call | tf_op jit(solution)/shard_map/insert/pallas_call | solution.py:269
  51.6 3.2 %collective-permute-start = (bf16[272,768]{1,0:T(8,128)(2,1)}, bf16[272,768]{1,0:T(8,128)(2,1)S(1)}, u32[]{:S(2)}, u32[]{:S(2)}) collective-permute-start(bf16[272,768]{1,0:T(8,128)(2,1)} %get-tuple-element.28), channel_id=1, source_target_pairs={{0,1},{1,2},{3,0},{4,5},{5,6},{7,4},{8,9},{9,10},{11,8},{12,13},{1... | collective-permute-start | bytes 1253384 | tf_op jit(solution)/shard_map/ppermute | solution.py:143
  54.8 2.1 %collective-permute-start.1 = (bf16[272,768]{1,0:T(8,128)(2,1)}, bf16[272,768]{1,0:T(8,128)(2,1)}, u32[]{:S(2)}, u32[]{:S(2)}) collective-permute-start(bf16[272,768]{1,0:T(8,128)(2,1)} %get-tuple-element.29), channel_id=1, source_target_pairs={{1,0},{2,1},{3,2},{5,4},{6,5},{7,6},{9,8},{10,9},{11,10},{13,12},{... | collective-permute-start | bytes 1253384 | tf_op jit(solution)/shard_map/ppermute | solution.py:143
  58.8 6.2 %collective-permute-done = bf16[272,768]{1,0:T(8,128)(2,1)S(1)} collective-permute-done((bf16[272,768]{1,0:T(8,128)(2,1)}, bf16[272,768]{1,0:T(8,128)(2,1)S(1)}, u32[]{:S(2)}, u32[]{:S(2)}) %collective-permute-start) | collective-permute-done | bytes 417824 | tf_op jit(solution)/shard_map/ppermute | solution.py:143
  65.0 10.0 %collective-permute-done.1 = bf16[272,768]{1,0:T(8,128)(2,1)} collective-permute-done((bf16[272,768]{1,0:T(8,128)(2,1)}, bf16[272,768]{1,0:T(8,128)(2,1)}, u32[]{:S(2)}, u32[]{:S(2)}) %collective-permute-start.1) | collective-permute-done | bytes 417824 | tf_op jit(solution)/shard_map/ppermute | solution.py:143
  75.0 6.6 %all-to-all-start.2 = ((bf16[8,128,768]{2,1,0:T(8,128)(2,1)}), bf16[8,128,768]{2,1,0:T(8,128)(2,1)}, u32[]{:S(2)}, u32[]{:S(2)}) async-start(bf16[8,128,768]{2,1,0:T(8,128)(2,1)} %spectrum.5), calls=%async_computation.2 | async-start | bytes 3145728 | tf_op jit(solution)/shard_map/all_to_all | solution.py:213
  85.2 4.0 %collective-permute-start.4 = (bf16[256,768]{1,0:T(8,128)(2,1)S(1)}, bf16[256,768]{1,0:T(8,128)(2,1)}, u32[]{:S(2)}, u32[]{:S(2)}) collective-permute-start(bf16[256,768]{1,0:T(8,128)(2,1)S(1)} %get-tuple-element.38), channel_id=1, source_target_pairs={{2,3},{1,2},{0,1},{6,7},{5,6},{4,5},{10,11},{9,10},{8,9},{14,15},{... | collective-permute-start | bytes 1179656 | tf_op jit(solution)/shard_map/ppermute | solution.py:143
  89.2 2.3 %collective-permute-start.5 = (bf16[256,768]{1,0:T(8,128)(2,1)S(1)}, bf16[256,768]{1,0:T(8,128)(2,1)}, u32[]{:S(2)}, u32[]{:S(2)}) collective-permute-start(bf16[256,768]{1,0:T(8,128)(2,1)S(1)} %get-tuple-element.36), channel_id=1, source_target_pairs={{3,1},{1,3},{0,2},{7,5},{5,7},{4,6},{11,9},{9,11},{8,10},{15,13},{... | collective-permute-start | bytes 1179656 | tf_op jit(solution)/shard_map/ppermute | solution.py:143
  92.7 16.5 %collective-permute-done.3 = bf16[256,768]{1,0:T(8,128)(2,1)S(1)} collective-permute-done((bf16[256,768]{1,0:T(8,128)(2,1)S(1)}, bf16[256,768]{1,0:T(8,128)(2,1)S(1)}, u32[]{:S(2)}, u32[]{:S(2)}) %collective-permute-start.3) | collective-permute-done | bytes 393248 | tf_op jit(solution)/shard_map/ppermute | solution.py:143
  110.0 2.8 %insert.5 = bf16[3,256,768]{2,1,0:T(8,128)(2,1)S(1)} custom-call(bf16[8,128,768]{2,1,0:T(8,128)(2,1)} %all-to-all-done.2.received, s32[1,1024]{1,0:T(1,128)S(1)} %reshape_reshape.7.codes), custom_call_target="tpu_custom_call" | custom-call | tf_op jit(solution)/shard_map/insert/pallas_call | solution.py:269
  115.1 7.0 %collective-permute-done.5 = bf16[256,768]{1,0:T(8,128)(2,1)} collective-permute-done((bf16[256,768]{1,0:T(8,128)(2,1)S(1)}, bf16[256,768]{1,0:T(8,128)(2,1)}, u32[]{:S(2)}, u32[]{:S(2)}) %collective-permute-start.5) | collective-permute-done | bytes 393248 | tf_op jit(solution)/shard_map/ppermute | solution.py:143
  122.1 2.2 %fusion.11 = bf16[256,768]{1,0:T(8,128)(2,1)} fusion(bf16[256,768]{1,0:T(8,128)(2,1)} %collective-permute-done.4, bf16[256,768]{1,0:T(8,128)(2,1)} %collective-permute-done.5, bf16[256,768]{1,0:T(8,128)(2,1)S(1)} %copy-done.19, pred[]{:T(512)S(6)} %eq.277, pred[]{:T(512)S(6)} %eq.276, pred[]{:T(512)S(6)} %eq.275, bf16[3,256,768]{2,1,0:T(8,128)(2,1)S(1)} %copy-done.3), kind=kLoop, calls=%fused_computation.23 | loop fusion | flops 2162688 | bytes 2752515 | tf_op jit(solution)/shard_map/convert_element_type | solution.py:299
  124.3 2.4 %collective-permute-start.7 = (bf16[256,768]{1,0:T(8,128)(2,1)}, bf16[256,768]{1,0:T(8,128)(2,1)S(1)}, u32[]{:S(2)}, u32[]{:S(2)}) collective-permute-start(bf16[256,768]{1,0:T(8,128)(2,1)} %get-tuple-element.39), channel_id=1, source_target_pairs={{0,1},{1,2},{3,0},{4,5},{5,6},{7,4},{8,9},{9,10},{11,8},{12,13},{1... | collective-permute-start | bytes 1179656 | tf_op jit(solution)/shard_map/ppermute | solution.py:143
  128.0 4.6 %collective-permute-start.9 = (bf16[256,768]{1,0:T(8,128)(2,1)}, bf16[256,768]{1,0:T(8,128)(2,1)}, u32[]{:S(2)}, u32[]{:S(2)}) collective-permute-start(bf16[256,768]{1,0:T(8,128)(2,1)} %get-tuple-element.40), channel_id=1, source_target_pairs={{1,0},{2,1},{3,2},{5,4},{6,5},{7,6},{9,8},{10,9},{11,10},{13,12},{... | collective-permute-start | bytes 1179656 | tf_op jit(solution)/shard_map/ppermute | solution.py:143
  137.7 10.4 %collective-permute-done.8 = bf16[256,768]{1,0:T(8,128)(2,1)} collective-permute-done((bf16[256,768]{1,0:T(8,128)(2,1)}, bf16[256,768]{1,0:T(8,128)(2,1)}, u32[]{:S(2)}, u32[]{:S(2)}) %collective-permute-start.8) | collective-permute-done | bytes 393248 | tf_op jit(solution)/shard_map/ppermute | solution.py:143
  148.1 18.0 %collective-permute-done.9 = bf16[256,768]{1,0:T(8,128)(2,1)} collective-permute-done((bf16[256,768]{1,0:T(8,128)(2,1)}, bf16[256,768]{1,0:T(8,128)(2,1)}, u32[]{:S(2)}, u32[]{:S(2)}) %collective-permute-start.9) | collective-permute-done | bytes 393248 | tf_op jit(solution)/shard_map/ppermute | solution.py:143
  167.5 1.5 fusion.4
  (123 shorter events, 34.4 us)
Async XLA Ops:
  2.0 2.7 %copy-start.8 = (f32[384,32]{1,0:T(8,128)}, f32[384,32]{1,0:T(8,128)S(1)}, u32[]{:S(2)}) copy-start(f32[384,32]{1,0:T(8,128)S(1)} %copy.67.row_factors) | copy-start | bytes 147460
  4.7 1.7 copy-start
  13.3 5.1 %copy-start.1 = (bf16[8,384,384]{2,1,0:T(8,128)(2,1)S(1)}, bf16[8,384,384]{2,1,0:T(8,128)(2,1)}, u32[]{:S(2)}) copy-start(bf16[8,384,384]{2,1,0:T(8,128)(2,1)} %images.5) | copy-start | bytes 7077892
  13.3 5.1 %copy-start.5 = (bf16[768,768]{1,0:T(8,128)(2,1)S(1)}, bf16[768,768]{1,0:T(8,128)(2,1)}, u32[]{:S(2)}) copy-start(bf16[768,768]{1,0:T(8,128)(2,1)} %constant.241.clone.right) | copy-start | bytes 3538948
  13.3 24.8 %all-to-all-start = ((bf16[8,144,768]{2,1,0:T(8,128)(2,1)}), bf16[8,144,768]{2,1,0:T(8,128)(2,1)}, u32[]{:S(2)}, u32[]{:S(2)}) async-start(bf16[8,144,768]{2,1,0:T(8,128)(2,1)} %copy-done.6), calls=%async_computation | async-start | bytes 3538944 | tf_op jit(solution)/shard_map/all_to_all | solution.py:213
  21.1 3.8 %copy-start.12 = (bf16[256,384]{1,0:T(8,128)(2,1)S(1)}, bf16[256,384]{1,0:T(8,128)(2,1)}, u32[]{:S(2)}) copy-start(bf16[256,384]{1,0:T(8,128)(2,1)} %constant.244.clone.left) | copy-start | bytes 589828
  28.8 17.5 %copy-start.15 = (s32[768,384]{1,0:T(8,128)S(1)}, s32[768,384]{1,0:T(8,128)}, u32[]{:S(2)}) copy-start(s32[768,384]{1,0:T(8,128)} %param.18) | copy-start | bytes 3538948
  38.1 36.8 %all-to-all-start.1 = ((bf16[8,128,768]{2,1,0:T(8,128)(2,1)}), bf16[8,128,768]{2,1,0:T(8,128)(2,1)S(1)}, u32[]{:S(2)}, u32[]{:S(2)}) async-start(bf16[8,128,768]{2,1,0:T(8,128)(2,1)} %copy-done.7), calls=%async_computation.1 | async-start | bytes 3145728 | tf_op jit(solution)/shard_map/all_to_all | solution.py:213
  50.4 6.5 %copy-start.20 = (f32[16]{0:T(128)S(1)}, f32[16]{0:T(128)}, u32[]{:S(2)}) copy-start(f32[16]{0:T(128)} %param.16) | copy-start | bytes 196
  51.6 13.4 %collective-permute-start = (bf16[272,768]{1,0:T(8,128)(2,1)}, bf16[272,768]{1,0:T(8,128)(2,1)S(1)}, u32[]{:S(2)}, u32[]{:S(2)}) collective-permute-start(bf16[272,768]{1,0:T(8,128)(2,1)} %get-tuple-element.28), channel_id=1, source_target_pairs={{0,1},{1,2},{3,0},{4,5},{5,6},{7,4},{8,9},{9,10},{11,8},{12,13},{1... | collective-permute-start | bytes 1253384 | tf_op jit(solution)/shard_map/ppermute | solution.py:143
  54.8 20.2 %collective-permute-start.1 = (bf16[272,768]{1,0:T(8,128)(2,1)}, bf16[272,768]{1,0:T(8,128)(2,1)}, u32[]{:S(2)}, u32[]{:S(2)}) collective-permute-start(bf16[272,768]{1,0:T(8,128)(2,1)} %get-tuple-element.29), channel_id=1, source_target_pairs={{1,0},{2,1},{3,2},{5,4},{6,5},{7,6},{9,8},{10,9},{11,10},{13,12},{... | collective-permute-start | bytes 1253384 | tf_op jit(solution)/shard_map/ppermute | solution.py:143
  57.5 34.0 %collective-permute-start.2 = (bf16[272,768]{1,0:T(8,128)(2,1)}, bf16[272,768]{1,0:T(8,128)(2,1)}, u32[]{:S(2)}, u32[]{:S(2)}) collective-permute-start(bf16[272,768]{1,0:T(8,128)(2,1)} %get-tuple-element.27), channel_id=1, source_target_pairs={{0,2},{2,0},{3,1},{4,6},{6,4},{7,5},{8,10},{10,8},{11,9},{12,14},{... | collective-permute-start | bytes 1253384 | tf_op jit(solution)/shard_map/ppermute | solution.py:143
  75.0 35.1 %all-to-all-start.2 = ((bf16[8,128,768]{2,1,0:T(8,128)(2,1)}), bf16[8,128,768]{2,1,0:T(8,128)(2,1)}, u32[]{:S(2)}, u32[]{:S(2)}) async-start(bf16[8,128,768]{2,1,0:T(8,128)(2,1)} %spectrum.5), calls=%async_computation.2 | async-start | bytes 3145728 | tf_op jit(solution)/shard_map/all_to_all | solution.py:213
  83.9 25.3 %collective-permute-start.3 = (bf16[256,768]{1,0:T(8,128)(2,1)S(1)}, bf16[256,768]{1,0:T(8,128)(2,1)S(1)}, u32[]{:S(2)}, u32[]{:S(2)}) collective-permute-start(bf16[256,768]{1,0:T(8,128)(2,1)S(1)} %get-tuple-element.37), channel_id=1, source_target_pairs={{3,2},{2,1},{0,3},{7,6},{6,5},{4,7},{11,10},{10,9},{8,11},{15,14},... | collective-permute-start | bytes 1179656 | tf_op jit(solution)/shard_map/ppermute | solution.py:143
  85.2 24.1 %collective-permute-start.4 = (bf16[256,768]{1,0:T(8,128)(2,1)S(1)}, bf16[256,768]{1,0:T(8,128)(2,1)}, u32[]{:S(2)}, u32[]{:S(2)}) collective-permute-start(bf16[256,768]{1,0:T(8,128)(2,1)S(1)} %get-tuple-element.38), channel_id=1, source_target_pairs={{2,3},{1,2},{0,1},{6,7},{5,6},{4,5},{10,11},{9,10},{8,9},{14,15},{... | collective-permute-start | bytes 1179656 | tf_op jit(solution)/shard_map/ppermute | solution.py:143
  89.2 32.9 %collective-permute-start.5 = (bf16[256,768]{1,0:T(8,128)(2,1)S(1)}, bf16[256,768]{1,0:T(8,128)(2,1)}, u32[]{:S(2)}, u32[]{:S(2)}) collective-permute-start(bf16[256,768]{1,0:T(8,128)(2,1)S(1)} %get-tuple-element.36), channel_id=1, source_target_pairs={{3,1},{1,3},{0,2},{7,5},{5,7},{4,6},{11,9},{9,11},{8,10},{15,13},{... | collective-permute-start | bytes 1179656 | tf_op jit(solution)/shard_map/ppermute | solution.py:143
  114.0 8.1 %copy-start.3 = (bf16[3,256,768]{2,1,0:T(8,128)(2,1)S(1)}, bf16[3,256,768]{2,1,0:T(8,128)(2,1)}, u32[]{:S(2)}) copy-start(bf16[3,256,768]{2,1,0:T(8,128)(2,1)} %copy-done.2) | copy-start | bytes 3538948
  114.0 8.1 %copy-start.19 = (bf16[256,768]{1,0:T(8,128)(2,1)S(1)}, bf16[256,768]{1,0:T(8,128)(2,1)}, u32[]{:S(2)}) copy-start(bf16[256,768]{1,0:T(8,128)(2,1)} %copy-done.18) | copy-start | bytes 1179652
  115.1 17.7 %copy-start.16 = (s32[768,384]{1,0:T(8,128)S(1)}, s32[768,384]{1,0:T(8,128)}, u32[]{:S(2)}) copy-start(s32[768,384]{1,0:T(8,128)} %param.18) | copy-start | bytes 3538948
  124.3 43.2 %collective-permute-start.6 = (bf16[256,768]{1,0:T(8,128)(2,1)}, bf16[256,768]{1,0:T(8,128)(2,1)}, u32[]{:S(2)}, u32[]{:S(2)}) collective-permute-start(bf16[256,768]{1,0:T(8,128)(2,1)} %fusion.11), channel_id=1, source_target_pairs={{0,16},{4,20},{8,24},{12,28},{16,0},{20,4},{24,8},{28,12},{1,17},{... | collective-permute-start | bytes 1179656 | tf_op jit(solution)/shard_map/ppermute | solution.py:299
  124.3 13.4 %collective-permute-start.7 = (bf16[256,768]{1,0:T(8,128)(2,1)}, bf16[256,768]{1,0:T(8,128)(2,1)S(1)}, u32[]{:S(2)}, u32[]{:S(2)}) collective-permute-start(bf16[256,768]{1,0:T(8,128)(2,1)} %get-tuple-element.39), channel_id=1, source_target_pairs={{0,1},{1,2},{3,0},{4,5},{5,6},{7,4},{8,9},{9,10},{11,8},{12,13},{1... | collective-permute-start | bytes 1179656 | tf_op jit(solution)/shard_map/ppermute | solution.py:143
  126.7 21.3 %collective-permute-start.8 = (bf16[256,768]{1,0:T(8,128)(2,1)}, bf16[256,768]{1,0:T(8,128)(2,1)}, u32[]{:S(2)}, u32[]{:S(2)}) collective-permute-start(bf16[256,768]{1,0:T(8,128)(2,1)} %get-tuple-element.41), channel_id=1, source_target_pairs={{0,2},{2,0},{3,1},{4,6},{6,4},{7,5},{8,10},{10,8},{11,9},{12,14},{... | collective-permute-start | bytes 1179656 | tf_op jit(solution)/shard_map/ppermute | solution.py:143
  128.0 38.0 %collective-permute-start.9 = (bf16[256,768]{1,0:T(8,128)(2,1)}, bf16[256,768]{1,0:T(8,128)(2,1)}, u32[]{:S(2)}, u32[]{:S(2)}) collective-permute-start(bf16[256,768]{1,0:T(8,128)(2,1)} %get-tuple-element.40), channel_id=1, source_target_pairs={{1,0},{2,1},{3,2},{5,4},{6,5},{7,6},{9,8},{10,9},{11,10},{13,12},{... | collective-permute-start | bytes 1179656 | tf_op jit(solution)/shard_map/ppermute | solution.py:143
  136.7 30.8 %copy-start.17 = (bf16[48,16,768]{2,1,0:T(8,128)(2,1)S(1)}, bf16[48,16,768]{2,1,0:T(8,128)(2,1)}, u32[]{:S(2)}) copy-start(bf16[48,16,768]{2,1,0:T(8,128)(2,1)} %param.19) | copy-start | bytes 3538948
  (10 other events, 9.7 us)

commit v8 on v7

--- a/solution.py
+++ b/solution.py
@@ -32,22 +32,103 @@
     return cosine, -sine, table_right
 
 
-def spectrum_kernel(runs, images, left, right, row_factors, col_factors, *rest):
-    *meta, out, joined = rest
+def spread(iota, values):
+    out = jnp.full(iota.shape, values[0])
+    for p in range(1, len(values)):
+        out = jnp.where(iota == p, values[p], out)
+    return out
+
+
+def phase_angle(freq, shift, length):
+    turns = freq * shift
+    turns = turns - length * jnp.floor(turns * (1.0 / length))
+    return (2.0 * math.pi / length) * turns
+
+
+def centred(freq, length):
+    return jnp.where(freq < length // 2, freq, freq - length) * (1.0 / length)
+
+
+def spectrum_kernel(
+    runs,
+    with_meta,
+    classes,
+    shifts,
+    defocus_class,
+    defocus,
+    run_counts,
+    images_in,
+    left_in,
+    right_in,
+    out,
+    images,
+    left,
+    right,
+    joined,
+    block,
+    load_sems,
+    send_sem,
+):
     particles, length = images.shape[0], images.shape[1]
     owners = out.shape[0]
     rows_each = runs[0][1] - runs[0][0]
     rows = owners * rows_each
-    for block in meta:
+    loads = [pltpu.make_async_copy(left_in, left, load_sems.at[0])]
+    for p in range(particles):
+        loads.append(pltpu.make_async_copy(images_in.at[p], images.at[p], load_sems.at[1 + p]))
+    loads.append(pltpu.make_async_copy(right_in, right, load_sems.at[1 + particles]))
+    for load in loads:
+        load.start()
+
+    every = range(particles)
+    focus = [defocus[defocus_class[p]] for p in every]
+    shift_x = [shifts[p, 0].astype(jnp.float32) for p in every]
+    shift_y = [shifts[p, 1].astype(jnp.float32) for p in every]
+    sublane = lax.broadcasted_iota(jnp.int32, (particles, length), 0)
+    freq_x = lax.broadcasted_iota(jnp.int32, (particles, length), 1).astype(jnp.float32)
+    phase_x = phase_angle(freq_x, spread(sublane, shift_x), length)
+    angle_x = spread(sublane, focus) * centred(freq_x, length) * centred(freq_x, length)
+    col = [jnp.sin(phase_x), jnp.cos(phase_x), jnp.sin(angle_x), jnp.cos(angle_x)]
+    lane = lax.broadcasted_iota(jnp.int32, (rows, LANES), 1)
+    which = lane % particles
+    quantity = lane // particles
+    row_at = lax.broadcasted_iota(jnp.int32, (rows, LANES), 0)
+    owner = row_at // rows_each
+    freq_y = row_at - owner * rows_each + spread(owner, [begin for begin, _ in runs])
+    freq_y = freq_y.astype(jnp.float32)
+    phase_y = phase_angle(freq_y, spread(which, shift_y), length)
+    angle_y = spread(which, focus) * centred(freq_y, length) * centred(freq_y, length)
+    angles = jnp.where(quantity < 2, phase_y, angle_y + PHASE_OFFSET)
+    row = jnp.sin(angles + jnp.where(quantity % 2 == 1, 0.5 * math.pi, 0.0))
+
+    if with_meta:
+        digits = jnp.zeros((META_ROWS, LANES), jnp.int32)
+        at_row = lax.broadcasted_iota(jnp.int32, (META_ROWS, LANES), 0) % particles
+        at_lane = lax.broadcasted_iota(jnp.int32, (META_ROWS, LANES), 1)
+        ends = [[run_counts[p, 0] for p in every]]
+        for s in range(1, run_counts.shape[1] - 1):
+            ends.append([ends[-1][p] + run_counts[p, s] for p in every])
+        fields = [[classes[p] for p in every], [defocus_class[p] for p in every], *ends]
+        for f, values in enumerate(fields):
+            value = spread(at_row, values)
+            digits = jnp.where(at_lane == f, value // META_BASE, digits)
+            digits = jnp.where(at_lane == f + len(fields), value % META_BASE, digits)
+        digits = digits.astype(jnp.float32).astype(jnp.bfloat16)
         for d in range(owners):
-            out[d, particles * rows_each :, :] = block[...]
+            block[d, particles * rows_each :, :] = jnp.zeros(
+                (META_ROWS, 2 * length), jnp.bfloat16
+            )
+            block[d, particles * rows_each :, :LANES] = digits
+
+    loads[0].wait()
     table = left[...]
     for p in range(particles):
+        loads[1 + p].wait()
         section = jnp.dot(table, images[p], preferred_element_type=jnp.float32)
         section = section.astype(jnp.bfloat16)
         joined[p * rows : (p + 1) * rows, :length] = section[:rows]
         joined[p * rows : (p + 1) * rows, length:] = section[rows:]
-    factors = jnp.concatenate([row_factors[begin:end, :] for begin, end in runs], axis=0)
+    loads[1 + particles].wait()
     for first in range(0, particles, 2):
         spectrum = jnp.dot(
             joined[first * rows : (first + 2) * rows, :],
@@ -57,24 +138,22 @@
         for p in range(first, first + 2):
             part = spectrum[(p - first) * rows : (p - first + 1) * rows]
             real_part, imag_part = part[:, :length], part[:, length:]
-
-            def row(q):
-                at = q * particles + p
-                return factors[:, at : at + 1]
-
-            def col(q):
-                at = q * particles + p
-                return col_factors[at : at + 1, :]
-
-            transfer = -(row(2) * col(3) + row(3) * col(2))
-            cosine = transfer * (row(1) * col(1) - row(0) * col(0))
-            sine = transfer * (row(0) * col(1) + row(1) * col(0))
+            row_sin, row_cos, row_ctf_sin, row_ctf_cos = [
+                row[:, q * particles + p : q * particles + p + 1] for q in range(4)
+            ]
+            col_sin, col_cos, col_ctf_sin, col_ctf_cos = [part[p : p + 1, :] for part in col]
+            transfer = -(row_ctf_sin * col_ctf_cos + row_ctf_cos * col_ctf_sin)
+            cosine = transfer * (row_cos * col_cos - row_sin * col_sin)
+            sine = transfer * (row_sin * col_cos + row_cos * col_sin)
             real_new = real_part * cosine + imag_part * sine
             imag_new = imag_part * cosine - real_part * sine
             weighted = jnp.concatenate([real_new, imag_new], axis=1).astype(jnp.bfloat16)
-            out[:, p * rows_each : (p + 1) * rows_each, :] = weighted.reshape(
+            block[:, p * rows_each : (p + 1) * rows_each, :] = weighted.reshape(
                 owners, rows_each, 2 * length
             )
+    send = pltpu.make_async_copy(block, out, send_sem)
+    send.start()
+    send.wait()
 
 
 def insert_kernel(bins, meta_at, received, codes, out):
@@ -103,28 +182,10 @@
     return [pl.BlockSpec(memory_space=pltpu.VMEM)] * count
 
 
-def lookup(values, indices):
-    matches = indices[:, None] == jnp.arange(values.shape[0], dtype=jnp.int32)[None, :]
-    return jnp.sum(jnp.where(matches, values[None, :], 0.0), axis=1)
-
-
 def centred_square(freq, length):
     half_length = length // 2
     value = ((freq + half_length) % length - half_length).astype(jnp.float32) / length
     return value * value
-
-
-def trig_factors(shift, focus, freq, offset, length, axis):
-    if axis == 0:
-        freq, shift, focus = freq[:, None], shift[None, :], focus[None, :]
-    else:
-        freq, shift, focus = freq[None, :], shift[:, None], focus[:, None]
-    turns = (freq * shift) % length
-    phase = 2.0 * math.pi / length * turns.astype(jnp.float32)
-    angle = focus * centred_square(freq, length) + offset
-    return jnp.concatenate(
-        [jnp.sin(phase), jnp.cos(phase), jnp.sin(angle), jnp.cos(angle)], axis=1 - axis
-    )
 
 
 def slab_exchange(parts, place, slab_count, batch_count, swapped):
@@ -166,18 +227,10 @@
     swaps = [mirrored and swapped for _, swapped in CHUNKS]
     freq = jnp.arange(length, dtype=jnp.int32)
 
-    ends = jnp.cumsum(run_counts, axis=1)[:, : slab_count - 1]
-    meta = jnp.concatenate([classes[:, None], defocus_class[:, None], ends], axis=1)
-    fields = meta.shape[1]
-    digits = jnp.concatenate([meta // META_BASE, meta % META_BASE], axis=1).astype(jnp.bfloat16)
-    digits = jnp.concatenate([digits] * (META_ROWS // particles), axis=0)
-    digits = jnp.pad(digits, ((0, META_ROWS - len(digits)), (0, 2 * length - 2 * fields)))
+    fields = slab_count + 1
 
     cosine, minus_sine, table_right = dft_tables(length)
     table_right = jnp.asarray(table_right.astype(jnp.bfloat16))
-    focus = lookup(defocus, defocus_class)
-    row_factors = trig_factors(shifts[:, 1], focus, freq, PHASE_OFFSET, length, 0)
-    col_factors = trig_factors(shifts[:, 0], focus, freq, 0.0, length, 1)
     received = []
     weighted = []
     for c, each in enumerate(sizes):
@@ -186,28 +239,37 @@
         order = (block[:, None] * rows + starts[c] + np.arange(each)[None, :]).reshape(-1)
         left = np.concatenate([cosine[order], minus_sine[order]], axis=0)
         runs = [(k * rows + starts[c], k * rows + starts[c] + each) for k in block.tolist()]
-        extra = (digits,) if c == 0 else ()
-        block_rows = particles * each + META_ROWS * len(extra)
+        with_meta = c == 0
+        block_rows = particles * each + META_ROWS * with_meta
+        block_shape = (batch_count, block_rows, 2 * length)
+        smem = pl.BlockSpec(memory_space=pltpu.SMEM)
+        hbm = pl.BlockSpec(memory_space=pltpu.HBM)
         send = pl.pallas_call(
-            functools.partial(spectrum_kernel, runs),
-            out_shape=jax.ShapeDtypeStruct((batch_count, block_rows, 2 * length), jnp.bfloat16),
-            in_specs=whole_vmem(5 + len(extra)),
-            out_specs=pl.BlockSpec(memory_space=pltpu.VMEM),
-            scratch_shapes=[pltpu.VMEM((particles * chunk_rows, 2 * length), jnp.bfloat16)],
+            functools.partial(spectrum_kernel, runs, with_meta),
+            out_shape=jax.ShapeDtypeStruct(block_shape, jnp.bfloat16),
+            in_specs=[smem] * 5 + [hbm] * 3,
+            out_specs=hbm,
+            scratch_shapes=[
+                pltpu.VMEM((particles, length, length), jnp.bfloat16),
+                pltpu.VMEM((2 * chunk_rows, length), jnp.bfloat16),
+                pltpu.VMEM((2 * length, 2 * length), jnp.bfloat16),
+                pltpu.VMEM((particles * chunk_rows, 2 * length), jnp.bfloat16),
+                pltpu.VMEM(block_shape, jnp.bfloat16),
+                pltpu.SemaphoreType.DMA((particles + 2,)),
+                pltpu.SemaphoreType.DMA,
+            ],
             compiler_params=pltpu.CompilerParams(vmem_limit_bytes=VMEM_LIMIT),
-            cost_estimate=pl.CostEstimate(
-                flops=0,
-                bytes_accessed=0,
-                transcendentals=0,
-            ),
+            cost_estimate=pl.CostEstimate(flops=0, bytes_accessed=0, transcendentals=0),
             name="spectrum",
         )(
+            classes,
+            shifts,
+            defocus_class,
+            defocus,
+            run_counts,
             images,
             jnp.asarray(left.astype(jnp.bfloat16)),
             table_right,
-            row_factors,
-            col_factors,
-            *extra,
         )
         weighted.append(send)
         received.append(lax.all_to_all(send, "batch", 0, 0, tiled=True))
@@ -263,9 +325,7 @@
         if c + 1 < len(sizes):
             codes_in, _ = lax.optimization_barrier((codes_in, weighted[c + 1]))
         if c > 0 and mirrored:
-            near = [arrived[c - 1][0], arrived[c - 1][2]]
-            codes_in, *near = lax.optimization_barrier((codes_in, *near))
-            arrived[c - 1][0], arrived[c - 1][2] = near[:2]
+            codes_in, arrived[c - 1][2] = lax.optimization_barrier((codes_in, arrived[c - 1][2]))
         parts = pl.pallas_call(
             functools.partial(insert_kernel, bins, meta_at),
             out_shape=jax.ShapeDtypeStruct(
@@ -295,6 +355,8 @@
         for block in arrived[c]:
             sums[c] = sums[c] + block[: each * planes].astype(jnp.float32)
         if swaps[c]:
+            if c + 1 < len(sizes):
+                sums[c], arrived[-1][0] = lax.optimization_barrier((sums[c], arrived[-1][0]))
             over = [(b, (b + half_batch) % batch_count) for b in range(batch_count)]
             sums[c] = lax.ppermute(sums[c].astype(jnp.bfloat16), "batch", over)
 

time: 171 us -> 176 us (1.029)
  the two profiles are of different devices: /device:TPU:9 before, /device:TPU:11 now
where the time goes in v8:
time: 176 us; the launch traced here: 174 us
  waiting for transfers between devices  60 us (34%)
  starting transfers between devices  41.6 us (24%)
  Pallas kernels  28 us (16%)
  local copies, waits for them, and re-layouts  26.3 us (15%)
  other arithmetic  14.2 us (8%)
  matrix products  3.45 us (2%)
    ppermute x9, waiting for transfers between devices, slab_exchange(): arrived.append(lax.ppermute(block, ('batch', 'slab'), perm))  48.7 us
    ppermute x9, starting transfers between devices, slab_exchange(): arrived.append(lax.ppermute(block, ('batch', 'slab'), perm))  23.3 us
    pallas_call x3, Pallas kernels, per_device(): pl.pallas_call(functools.partial(spectrum_kernel, runs, with_meta), out_s...  19.2 us
    unnamed x74, local copies, waits for them, and re-layouts  18.2 us
    all_to_all x3, starting transfers between devices, per_device(): received.append(lax.all_to_all(send, 'batch', 0, 0, tiled=True))  16 us
    all_to_all x3, waiting for transfers between devices, per_device(): received.append(lax.all_to_all(send, 'batch', 0, 0, tiled=True))  11.4 us
    pallas_call x3, Pallas kernels, per_device(): pl.pallas_call(functools.partial(insert_kernel, bins, meta_at), out_shape...  8.77 us
    add x3, other arithmetic, per_device(): sums[c] = sums[c] + block[:each * planes].astype(jnp.float32)  4.6 us
  transfers between devices with their start and end apart: 13, of which 5 were waited for; matrix products, arithmetic and copies ran while one was open for 15% of the time, Pallas kernels for 12%

profile of v8, /device:TPU:11, one launch (start us, length us, event | category | flops | bytes accessed | tf_op | source)
XLA Modules:
  0.0 174.2 jit_solution(15824171020262083622)
XLA Ops:
  1.5 1.7 copy-done
  7.3 6.7 %spectrum.3 = bf16[8,144,768]{2,1,0:T(8,128)(2,1)S(1)} custom-call(s32[8]{0:T(128)S(1)} %copy-done.17, s32[8,2]{1,0:T(8,128)S(1)} %copy.70.shifts, s32[8]{0:T(128)S(1)} %copy-done.20, f32[16]{0:T(128)S(1)} %copy-done.14, s32[8,4]{1,0:T(8,128)S(1)} %copy.71.run_counts, bf16[8,384,384]{2,1,0:T(8,128)(2,1)S(1)} %copy-done, bf16[256,384]{1,0:T(8,128)(2,1)S(1)} %copy-done.13, ...), custom_call_target="tpu_custom_call" | custom-call | tf_op jit(solution)/shard_map/spectrum/pallas_call | solution.py:247
  15.2 5.3 %all-to-all-start = ((bf16[8,144,768]{2,1,0:T(8,128)(2,1)}), bf16[8,144,768]{2,1,0:T(8,128)(2,1)}, u32[]{:S(2)}, u32[]{:S(2)}) async-start(bf16[8,144,768]{2,1,0:T(8,128)(2,1)} %copy-done.8), calls=%async_computation | async-start | bytes 3538944 | tf_op jit(solution)/shard_map/all_to_all | solution.py:275
  22.2 6.3 %spectrum.4 = bf16[8,128,768]{2,1,0:T(8,128)(2,1)S(1)} custom-call(s32[8]{0:T(128)S(1)} %copy-done.18, s32[8,2]{1,0:T(8,128)S(1)} %copy.70.shifts, s32[8]{0:T(128)S(1)} %copy-done.21, f32[16]{0:T(128)S(1)} %copy-done.15, s32[8,4]{1,0:T(8,128)S(1)} %copy.71.run_counts, bf16[8,384,384]{2,1,0:T(8,128)(2,1)S(1)} %copy-done.1, bf16[256,384]{1,0:T(8,128)(2,1)S(1)} %copy-done.12, ...), custom_call_target="tpu_custom_call" | custom-call | tf_op jit(solution)/shard_map/spectrum/pallas_call | solution.py:247
  30.8 11.4 %all-to-all-done.received = bf16[8,144,768]{2,1,0:T(8,128)(2,1)} async-done(((bf16[8,144,768]{2,1,0:T(8,128)(2,1)}), bf16[8,144,768]{2,1,0:T(8,128)(2,1)}, u32[]{:S(2)}, u32[]{:S(2)}) %all-to-all-start) | async-done | bytes 1769504 | tf_op jit(solution)/shard_map/all_to_all | solution.py:275
  42.2 5.8 %all-to-all-start.1 = ((bf16[8,128,768]{2,1,0:T(8,128)(2,1)}), bf16[8,128,768]{2,1,0:T(8,128)(2,1)}, u32[]{:S(2)}, u32[]{:S(2)}) async-start(bf16[8,128,768]{2,1,0:T(8,128)(2,1)} %copy-done.9), calls=%async_computation.1 | async-start | bytes 3145728 | tf_op jit(solution)/shard_map/all_to_all | solution.py:275
  56.6 3.2 %insert.3 = bf16[3,272,768]{2,1,0:T(8,128)(2,1)S(1)} custom-call(bf16[8,144,768]{2,1,0:T(8,128)(2,1)} %all-to-all-done.received, s32[1,1152]{1,0:T(1,128)S(1)} %reshape.200.codes), custom_call_target="tpu_custom_call" | custom-call | tf_op jit(solution)/shard_map/insert/pallas_call | solution.py:329
  61.3 2.1 %collective-permute-start.2 = (bf16[272,768]{1,0:T(8,128)(2,1)}, bf16[272,768]{1,0:T(8,128)(2,1)}, u32[]{:S(2)}, u32[]{:S(2)}) collective-permute-start(bf16[272,768]{1,0:T(8,128)(2,1)} %get-tuple-element.28), channel_id=1, source_target_pairs={{1,0},{2,1},{3,2},{5,4},{6,5},{7,6},{9,8},{10,9},{11,10},{13,12},{... | collective-permute-start | bytes 1253384 | tf_op jit(solution)/shard_map/ppermute | solution.py:204
  65.7 6.3 %spectrum.5 = bf16[8,128,768]{2,1,0:T(8,128)(2,1)S(1)} custom-call(s32[8]{0:T(128)S(1)} %copy-done.19, s32[8,2]{1,0:T(8,128)S(1)} %copy.70.shifts, s32[8]{0:T(128)S(1)} %copy-done.22, f32[16]{0:T(128)S(1)} %copy-done.16, s32[8,4]{1,0:T(8,128)S(1)} %copy.71.run_counts, bf16[8,384,384]{2,1,0:T(8,128)(2,1)S(1)} %copy-done.1, bf16[256,384]{1,0:T(8,128)(2,1)S(1)} %copy-done.11, ...), custom_call_target="tpu_custom_call" | custom-call | tf_op jit(solution)/shard_map/spectrum/pallas_call | solution.py:247
  76.0 4.0 %collective-permute-start = (bf16[272,768]{1,0:T(8,128)(2,1)}, bf16[272,768]{1,0:T(8,128)(2,1)}, u32[]{:S(2)}, u32[]{:S(2)}) collective-permute-start(bf16[272,768]{1,0:T(8,128)(2,1)} %get-tuple-element.27), channel_id=1, source_target_pairs={{0,1},{1,2},{3,0},{4,5},{5,6},{7,4},{8,9},{9,10},{11,8},{12,13},{1... | collective-permute-start | bytes 1253384 | tf_op jit(solution)/shard_map/ppermute | solution.py:204
  81.9 4.9 %all-to-all-start.2 = ((bf16[8,128,768]{2,1,0:T(8,128)(2,1)}), bf16[8,128,768]{2,1,0:T(8,128)(2,1)}, u32[]{:S(2)}, u32[]{:S(2)}) async-start(bf16[8,128,768]{2,1,0:T(8,128)(2,1)} %copy-done.10), calls=%async_computation.2 | async-start | bytes 3145728 | tf_op jit(solution)/shard_map/all_to_all | solution.py:275
  86.8 2.8 %insert.4 = bf16[3,256,768]{2,1,0:T(8,128)(2,1)S(1)} custom-call(bf16[8,128,768]{2,1,0:T(8,128)(2,1)} %all-to-all-done.1.received, s32[1,1024]{1,0:T(1,128)S(1)} %reshape_reshape.6.codes), custom_call_target="tpu_custom_call" | custom-call | tf_op jit(solution)/shard_map/insert/pallas_call | solution.py:329
  90.5 3.5 %collective-permute-start.3 = (bf16[256,768]{1,0:T(8,128)(2,1)S(1)}, bf16[256,768]{1,0:T(8,128)(2,1)S(1)}, u32[]{:S(2)}, u32[]{:S(2)}) collective-permute-start(bf16[256,768]{1,0:T(8,128)(2,1)S(1)} %get-tuple-element.41), channel_id=1, source_target_pairs={{2,3},{1,2},{0,1},{6,7},{5,6},{4,5},{10,11},{9,10},{8,9},{14,15},{... | collective-permute-start | bytes 1179656 | tf_op jit(solution)/shard_map/ppermute | solution.py:204
  94.0 4.0 %collective-permute-start.5 = (bf16[256,768]{1,0:T(8,128)(2,1)S(1)}, bf16[256,768]{1,0:T(8,128)(2,1)}, u32[]{:S(2)}, u32[]{:S(2)}) collective-permute-start(bf16[256,768]{1,0:T(8,128)(2,1)S(1)} %get-tuple-element.40), channel_id=1, source_target_pairs={{3,1},{1,3},{0,2},{7,5},{5,7},{4,6},{11,9},{9,11},{8,10},{15,13},{... | collective-permute-start | bytes 1179656 | tf_op jit(solution)/shard_map/ppermute | solution.py:204
  101.3 5.1 %collective-permute-done.3 = bf16[256,768]{1,0:T(8,128)(2,1)S(1)} collective-permute-done((bf16[256,768]{1,0:T(8,128)(2,1)S(1)}, bf16[256,768]{1,0:T(8,128)(2,1)S(1)}, u32[]{:S(2)}, u32[]{:S(2)}) %collective-permute-start.3) | collective-permute-done | bytes 393248 | tf_op jit(solution)/shard_map/ppermute | solution.py:204
  107.2 2.8 %insert.5 = bf16[3,256,768]{2,1,0:T(8,128)(2,1)S(1)} custom-call(bf16[8,128,768]{2,1,0:T(8,128)(2,1)} %all-to-all-done.2.received, s32[1,1024]{1,0:T(1,128)S(1)} %reshape_reshape.7.codes), custom_call_target="tpu_custom_call" | custom-call | tf_op jit(solution)/shard_map/insert/pallas_call | solution.py:329
  111.6 19.6 %collective-permute-done.5 = bf16[256,768]{1,0:T(8,128)(2,1)} collective-permute-done((bf16[256,768]{1,0:T(8,128)(2,1)S(1)}, bf16[256,768]{1,0:T(8,128)(2,1)}, u32[]{:S(2)}, u32[]{:S(2)}) %collective-permute-start.5) | collective-permute-done | bytes 393248 | tf_op jit(solution)/shard_map/ppermute | solution.py:204
  131.2 1.9 %collective-permute-start.6 = (bf16[256,768]{1,0:T(8,128)(2,1)}, bf16[256,768]{1,0:T(8,128)(2,1)}, u32[]{:S(2)}, u32[]{:S(2)}) collective-permute-start(bf16[256,768]{1,0:T(8,128)(2,1)} %get-tuple-element.36), channel_id=1, source_target_pairs={{0,1},{1,2},{3,0},{4,5},{5,6},{7,4},{8,9},{9,10},{11,8},{12,13},{1... | collective-permute-start | bytes 1179656 | tf_op jit(solution)/shard_map/ppermute | solution.py:204
  134.4 4.0 %collective-permute-start.9 = (bf16[256,768]{1,0:T(8,128)(2,1)}, bf16[256,768]{1,0:T(8,128)(2,1)}, u32[]{:S(2)}, u32[]{:S(2)}) collective-permute-start(bf16[256,768]{1,0:T(8,128)(2,1)} %get-tuple-element.37), channel_id=1, source_target_pairs={{1,0},{2,1},{3,2},{5,4},{6,5},{7,6},{9,8},{10,9},{11,10},{13,12},{... | collective-permute-start | bytes 1179656 | tf_op jit(solution)/shard_map/ppermute | solution.py:204
  139.9 1.6 fusion.12
  144.6 2.3 %collective-permute-start.7 = (bf16[256,768]{1,0:T(8,128)(2,1)S(1)}, bf16[256,768]{1,0:T(8,128)(2,1)S(1)}, u32[]{:S(2)}, u32[]{:S(2)}) collective-permute-start(bf16[256,768]{1,0:T(8,128)(2,1)S(1)} %fusion.10), channel_id=1, source_target_pairs={{0,16},{4,20},{8,24},{12,28},{16,0},{20,4},{24,8},{28,12},{1,17},{... | collective-permute-start | bytes 1179656 | tf_op jit(solution)/shard_map/ppermute | solution.py:361
  147.0 6.6 %collective-permute-done.8 = bf16[256,768]{1,0:T(8,128)(2,1)} collective-permute-done((bf16[256,768]{1,0:T(8,128)(2,1)}, bf16[256,768]{1,0:T(8,128)(2,1)}, u32[]{:S(2)}, u32[]{:S(2)}) %collective-permute-start.8) | collective-permute-done | bytes 393248 | tf_op jit(solution)/shard_map/ppermute | solution.py:204
  153.6 17.3 %collective-permute-done.9 = bf16[256,768]{1,0:T(8,128)(2,1)} collective-permute-done((bf16[256,768]{1,0:T(8,128)(2,1)}, bf16[256,768]{1,0:T(8,128)(2,1)}, u32[]{:S(2)}, u32[]{:S(2)}) %collective-permute-start.9) | collective-permute-done | bytes 393248 | tf_op jit(solution)/shard_map/ppermute | solution.py:204
  170.9 1.5 fusion.8
  (133 shorter events, 43.1 us)
Async XLA Ops:
  15.2 5.3 %copy-start.1 = (bf16[8,384,384]{2,1,0:T(8,128)(2,1)S(1)}, bf16[8,384,384]{2,1,0:T(8,128)(2,1)}, u32[]{:S(2)}) copy-start(bf16[8,384,384]{2,1,0:T(8,128)(2,1)} %images_in.5) | copy-start | bytes 7077892
  15.2 5.3 %copy-start.7 = (bf16[768,768]{1,0:T(8,128)(2,1)S(1)}, bf16[768,768]{1,0:T(8,128)(2,1)}, u32[]{:S(2)}) copy-start(bf16[768,768]{1,0:T(8,128)(2,1)} %constant.177.clone.right_in) | copy-start | bytes 3538948
  15.2 5.3 %copy-start.15 = (f32[16]{0:T(128)S(1)}, f32[16]{0:T(128)}, u32[]{:S(2)}) copy-start(f32[16]{0:T(128)} %defocus.5) | copy-start | bytes 196
  15.2 5.3 %copy-start.18 = (s32[8]{0:T(128)S(1)}, s32[8]{0:T(128)}, u32[]{:S(2)}) copy-start(s32[8]{0:T(128)} %classes.5) | copy-start | bytes 100
  15.2 27.0 %all-to-all-start = ((bf16[8,144,768]{2,1,0:T(8,128)(2,1)}), bf16[8,144,768]{2,1,0:T(8,128)(2,1)}, u32[]{:S(2)}, u32[]{:S(2)}) async-start(bf16[8,144,768]{2,1,0:T(8,128)(2,1)} %copy-done.8), calls=%async_computation | async-start | bytes 3538944 | tf_op jit(solution)/shard_map/all_to_all | solution.py:275
  42.2 39.7 %all-to-all-start.1 = ((bf16[8,128,768]{2,1,0:T(8,128)(2,1)}), bf16[8,128,768]{2,1,0:T(8,128)(2,1)}, u32[]{:S(2)}, u32[]{:S(2)}) async-start(bf16[8,128,768]{2,1,0:T(8,128)(2,1)} %copy-done.9), calls=%async_computation.1 | async-start | bytes 3145728 | tf_op jit(solution)/shard_map/all_to_all | solution.py:275
  59.8 3.6 %copy-start.16 = (f32[16]{0:T(128)S(1)}, f32[16]{0:T(128)}, u32[]{:S(2)}) copy-start(f32[16]{0:T(128)} %defocus.5) | copy-start | bytes 196
  59.8 4.3 %copy-start.19 = (s32[8]{0:T(128)S(1)}, s32[8]{0:T(128)}, u32[]{:S(2)}) copy-start(s32[8]{0:T(128)} %classes.5) | copy-start | bytes 100
  61.3 20.6 %collective-permute-start.2 = (bf16[272,768]{1,0:T(8,128)(2,1)}, bf16[272,768]{1,0:T(8,128)(2,1)}, u32[]{:S(2)}, u32[]{:S(2)}) collective-permute-start(bf16[272,768]{1,0:T(8,128)(2,1)} %get-tuple-element.28), channel_id=1, source_target_pairs={{1,0},{2,1},{3,2},{5,4},{6,5},{7,6},{9,8},{10,9},{11,10},{13,12},{... | collective-permute-start | bytes 1253384 | tf_op jit(solution)/shard_map/ppermute | solution.py:204
  74.8 24.5 %collective-permute-start.1 = (bf16[272,768]{1,0:T(8,128)(2,1)}, bf16[272,768]{1,0:T(8,128)(2,1)S(1)}, u32[]{:S(2)}, u32[]{:S(2)}) collective-permute-start(bf16[272,768]{1,0:T(8,128)(2,1)} %get-tuple-element.29), channel_id=1, source_target_pairs={{0,2},{2,0},{3,1},{4,6},{6,4},{7,5},{8,10},{10,8},{11,9},{12,14},{... | collective-permute-start | bytes 1253384 | tf_op jit(solution)/shard_map/ppermute | solution.py:204
  76.0 23.2 %collective-permute-start = (bf16[272,768]{1,0:T(8,128)(2,1)}, bf16[272,768]{1,0:T(8,128)(2,1)}, u32[]{:S(2)}, u32[]{:S(2)}) collective-permute-start(bf16[272,768]{1,0:T(8,128)(2,1)} %get-tuple-element.27), channel_id=1, source_target_pairs={{0,1},{1,2},{3,0},{4,5},{5,6},{7,4},{8,9},{9,10},{11,8},{12,13},{1... | collective-permute-start | bytes 1253384 | tf_op jit(solution)/shard_map/ppermute | solution.py:204
  81.9 25.3 %all-to-all-start.2 = ((bf16[8,128,768]{2,1,0:T(8,128)(2,1)}), bf16[8,128,768]{2,1,0:T(8,128)(2,1)}, u32[]{:S(2)}, u32[]{:S(2)}) async-start(bf16[8,128,768]{2,1,0:T(8,128)(2,1)} %copy-done.10), calls=%async_computation.2 | async-start | bytes 3145728 | tf_op jit(solution)/shard_map/all_to_all | solution.py:275
  90.5 15.9 %collective-permute-start.3 = (bf16[256,768]{1,0:T(8,128)(2,1)S(1)}, bf16[256,768]{1,0:T(8,128)(2,1)S(1)}, u32[]{:S(2)}, u32[]{:S(2)}) collective-permute-start(bf16[256,768]{1,0:T(8,128)(2,1)S(1)} %get-tuple-element.41), channel_id=1, source_target_pairs={{2,3},{1,2},{0,1},{6,7},{5,6},{4,5},{10,11},{9,10},{8,9},{14,15},{... | collective-permute-start | bytes 1179656 | tf_op jit(solution)/shard_map/ppermute | solution.py:204
  94.0 37.3 %collective-permute-start.5 = (bf16[256,768]{1,0:T(8,128)(2,1)S(1)}, bf16[256,768]{1,0:T(8,128)(2,1)}, u32[]{:S(2)}, u32[]{:S(2)}) collective-permute-start(bf16[256,768]{1,0:T(8,128)(2,1)S(1)} %get-tuple-element.40), channel_id=1, source_target_pairs={{3,1},{1,3},{0,2},{7,5},{5,7},{4,6},{11,9},{9,11},{8,10},{15,13},{... | collective-permute-start | bytes 1179656 | tf_op jit(solution)/shard_map/ppermute | solution.py:204
  98.0 43.6 %collective-permute-start.4 = (bf16[256,768]{1,0:T(8,128)(2,1)}, bf16[256,768]{1,0:T(8,128)(2,1)}, u32[]{:S(2)}, u32[]{:S(2)}) collective-permute-start(bf16[256,768]{1,0:T(8,128)(2,1)} %get-tuple-element.39), channel_id=1, source_target_pairs={{3,2},{2,1},{0,3},{7,6},{6,5},{4,7},{11,10},{10,9},{8,11},{15,14},... | collective-permute-start | bytes 1179656 | tf_op jit(solution)/shard_map/ppermute | solution.py:204
  99.3 10.8 %copy-start.25 = (bf16[272,768]{1,0:T(8,128)(2,1)}, bf16[272,768]{1,0:T(8,128)(2,1)S(1)}, u32[]{:S(2)}) copy-start(bf16[272,768]{1,0:T(8,128)(2,1)S(1)} %collective-permute-done.1) | copy-start | bytes 1253380
  101.3 9.0 %copy-start.29 = (s32[64,5]{0,1:T(8,128)S(1)}, s32[64,5]{0,1:T(8,128)}, u32[]{:S(2)}) copy-start(s32[64,5]{0,1:T(8,128)} %copy-done.28) | copy-start | bytes 3844
  110.5 28.2 %copy-start.23 = (s32[768,384]{1,0:T(8,128)S(1)}, s32[768,384]{1,0:T(8,128)}, u32[]{:S(2)}) copy-start(s32[768,384]{1,0:T(8,128)} %param.18) | copy-start | bytes 3538948
  131.2 13.3 %collective-permute-start.6 = (bf16[256,768]{1,0:T(8,128)(2,1)}, bf16[256,768]{1,0:T(8,128)(2,1)}, u32[]{:S(2)}, u32[]{:S(2)}) collective-permute-start(bf16[256,768]{1,0:T(8,128)(2,1)} %get-tuple-element.36), channel_id=1, source_target_pairs={{0,1},{1,2},{3,0},{4,5},{5,6},{7,4},{8,9},{9,10},{11,8},{12,13},{1... | collective-permute-start | bytes 1179656 | tf_op jit(solution)/shard_map/ppermute | solution.py:204
  133.1 20.4 %collective-permute-start.8 = (bf16[256,768]{1,0:T(8,128)(2,1)}, bf16[256,768]{1,0:T(8,128)(2,1)}, u32[]{:S(2)}, u32[]{:S(2)}) collective-permute-start(bf16[256,768]{1,0:T(8,128)(2,1)} %get-tuple-element.38), channel_id=1, source_target_pairs={{0,2},{2,0},{3,1},{4,6},{6,4},{7,5},{8,10},{10,8},{11,9},{12,14},{... | collective-permute-start | bytes 1179656 | tf_op jit(solution)/shard_map/ppermute | solution.py:204
  134.4 36.5 %collective-permute-start.9 = (bf16[256,768]{1,0:T(8,128)(2,1)}, bf16[256,768]{1,0:T(8,128)(2,1)}, u32[]{:S(2)}, u32[]{:S(2)}) collective-permute-start(bf16[256,768]{1,0:T(8,128)(2,1)} %get-tuple-element.37), channel_id=1, source_target_pairs={{1,0},{2,1},{3,2},{5,4},{6,5},{7,6},{9,8},{10,9},{11,10},{13,12},{... | collective-permute-start | bytes 1179656 | tf_op jit(solution)/shard_map/ppermute | solution.py:204
  144.5 26.4 %copy-start.5 = (bf16[3,256,768]{2,1,0:T(8,128)(2,1)S(1)}, bf16[3,256,768]{2,1,0:T(8,128)(2,1)}, u32[]{:S(2)}) copy-start(bf16[3,256,768]{2,1,0:T(8,128)(2,1)} %copy-done.4) | copy-start | bytes 3538948
  144.6 27.9 %collective-permute-start.7 = (bf16[256,768]{1,0:T(8,128)(2,1)S(1)}, bf16[256,768]{1,0:T(8,128)(2,1)S(1)}, u32[]{:S(2)}, u32[]{:S(2)}) collective-permute-start(bf16[256,768]{1,0:T(8,128)(2,1)S(1)} %fusion.10), channel_id=1, source_target_pairs={{0,16},{4,20},{8,24},{12,28},{16,0},{20,4},{24,8},{28,12},{1,17},{... | collective-permute-start | bytes 1179656 | tf_op jit(solution)/shard_map/ppermute | solution.py:361
  147.0 25.5 %copy-start.24 = (bf16[48,16,768]{2,1,0:T(8,128)(2,1)S(1)}, bf16[48,16,768]{2,1,0:T(8,128)(2,1)}, u32[]{:S(2)}) copy-start(bf16[48,16,768]{2,1,0:T(8,128)(2,1)} %param.19) | copy-start | bytes 3538948
  (21 other events, 26.0 us)

commit v9 on v8

--- a/solution.py
+++ b/solution.py
@@ -16,7 +16,8 @@
 META_BASE = 32
 META_ROWS = 16
 LANES = 128
-VMEM_LIMIT = 48 * 1024 * 1024
+SPECTRUM_VMEM = 60 * 1024 * 1024
+INSERT_VMEM = 32 * 1024 * 1024
 
 
 def dft_tables(length):
@@ -39,10 +40,21 @@
     return out
 
 
-def phase_angle(freq, shift, length):
-    turns = freq * shift
-    turns = turns - length * jnp.floor(turns * (1.0 / length))
-    return (2.0 * math.pi / length) * turns
+def sin_turns(turns):
+    half = jnp.floor(2.0 * turns + 0.5)
+    x = (2.0 * math.pi) * (turns - 0.5 * half)
+    sign = 1.0 - 2.0 * (half - 2.0 * jnp.floor(0.5 * half))
+    square = x * x
+    series = jnp.full(x.shape, -1.0 / math.factorial(11), jnp.float32)
+    for power in (9, 7, 5, 3, 1):
+        series = series * square + (1.0 if power % 4 == 1 else -1.0) / math.factorial(power)
+    return sign * x * series
+
+
+def phase_turns(freq, shift, length):
+    steps = freq * shift
+    steps = steps - length * jnp.floor(steps * (1.0 / length))
+    return steps * (1.0 / length)
 
 
 def centred(freq, length):
@@ -67,7 +79,7 @@
     joined,
     block,
     load_sems,
-    send_sem,
+    send_sems,
 ):
     particles, length = images.shape[0], images.shape[1]
     owners = out.shape[0]
@@ -82,13 +94,14 @@
 
     every = range(particles)
     focus = [defocus[defocus_class[p]] for p in every]
-    shift_x = [shifts[p, 0].astype(jnp.float32) for p in every]
-    shift_y = [shifts[p, 1].astype(jnp.float32) for p in every]
+    shift_x = [shifts[0, p].astype(jnp.float32) for p in every]
+    shift_y = [shifts[1, p].astype(jnp.float32) for p in every]
     sublane = lax.broadcasted_iota(jnp.int32, (particles, length), 0)
     freq_x = lax.broadcasted_iota(jnp.int32, (particles, length), 1).astype(jnp.float32)
-    phase_x = phase_angle(freq_x, spread(sublane, shift_x), length)
+    phase_x = phase_turns(freq_x, spread(sublane, shift_x), length)
     angle_x = spread(sublane, focus) * centred(freq_x, length) * centred(freq_x, length)
-    col = [jnp.sin(phase_x), jnp.cos(phase_x), jnp.sin(angle_x), jnp.cos(angle_x)]
+    angle_x = angle_x * (0.5 / math.pi)
+    col = [sin_turns(at) for at in (phase_x, phase_x + 0.25, angle_x, angle_x + 0.25)]
     lane = lax.broadcasted_iota(jnp.int32, (rows, LANES), 1)
     which = lane % particles
     quantity = lane // particles
@@ -96,18 +109,19 @@
     owner = row_at // rows_each
     freq_y = row_at - owner * rows_each + spread(owner, [begin for begin, _ in runs])
     freq_y = freq_y.astype(jnp.float32)
-    phase_y = phase_angle(freq_y, spread(which, shift_y), length)
+    phase_y = phase_turns(freq_y, spread(which, shift_y), length)
     angle_y = spread(which, focus) * centred(freq_y, length) * centred(freq_y, length)
-    angles = jnp.where(quantity < 2, phase_y, angle_y + PHASE_OFFSET)
-    row = jnp.sin(angles + jnp.where(quantity % 2 == 1, 0.5 * math.pi, 0.0))
+    angle_y = (angle_y + PHASE_OFFSET) * (0.5 / math.pi)
+    row = jnp.where(quantity < 2, phase_y, angle_y)
+    row = sin_turns(row + jnp.where(quantity % 2 == 1, 0.25, 0.0))
 
     if with_meta:
         digits = jnp.zeros((META_ROWS, LANES), jnp.int32)
         at_row = lax.broadcasted_iota(jnp.int32, (META_ROWS, LANES), 0) % particles
         at_lane = lax.broadcasted_iota(jnp.int32, (META_ROWS, LANES), 1)
-        ends = [[run_counts[p, 0] for p in every]]
-        for s in range(1, run_counts.shape[1] - 1):
-            ends.append([ends[-1][p] + run_counts[p, s] for p in every])
+        ends = [[run_counts[0, p] for p in every]]
+        for s in range(1, run_counts.shape[0] - 1):
+            ends.append([ends[-1][p] + run_counts[s, p] for p in every])
         fields = [[classes[p] for p in every], [defocus_class[p] for p in every], *ends]
         for f, values in enumerate(fields):
             value = spread(at_row, values)
@@ -129,6 +143,7 @@
         joined[p * rows : (p + 1) * rows, :length] = section[:rows]
         joined[p * rows : (p + 1) * rows, length:] = section[rows:]
     loads[1 + particles].wait()
+    sends = []
     for first in range(0, particles, 2):
         spectrum = jnp.dot(
             joined[first * rows : (first + 2) * rows, :],
@@ -151,9 +166,15 @@
             block[:, p * rows_each : (p + 1) * rows_each, :] = weighted.reshape(
                 owners, rows_each, 2 * length
             )
-    send = pltpu.make_async_copy(block, out, send_sem)
-    send.start()
-    send.wait()
+        done = pl.ds(first * rows_each, 2 * rows_each)
+        if with_meta and first + 2 == particles:
+            done = pl.ds(first * rows_each, 2 * rows_each + META_ROWS)
+        sends.append(
+            pltpu.make_async_copy(block.at[:, done], out.at[:, done], send_sems.at[first // 2])
+        )
+        sends[-1].start()
+    for send in sends:
+        send.wait()
 
 
 def insert_kernel(bins, meta_at, received, codes, out):
@@ -188,12 +209,21 @@
     return value * value
 
 
-def slab_exchange(parts, place, slab_count, batch_count, swapped):
+def slab_roles(batch_count, swapped):
+    roles = list(range(batch_count))
+    half = batch_count // 2
+    if swapped:
+        for b in range(1, half, 2):
+            roles[b], roles[half + b - 1] = half + b - 1, b
+    return roles
+
+
+def slab_exchange(parts, place, slab_count, roles):
     arrived = []
     for shift in range(1, slab_count):
         perm = []
-        for b in range(batch_count):
-            upper = (b >= batch_count // 2) != swapped
+        for b, role in enumerate(roles):
+            upper = role >= len(roles) // 2
             for source in range(slab_count):
                 target = (source + shift) % slab_count
                 if target < slab_count - 1:
@@ -224,7 +254,7 @@
     half_batch = batch_count // 2
     sizes = [rows * share // SHARES for share, _ in CHUNKS]
     starts = [sum(sizes[:c]) for c in range(len(CHUNKS))]
-    swaps = [mirrored and swapped for _, swapped in CHUNKS]
+    roles = [slab_roles(batch_count, mirrored and swapped) for _, swapped in CHUNKS]
     freq = jnp.arange(length, dtype=jnp.int32)
 
     fields = slab_count + 1
@@ -235,7 +265,7 @@
     weighted = []
     for c, each in enumerate(sizes):
         chunk_rows = batch_count * each
-        block = np.roll(np.arange(batch_count), -half_batch if swaps[c] else 0)
+        block = np.array(roles[c])
         order = (block[:, None] * rows + starts[c] + np.arange(each)[None, :]).reshape(-1)
         left = np.concatenate([cosine[order], minus_sine[order]], axis=0)
         runs = [(k * rows + starts[c], k * rows + starts[c] + each) for k in block.tolist()]
@@ -256,17 +286,17 @@
                 pltpu.VMEM((particles * chunk_rows, 2 * length), jnp.bfloat16),
                 pltpu.VMEM(block_shape, jnp.bfloat16),
                 pltpu.SemaphoreType.DMA((particles + 2,)),
-                pltpu.SemaphoreType.DMA,
+                pltpu.SemaphoreType.DMA((particles // 2,)),
             ],
-            compiler_params=pltpu.CompilerParams(vmem_limit_bytes=VMEM_LIMIT),
+            compiler_params=pltpu.CompilerParams(vmem_limit_bytes=SPECTRUM_VMEM),
             cost_estimate=pl.CostEstimate(flops=0, bytes_accessed=0, transcendentals=0),
             name="spectrum",
         )(
             classes,
-            shifts,
+            shifts.T,
             defocus_class,
             defocus,
-            run_counts,
+            run_counts.T,
             images,
             jnp.asarray(left.astype(jnp.bfloat16)),
             table_right,
@@ -299,7 +329,9 @@
         )
 
     window_slabs = 3 if mirrored else slab_count
-    blocks = [(batch + half_batch) % batch_count if swap else batch for swap in swaps]
+    blocks = [
+        sum(jnp.where(batch == b, block, 0) for b, block in enumerate(role)) for role in roles
+    ]
     layer_planes = find_planes(meta_layer)
     places, codes = [], []
     for c, each in enumerate(sizes):
@@ -322,10 +354,12 @@
         bins = each * planes
         extra_rows = META_ROWS if c == 0 and mirrored else 0
         codes_in = codes[c]
-        if c + 1 < len(sizes):
-            codes_in, _ = lax.optimization_barrier((codes_in, weighted[c + 1]))
+        if c == 0:
+            codes_in, _ = lax.optimization_barrier((codes_in, weighted[1:]))
         if c > 0 and mirrored:
-            codes_in, arrived[c - 1][2] = lax.optimization_barrier((codes_in, arrived[c - 1][2]))
+            codes_in, arrived[c - 1][0], arrived[c - 1][2] = lax.optimization_barrier(
+                (codes_in, arrived[c - 1][0], arrived[c - 1][2])
+            )
         parts = pl.pallas_call(
             functools.partial(insert_kernel, bins, meta_at),
             out_shape=jax.ShapeDtypeStruct(
@@ -333,7 +367,7 @@
             ),
             in_specs=whole_vmem(2),
             out_specs=pl.BlockSpec(memory_space=pltpu.VMEM),
-            compiler_params=pltpu.CompilerParams(vmem_limit_bytes=VMEM_LIMIT),
+            compiler_params=pltpu.CompilerParams(vmem_limit_bytes=INSERT_VMEM),
             cost_estimate=pl.CostEstimate(
                 flops=0,
                 bytes_accessed=0,
@@ -346,7 +380,7 @@
             continue
         for before in arrived:
             before[1], _ = lax.optimization_barrier((before[1], parts))
-        arrived.append(slab_exchange(parts, places[c], slab_count, batch_count, swaps[c]))
+        arrived.append(slab_exchange(parts, places[c], slab_count, roles[c]))
         own = choose(parts[:, :bins], places[c]).astype(jnp.float32)
         sums.append(jnp.where(places[c] == slab_count - 1, 0.0, own))
     for c, each in enumerate(sizes):
@@ -354,11 +388,14 @@
             break
         for block in arrived[c]:
             sums[c] = sums[c] + block[: each * planes].astype(jnp.float32)
-        if swaps[c]:
+        over = [(b, block) for b, block in enumerate(roles[c]) if b != block]
+        if over:
             if c + 1 < len(sizes):
-                sums[c], arrived[-1][0] = lax.optimization_barrier((sums[c], arrived[-1][0]))
-            over = [(b, (b + half_batch) % batch_count) for b in range(batch_count)]
-            sums[c] = lax.ppermute(sums[c].astype(jnp.bfloat16), "batch", over)
+                sums[c], arrived[c + 1][2] = lax.optimization_barrier(
+                    (sums[c], arrived[c + 1][2])
+                )
+            handed = lax.ppermute(sums[c].astype(jnp.bfloat16), "batch", over)
+            sums[c] = jnp.where(blocks[c] == batch, sums[c], handed.astype(jnp.float32))
 
     meta_all = [meta_layer]
     if mirrored:

time: 176 us -> 155 us (0.88)
  the two profiles are of different devices: /device:TPU:11 before, /device:TPU:0 now
where the time goes in v9:
time: 155 us; the launch traced here: 154 us
  waiting for transfers between devices  62 us (40%)
  starting transfers between devices  45.6 us (29%)
  Pallas kernels  27.5 us (18%)
  other arithmetic  11 us (7%)
  local copies, waits for them, and re-layouts  4.2 us (3%)
  matrix products  3.46 us (2%)
    ppermute x9, waiting for transfers between devices, slab_exchange(): arrived.append(lax.ppermute(block, ('batch', 'slab'), perm))  52.3 us
    ppermute x9, starting transfers between devices, slab_exchange(): arrived.append(lax.ppermute(block, ('batch', 'slab'), perm))  30.8 us
    pallas_call x3, Pallas kernels, per_device(): pl.pallas_call(functools.partial(spectrum_kernel, runs, with_meta), out_s...  20.1 us
    all_to_all x3, starting transfers between devices, per_device(): received.append(lax.all_to_all(send, 'batch', 0, 0, tiled=True))  13.9 us
    all_to_all x3, waiting for transfers between devices, per_device(): received.append(lax.all_to_all(send, 'batch', 0, 0, tiled=True))  9.7 us
    pallas_call x3, Pallas kernels, per_device(): pl.pallas_call(functools.partial(insert_kernel, bins, meta_at), out_shape...  7.31 us
    add x3, other arithmetic, per_device(): sums[c] = sums[c] + block[:each * planes].astype(jnp.float32)  4.4 us
    select_n x3, other arithmetic, choose(): chosen = jnp.where(index == d, parts[d], chosen)  3.28 us
  transfers between devices with their start and end apart: 13, of which 9 were waited for; matrix products, arithmetic and copies ran while one was open for 10% of the time, Pallas kernels for 13%

profile of v9, /device:TPU:0, one launch (start us, length us, event | category | flops | bytes accessed | tf_op | source)
XLA Modules:
  0.0 154.1 jit_solution(17016446920971039829)
XLA Ops:
  0.0 6.8 %spectrum.3 = bf16[8,144,768]{2,1,0:T(8,128)(2,1)} custom-call(s32[8]{0:T(128)} %classes.5, s32[2,8]{1,0:T(2,128)} %bitcast.90, s32[8]{0:T(128)} %defocus_class.5, f32[16]{0:T(128)} %defocus.5, s32[4,8]{1,0:T(4,128)} %bitcast.87, bf16[8,384,384]{2,1,0:T(8,128)(2,1)} %images_in.5, bf16[256,384]{1,0:T(8,128)(2,1)} %constant.169.clone.left_in, ...), custom_call_target="tpu_custom_call" | custom-call | tf_op jit(solution)/shard_map/spectrum/pallas_call | solution.py:277
  6.8 5.2 %all-to-all-start = ((bf16[8,144,768]{2,1,0:T(8,128)(2,1)}), bf16[8,144,768]{2,1,0:T(8,128)(2,1)S(1)}, u32[]{:S(2)}, u32[]{:S(2)}) async-start(bf16[8,144,768]{2,1,0:T(8,128)(2,1)} %spectrum.3), calls=%async_computation | async-start | bytes 3538944 | tf_op jit(solution)/shard_map/all_to_all | solution.py:305
  11.9 6.7 %spectrum.4 = bf16[8,128,768]{2,1,0:T(8,128)(2,1)} custom-call(s32[8]{0:T(128)} %classes.5, s32[2,8]{1,0:T(2,128)} %bitcast.91, s32[8]{0:T(128)} %defocus_class.5, f32[16]{0:T(128)} %defocus.5, s32[4,8]{1,0:T(4,128)} %bitcast.88, bf16[8,384,384]{2,1,0:T(8,128)(2,1)} %images_in.5, bf16[256,384]{1,0:T(8,128)(2,1)} %constant.170.clone.left_in, ...), custom_call_target="tpu_custom_call" | custom-call | tf_op jit(solution)/shard_map/spectrum/pallas_call | solution.py:277
  18.6 6.7 %spectrum.5 = bf16[8,128,768]{2,1,0:T(8,128)(2,1)} custom-call(s32[8]{0:T(128)} %classes.5, s32[2,8]{1,0:T(2,128)} %bitcast.92, s32[8]{0:T(128)} %defocus_class.5, f32[16]{0:T(128)} %defocus.5, s32[4,8]{1,0:T(4,128)} %bitcast.89, bf16[8,384,384]{2,1,0:T(8,128)(2,1)} %images_in.5, bf16[256,384]{1,0:T(8,128)(2,1)} %constant.171.clone.left_in, ...), custom_call_target="tpu_custom_call" | custom-call | tf_op jit(solution)/shard_map/spectrum/pallas_call | solution.py:277
  25.4 9.7 %all-to-all-done.received = bf16[8,144,768]{2,1,0:T(8,128)(2,1)S(1)} async-done(((bf16[8,144,768]{2,1,0:T(8,128)(2,1)}), bf16[8,144,768]{2,1,0:T(8,128)(2,1)S(1)}, u32[]{:S(2)}, u32[]{:S(2)}) %all-to-all-start) | async-done | bytes 1769504 | tf_op jit(solution)/shard_map/all_to_all | solution.py:305
  35.1 4.5 %all-to-all-start.1 = ((bf16[8,128,768]{2,1,0:T(8,128)(2,1)}), bf16[8,128,768]{2,1,0:T(8,128)(2,1)}, u32[]{:S(2)}, u32[]{:S(2)}) async-start(bf16[8,128,768]{2,1,0:T(8,128)(2,1)} %spectrum.4), calls=%async_computation.1 | async-start | bytes 3145728 | tf_op jit(solution)/shard_map/all_to_all | solution.py:305
  40.9 1.7 %insert.3 = bf16[3,272,768]{2,1,0:T(8,128)(2,1)S(1)} custom-call(bf16[8,144,768]{2,1,0:T(8,128)(2,1)S(1)} %all-to-all-done.received, s32[1,1152]{1,0:T(1,128)S(1)} %reshape.197.codes), custom_call_target="tpu_custom_call" | custom-call | tf_op jit(solution)/shard_map/insert/pallas_call | solution.py:363
  43.5 3.5 %collective-permute-start = (bf16[272,768]{1,0:T(8,128)(2,1)S(1)}, bf16[272,768]{1,0:T(8,128)(2,1)S(1)}, u32[]{:S(2)}, u32[]{:S(2)}) collective-permute-start(bf16[272,768]{1,0:T(8,128)(2,1)S(1)} %get-tuple-element.30), channel_id=1, source_target_pairs={{0,1},{1,2},{3,0},{4,5},{5,6},{7,4},{8,9},{9,10},{11,8},{12,13},{1... | collective-permute-start | bytes 1253384 | tf_op jit(solution)/shard_map/ppermute | solution.py:234
  49.2 5.6 %collective-permute-start.2 = (bf16[272,768]{1,0:T(8,128)(2,1)}, bf16[272,768]{1,0:T(8,128)(2,1)}, u32[]{:S(2)}, u32[]{:S(2)}) collective-permute-start(bf16[272,768]{1,0:T(8,128)(2,1)} %get-tuple-element.29), channel_id=1, source_target_pairs={{0,2},{2,0},{3,1},{4,6},{6,4},{7,5},{8,10},{10,8},{11,9},{12,14},{... | collective-permute-start | bytes 1253384 | tf_op jit(solution)/shard_map/ppermute | solution.py:234
  55.1 4.5 %collective-permute-done = bf16[272,768]{1,0:T(8,128)(2,1)S(1)} collective-permute-done((bf16[272,768]{1,0:T(8,128)(2,1)S(1)}, bf16[272,768]{1,0:T(8,128)(2,1)S(1)}, u32[]{:S(2)}, u32[]{:S(2)}) %collective-permute-start) | collective-permute-done | bytes 417824 | tf_op jit(solution)/shard_map/ppermute | solution.py:234
  59.7 8.2 %collective-permute-done.1 = bf16[272,768]{1,0:T(8,128)(2,1)S(1)} collective-permute-done((bf16[272,768]{1,0:T(8,128)(2,1)S(1)}, bf16[272,768]{1,0:T(8,128)(2,1)S(1)}, u32[]{:S(2)}, u32[]{:S(2)}) %collective-permute-start.1) | collective-permute-done | bytes 417824 | tf_op jit(solution)/shard_map/ppermute | solution.py:234
  67.8 4.3 %all-to-all-start.2 = ((bf16[8,128,768]{2,1,0:T(8,128)(2,1)}), bf16[8,128,768]{2,1,0:T(8,128)(2,1)}, u32[]{:S(2)}, u32[]{:S(2)}) async-start(bf16[8,128,768]{2,1,0:T(8,128)(2,1)} %spectrum.5), calls=%async_computation.2 | async-start | bytes 3145728 | tf_op jit(solution)/shard_map/all_to_all | solution.py:305
  72.1 2.8 %insert.4 = bf16[3,256,768]{2,1,0:T(8,128)(2,1)S(1)} custom-call(bf16[8,128,768]{2,1,0:T(8,128)(2,1)} %all-to-all-done.1.received, s32[1,1024]{1,0:T(1,128)S(1)} %reshape_reshape.6.codes), custom_call_target="tpu_custom_call" | custom-call | tf_op jit(solution)/shard_map/insert/pallas_call | solution.py:363
  76.1 4.1 %collective-permute-start.3 = (bf16[256,768]{1,0:T(8,128)(2,1)}, bf16[256,768]{1,0:T(8,128)(2,1)}, u32[]{:S(2)}, u32[]{:S(2)}) collective-permute-start(bf16[256,768]{1,0:T(8,128)(2,1)} %get-tuple-element.42), channel_id=1, source_target_pairs={{0,1},{1,2},{3,0},{7,6},{6,5},{4,7},{8,9},{9,10},{11,8},{15,14},{1... | collective-permute-start | bytes 1179656 | tf_op jit(solution)/shard_map/ppermute | solution.py:234
  81.5 5.5 %collective-permute-start.5 = (bf16[256,768]{1,0:T(8,128)(2,1)}, bf16[256,768]{1,0:T(8,128)(2,1)}, u32[]{:S(2)}, u32[]{:S(2)}) collective-permute-start(bf16[256,768]{1,0:T(8,128)(2,1)} %get-tuple-element.41), channel_id=1, source_target_pairs={{0,2},{2,0},{3,1},{7,5},{5,7},{4,6},{8,10},{10,8},{11,9},{15,13},{... | collective-permute-start | bytes 1179656 | tf_op jit(solution)/shard_map/ppermute | solution.py:234
  89.1 2.7 %collective-permute-done.3 = bf16[256,768]{1,0:T(8,128)(2,1)} collective-permute-done((bf16[256,768]{1,0:T(8,128)(2,1)}, bf16[256,768]{1,0:T(8,128)(2,1)}, u32[]{:S(2)}, u32[]{:S(2)}) %collective-permute-start.3) | collective-permute-done | bytes 393248 | tf_op jit(solution)/shard_map/ppermute | solution.py:234
  91.8 2.5 %collective-permute-done.4 = bf16[256,768]{1,0:T(8,128)(2,1)} collective-permute-done((bf16[256,768]{1,0:T(8,128)(2,1)}, bf16[256,768]{1,0:T(8,128)(2,1)}, u32[]{:S(2)}, u32[]{:S(2)}) %collective-permute-start.4) | collective-permute-done | bytes 393248 | tf_op jit(solution)/shard_map/ppermute | solution.py:234
  94.3 2.8 %insert.5 = bf16[3,256,768]{2,1,0:T(8,128)(2,1)S(1)} custom-call(bf16[8,128,768]{2,1,0:T(8,128)(2,1)} %all-to-all-done.2.received, s32[1,1024]{1,0:T(1,128)S(1)} %reshape_reshape.7.codes), custom_call_target="tpu_custom_call" | custom-call | tf_op jit(solution)/shard_map/insert/pallas_call | solution.py:363
  100.9 10.3 %collective-permute-done.5 = bf16[256,768]{1,0:T(8,128)(2,1)} collective-permute-done((bf16[256,768]{1,0:T(8,128)(2,1)}, bf16[256,768]{1,0:T(8,128)(2,1)}, u32[]{:S(2)}, u32[]{:S(2)}) %collective-permute-start.5) | collective-permute-done | bytes 393248 | tf_op jit(solution)/shard_map/ppermute | solution.py:234
  111.2 5.5 %collective-permute-start.8 = (bf16[256,768]{1,0:T(8,128)(2,1)}, bf16[256,768]{1,0:T(8,128)(2,1)}, u32[]{:S(2)}, u32[]{:S(2)}) collective-permute-start(bf16[256,768]{1,0:T(8,128)(2,1)} %get-tuple-element.38), channel_id=1, source_target_pairs={{0,1},{1,2},{3,0},{4,5},{5,6},{7,4},{8,9},{9,10},{11,8},{12,13},{1... | collective-permute-start | bytes 1179656 | tf_op jit(solution)/shard_map/ppermute | solution.py:234
  116.7 2.7 %collective-permute-start.9 = (bf16[256,768]{1,0:T(8,128)(2,1)}, bf16[256,768]{1,0:T(8,128)(2,1)}, u32[]{:S(2)}, u32[]{:S(2)}) collective-permute-start(bf16[256,768]{1,0:T(8,128)(2,1)} %get-tuple-element.39), channel_id=1, source_target_pairs={{0,2},{2,0},{3,1},{4,6},{6,4},{7,5},{8,10},{10,8},{11,9},{12,14},{... | collective-permute-start | bytes 1179656 | tf_op jit(solution)/shard_map/ppermute | solution.py:234
  119.6 1.7 %fusion.2 = s32[256,384]{1,0:T(8,128)S(1)} fusion(s32[256]{0:T(256)S(1)} %bitcast.93, s32[256,384]{1,0:T(8,128)S(1)} %convert_reduce_fusion, s32[768,384]{1,0:T(8,128)} %param.18), kind=kOutput, calls=%fused_computation.4 | convolution fusion | flops 151781376 | bytes 1967104 | tf_op jit(solution)/shard_map/dot_general | solution.py:320
  127.1 5.7 %collective-permute-done.8 = bf16[256,768]{1,0:T(8,128)(2,1)} collective-permute-done((bf16[256,768]{1,0:T(8,128)(2,1)}, bf16[256,768]{1,0:T(8,128)(2,1)}, u32[]{:S(2)}, u32[]{:S(2)}) %collective-permute-start.8) | collective-permute-done | bytes 393248 | tf_op jit(solution)/shard_map/ppermute | solution.py:234
  132.8 16.8 %collective-permute-done.9 = bf16[256,768]{1,0:T(8,128)(2,1)} collective-permute-done((bf16[256,768]{1,0:T(8,128)(2,1)}, bf16[256,768]{1,0:T(8,128)(2,1)}, u32[]{:S(2)}, u32[]{:S(2)}) %collective-permute-start.9) | collective-permute-done | bytes 393248 | tf_op jit(solution)/shard_map/ppermute | solution.py:234
  (81 shorter events, 23.2 us)
Async XLA Ops:
  6.8 28.3 %all-to-all-start = ((bf16[8,144,768]{2,1,0:T(8,128)(2,1)}), bf16[8,144,768]{2,1,0:T(8,128)(2,1)S(1)}, u32[]{:S(2)}, u32[]{:S(2)}) async-start(bf16[8,144,768]{2,1,0:T(8,128)(2,1)} %spectrum.3), calls=%async_computation | async-start | bytes 3538944 | tf_op jit(solution)/shard_map/all_to_all | solution.py:305
  25.4 14.6 %copy-start.2 = (s32[768,384]{1,0:T(8,128)S(1)}, s32[768,384]{1,0:T(8,128)}, u32[]{:S(2)}) copy-start(s32[768,384]{1,0:T(8,128)} %param.18) | copy-start | bytes 3538948
  35.1 32.7 %all-to-all-start.1 = ((bf16[8,128,768]{2,1,0:T(8,128)(2,1)}), bf16[8,128,768]{2,1,0:T(8,128)(2,1)}, u32[]{:S(2)}, u32[]{:S(2)}) async-start(bf16[8,128,768]{2,1,0:T(8,128)(2,1)} %spectrum.4), calls=%async_computation.1 | async-start | bytes 3145728 | tf_op jit(solution)/shard_map/all_to_all | solution.py:305
  42.6 5.7 %copy-start.5 = (f32[16]{0:T(128)S(1)}, f32[16]{0:T(128)}, u32[]{:S(2)}) copy-start(f32[16]{0:T(128)} %defocus.5) | copy-start | bytes 196
  43.5 16.2 %collective-permute-start = (bf16[272,768]{1,0:T(8,128)(2,1)S(1)}, bf16[272,768]{1,0:T(8,128)(2,1)S(1)}, u32[]{:S(2)}, u32[]{:S(2)}) collective-permute-start(bf16[272,768]{1,0:T(8,128)(2,1)S(1)} %get-tuple-element.30), channel_id=1, source_target_pairs={{0,1},{1,2},{3,0},{4,5},{5,6},{7,4},{8,9},{9,10},{11,8},{12,13},{1... | collective-permute-start | bytes 1253384 | tf_op jit(solution)/shard_map/ppermute | solution.py:234
  46.9 20.9 %collective-permute-start.1 = (bf16[272,768]{1,0:T(8,128)(2,1)S(1)}, bf16[272,768]{1,0:T(8,128)(2,1)S(1)}, u32[]{:S(2)}, u32[]{:S(2)}) collective-permute-start(bf16[272,768]{1,0:T(8,128)(2,1)S(1)} %get-tuple-element.31), channel_id=1, source_target_pairs={{1,0},{2,1},{3,2},{5,4},{6,5},{7,6},{9,8},{10,9},{11,10},{13,12},{... | collective-permute-start | bytes 1253384 | tf_op jit(solution)/shard_map/ppermute | solution.py:234
  49.2 39.4 %collective-permute-start.2 = (bf16[272,768]{1,0:T(8,128)(2,1)}, bf16[272,768]{1,0:T(8,128)(2,1)}, u32[]{:S(2)}, u32[]{:S(2)}) collective-permute-start(bf16[272,768]{1,0:T(8,128)(2,1)} %get-tuple-element.29), channel_id=1, source_target_pairs={{0,2},{2,0},{3,1},{4,6},{6,4},{7,5},{8,10},{10,8},{11,9},{12,14},{... | collective-permute-start | bytes 1253384 | tf_op jit(solution)/shard_map/ppermute | solution.py:234
  67.8 26.4 %all-to-all-start.2 = ((bf16[8,128,768]{2,1,0:T(8,128)(2,1)}), bf16[8,128,768]{2,1,0:T(8,128)(2,1)}, u32[]{:S(2)}, u32[]{:S(2)}) async-start(bf16[8,128,768]{2,1,0:T(8,128)(2,1)} %spectrum.5), calls=%async_computation.2 | async-start | bytes 3145728 | tf_op jit(solution)/shard_map/all_to_all | solution.py:305
  76.1 15.7 %collective-permute-start.3 = (bf16[256,768]{1,0:T(8,128)(2,1)}, bf16[256,768]{1,0:T(8,128)(2,1)}, u32[]{:S(2)}, u32[]{:S(2)}) collective-permute-start(bf16[256,768]{1,0:T(8,128)(2,1)} %get-tuple-element.42), channel_id=1, source_target_pairs={{0,1},{1,2},{3,0},{7,6},{6,5},{4,7},{8,9},{9,10},{11,8},{15,14},{1... | collective-permute-start | bytes 1179656 | tf_op jit(solution)/shard_map/ppermute | solution.py:234
  80.2 14.1 %collective-permute-start.4 = (bf16[256,768]{1,0:T(8,128)(2,1)}, bf16[256,768]{1,0:T(8,128)(2,1)}, u32[]{:S(2)}, u32[]{:S(2)}) collective-permute-start(bf16[256,768]{1,0:T(8,128)(2,1)} %get-tuple-element.43), channel_id=1, source_target_pairs={{1,0},{2,1},{3,2},{6,7},{5,6},{4,5},{9,8},{10,9},{11,10},{14,15},{... | collective-permute-start | bytes 1179656 | tf_op jit(solution)/shard_map/ppermute | solution.py:234
  81.5 29.7 %collective-permute-start.5 = (bf16[256,768]{1,0:T(8,128)(2,1)}, bf16[256,768]{1,0:T(8,128)(2,1)}, u32[]{:S(2)}, u32[]{:S(2)}) collective-permute-start(bf16[256,768]{1,0:T(8,128)(2,1)} %get-tuple-element.41), channel_id=1, source_target_pairs={{0,2},{2,0},{3,1},{7,5},{5,7},{4,6},{8,10},{10,8},{11,9},{15,13},{... | collective-permute-start | bytes 1179656 | tf_op jit(solution)/shard_map/ppermute | solution.py:234
  97.1 1.4 copy-start
  98.5 27.7 %collective-permute-start.6 = (bf16[256,768]{1,0:T(8,128)(2,1)}, bf16[256,768]{1,0:T(8,128)(2,1)}, u32[]{:S(2)}, u32[]{:S(2)}) collective-permute-start(bf16[256,768]{1,0:T(8,128)(2,1)} %get-tuple-element.40), channel_id=1, source_target_pairs={{1,0},{2,1},{3,2},{5,4},{6,5},{7,6},{9,8},{10,9},{11,10},{13,12},{... | collective-permute-start | bytes 1179656 | tf_op jit(solution)/shard_map/ppermute | solution.py:234
  111.2 21.7 %collective-permute-start.8 = (bf16[256,768]{1,0:T(8,128)(2,1)}, bf16[256,768]{1,0:T(8,128)(2,1)}, u32[]{:S(2)}, u32[]{:S(2)}) collective-permute-start(bf16[256,768]{1,0:T(8,128)(2,1)} %get-tuple-element.38), channel_id=1, source_target_pairs={{0,1},{1,2},{3,0},{4,5},{5,6},{7,4},{8,9},{9,10},{11,8},{12,13},{1... | collective-permute-start | bytes 1179656 | tf_op jit(solution)/shard_map/ppermute | solution.py:234
  116.7 33.0 %collective-permute-start.9 = (bf16[256,768]{1,0:T(8,128)(2,1)}, bf16[256,768]{1,0:T(8,128)(2,1)}, u32[]{:S(2)}, u32[]{:S(2)}) collective-permute-start(bf16[256,768]{1,0:T(8,128)(2,1)} %get-tuple-element.39), channel_id=1, source_target_pairs={{0,2},{2,0},{3,1},{4,6},{6,4},{7,5},{8,10},{10,8},{11,9},{12,14},{... | collective-permute-start | bytes 1179656 | tf_op jit(solution)/shard_map/ppermute | solution.py:234
  123.0 1.6 %copy-start.4 = (f32[48,16]{1,0:T(8,128)S(1)}, f32[48,16]{1,0:T(8,128)}, u32[]{:S(2)}) copy-start(f32[48,16]{1,0:T(8,128)} %copy.53) | copy-start | bytes 9220
  126.2 23.5 %copy-start.1 = (bf16[3,256,768]{2,1,0:T(8,128)(2,1)S(1)}, bf16[3,256,768]{2,1,0:T(8,128)(2,1)}, u32[]{:S(2)}) copy-start(bf16[3,256,768]{2,1,0:T(8,128)(2,1)} %copy-done) | copy-start | bytes 3538948
  126.2 25.0 %collective-permute-start.7 = (bf16[256,768]{1,0:T(8,128)(2,1)S(1)}, bf16[256,768]{1,0:T(8,128)(2,1)S(1)}, u32[]{:S(2)}, u32[]{:S(2)}) collective-permute-start(bf16[256,768]{1,0:T(8,128)(2,1)S(1)} %convert_element_type.130), channel_id=1, source_target_pairs={{4,16},{12,24},{16,4},{24,12},{5,17},{13,25},{17,5},{25,13},{6,18}... | collective-permute-start | bytes 1179656 | tf_op jit(solution)/shard_map/ppermute | solution.py:397
  151.2 1.3 copy-start.3

commit v10 on v9

--- a/solution.py
+++ b/solution.py
@@ -11,7 +11,7 @@
 
 TAU_PRIOR = 4.0
 PHASE_OFFSET = 0.1
-CHUNKS = ((2, False), (2, True), (2, False))
+CHUNKS = ((2, True), (2, True), (2, False))
 SHARES = 6
 META_BASE = 32
 META_ROWS = 16
@@ -61,26 +61,14 @@
     return jnp.where(freq < length // 2, freq, freq - length) * (1.0 / length)
 
 
-def spectrum_kernel(
-    runs,
-    with_meta,
-    classes,
-    shifts,
-    defocus_class,
-    defocus,
-    run_counts,
-    images_in,
-    left_in,
-    right_in,
-    out,
-    images,
-    left,
-    right,
-    joined,
-    block,
-    load_sems,
-    send_sems,
-):
+def spectrum_kernel(runs, meta_from, *refs):
+    classes, shifts, defocus_class, defocus, run_counts, images_in, left_in, right_in, *refs = refs
+    if meta_from == "operand":
+        meta_in, *refs = refs
+    out, *refs = refs
+    if meta_from == "scalars":
+        meta_out, *refs = refs
+    images, left, right, joined, block, load_sems, send_sems = refs
     particles, length = images.shape[0], images.shape[1]
     owners = out.shape[0]
     rows_each = runs[0][1] - runs[0][0]
@@ -103,21 +91,26 @@
     angle_x = angle_x * (0.5 / math.pi)
     col = [sin_turns(at) for at in (phase_x, phase_x + 0.25, angle_x, angle_x + 0.25)]
     lane = lax.broadcasted_iota(jnp.int32, (rows, LANES), 1)
-    which = lane % particles
-    quantity = lane // particles
+    which = lane & (particles - 1)
+    quantity = (lane - which) * (1.0 / particles)
     row_at = lax.broadcasted_iota(jnp.int32, (rows, LANES), 0)
-    owner = row_at // rows_each
-    freq_y = row_at - owner * rows_each + spread(owner, [begin for begin, _ in runs])
+    freq_y = row_at + runs[0][0]
+    for d in range(1, owners):
+        freq_y = jnp.where(row_at >= d * rows_each, row_at + (runs[d][0] - d * rows_each), freq_y)
     freq_y = freq_y.astype(jnp.float32)
     phase_y = phase_turns(freq_y, spread(which, shift_y), length)
     angle_y = spread(which, focus) * centred(freq_y, length) * centred(freq_y, length)
     angle_y = (angle_y + PHASE_OFFSET) * (0.5 / math.pi)
-    row = jnp.where(quantity < 2, phase_y, angle_y)
-    row = sin_turns(row + jnp.where(quantity % 2 == 1, 0.25, 0.0))
-
-    if with_meta:
+    row = jnp.where(quantity < 2.0, phase_y, angle_y)
+    row = sin_turns(row + jnp.where((quantity == 1.0) | (quantity == 3.0), 0.25, 0.0))
+
+    if meta_from == "operand":
+        for d in range(owners):
+            block[d, particles * rows_each :, :] = meta_in[...]
+    if meta_from == "scalars":
         digits = jnp.zeros((META_ROWS, LANES), jnp.int32)
-        at_row = lax.broadcasted_iota(jnp.int32, (META_ROWS, LANES), 0) % particles
+        at_row = lax.broadcasted_iota(jnp.int32, (META_ROWS, LANES), 0)
+        at_row = at_row & (particles - 1)
         at_lane = lax.broadcasted_iota(jnp.int32, (META_ROWS, LANES), 1)
         ends = [[run_counts[0, p] for p in every]]
         for s in range(1, run_counts.shape[0] - 1):
@@ -128,6 +121,7 @@
             digits = jnp.where(at_lane == f, value // META_BASE, digits)
             digits = jnp.where(at_lane == f + len(fields), value % META_BASE, digits)
         digits = digits.astype(jnp.float32).astype(jnp.bfloat16)
+        meta_out[...] = digits
         for d in range(owners):
             block[d, particles * rows_each :, :] = jnp.zeros(
                 (META_ROWS, 2 * length), jnp.bfloat16
@@ -167,7 +161,7 @@
                 owners, rows_each, 2 * length
             )
         done = pl.ds(first * rows_each, 2 * rows_each)
-        if with_meta and first + 2 == particles:
+        if meta_from and first + 2 == particles:
             done = pl.ds(first * rows_each, 2 * rows_each + META_ROWS)
         sends.append(
             pltpu.make_async_copy(block.at[:, done], out.at[:, done], send_sems.at[first // 2])
@@ -177,26 +171,15 @@
         send.wait()
 
 
-def insert_kernel(bins, meta_at, received, codes, out):
-    sources = received.shape[0]
+def insert_kernel(received, codes, out):
+    windows, bins, _ = out.shape
     rows = received[...].reshape(-1, received.shape[2])
     codes_all = codes[...]
-    for k in range(out.shape[0]):
+    for k in range(windows):
         bin_index = lax.broadcasted_iota(jnp.int32, (bins, 1), 0) + k * bins
         hot = jnp.where(codes_all == bin_index, 1.0, 0.0).astype(jnp.bfloat16)
         total = jnp.dot(hot, rows, preferred_element_type=jnp.float32)
-        out[k, :bins, :] = total.astype(out.dtype)
-        if out.shape[1] > bins:
-            tiles = out.shape[2] // LANES
-            first_half = lax.broadcasted_iota(jnp.int32, (META_ROWS, LANES), 0) < META_ROWS // 2
-            for i in range(min(sources, tiles)):
-                low = received[i, meta_at : meta_at + META_ROWS, :LANES]
-                if i + tiles < sources:
-                    high = received[i + tiles, meta_at : meta_at + META_ROWS, :LANES]
-                    low = jnp.where(
-                        first_half, low.astype(jnp.float32), high.astype(jnp.float32)
-                    ).astype(low.dtype)
-                out[k, bins:, i * LANES : (i + 1) * LANES] = low
+        out[k] = total.astype(out.dtype)
 
 
 def whole_vmem(count):
@@ -249,8 +232,7 @@
     batch = lax.axis_index("batch")
     slab = lax.axis_index("slab")
     rows, planes, _ = ref.shape
-    mirrored = slab_count == 4 and batch_count % 2 == 0 and 2 * particles <= META_ROWS
-    mirrored = mirrored and batch_count * LANES <= 4 * length
+    mirrored = slab_count == 4 and batch_count % 2 == 0
     half_batch = batch_count // 2
     sizes = [rows * share // SHARES for share, _ in CHUNKS]
     starts = [sum(sizes[:c]) for c in range(len(CHUNKS))]
@@ -269,16 +251,19 @@
         order = (block[:, None] * rows + starts[c] + np.arange(each)[None, :]).reshape(-1)
         left = np.concatenate([cosine[order], minus_sine[order]], axis=0)
         runs = [(k * rows + starts[c], k * rows + starts[c] + each) for k in block.tolist()]
-        with_meta = c == 0
-        block_rows = particles * each + META_ROWS * with_meta
+        last = c + 1 == len(sizes)
+        meta_from = "scalars" if c == 0 else "operand" if last else None
+        block_rows = particles * each + (META_ROWS if meta_from else 0)
         block_shape = (batch_count, block_rows, 2 * length)
         smem = pl.BlockSpec(memory_space=pltpu.SMEM)
         hbm = pl.BlockSpec(memory_space=pltpu.HBM)
-        send = pl.pallas_call(
-            functools.partial(spectrum_kernel, runs, with_meta),
-            out_shape=jax.ShapeDtypeStruct(block_shape, jnp.bfloat16),
-            in_specs=[smem] * 5 + [hbm] * 3,
-            out_specs=hbm,
+        vmem = pl.BlockSpec(memory_space=pltpu.VMEM)
+        send, *meta_out = pl.pallas_call(
+            functools.partial(spectrum_kernel, runs, meta_from),
+            out_shape=[jax.ShapeDtypeStruct(block_shape, jnp.bfloat16)]
+            + [jax.ShapeDtypeStruct((META_ROWS, LANES), jnp.bfloat16)] * (c == 0),
+            in_specs=[smem] * 5 + [hbm] * 3 + [vmem] * last,
+            out_specs=[hbm] + [vmem] * (c == 0),
             scratch_shapes=[
                 pltpu.VMEM((particles, length, length), jnp.bfloat16),
                 pltpu.VMEM((2 * chunk_rows, length), jnp.bfloat16),
@@ -300,7 +285,18 @@
             images,
             jnp.asarray(left.astype(jnp.bfloat16)),
             table_right,
+            *([digits] if last else []),
         )
+        if c == 0:
+            own_digits = meta_out[0]
+        if c == 1:
+            own_digits, send = lax.optimization_barrier((own_digits, send))
+            layers = [own_digits]
+            for step in range(1, slab_count):
+                ring = [(s, (s + step) % slab_count) for s in range(slab_count)]
+                layers.append(lax.ppermute(own_digits, "slab", ring))
+            digits = jnp.concatenate([layer[:, : 2 * fields] for layer in layers], axis=1)
+            digits = jnp.pad(digits, ((0, 0), (0, 2 * length - digits.shape[1])))
         weighted.append(send)
         received.append(lax.all_to_all(send, "batch", 0, 0, tiled=True))
 
@@ -308,8 +304,11 @@
         whole = rows_in.astype(jnp.int32).reshape(-1, 2 * fields)
         return whole[:, :fields] * META_BASE + whole[:, fields:]
 
-    meta_at = particles * sizes[0]
-    meta_layer = read_digits(received[0][:, meta_at : meta_at + particles, : 2 * fields])
+    at = [particles * each for each in sizes]
+    layer_digits = received[0][:, at[0] : at[0] + particles, : 2 * fields]
+    meta_layer = read_digits(layer_digits)
+    all_digits = received[-1][:, at[-1] : at[-1] + particles, : slab_count * 2 * fields]
+    meta_all = read_digits(all_digits)
 
     class_count = dest_map.shape[0]
 
@@ -345,26 +344,21 @@
         places.append(place)
         code = owner_place * (each * planes) + jnp.arange(each)[None, :] * planes
         code = (code + plane % planes).reshape(batch_count, particles * each)
-        if c == 0:
+        if c in (0, len(sizes) - 1):
             code = jnp.pad(code, ((0, 0), (0, META_ROWS)), constant_values=-1)
         codes.append(code.reshape(1, -1))
 
     sums, arrived = [], []
     for c, each in enumerate(sizes):
         bins = each * planes
-        extra_rows = META_ROWS if c == 0 and mirrored else 0
         codes_in = codes[c]
         if c == 0:
             codes_in, _ = lax.optimization_barrier((codes_in, weighted[1:]))
         if c > 0 and mirrored:
-            codes_in, arrived[c - 1][0], arrived[c - 1][2] = lax.optimization_barrier(
-                (codes_in, arrived[c - 1][0], arrived[c - 1][2])
-            )
+            codes_in, arrived[c - 1][2] = lax.optimization_barrier((codes_in, arrived[c - 1][2]))
         parts = pl.pallas_call(
-            functools.partial(insert_kernel, bins, meta_at),
-            out_shape=jax.ShapeDtypeStruct(
-                (window_slabs, bins + extra_rows, 2 * length), jnp.bfloat16
-            ),
+            insert_kernel,
+            out_shape=jax.ShapeDtypeStruct((window_slabs, bins, 2 * length), jnp.bfloat16),
             in_specs=whole_vmem(2),
             out_specs=pl.BlockSpec(memory_space=pltpu.VMEM),
             compiler_params=pltpu.CompilerParams(vmem_limit_bytes=INSERT_VMEM),
@@ -381,13 +375,13 @@
         for before in arrived:
             before[1], _ = lax.optimization_barrier((before[1], parts))
         arrived.append(slab_exchange(parts, places[c], slab_count, roles[c]))
-        own = choose(parts[:, :bins], places[c]).astype(jnp.float32)
+        own = choose(parts, places[c]).astype(jnp.float32)
         sums.append(jnp.where(places[c] == slab_count - 1, 0.0, own))
     for c, each in enumerate(sizes):
         if not mirrored:
             break
         for block in arrived[c]:
-            sums[c] = sums[c] + block[: each * planes].astype(jnp.float32)
+            sums[c] = sums[c] + block.astype(jnp.float32)
         over = [(b, block) for b, block in enumerate(roles[c]) if b != block]
         if over:
             if c + 1 < len(sizes):
@@ -397,25 +391,10 @@
             handed = lax.ppermute(sums[c].astype(jnp.bfloat16), "batch", over)
             sums[c] = jnp.where(blocks[c] == batch, sums[c], handed.astype(jnp.float32))
 
-    meta_all = [meta_layer]
-    if mirrored:
-        for block in [block[sizes[0] * planes :] for block in arrived[0]]:
-            block = block.reshape(META_ROWS, -1, LANES)
-            halves = (block[:particles], block[particles : 2 * particles])
-            low = jnp.concatenate(halves, axis=1)[:, :batch_count, : 2 * fields]
-            meta_all.append(read_digits(low.transpose(1, 0, 2)))
-    else:
-        for step in range(1, slab_count):
-            ring = [(s, (s + step) % slab_count) for s in range(slab_count)]
-            meta_all.append(lax.ppermute(meta_layer, "slab", ring))
-    meta_all = jnp.concatenate(meta_all, axis=0)
-
     own_freq = batch * rows + jnp.arange(rows, dtype=jnp.int32)
     own_plane = pick_block(find_planes(meta_all), batch) - slab * planes
     focus_count = defocus.shape[0]
     focus_hot = (meta_all[:, 1:2] == jnp.arange(focus_count)[None, :]).astype(jnp.bfloat16)
-    if mirrored:
-        own_plane = jnp.where(places[0] == slab_count - 1, -1, own_plane)
     bin_hot = (own_plane.T[:, None, :] == jnp.arange(planes)[None, :, None]).astype(jnp.bfloat16)
     counts = jnp.einsum("kzp,pd->kzd", bin_hot, focus_hot, preferred_element_type=jnp.float32)
     row_angle = 2.0 * (

time: 155 us -> 163 us (1.052)
  waiting for transfers between devices: 62 us -> 78.7 us
  starting transfers between devices: 45.6 us -> 39.6 us
  other arithmetic: 11 us -> 8.22 us
    all_to_all x3, waiting for transfers between devices: 9.7 us -> 22.9 us  [per_device(): received.append(lax.all_to_all(send, 'batch', 0, 0, tiled=True))]
    ppermute x9, starting transfers between devices: 30.8 us -> 20.1 us  [slab_exchange(): arrived.append(lax.ppermute(block, ('batch', 'slab'), perm))]
    ppermute x0 -> x3, starting transfers between devices: none -> 4.67 us  [per_device(): layers.append(lax.ppermute(own_digits, 'slab', ring))]
    ppermute x0 -> x3, waiting for transfers between devices: none -> 2.55 us  [per_device(): layers.append(lax.ppermute(own_digits, 'slab', ring))]
    add x3, other arithmetic: 4.4 us -> 2.1 us  [per_device(): sums[c] = sums[c] + block.astype(jnp.float32)]
    select_n x3, other arithmetic: 3.28 us -> 1.36 us  [choose(): chosen = jnp.where(index == d, parts[d], chosen)]
  transfers between devices with their start and end apart: 13 -> 17, of which waited for: 9 -> 10; matrix products, arithmetic and copies ran while one was open for 10% -> 8% of each run, Pallas kernels for 13% -> 12%
where the time goes in v10:
time: 163 us; the launch traced here: 162 us
  waiting for transfers between devices  78.7 us (48%)
  starting transfers between devices  39.6 us (24%)
  Pallas kernels  27.2 us (17%)
  other arithmetic  8.22 us (5%)
  local copies, waits for them, and re-layouts  3.86 us (2%)
  matrix products  3.46 us (2%)
    ppermute x9, waiting for transfers between devices, slab_exchange(): arrived.append(lax.ppermute(block, ('batch', 'slab'), perm))  53.3 us
    all_to_all x3, waiting for transfers between devices, per_device(): received.append(lax.all_to_all(send, 'batch', 0, 0, tiled=True))  22.9 us
    pallas_call x3, Pallas kernels, per_device(): pl.pallas_call(functools.partial(spectrum_kernel, runs, meta_from), out_s...  21 us
    ppermute x9, starting transfers between devices, slab_exchange(): arrived.append(lax.ppermute(block, ('batch', 'slab'), perm))  20.1 us
    all_to_all x3, starting transfers between devices, per_device(): received.append(lax.all_to_all(send, 'batch', 0, 0, tiled=True))  13.4 us
    pallas_call x3, Pallas kernels, per_device(): pl.pallas_call(insert_kernel, out_shape=jax.ShapeDtypeStruct((window_slab...  6.25 us
    ppermute x3, starting transfers between devices, per_device(): layers.append(lax.ppermute(own_digits, 'slab', ring))  4.67 us
  transfers between devices with their start and end apart: 17, of which 10 were waited for; matrix products, arithmetic and copies ran while one was open for 8% of the time, Pallas kernels for 12%

profile of v10, /device:TPU:0, one launch (start us, length us, event | category | flops | bytes accessed | tf_op | source)
XLA Modules:
  0.0 161.7 jit_solution(13371382098246780958)
XLA Ops:
  0.0 7.4 %spectrum.3 = (bf16[8,144,768]{2,1,0:T(8,128)(2,1)}, bf16[16,128]{1,0:T(8,128)(2,1)}) custom-call(s32[8]{0:T(128)} %refs_0_.5, s32[2,8]{1,0:T(2,128)} %bitcast.68, s32[8]{0:T(128)} %refs_2_.5, f32[16]{0:T(128)} %refs_3_.5, s32[4,8]{1,0:T(4,128)} %bitcast.65, bf16[8,384,384]{2,1,0:T(8,128)(2,1)} %refs_5_.5, bf16[256,384]{1,0:T(8,128)(2,1)} %constant.172.clone.refs_6_, ...), custom_call_target="tpu_custom_call" | custom-call | tf_op jit(solution)/shard_map/spectrum/pallas_call | solution.py:261
  7.4 5.2 %all-to-all-start = ((bf16[8,144,768]{2,1,0:T(8,128)(2,1)}), bf16[8,144,768]{2,1,0:T(8,128)(2,1)S(1)}, u32[]{:S(2)}, u32[]{:S(2)}) async-start(bf16[8,144,768]{2,1,0:T(8,128)(2,1)} %get-tuple-element.21), calls=%async_computation | async-start | bytes 3538944 | tf_op jit(solution)/shard_map/all_to_all | solution.py:301
  12.6 6.8 %spectrum.4 = bf16[8,128,768]{2,1,0:T(8,128)(2,1)} custom-call(s32[8]{0:T(128)} %refs_0_.5, s32[2,8]{1,0:T(2,128)} %bitcast.69, s32[8]{0:T(128)} %refs_2_.5, f32[16]{0:T(128)} %refs_3_.5, s32[4,8]{1,0:T(4,128)} %bitcast.66, bf16[8,384,384]{2,1,0:T(8,128)(2,1)} %refs_5_.5, bf16[256,384]{1,0:T(8,128)(2,1)} %constant.173.clone.refs_6_, ...), custom_call_target="tpu_custom_call" | custom-call | tf_op jit(solution)/shard_map/spectrum/pallas_call | solution.py:261
  19.4 3.7 %collective-permute-start.2 = (bf16[16,128]{1,0:T(8,128)(2,1)S(1)}, bf16[16,128]{1,0:T(8,128)(2,1)S(1)}, u32[]{:S(2)}, u32[]{:S(2)}) collective-permute-start(bf16[16,128]{1,0:T(8,128)(2,1)S(1)} %copy-done.5), channel_id=1, source_target_pairs={{0,3},{1,0},{2,1},{3,2},{4,7},{5,4},{6,5},{7,6},{8,11},{9,8},{10,9... | collective-permute-start | bytes 12296 | tf_op jit(solution)/shard_map/ppermute | solution.py:297
  25.9 1.6 %collective-permute-done.1 = bf16[16,128]{1,0:T(8,128)(2,1)S(1)} collective-permute-done((bf16[16,128]{1,0:T(8,128)(2,1)S(1)}, bf16[16,128]{1,0:T(8,128)(2,1)S(1)}, u32[]{:S(2)}, u32[]{:S(2)}) %collective-permute-start.1) | collective-permute-done | bytes 4128 | tf_op jit(solution)/shard_map/ppermute | solution.py:297
  29.2 6.8 %spectrum.5 = bf16[8,144,768]{2,1,0:T(8,128)(2,1)} custom-call(s32[8]{0:T(128)} %refs_0_.5, s32[2,8]{1,0:T(2,128)} %bitcast.70, s32[8]{0:T(128)} %refs_2_.5, f32[16]{0:T(128)} %refs_3_.5, s32[4,8]{1,0:T(4,128)} %bitcast.67, bf16[8,384,384]{2,1,0:T(8,128)(2,1)} %refs_5_.5, bf16[256,384]{1,0:T(8,128)(2,1)} %constant.174.clone.refs_6_, ...), custom_call_target="tpu_custom_call" | custom-call | tf_op jit(solution)/shard_map/spectrum/pallas_call | solution.py:261
  36.0 4.6 %all-to-all-start.2 = ((bf16[8,144,768]{2,1,0:T(8,128)(2,1)}), bf16[8,144,768]{2,1,0:T(8,128)(2,1)}, u32[]{:S(2)}, u32[]{:S(2)}) async-start(bf16[8,144,768]{2,1,0:T(8,128)(2,1)} %spectrum.5), calls=%async_computation.2 | async-start | bytes 3538944 | tf_op jit(solution)/shard_map/all_to_all | solution.py:301
  42.2 1.7 %insert.3 = bf16[3,256,768]{2,1,0:T(8,128)(2,1)S(1)} custom-call(bf16[8,144,768]{2,1,0:T(8,128)(2,1)S(1)} %all-to-all-done.received, s32[1,1152]{1,0:T(1,128)S(1)} %reshape.182.codes), custom_call_target="tpu_custom_call" | custom-call | tf_op jit(solution)/shard_map/insert/pallas_call | solution.py:359
  43.9 19.7 %all-to-all-done.2.received = bf16[8,144,768]{2,1,0:T(8,128)(2,1)} async-done(((bf16[8,144,768]{2,1,0:T(8,128)(2,1)}), bf16[8,144,768]{2,1,0:T(8,128)(2,1)}, u32[]{:S(2)}, u32[]{:S(2)}) %all-to-all-start.2) | async-done | bytes 1769504 | tf_op jit(solution)/shard_map/all_to_all | solution.py:301
  63.6 3.6 %all-to-all-start.1 = ((bf16[8,128,768]{2,1,0:T(8,128)(2,1)}), bf16[8,128,768]{2,1,0:T(8,128)(2,1)S(1)}, u32[]{:S(2)}, u32[]{:S(2)}) async-start(bf16[8,128,768]{2,1,0:T(8,128)(2,1)} %spectrum.4), calls=%async_computation.1 | async-start | bytes 3145728 | tf_op jit(solution)/shard_map/all_to_all | solution.py:301
  68.3 3.0 %collective-permute-start.3 = (bf16[256,768]{1,0:T(8,128)(2,1)}, bf16[256,768]{1,0:T(8,128)(2,1)S(1)}, u32[]{:S(2)}, u32[]{:S(2)}) collective-permute-start(bf16[256,768]{1,0:T(8,128)(2,1)} %get-tuple-element.51), channel_id=1, source_target_pairs={{0,1},{1,2},{3,0},{7,6},{6,5},{4,7},{8,9},{9,10},{11,8},{15,14},{1... | collective-permute-start | bytes 1179656 | tf_op jit(solution)/shard_map/ppermute | solution.py:217
  72.7 5.6 %collective-permute-start.4 = (bf16[256,768]{1,0:T(8,128)(2,1)}, bf16[256,768]{1,0:T(8,128)(2,1)}, u32[]{:S(2)}, u32[]{:S(2)}) collective-permute-start(bf16[256,768]{1,0:T(8,128)(2,1)} %get-tuple-element.53), channel_id=1, source_target_pairs={{0,2},{2,0},{3,1},{7,5},{5,7},{4,6},{8,10},{10,8},{11,9},{15,13},{... | collective-permute-start | bytes 1179656 | tf_op jit(solution)/shard_map/ppermute | solution.py:217
  79.8 1.7 %fusion.2 = s32[256,384]{1,0:T(8,128)S(1)} fusion(s32[256]{0:T(256)S(1)} %get-tuple-element.38, s32[256,384]{1,0:T(8,128)S(1)} %convert_reduce_fusion, s32[768,384]{1,0:T(8,128)} %param.18), kind=kOutput, calls=%fused_computation.4 | convolution fusion | flops 151781376 | bytes 1967104 | tf_op jit(solution)/shard_map/dot_general | solution.py:319
  81.9 3.1 %collective-permute-done.5 = bf16[256,768]{1,0:T(8,128)(2,1)} collective-permute-done((bf16[256,768]{1,0:T(8,128)(2,1)}, bf16[256,768]{1,0:T(8,128)(2,1)}, u32[]{:S(2)}, u32[]{:S(2)}) %collective-permute-start.5) | collective-permute-done | bytes 393248 | tf_op jit(solution)/shard_map/ppermute | solution.py:217
  84.9 3.2 %all-to-all-done.1.received = bf16[8,128,768]{2,1,0:T(8,128)(2,1)S(1)} async-done(((bf16[8,128,768]{2,1,0:T(8,128)(2,1)}), bf16[8,128,768]{2,1,0:T(8,128)(2,1)S(1)}, u32[]{:S(2)}, u32[]{:S(2)}) %all-to-all-start.1) | async-done | bytes 1572896 | tf_op jit(solution)/shard_map/all_to_all | solution.py:301
  92.5 7.0 %collective-permute-done.4 = bf16[256,768]{1,0:T(8,128)(2,1)} collective-permute-done((bf16[256,768]{1,0:T(8,128)(2,1)}, bf16[256,768]{1,0:T(8,128)(2,1)}, u32[]{:S(2)}, u32[]{:S(2)}) %collective-permute-start.4) | collective-permute-done | bytes 393248 | tf_op jit(solution)/shard_map/ppermute | solution.py:217
  99.5 1.9 %collective-permute-start.8 = (bf16[256,768]{1,0:T(8,128)(2,1)S(1)}, bf16[256,768]{1,0:T(8,128)(2,1)S(1)}, u32[]{:S(2)}, u32[]{:S(2)}) collective-permute-start(bf16[256,768]{1,0:T(8,128)(2,1)S(1)} %get-tuple-element.48), channel_id=1, source_target_pairs={{0,1},{1,2},{3,0},{7,6},{6,5},{4,7},{8,9},{9,10},{11,8},{15,14},{1... | collective-permute-start | bytes 1179656 | tf_op jit(solution)/shard_map/ppermute | solution.py:217
  101.4 1.9 %collective-permute-start.9 = (bf16[256,768]{1,0:T(8,128)(2,1)S(1)}, bf16[256,768]{1,0:T(8,128)(2,1)S(1)}, u32[]{:S(2)}, u32[]{:S(2)}) collective-permute-start(bf16[256,768]{1,0:T(8,128)(2,1)S(1)} %get-tuple-element.49), channel_id=1, source_target_pairs={{0,2},{2,0},{3,1},{7,5},{5,7},{4,6},{8,10},{10,8},{11,9},{15,13},{... | collective-permute-start | bytes 1179656 | tf_op jit(solution)/shard_map/ppermute | solution.py:217
  103.5 3.2 %insert.5 = bf16[3,256,768]{2,1,0:T(8,128)(2,1)S(1)} custom-call(bf16[8,144,768]{2,1,0:T(8,128)(2,1)} %all-to-all-done.2.received, s32[1,1152]{1,0:T(1,128)S(1)} %reshape.184.codes), custom_call_target="tpu_custom_call" | custom-call | tf_op jit(solution)/shard_map/insert/pallas_call | solution.py:359
  110.3 17.0 %collective-permute-done.9 = bf16[256,768]{1,0:T(8,128)(2,1)S(1)} collective-permute-done((bf16[256,768]{1,0:T(8,128)(2,1)S(1)}, bf16[256,768]{1,0:T(8,128)(2,1)S(1)}, u32[]{:S(2)}, u32[]{:S(2)}) %collective-permute-start.9) | collective-permute-done | bytes 393248 | tf_op jit(solution)/shard_map/ppermute | solution.py:217
  127.4 1.9 %collective-permute-start.12 = (bf16[256,768]{1,0:T(8,128)(2,1)S(1)}, bf16[256,768]{1,0:T(8,128)(2,1)S(1)}, u32[]{:S(2)}, u32[]{:S(2)}) collective-permute-start(bf16[256,768]{1,0:T(8,128)(2,1)S(1)} %get-tuple-element.45), channel_id=1, source_target_pairs={{0,1},{1,2},{3,0},{4,5},{5,6},{7,4},{8,9},{9,10},{11,8},{12,13},{1... | collective-permute-start | bytes 1179656 | tf_op jit(solution)/shard_map/ppermute | solution.py:217
  129.3 1.9 %collective-permute-start.13 = (bf16[256,768]{1,0:T(8,128)(2,1)S(1)}, bf16[256,768]{1,0:T(8,128)(2,1)S(1)}, u32[]{:S(2)}, u32[]{:S(2)}) collective-permute-start(bf16[256,768]{1,0:T(8,128)(2,1)S(1)} %get-tuple-element.46), channel_id=1, source_target_pairs={{0,2},{2,0},{3,1},{4,6},{6,4},{7,5},{8,10},{10,8},{11,9},{12,14},{... | collective-permute-start | bytes 1179656 | tf_op jit(solution)/shard_map/ppermute | solution.py:217
  132.4 10.8 %collective-permute-done.12 = bf16[256,768]{1,0:T(8,128)(2,1)S(1)} collective-permute-done((bf16[256,768]{1,0:T(8,128)(2,1)S(1)}, bf16[256,768]{1,0:T(8,128)(2,1)S(1)}, u32[]{:S(2)}, u32[]{:S(2)}) %collective-permute-start.12) | collective-permute-done | bytes 393248 | tf_op jit(solution)/shard_map/ppermute | solution.py:217
  143.1 15.3 %collective-permute-done.13 = bf16[256,768]{1,0:T(8,128)(2,1)S(1)} collective-permute-done((bf16[256,768]{1,0:T(8,128)(2,1)S(1)}, bf16[256,768]{1,0:T(8,128)(2,1)S(1)}, u32[]{:S(2)}, u32[]{:S(2)}) %collective-permute-start.13) | collective-permute-done | bytes 393248 | tf_op jit(solution)/shard_map/ppermute | solution.py:217
  (80 shorter events, 22.6 us)
Async XLA Ops:
  7.4 28.6 %all-to-all-start = ((bf16[8,144,768]{2,1,0:T(8,128)(2,1)}), bf16[8,144,768]{2,1,0:T(8,128)(2,1)S(1)}, u32[]{:S(2)}, u32[]{:S(2)}) async-start(bf16[8,144,768]{2,1,0:T(8,128)(2,1)} %get-tuple-element.21), calls=%async_computation | async-start | bytes 3538944 | tf_op jit(solution)/shard_map/all_to_all | solution.py:301
  12.5 6.9 %copy-start.5 = (bf16[16,128]{1,0:T(8,128)(2,1)S(1)}, bf16[16,128]{1,0:T(8,128)(2,1)}, u32[]{:S(2)}) copy-start(bf16[16,128]{1,0:T(8,128)(2,1)} %get-tuple-element.24) | copy-start | bytes 12292
  12.5 11.6 %copy-start.4 = (f32[16]{0:T(128)S(1)}, f32[16]{0:T(128)}, u32[]{:S(2)}) copy-start(f32[16]{0:T(128)} %refs_3_.5) | copy-start | bytes 196
  19.4 6.5 %collective-permute-start.2 = (bf16[16,128]{1,0:T(8,128)(2,1)S(1)}, bf16[16,128]{1,0:T(8,128)(2,1)S(1)}, u32[]{:S(2)}, u32[]{:S(2)}) collective-permute-start(bf16[16,128]{1,0:T(8,128)(2,1)S(1)} %copy-done.5), channel_id=1, source_target_pairs={{0,3},{1,0},{2,1},{3,2},{4,7},{5,4},{6,5},{7,6},{8,11},{9,8},{10,9... | collective-permute-start | bytes 12296 | tf_op jit(solution)/shard_map/ppermute | solution.py:297
  23.1 4.5 %collective-permute-start.1 = (bf16[16,128]{1,0:T(8,128)(2,1)S(1)}, bf16[16,128]{1,0:T(8,128)(2,1)S(1)}, u32[]{:S(2)}, u32[]{:S(2)}) collective-permute-start(bf16[16,128]{1,0:T(8,128)(2,1)S(1)} %copy-done.5), channel_id=1, source_target_pairs={{0,2},{1,3},{2,0},{3,1},{4,6},{5,7},{6,4},{7,5},{8,10},{9,11},{10,... | collective-permute-start | bytes 12296 | tf_op jit(solution)/shard_map/ppermute | solution.py:297
  23.1 5.4 %collective-permute-start = (bf16[16,128]{1,0:T(8,128)(2,1)S(1)}, bf16[16,128]{1,0:T(8,128)(2,1)S(1)}, u32[]{:S(2)}, u32[]{:S(2)}) collective-permute-start(bf16[16,128]{1,0:T(8,128)(2,1)S(1)} %copy-done.5), channel_id=1, source_target_pairs={{0,1},{1,2},{2,3},{3,0},{4,5},{5,6},{6,7},{7,4},{8,9},{9,10},{10,1... | collective-permute-start | bytes 12296 | tf_op jit(solution)/shard_map/ppermute | solution.py:297
  36.0 5.1 %copy-start = (s32[768,384]{1,0:T(8,128)S(1)}, s32[768,384]{1,0:T(8,128)}, u32[]{:S(2)}) copy-start(s32[768,384]{1,0:T(8,128)} %param.18) | copy-start | bytes 3538948
  36.0 27.6 %all-to-all-start.2 = ((bf16[8,144,768]{2,1,0:T(8,128)(2,1)}), bf16[8,144,768]{2,1,0:T(8,128)(2,1)}, u32[]{:S(2)}, u32[]{:S(2)}) async-start(bf16[8,144,768]{2,1,0:T(8,128)(2,1)} %spectrum.5), calls=%async_computation.2 | async-start | bytes 3538944 | tf_op jit(solution)/shard_map/all_to_all | solution.py:301
  63.6 24.5 %all-to-all-start.1 = ((bf16[8,128,768]{2,1,0:T(8,128)(2,1)}), bf16[8,128,768]{2,1,0:T(8,128)(2,1)S(1)}, u32[]{:S(2)}, u32[]{:S(2)}) async-start(bf16[8,128,768]{2,1,0:T(8,128)(2,1)} %spectrum.4), calls=%async_computation.1 | async-start | bytes 3145728 | tf_op jit(solution)/shard_map/all_to_all | solution.py:301
  68.3 38.3 %collective-permute-start.3 = (bf16[256,768]{1,0:T(8,128)(2,1)}, bf16[256,768]{1,0:T(8,128)(2,1)S(1)}, u32[]{:S(2)}, u32[]{:S(2)}) collective-permute-start(bf16[256,768]{1,0:T(8,128)(2,1)} %get-tuple-element.51), channel_id=1, source_target_pairs={{0,1},{1,2},{3,0},{7,6},{6,5},{4,7},{8,9},{9,10},{11,8},{15,14},{1... | collective-permute-start | bytes 1179656 | tf_op jit(solution)/shard_map/ppermute | solution.py:217
  71.4 13.6 %collective-permute-start.5 = (bf16[256,768]{1,0:T(8,128)(2,1)}, bf16[256,768]{1,0:T(8,128)(2,1)}, u32[]{:S(2)}, u32[]{:S(2)}) collective-permute-start(bf16[256,768]{1,0:T(8,128)(2,1)} %get-tuple-element.52), channel_id=1, source_target_pairs={{1,0},{2,1},{3,2},{6,7},{5,6},{4,5},{9,8},{10,9},{11,10},{14,15},{... | collective-permute-start | bytes 1179656 | tf_op jit(solution)/shard_map/ppermute | solution.py:217
  72.7 26.8 %collective-permute-start.4 = (bf16[256,768]{1,0:T(8,128)(2,1)}, bf16[256,768]{1,0:T(8,128)(2,1)}, u32[]{:S(2)}, u32[]{:S(2)}) collective-permute-start(bf16[256,768]{1,0:T(8,128)(2,1)} %get-tuple-element.53), channel_id=1, source_target_pairs={{0,2},{2,0},{3,1},{7,5},{5,7},{4,6},{8,10},{10,8},{11,9},{15,13},{... | collective-permute-start | bytes 1179656 | tf_op jit(solution)/shard_map/ppermute | solution.py:217
  89.5 1.4 copy-start.2
  89.5 1.4 copy-start.3
  89.7 13.8 %collective-permute-start.6 = (bf16[256,768]{1,0:T(8,128)(2,1)S(1)}, bf16[256,768]{1,0:T(8,128)(2,1)S(1)}, u32[]{:S(2)}, u32[]{:S(2)}) collective-permute-start(bf16[256,768]{1,0:T(8,128)(2,1)S(1)} %get-tuple-element.50), channel_id=1, source_target_pairs={{1,0},{2,1},{3,2},{6,7},{5,6},{4,5},{9,8},{10,9},{11,10},{14,15},{... | collective-permute-start | bytes 1179656 | tf_op jit(solution)/shard_map/ppermute | solution.py:217
  99.5 31.7 %collective-permute-start.8 = (bf16[256,768]{1,0:T(8,128)(2,1)S(1)}, bf16[256,768]{1,0:T(8,128)(2,1)S(1)}, u32[]{:S(2)}, u32[]{:S(2)}) collective-permute-start(bf16[256,768]{1,0:T(8,128)(2,1)S(1)} %get-tuple-element.48), channel_id=1, source_target_pairs={{0,1},{1,2},{3,0},{7,6},{6,5},{4,7},{8,9},{9,10},{11,8},{15,14},{1... | collective-permute-start | bytes 1179656 | tf_op jit(solution)/shard_map/ppermute | solution.py:217
  101.4 26.0 %collective-permute-start.9 = (bf16[256,768]{1,0:T(8,128)(2,1)S(1)}, bf16[256,768]{1,0:T(8,128)(2,1)S(1)}, u32[]{:S(2)}, u32[]{:S(2)}) collective-permute-start(bf16[256,768]{1,0:T(8,128)(2,1)S(1)} %get-tuple-element.49), channel_id=1, source_target_pairs={{0,2},{2,0},{3,1},{7,5},{5,7},{4,6},{8,10},{10,8},{11,9},{15,13},{... | collective-permute-start | bytes 1179656 | tf_op jit(solution)/shard_map/ppermute | solution.py:217
  108.1 24.2 %collective-permute-start.7 = (bf16[256,768]{1,0:T(8,128)(2,1)S(1)}, bf16[256,768]{1,0:T(8,128)(2,1)S(1)}, u32[]{:S(2)}, u32[]{:S(2)}) collective-permute-start(bf16[256,768]{1,0:T(8,128)(2,1)S(1)} %convert_element_type.114), channel_id=1, source_target_pairs={{4,16},{12,24},{16,4},{24,12},{5,17},{13,25},{17,5},{25,13},{6,18}... | collective-permute-start | bytes 1179656 | tf_op jit(solution)/shard_map/ppermute | solution.py:391
  108.9 22.6 %collective-permute-start.10 = (bf16[256,768]{1,0:T(8,128)(2,1)S(1)}, bf16[256,768]{1,0:T(8,128)(2,1)S(1)}, u32[]{:S(2)}, u32[]{:S(2)}) collective-permute-start(bf16[256,768]{1,0:T(8,128)(2,1)S(1)} %get-tuple-element.47), channel_id=1, source_target_pairs={{1,0},{2,1},{3,2},{5,4},{6,5},{7,6},{9,8},{10,9},{11,10},{13,12},{... | collective-permute-start | bytes 1179656 | tf_op jit(solution)/shard_map/ppermute | solution.py:217
  127.4 15.8 %collective-permute-start.12 = (bf16[256,768]{1,0:T(8,128)(2,1)S(1)}, bf16[256,768]{1,0:T(8,128)(2,1)S(1)}, u32[]{:S(2)}, u32[]{:S(2)}) collective-permute-start(bf16[256,768]{1,0:T(8,128)(2,1)S(1)} %get-tuple-element.45), channel_id=1, source_target_pairs={{0,1},{1,2},{3,0},{4,5},{5,6},{7,4},{8,9},{9,10},{11,8},{12,13},{1... | collective-permute-start | bytes 1179656 | tf_op jit(solution)/shard_map/ppermute | solution.py:217
  129.3 29.2 %collective-permute-start.13 = (bf16[256,768]{1,0:T(8,128)(2,1)S(1)}, bf16[256,768]{1,0:T(8,128)(2,1)S(1)}, u32[]{:S(2)}, u32[]{:S(2)}) collective-permute-start(bf16[256,768]{1,0:T(8,128)(2,1)S(1)} %get-tuple-element.46), channel_id=1, source_target_pairs={{0,2},{2,0},{3,1},{4,6},{6,4},{7,5},{8,10},{10,8},{11,9},{12,14},{... | collective-permute-start | bytes 1179656 | tf_op jit(solution)/shard_map/ppermute | solution.py:217
  131.6 27.2 %collective-permute-start.11 = (bf16[256,768]{1,0:T(8,128)(2,1)S(1)}, bf16[256,768]{1,0:T(8,128)(2,1)S(1)}, u32[]{:S(2)}, u32[]{:S(2)}) collective-permute-start(bf16[256,768]{1,0:T(8,128)(2,1)S(1)} %convert_element_type.126), channel_id=1, source_target_pairs={{4,16},{12,24},{16,4},{24,12},{5,17},{13,25},{17,5},{25,13},{6,18}... | collective-permute-start | bytes 1179656 | tf_op jit(solution)/shard_map/ppermute | solution.py:391
  158.8 1.3 copy-start.1

commit v11 on v10

--- a/solution.py
+++ b/solution.py
@@ -20,17 +20,12 @@
 INSERT_VMEM = 32 * 1024 * 1024
 
 
-def dft_tables(length):
+def dft_table(length):
     index = np.arange(length, dtype=np.int32)
     turns = index[:, None] * index[None, :] % length
     angle = np.float32(2.0 * math.pi / length) * turns.astype(np.float32)
     factor = np.float32(1.0 / math.sqrt(length))
-    cosine = np.cos(angle) * factor
-    sine = np.sin(angle) * factor
-    upper_rows = np.concatenate([cosine, -sine], axis=1)
-    lower_rows = np.concatenate([sine, cosine], axis=1)
-    table_right = np.concatenate([upper_rows, lower_rows], axis=0)
-    return cosine, -sine, table_right
+    return np.concatenate([np.cos(angle) * factor, -(np.sin(angle) * factor)], axis=1)
 
 
 def spread(iota, values):
@@ -62,7 +57,7 @@
 
 
 def spectrum_kernel(runs, meta_from, *refs):
-    classes, shifts, defocus_class, defocus, run_counts, images_in, left_in, right_in, *refs = refs
+    classes, shifts, defocus_class, defocus, run_counts, images_in, upper_in, *refs = refs
     if meta_from == "operand":
         meta_in, *refs = refs
     out, *refs = refs
@@ -73,10 +68,9 @@
     owners = out.shape[0]
     rows_each = runs[0][1] - runs[0][0]
     rows = owners * rows_each
-    loads = [pltpu.make_async_copy(left_in, left, load_sems.at[0])]
+    loads = [pltpu.make_async_copy(upper_in, right.at[:length], load_sems.at[0])]
     for p in range(particles):
         loads.append(pltpu.make_async_copy(images_in.at[p], images.at[p], load_sems.at[1 + p]))
-    loads.append(pltpu.make_async_copy(right_in, right, load_sems.at[1 + particles]))
     for load in loads:
         load.start()
 
@@ -129,16 +123,21 @@
             block[d, particles * rows_each :, :LANES] = digits
 
     loads[0].wait()
+    for d, (begin, end) in enumerate(runs):
+        here = slice(d * rows_each, (d + 1) * rows_each)
+        left[here, :] = right[begin:end, :length]
+        left[rows + here.start : rows + here.stop, :] = right[begin:end, length:]
+    right[length:, :length] = -right[:length, length:]
+    right[length:, length:] = right[:length, :length]
     table = left[...]
-    for p in range(particles):
-        loads[1 + p].wait()
-        section = jnp.dot(table, images[p], preferred_element_type=jnp.float32)
-        section = section.astype(jnp.bfloat16)
-        joined[p * rows : (p + 1) * rows, :length] = section[:rows]
-        joined[p * rows : (p + 1) * rows, length:] = section[rows:]
-    loads[1 + particles].wait()
     sends = []
     for first in range(0, particles, 2):
+        for p in range(first, first + 2):
+            loads[1 + p].wait()
+            section = jnp.dot(table, images[p], preferred_element_type=jnp.float32)
+            section = section.astype(jnp.bfloat16)
+            joined[p * rows : (p + 1) * rows, :length] = section[:rows]
+            joined[p * rows : (p + 1) * rows, length:] = section[rows:]
         spectrum = jnp.dot(
             joined[first * rows : (first + 2) * rows, :],
             right[...],
@@ -241,16 +240,12 @@
 
     fields = slab_count + 1
 
-    cosine, minus_sine, table_right = dft_tables(length)
-    table_right = jnp.asarray(table_right.astype(jnp.bfloat16))
+    table_upper = jnp.asarray(dft_table(length).astype(jnp.bfloat16))
     received = []
     weighted = []
     for c, each in enumerate(sizes):
         chunk_rows = batch_count * each
-        block = np.array(roles[c])
-        order = (block[:, None] * rows + starts[c] + np.arange(each)[None, :]).reshape(-1)
-        left = np.concatenate([cosine[order], minus_sine[order]], axis=0)
-        runs = [(k * rows + starts[c], k * rows + starts[c] + each) for k in block.tolist()]
+        runs = [(k * rows + starts[c], k * rows + starts[c] + each) for k in roles[c]]
         last = c + 1 == len(sizes)
         meta_from = "scalars" if c == 0 else "operand" if last else None
         block_rows = particles * each + (META_ROWS if meta_from else 0)
@@ -262,7 +257,7 @@
             functools.partial(spectrum_kernel, runs, meta_from),
             out_shape=[jax.ShapeDtypeStruct(block_shape, jnp.bfloat16)]
             + [jax.ShapeDtypeStruct((META_ROWS, LANES), jnp.bfloat16)] * (c == 0),
-            in_specs=[smem] * 5 + [hbm] * 3 + [vmem] * last,
+            in_specs=[smem] * 5 + [hbm] * 2 + [vmem] * last,
             out_specs=[hbm] + [vmem] * (c == 0),
             scratch_shapes=[
                 pltpu.VMEM((particles, length, length), jnp.bfloat16),
@@ -270,7 +265,7 @@
                 pltpu.VMEM((2 * length, 2 * length), jnp.bfloat16),
                 pltpu.VMEM((particles * chunk_rows, 2 * length), jnp.bfloat16),
                 pltpu.VMEM(block_shape, jnp.bfloat16),
-                pltpu.SemaphoreType.DMA((particles + 2,)),
+                pltpu.SemaphoreType.DMA((particles + 1,)),
                 pltpu.SemaphoreType.DMA((particles // 2,)),
             ],
             compiler_params=pltpu.CompilerParams(vmem_limit_bytes=SPECTRUM_VMEM),
@@ -283,8 +278,7 @@
             defocus,
             run_counts.T,
             images,
-            jnp.asarray(left.astype(jnp.bfloat16)),
-            table_right,
+            table_upper,
             *([digits] if last else []),
         )
         if c == 0:
@@ -297,6 +291,8 @@
                 layers.append(lax.ppermute(own_digits, "slab", ring))
             digits = jnp.concatenate([layer[:, : 2 * fields] for layer in layers], axis=1)
             digits = jnp.pad(digits, ((0, 0), (0, 2 * length - digits.shape[1])))
+        if c > 0:
+            send, received[-1] = lax.optimization_barrier((send, received[-1]))
         weighted.append(send)
         received.append(lax.all_to_all(send, "batch", 0, 0, tiled=True))
 
@@ -355,7 +351,9 @@
         if c == 0:
             codes_in, _ = lax.optimization_barrier((codes_in, weighted[1:]))
         if c > 0 and mirrored:
-            codes_in, arrived[c - 1][2] = lax.optimization_barrier((codes_in, arrived[c - 1][2]))
+            codes_in, arrived[c - 1][0], arrived[c - 1][2] = lax.optimization_barrier(
+                (codes_in, arrived[c - 1][0], arrived[c - 1][2])
+            )
         parts = pl.pallas_call(
             insert_kernel,
             out_shape=jax.ShapeDtypeStruct((window_slabs, bins, 2 * length), jnp.bfloat16),

time: 163 us -> 179 us (1.098)
  the two profiles are of different devices: /device:TPU:0 before, /device:TPU:11 now
where the time goes in v11:
time: 179 us; the launch traced here: 178 us
  waiting for transfers between devices  76.8 us (43%)
  starting transfers between devices  54.8 us (31%)
  Pallas kernels  30.4 us (17%)
  other arithmetic  9.93 us (6%)
  matrix products  3.46 us (2%)
  local copies, waits for them, and re-layouts  2.22 us (1%)
    ppermute x9, waiting for transfers between devices, slab_exchange(): arrived.append(lax.ppermute(block, ('batch', 'slab'), perm))  50 us
    ppermute x9, starting transfers between devices, slab_exchange(): arrived.append(lax.ppermute(block, ('batch', 'slab'), perm))  29.2 us
    pallas_call x3, Pallas kernels, per_device(): pl.pallas_call(functools.partial(spectrum_kernel, runs, meta_from), out_s...  22.6 us
    all_to_all x3, waiting for transfers between devices, per_device(): received.append(lax.all_to_all(send, 'batch', 0, 0, tiled=True))  19.3 us
    all_to_all x3, starting transfers between devices, per_device(): received.append(lax.all_to_all(send, 'batch', 0, 0, tiled=True))  16.2 us
    pallas_call x3, Pallas kernels, per_device(): pl.pallas_call(insert_kernel, out_shape=jax.ShapeDtypeStruct((window_slab...  7.85 us
    ppermute x2, waiting for transfers between devices, per_device(): handed = lax.ppermute(sums[c].astype(jnp.bfloat16), 'batch', over)  6.73 us
    ppermute x2, starting transfers between devices, per_device(): handed = lax.ppermute(sums[c].astype(jnp.bfloat16), 'batch', over)  4.71 us
  transfers between devices with their start and end apart: 17, of which 9 were waited for; matrix products, arithmetic and copies ran while one was open for 7% of the time, Pallas kernels for 13%

profile of v11, /device:TPU:11, one launch (start us, length us, event | category | flops | bytes accessed | tf_op | source)
XLA Modules:
  0.0 178.2 jit_solution(17768954055010437364)
XLA Ops:
  0.0 7.9 %spectrum.3 = (bf16[8,144,768]{2,1,0:T(8,128)(2,1)}, bf16[16,128]{1,0:T(8,128)(2,1)}) custom-call(s32[8]{0:T(128)} %refs_0_.5, s32[2,8]{1,0:T(2,128)} %bitcast.66, s32[8]{0:T(128)} %refs_2_.5, f32[16]{0:T(128)} %refs_3_.5, s32[4,8]{1,0:T(4,128)} %bitcast.63, bf16[8,384,384]{2,1,0:T(8,128)(2,1)} %refs_5_.5, bf16[384,768]{1,0:T(8,128)(2,1)} %constant.165.clone.refs_6_), custom_call_target="tpu_custom_call" | custom-call | tf_op jit(solution)/shard_map/spectrum/pallas_call | solution.py:256
  7.9 4.6 %all-to-all-start = ((bf16[8,144,768]{2,1,0:T(8,128)(2,1)}), bf16[8,144,768]{2,1,0:T(8,128)(2,1)S(1)}, u32[]{:S(2)}, u32[]{:S(2)}) async-start(bf16[8,144,768]{2,1,0:T(8,128)(2,1)} %get-tuple-element.29), calls=%async_computation | async-start | bytes 3538944 | tf_op jit(solution)/shard_map/all_to_all | solution.py:297
  12.5 7.4 %spectrum.4 = bf16[8,128,768]{2,1,0:T(8,128)(2,1)} custom-call(s32[8]{0:T(128)} %refs_0_.5, s32[2,8]{1,0:T(2,128)} %bitcast.67, s32[8]{0:T(128)} %refs_2_.5, f32[16]{0:T(128)} %refs_3_.5, s32[4,8]{1,0:T(4,128)} %bitcast.64, bf16[8,384,384]{2,1,0:T(8,128)(2,1)} %refs_5_.5, bf16[384,768]{1,0:T(8,128)(2,1)} %constant.165.clone.refs_6_), custom_call_target="tpu_custom_call" | custom-call | tf_op jit(solution)/shard_map/spectrum/pallas_call | solution.py:256
  20.1 2.3 %collective-permute-start.1 = (bf16[16,128]{1,0:T(8,128)(2,1)S(1)}, bf16[16,128]{1,0:T(8,128)(2,1)S(1)}, u32[]{:S(2)}, u32[]{:S(2)}) collective-permute-start(bf16[16,128]{1,0:T(8,128)(2,1)S(1)} %copy-done.7), channel_id=1, source_target_pairs={{0,2},{1,3},{2,0},{3,1},{4,6},{5,7},{6,4},{7,5},{8,10},{9,11},{10,... | collective-permute-start | bytes 12296 | tf_op jit(solution)/shard_map/ppermute | solution.py:291
  22.4 2.2 %collective-permute-start = (bf16[16,128]{1,0:T(8,128)(2,1)S(1)}, bf16[16,128]{1,0:T(8,128)(2,1)S(1)}, u32[]{:S(2)}, u32[]{:S(2)}) collective-permute-start(bf16[16,128]{1,0:T(8,128)(2,1)S(1)} %copy-done.7), channel_id=1, source_target_pairs={{0,1},{1,2},{2,3},{3,0},{4,5},{5,6},{6,7},{7,4},{8,9},{9,10},{10,1... | collective-permute-start | bytes 12296 | tf_op jit(solution)/shard_map/ppermute | solution.py:291
  26.1 7.3 %spectrum.5 = bf16[8,144,768]{2,1,0:T(8,128)(2,1)} custom-call(s32[8]{0:T(128)} %refs_0_.5, s32[2,8]{1,0:T(2,128)} %bitcast.68, s32[8]{0:T(128)} %refs_2_.5, f32[16]{0:T(128)} %refs_3_.5, s32[4,8]{1,0:T(4,128)} %bitcast.65, bf16[8,384,384]{2,1,0:T(8,128)(2,1)} %refs_5_.5, bf16[384,768]{1,0:T(8,128)(2,1)} %constant.165.clone.refs_6_, ...), custom_call_target="tpu_custom_call" | custom-call | tf_op jit(solution)/shard_map/spectrum/pallas_call | solution.py:256
  34.1 5.8 %all-to-all-start.1 = ((bf16[8,128,768]{2,1,0:T(8,128)(2,1)}), bf16[8,128,768]{2,1,0:T(8,128)(2,1)}, u32[]{:S(2)}, u32[]{:S(2)}) async-start(bf16[8,128,768]{2,1,0:T(8,128)(2,1)} %spectrum.4), calls=%async_computation.1 | async-start | bytes 3145728 | tf_op jit(solution)/shard_map/all_to_all | solution.py:297
  40.7 18.6 %all-to-all-done.1.received = bf16[8,128,768]{2,1,0:T(8,128)(2,1)} async-done(((bf16[8,128,768]{2,1,0:T(8,128)(2,1)}), bf16[8,128,768]{2,1,0:T(8,128)(2,1)}, u32[]{:S(2)}, u32[]{:S(2)}) %all-to-all-start.1) | async-done | bytes 1572896 | tf_op jit(solution)/shard_map/all_to_all | solution.py:297
  59.4 5.8 %all-to-all-start.2 = ((bf16[8,144,768]{2,1,0:T(8,128)(2,1)}), bf16[8,144,768]{2,1,0:T(8,128)(2,1)}, u32[]{:S(2)}, u32[]{:S(2)}) async-start(bf16[8,144,768]{2,1,0:T(8,128)(2,1)} %spectrum.5), calls=%async_computation.2 | async-start | bytes 3538944 | tf_op jit(solution)/shard_map/all_to_all | solution.py:297
  69.4 4.0 %collective-permute-start.4 = (bf16[256,768]{1,0:T(8,128)(2,1)S(1)}, bf16[256,768]{1,0:T(8,128)(2,1)S(1)}, u32[]{:S(2)}, u32[]{:S(2)}) collective-permute-start(bf16[256,768]{1,0:T(8,128)(2,1)S(1)} %get-tuple-element.65), channel_id=1, source_target_pairs={{1,0},{2,1},{3,2},{6,7},{5,6},{4,5},{9,8},{10,9},{11,10},{14,15},{... | collective-permute-start | bytes 1179656 | tf_op jit(solution)/shard_map/ppermute | solution.py:216
  73.5 2.4 %collective-permute-start.5 = (bf16[256,768]{1,0:T(8,128)(2,1)}, bf16[256,768]{1,0:T(8,128)(2,1)}, u32[]{:S(2)}, u32[]{:S(2)}) collective-permute-start(bf16[256,768]{1,0:T(8,128)(2,1)} %get-tuple-element.63), channel_id=1, source_target_pairs={{0,2},{2,0},{3,1},{7,5},{5,7},{4,6},{8,10},{10,8},{11,9},{15,13},{... | collective-permute-start | bytes 1179656 | tf_op jit(solution)/shard_map/ppermute | solution.py:216
  76.0 2.8 %collective-permute-done.3 = bf16[256,768]{1,0:T(8,128)(2,1)S(1)} collective-permute-done((bf16[256,768]{1,0:T(8,128)(2,1)S(1)}, bf16[256,768]{1,0:T(8,128)(2,1)S(1)}, u32[]{:S(2)}, u32[]{:S(2)}) %collective-permute-start.3) | collective-permute-done | bytes 393248 | tf_op jit(solution)/shard_map/ppermute | solution.py:216
  78.8 11.3 %collective-permute-done.4 = bf16[256,768]{1,0:T(8,128)(2,1)S(1)} collective-permute-done((bf16[256,768]{1,0:T(8,128)(2,1)S(1)}, bf16[256,768]{1,0:T(8,128)(2,1)S(1)}, u32[]{:S(2)}, u32[]{:S(2)}) %collective-permute-start.4) | collective-permute-done | bytes 393248 | tf_op jit(solution)/shard_map/ppermute | solution.py:216
  90.1 2.9 %insert.4 = bf16[3,256,768]{2,1,0:T(8,128)(2,1)S(1)} custom-call(bf16[8,128,768]{2,1,0:T(8,128)(2,1)} %all-to-all-done.1.received, s32[1,1024]{1,0:T(1,128)S(1)} %reshape_reshape.3.codes), custom_call_target="tpu_custom_call" | custom-call | tf_op jit(solution)/shard_map/insert/pallas_call | solution.py:357
  95.6 8.1 %collective-permute-start.7 = (bf16[256,768]{1,0:T(8,128)(2,1)}, bf16[256,768]{1,0:T(8,128)(2,1)}, u32[]{:S(2)}, u32[]{:S(2)}) collective-permute-start(bf16[256,768]{1,0:T(8,128)(2,1)} %get-tuple-element.62), channel_id=1, source_target_pairs={{1,0},{2,1},{3,2},{6,7},{5,6},{4,5},{9,8},{10,9},{11,10},{14,15},{... | collective-permute-start | bytes 1179656 | tf_op jit(solution)/shard_map/ppermute | solution.py:216
  104.6 4.7 %collective-permute-start.9 = (bf16[256,768]{1,0:T(8,128)(2,1)}, bf16[256,768]{1,0:T(8,128)(2,1)}, u32[]{:S(2)}, u32[]{:S(2)}) collective-permute-start(bf16[256,768]{1,0:T(8,128)(2,1)} %get-tuple-element.60), channel_id=1, source_target_pairs={{0,2},{2,0},{3,1},{7,5},{5,7},{4,6},{8,10},{10,8},{11,9},{15,13},{... | collective-permute-start | bytes 1179656 | tf_op jit(solution)/shard_map/ppermute | solution.py:216
  109.3 10.5 %collective-permute-done.6 = bf16[256,768]{1,0:T(8,128)(2,1)S(1)} collective-permute-done((bf16[256,768]{1,0:T(8,128)(2,1)}, bf16[256,768]{1,0:T(8,128)(2,1)S(1)}, u32[]{:S(2)}, u32[]{:S(2)}) %collective-permute-start.6) | collective-permute-done | bytes 393248 | tf_op jit(solution)/shard_map/ppermute | solution.py:216
  124.2 3.2 %insert.5 = bf16[3,256,768]{2,1,0:T(8,128)(2,1)S(1)} custom-call(bf16[8,144,768]{2,1,0:T(8,128)(2,1)} %all-to-all-done.2.received, s32[1,1152]{1,0:T(1,128)S(1)} %reshape.184.codes), custom_call_target="tpu_custom_call" | custom-call | tf_op jit(solution)/shard_map/insert/pallas_call | solution.py:357
  128.8 2.8 %collective-permute-start.8 = (bf16[256,768]{1,0:T(8,128)(2,1)S(1)}, bf16[256,768]{1,0:T(8,128)(2,1)S(1)}, u32[]{:S(2)}, u32[]{:S(2)}) collective-permute-start(bf16[256,768]{1,0:T(8,128)(2,1)S(1)} %convert_element_type.114), channel_id=1, source_target_pairs={{4,16},{12,24},{16,4},{24,12},{5,17},{13,25},{17,5},{25,13},{6,18}... | collective-permute-start | bytes 1179656 | tf_op jit(solution)/shard_map/ppermute | solution.py:389
  131.7 1.9 %collective-permute-start.12 = (bf16[256,768]{1,0:T(8,128)(2,1)S(1)}, bf16[256,768]{1,0:T(8,128)(2,1)S(1)}, u32[]{:S(2)}, u32[]{:S(2)}) collective-permute-start(bf16[256,768]{1,0:T(8,128)(2,1)S(1)} %get-tuple-element.57), channel_id=1, source_target_pairs={{0,1},{1,2},{3,0},{4,5},{5,6},{7,4},{8,9},{9,10},{11,8},{12,13},{1... | collective-permute-start | bytes 1179656 | tf_op jit(solution)/shard_map/ppermute | solution.py:216
  134.9 4.2 %collective-permute-start.10 = (bf16[256,768]{1,0:T(8,128)(2,1)S(1)}, bf16[256,768]{1,0:T(8,128)(2,1)S(1)}, u32[]{:S(2)}, u32[]{:S(2)}) collective-permute-start(bf16[256,768]{1,0:T(8,128)(2,1)S(1)} %get-tuple-element.59), channel_id=1, source_target_pairs={{1,0},{2,1},{3,2},{5,4},{6,5},{7,6},{9,8},{10,9},{11,10},{13,12},{... | collective-permute-start | bytes 1179656 | tf_op jit(solution)/shard_map/ppermute | solution.py:216
  142.2 25.2 %collective-permute-done.10 = bf16[256,768]{1,0:T(8,128)(2,1)S(1)} collective-permute-done((bf16[256,768]{1,0:T(8,128)(2,1)S(1)}, bf16[256,768]{1,0:T(8,128)(2,1)S(1)}, u32[]{:S(2)}, u32[]{:S(2)}) %collective-permute-start.10) | collective-permute-done | bytes 393248 | tf_op jit(solution)/shard_map/ppermute | solution.py:216
  167.4 1.9 %collective-permute-start.11 = (bf16[256,768]{1,0:T(8,128)(2,1)S(1)}, bf16[256,768]{1,0:T(8,128)(2,1)S(1)}, u32[]{:S(2)}, u32[]{:S(2)}) collective-permute-start(bf16[256,768]{1,0:T(8,128)(2,1)S(1)} %convert_element_type.126), channel_id=1, source_target_pairs={{4,16},{12,24},{16,4},{24,12},{5,17},{13,25},{17,5},{25,13},{6,18}... | collective-permute-start | bytes 1179656 | tf_op jit(solution)/shard_map/ppermute | solution.py:389
  169.8 6.7 %collective-permute-done.11 = bf16[256,768]{1,0:T(8,128)(2,1)S(1)} collective-permute-done((bf16[256,768]{1,0:T(8,128)(2,1)S(1)}, bf16[256,768]{1,0:T(8,128)(2,1)S(1)}, u32[]{:S(2)}, u32[]{:S(2)}) %collective-permute-start.11) | collective-permute-done | bytes 393248 | tf_op jit(solution)/shard_map/ppermute | solution.py:389
  (84 shorter events, 23.0 us)
Async XLA Ops:
  7.9 26.1 %all-to-all-start = ((bf16[8,144,768]{2,1,0:T(8,128)(2,1)}), bf16[8,144,768]{2,1,0:T(8,128)(2,1)S(1)}, u32[]{:S(2)}, u32[]{:S(2)}) async-start(bf16[8,144,768]{2,1,0:T(8,128)(2,1)} %get-tuple-element.29), calls=%async_computation | async-start | bytes 3538944 | tf_op jit(solution)/shard_map/all_to_all | solution.py:297
  12.5 7.4 %copy-start.7 = (bf16[16,128]{1,0:T(8,128)(2,1)S(1)}, bf16[16,128]{1,0:T(8,128)(2,1)}, u32[]{:S(2)}) copy-start(bf16[16,128]{1,0:T(8,128)(2,1)} %get-tuple-element.32) | copy-start | bytes 12292
  19.9 4.7 %collective-permute-start.2 = (bf16[16,128]{1,0:T(8,128)(2,1)S(1)}, bf16[16,128]{1,0:T(8,128)(2,1)S(1)}, u32[]{:S(2)}, u32[]{:S(2)}) collective-permute-start(bf16[16,128]{1,0:T(8,128)(2,1)S(1)} %copy-done.7), channel_id=1, source_target_pairs={{0,3},{1,0},{2,1},{3,2},{4,7},{5,4},{6,5},{7,6},{8,11},{9,8},{10,9... | collective-permute-start | bytes 12296 | tf_op jit(solution)/shard_map/ppermute | solution.py:291
  20.1 4.5 %collective-permute-start.1 = (bf16[16,128]{1,0:T(8,128)(2,1)S(1)}, bf16[16,128]{1,0:T(8,128)(2,1)S(1)}, u32[]{:S(2)}, u32[]{:S(2)}) collective-permute-start(bf16[16,128]{1,0:T(8,128)(2,1)S(1)} %copy-done.7), channel_id=1, source_target_pairs={{0,2},{1,3},{2,0},{3,1},{4,6},{5,7},{6,4},{7,5},{8,10},{9,11},{10,... | collective-permute-start | bytes 12296 | tf_op jit(solution)/shard_map/ppermute | solution.py:291
  22.4 2.9 %collective-permute-start = (bf16[16,128]{1,0:T(8,128)(2,1)S(1)}, bf16[16,128]{1,0:T(8,128)(2,1)S(1)}, u32[]{:S(2)}, u32[]{:S(2)}) collective-permute-start(bf16[16,128]{1,0:T(8,128)(2,1)S(1)} %copy-done.7), channel_id=1, source_target_pairs={{0,1},{1,2},{2,3},{3,0},{4,5},{5,6},{6,7},{7,4},{8,9},{9,10},{10,1... | collective-permute-start | bytes 12296 | tf_op jit(solution)/shard_map/ppermute | solution.py:291
  33.4 6.8 %copy-start = (s32[768,384]{1,0:T(8,128)S(1)}, s32[768,384]{1,0:T(8,128)}, u32[]{:S(2)}) copy-start(s32[768,384]{1,0:T(8,128)} %param.15) | copy-start | bytes 3538948
  34.1 25.3 %all-to-all-start.1 = ((bf16[8,128,768]{2,1,0:T(8,128)(2,1)}), bf16[8,128,768]{2,1,0:T(8,128)(2,1)}, u32[]{:S(2)}, u32[]{:S(2)}) async-start(bf16[8,128,768]{2,1,0:T(8,128)(2,1)} %spectrum.4), calls=%async_computation.1 | async-start | bytes 3145728 | tf_op jit(solution)/shard_map/all_to_all | solution.py:297
  59.4 60.4 %all-to-all-start.2 = ((bf16[8,144,768]{2,1,0:T(8,128)(2,1)}), bf16[8,144,768]{2,1,0:T(8,128)(2,1)}, u32[]{:S(2)}, u32[]{:S(2)}) async-start(bf16[8,144,768]{2,1,0:T(8,128)(2,1)} %spectrum.5), calls=%async_computation.2 | async-start | bytes 3538944 | tf_op jit(solution)/shard_map/all_to_all | solution.py:297
  68.1 10.7 %collective-permute-start.3 = (bf16[256,768]{1,0:T(8,128)(2,1)S(1)}, bf16[256,768]{1,0:T(8,128)(2,1)S(1)}, u32[]{:S(2)}, u32[]{:S(2)}) collective-permute-start(bf16[256,768]{1,0:T(8,128)(2,1)S(1)} %get-tuple-element.64), channel_id=1, source_target_pairs={{0,1},{1,2},{3,0},{7,6},{6,5},{4,7},{8,9},{9,10},{11,8},{15,14},{1... | collective-permute-start | bytes 1179656 | tf_op jit(solution)/shard_map/ppermute | solution.py:216
  69.4 20.7 %collective-permute-start.4 = (bf16[256,768]{1,0:T(8,128)(2,1)S(1)}, bf16[256,768]{1,0:T(8,128)(2,1)S(1)}, u32[]{:S(2)}, u32[]{:S(2)}) collective-permute-start(bf16[256,768]{1,0:T(8,128)(2,1)S(1)} %get-tuple-element.65), channel_id=1, source_target_pairs={{1,0},{2,1},{3,2},{6,7},{5,6},{4,5},{9,8},{10,9},{11,10},{14,15},{... | collective-permute-start | bytes 1179656 | tf_op jit(solution)/shard_map/ppermute | solution.py:216
  73.5 31.1 %collective-permute-start.5 = (bf16[256,768]{1,0:T(8,128)(2,1)}, bf16[256,768]{1,0:T(8,128)(2,1)}, u32[]{:S(2)}, u32[]{:S(2)}) collective-permute-start(bf16[256,768]{1,0:T(8,128)(2,1)} %get-tuple-element.63), channel_id=1, source_target_pairs={{0,2},{2,0},{3,1},{7,5},{5,7},{4,6},{8,10},{10,8},{11,9},{15,13},{... | collective-permute-start | bytes 1179656 | tf_op jit(solution)/shard_map/ppermute | solution.py:216
  90.1 2.9 %copy-start.2 = (bf16[256,768]{1,0:T(8,128)(2,1)}, bf16[256,768]{1,0:T(8,128)(2,1)S(1)}, u32[]{:S(2)}) copy-start(bf16[256,768]{1,0:T(8,128)(2,1)S(1)} %collective-permute-done.4) | copy-start | bytes 1179652
  93.1 10.6 %copy-start.6 = (f32[16]{0:T(128)S(1)}, f32[16]{0:T(128)}, u32[]{:S(2)}) copy-start(f32[16]{0:T(128)} %refs_3_.5) | copy-start | bytes 196
  94.3 25.5 %collective-permute-start.6 = (bf16[256,768]{1,0:T(8,128)(2,1)}, bf16[256,768]{1,0:T(8,128)(2,1)S(1)}, u32[]{:S(2)}, u32[]{:S(2)}) collective-permute-start(bf16[256,768]{1,0:T(8,128)(2,1)} %get-tuple-element.61), channel_id=1, source_target_pairs={{0,1},{1,2},{3,0},{7,6},{6,5},{4,7},{8,9},{9,10},{11,8},{15,14},{1... | collective-permute-start | bytes 1179656 | tf_op jit(solution)/shard_map/ppermute | solution.py:216
  95.6 24.2 %collective-permute-start.7 = (bf16[256,768]{1,0:T(8,128)(2,1)}, bf16[256,768]{1,0:T(8,128)(2,1)}, u32[]{:S(2)}, u32[]{:S(2)}) collective-permute-start(bf16[256,768]{1,0:T(8,128)(2,1)} %get-tuple-element.62), channel_id=1, source_target_pairs={{1,0},{2,1},{3,2},{6,7},{5,6},{4,5},{9,8},{10,9},{11,10},{14,15},{... | collective-permute-start | bytes 1179656 | tf_op jit(solution)/shard_map/ppermute | solution.py:216
  104.6 22.8 %collective-permute-start.9 = (bf16[256,768]{1,0:T(8,128)(2,1)}, bf16[256,768]{1,0:T(8,128)(2,1)}, u32[]{:S(2)}, u32[]{:S(2)}) collective-permute-start(bf16[256,768]{1,0:T(8,128)(2,1)} %get-tuple-element.60), channel_id=1, source_target_pairs={{0,2},{2,0},{3,1},{7,5},{5,7},{4,6},{8,10},{10,8},{11,9},{15,13},{... | collective-permute-start | bytes 1179656 | tf_op jit(solution)/shard_map/ppermute | solution.py:216
  124.2 3.2 %copy-start.3 = (bf16[256,768]{1,0:T(8,128)(2,1)S(1)}, bf16[256,768]{1,0:T(8,128)(2,1)}, u32[]{:S(2)}) copy-start(bf16[256,768]{1,0:T(8,128)(2,1)} %copy-done.2) | copy-start | bytes 1179652
  128.8 10.4 %copy-start.5 = (bf16[256,768]{1,0:T(8,128)(2,1)S(1)}, bf16[256,768]{1,0:T(8,128)(2,1)}, u32[]{:S(2)}) copy-start(bf16[256,768]{1,0:T(8,128)(2,1)} %copy-done.4) | copy-start | bytes 1179652
  128.8 40.6 %collective-permute-start.8 = (bf16[256,768]{1,0:T(8,128)(2,1)S(1)}, bf16[256,768]{1,0:T(8,128)(2,1)S(1)}, u32[]{:S(2)}, u32[]{:S(2)}) collective-permute-start(bf16[256,768]{1,0:T(8,128)(2,1)S(1)} %convert_element_type.114), channel_id=1, source_target_pairs={{4,16},{12,24},{16,4},{24,12},{5,17},{13,25},{17,5},{25,13},{6,18}... | collective-permute-start | bytes 1179656 | tf_op jit(solution)/shard_map/ppermute | solution.py:389
  131.7 37.7 %collective-permute-start.12 = (bf16[256,768]{1,0:T(8,128)(2,1)S(1)}, bf16[256,768]{1,0:T(8,128)(2,1)S(1)}, u32[]{:S(2)}, u32[]{:S(2)}) collective-permute-start(bf16[256,768]{1,0:T(8,128)(2,1)S(1)} %get-tuple-element.57), channel_id=1, source_target_pairs={{0,1},{1,2},{3,0},{4,5},{5,6},{7,4},{8,9},{9,10},{11,8},{12,13},{1... | collective-permute-start | bytes 1179656 | tf_op jit(solution)/shard_map/ppermute | solution.py:216
  133.7 35.8 %collective-permute-start.13 = (bf16[256,768]{1,0:T(8,128)(2,1)S(1)}, bf16[256,768]{1,0:T(8,128)(2,1)S(1)}, u32[]{:S(2)}, u32[]{:S(2)}) collective-permute-start(bf16[256,768]{1,0:T(8,128)(2,1)S(1)} %get-tuple-element.58), channel_id=1, source_target_pairs={{0,2},{2,0},{3,1},{4,6},{6,4},{7,5},{8,10},{10,8},{11,9},{12,14},{... | collective-permute-start | bytes 1179656 | tf_op jit(solution)/shard_map/ppermute | solution.py:216
  134.9 32.5 %collective-permute-start.10 = (bf16[256,768]{1,0:T(8,128)(2,1)S(1)}, bf16[256,768]{1,0:T(8,128)(2,1)S(1)}, u32[]{:S(2)}, u32[]{:S(2)}) collective-permute-start(bf16[256,768]{1,0:T(8,128)(2,1)S(1)} %get-tuple-element.59), channel_id=1, source_target_pairs={{1,0},{2,1},{3,2},{5,4},{6,5},{7,6},{9,8},{10,9},{11,10},{13,12},{... | collective-permute-start | bytes 1179656 | tf_op jit(solution)/shard_map/ppermute | solution.py:216
  167.4 9.1 %collective-permute-start.11 = (bf16[256,768]{1,0:T(8,128)(2,1)S(1)}, bf16[256,768]{1,0:T(8,128)(2,1)S(1)}, u32[]{:S(2)}, u32[]{:S(2)}) collective-permute-start(bf16[256,768]{1,0:T(8,128)(2,1)S(1)} %convert_element_type.126), channel_id=1, source_target_pairs={{4,16},{12,24},{16,4},{24,12},{5,17},{13,25},{17,5},{25,13},{6,18}... | collective-permute-start | bytes 1179656 | tf_op jit(solution)/shard_map/ppermute | solution.py:389
  169.8 6.8 %copy-start.1 = (bf16[48,16,768]{2,1,0:T(8,128)(2,1)S(1)}, bf16[48,16,768]{2,1,0:T(8,128)(2,1)}, u32[]{:S(2)}) copy-start(bf16[48,16,768]{2,1,0:T(8,128)(2,1)} %param.16) | copy-start | bytes 3538948
  (1 other events, 0.7 us)

commit v12 on v10

--- a/solution.py
+++ b/solution.py
@@ -243,7 +243,6 @@
 
     cosine, minus_sine, table_right = dft_tables(length)
     table_right = jnp.asarray(table_right.astype(jnp.bfloat16))
-    received = []
     weighted = []
     for c, each in enumerate(sizes):
         chunk_rows = batch_count * each
@@ -298,7 +297,14 @@
             digits = jnp.concatenate([layer[:, : 2 * fields] for layer in layers], axis=1)
             digits = jnp.pad(digits, ((0, 0), (0, 2 * length - digits.shape[1])))
         weighted.append(send)
-        received.append(lax.all_to_all(send, "batch", 0, 0, tiled=True))
+
+    def exchange(send, behind):
+        send, behind = lax.optimization_barrier((send, behind))
+        return lax.all_to_all(send, "batch", 0, 0, tiled=True), behind
+
+    first = lax.all_to_all(weighted[0], "batch", 0, 0, tiled=True)
+    second, first = exchange(weighted[1], first)
+    received = [first, second]
 
     def read_digits(rows_in):
         whole = rows_in.astype(jnp.int32).reshape(-1, 2 * fields)
@@ -307,8 +313,6 @@
     at = [particles * each for each in sizes]
     layer_digits = received[0][:, at[0] : at[0] + particles, : 2 * fields]
     meta_layer = read_digits(layer_digits)
-    all_digits = received[-1][:, at[-1] : at[-1] + particles, : slab_count * 2 * fields]
-    meta_all = read_digits(all_digits)
 
     class_count = dest_map.shape[0]
 
@@ -355,7 +359,9 @@
         if c == 0:
             codes_in, _ = lax.optimization_barrier((codes_in, weighted[1:]))
         if c > 0 and mirrored:
-            codes_in, arrived[c - 1][2] = lax.optimization_barrier((codes_in, arrived[c - 1][2]))
+            codes_in, arrived[c - 1][0], arrived[c - 1][2] = lax.optimization_barrier(
+                (codes_in, arrived[c - 1][0], arrived[c - 1][2])
+            )
         parts = pl.pallas_call(
             insert_kernel,
             out_shape=jax.ShapeDtypeStruct((window_slabs, bins, 2 * length), jnp.bfloat16),
@@ -371,10 +377,15 @@
         )(received[c], codes_in)
         if not mirrored:
             sums.append(lax.psum_scatter(parts, "slab", scatter_dimension=0, tiled=False))
+            if c + 2 < len(sizes):
+                received.append(lax.all_to_all(weighted[c + 2], "batch", 0, 0, tiled=True))
             continue
         for before in arrived:
             before[1], _ = lax.optimization_barrier((before[1], parts))
         arrived.append(slab_exchange(parts, places[c], slab_count, roles[c]))
+        if c + 2 < len(sizes):
+            third, arrived[c][2] = exchange(weighted[c + 2], arrived[c][2])
+            received.append(third)
         own = choose(parts, places[c]).astype(jnp.float32)
         sums.append(jnp.where(places[c] == slab_count - 1, 0.0, own))
     for c, each in enumerate(sizes):
@@ -385,11 +396,12 @@
         over = [(b, block) for b, block in enumerate(roles[c]) if b != block]
         if over:
             if c + 1 < len(sizes):
-                sums[c], arrived[c + 1][2] = lax.optimization_barrier(
-                    (sums[c], arrived[c + 1][2])
-                )
+                sums[c], arrived[-1][2] = lax.optimization_barrier((sums[c], arrived[-1][2]))
             handed = lax.ppermute(sums[c].astype(jnp.bfloat16), "batch", over)
             sums[c] = jnp.where(blocks[c] == batch, sums[c], handed.astype(jnp.float32))
+
+    all_digits = received[-1][:, at[-1] : at[-1] + particles, : slab_count * 2 * fields]
+    meta_all = read_digits(all_digits)
 
     own_freq = batch * rows + jnp.arange(rows, dtype=jnp.int32)
     own_plane = pick_block(find_planes(meta_all), batch) - slab * planes

time: 163 us -> 167 us (1.025)
  starting transfers between devices: 39.6 us -> 58.6 us
  waiting for transfers between devices: 78.7 us -> 62 us
  other arithmetic: 8.22 us -> 9.93 us
    ppermute x9, starting transfers between devices: 20.1 us -> 38.5 us  [slab_exchange(): arrived.append(lax.ppermute(block, ('batch', 'slab'), perm))]
    all_to_all x3, waiting for transfers between devices: 22.9 us -> 7.72 us  [the longest x2 7.72 us: exchange(): return (lax.all_to_all(send, 'batch', 0, 0, tiled=True), behind)]
    ppermute x9, waiting for transfers between devices: 53.3 us -> 49.9 us  [slab_exchange(): arrived.append(lax.ppermute(block, ('batch', 'slab'), perm))]
    ppermute x3, waiting for transfers between devices: 2.55 us -> 4.39 us  [per_device(): layers.append(lax.ppermute(own_digits, 'slab', ring))]
  transfers between devices with their start and end apart: 17 -> 17, of which waited for: 10 -> 10; matrix products, arithmetic and copies ran while one was open for 8% -> 8% of each run, Pallas kernels for 12% -> 13%
where the time goes in v12:
time: 167 us; the launch traced here: 166 us
  waiting for transfers between devices  62 us (37%)
  starting transfers between devices  58.6 us (35%)
  Pallas kernels  28.8 us (17%)
  other arithmetic  9.93 us (6%)
  matrix products  3.46 us (2%)
  local copies, waits for them, and re-layouts  2.75 us (2%)
    ppermute x9, waiting for transfers between devices, slab_exchange(): arrived.append(lax.ppermute(block, ('batch', 'slab'), perm))  49.9 us
    ppermute x9, starting transfers between devices, slab_exchange(): arrived.append(lax.ppermute(block, ('batch', 'slab'), perm))  38.5 us
    pallas_call x3, Pallas kernels, per_device(): pl.pallas_call(functools.partial(spectrum_kernel, runs, meta_from), out_s...  20.9 us
    all_to_all x2, starting transfers between devices, exchange(): return (lax.all_to_all(send, 'batch', 0, 0, tiled=True), behind)  8.93 us
    pallas_call x3, Pallas kernels, per_device(): pl.pallas_call(insert_kernel, out_shape=jax.ShapeDtypeStruct((window_slab...  7.8 us
    all_to_all x2, waiting for transfers between devices, exchange(): return (lax.all_to_all(send, 'batch', 0, 0, tiled=True), behind)  7.72 us
    all_to_all x1, starting transfers between devices, per_device(): first = lax.all_to_all(weighted[0], 'batch', 0, 0, tiled=True)  5.18 us
    ppermute x3, starting transfers between devices, per_device(): layers.append(lax.ppermute(own_digits, 'slab', ring))  4.67 us
  transfers between devices with their start and end apart: 17, of which 10 were waited for; matrix products, arithmetic and copies ran while one was open for 8% of the time, Pallas kernels for 13%

profile of v12, /device:TPU:0, one launch (start us, length us, event | category | flops | bytes accessed | tf_op | source)
XLA Modules:
  0.0 166.1 jit_solution(1952253226046573013)
XLA Ops:
  0.0 7.4 %spectrum.3 = (bf16[8,144,768]{2,1,0:T(8,128)(2,1)}, bf16[16,128]{1,0:T(8,128)(2,1)}) custom-call(s32[8]{0:T(128)} %refs_0_.5, s32[2,8]{1,0:T(2,128)} %bitcast.66, s32[8]{0:T(128)} %refs_2_.5, f32[16]{0:T(128)} %refs_3_.5, s32[4,8]{1,0:T(4,128)} %bitcast.63, bf16[8,384,384]{2,1,0:T(8,128)(2,1)} %refs_5_.5, bf16[256,384]{1,0:T(8,128)(2,1)} %constant.172.clone.refs_6_, ...), custom_call_target="tpu_custom_call" | custom-call | tf_op jit(solution)/shard_map/spectrum/pallas_call | solution.py:260
  7.4 5.2 %all-to-all-start = ((bf16[8,144,768]{2,1,0:T(8,128)(2,1)}), bf16[8,144,768]{2,1,0:T(8,128)(2,1)S(1)}, u32[]{:S(2)}, u32[]{:S(2)}) async-start(bf16[8,144,768]{2,1,0:T(8,128)(2,1)} %get-tuple-element.29), calls=%async_computation | async-start | bytes 3538944 | tf_op jit(solution)/shard_map/all_to_all | solution.py:305
  12.6 6.8 %spectrum.4 = bf16[8,128,768]{2,1,0:T(8,128)(2,1)} custom-call(s32[8]{0:T(128)} %refs_0_.5, s32[2,8]{1,0:T(2,128)} %bitcast.67, s32[8]{0:T(128)} %refs_2_.5, f32[16]{0:T(128)} %refs_3_.5, s32[4,8]{1,0:T(4,128)} %bitcast.64, bf16[8,384,384]{2,1,0:T(8,128)(2,1)} %refs_5_.5, bf16[256,384]{1,0:T(8,128)(2,1)} %constant.173.clone.refs_6_, ...), custom_call_target="tpu_custom_call" | custom-call | tf_op jit(solution)/shard_map/spectrum/pallas_call | solution.py:260
  19.4 3.7 %collective-permute-start.2 = (bf16[16,128]{1,0:T(8,128)(2,1)S(1)}, bf16[16,128]{1,0:T(8,128)(2,1)S(1)}, u32[]{:S(2)}, u32[]{:S(2)}) collective-permute-start(bf16[16,128]{1,0:T(8,128)(2,1)S(1)} %copy-done.7), channel_id=1, source_target_pairs={{0,3},{1,0},{2,1},{3,2},{4,7},{5,4},{6,5},{7,6},{8,11},{9,8},{10,9... | collective-permute-start | bytes 12296 | tf_op jit(solution)/shard_map/ppermute | solution.py:296
  24.4 3.2 %collective-permute-done.1 = bf16[16,128]{1,0:T(8,128)(2,1)S(1)} collective-permute-done((bf16[16,128]{1,0:T(8,128)(2,1)S(1)}, bf16[16,128]{1,0:T(8,128)(2,1)S(1)}, u32[]{:S(2)}, u32[]{:S(2)}) %collective-permute-start.1) | collective-permute-done | bytes 4128 | tf_op jit(solution)/shard_map/ppermute | solution.py:296
  29.2 6.8 %spectrum.5 = bf16[8,144,768]{2,1,0:T(8,128)(2,1)} custom-call(s32[8]{0:T(128)} %refs_0_.5, s32[2,8]{1,0:T(2,128)} %bitcast.68, s32[8]{0:T(128)} %refs_2_.5, f32[16]{0:T(128)} %refs_3_.5, s32[4,8]{1,0:T(4,128)} %bitcast.65, bf16[8,384,384]{2,1,0:T(8,128)(2,1)} %refs_5_.5, bf16[256,384]{1,0:T(8,128)(2,1)} %constant.174.clone.refs_6_, ...), custom_call_target="tpu_custom_call" | custom-call | tf_op jit(solution)/shard_map/spectrum/pallas_call | solution.py:260
  36.3 4.6 %all-to-all-start.1 = ((bf16[8,128,768]{2,1,0:T(8,128)(2,1)}), bf16[8,128,768]{2,1,0:T(8,128)(2,1)}, u32[]{:S(2)}, u32[]{:S(2)}) async-start(bf16[8,128,768]{2,1,0:T(8,128)(2,1)} %spectrum.4), calls=%async_computation.1 | async-start | bytes 3145728 | tf_op jit(solution)/shard_map/all_to_all | solution.py:303
  41.9 1.7 %insert.3 = bf16[3,256,768]{2,1,0:T(8,128)(2,1)S(1)} custom-call(bf16[8,144,768]{2,1,0:T(8,128)(2,1)S(1)} %all-to-all-done.received, s32[1,1152]{1,0:T(1,128)S(1)} %reshape.182.codes), custom_call_target="tpu_custom_call" | custom-call | tf_op jit(solution)/shard_map/insert/pallas_call | solution.py:365
  45.7 8.4 %collective-permute-done.4 = bf16[256,768]{1,0:T(8,128)(2,1)S(1)} collective-permute-done((bf16[256,768]{1,0:T(8,128)(2,1)S(1)}, bf16[256,768]{1,0:T(8,128)(2,1)S(1)}, u32[]{:S(2)}, u32[]{:S(2)}) %collective-permute-start.4) | collective-permute-done | bytes 393248 | tf_op jit(solution)/shard_map/ppermute | solution.py:217
  54.1 7.7 %all-to-all-done.1.received = bf16[8,128,768]{2,1,0:T(8,128)(2,1)} async-done(((bf16[8,128,768]{2,1,0:T(8,128)(2,1)}), bf16[8,128,768]{2,1,0:T(8,128)(2,1)}, u32[]{:S(2)}, u32[]{:S(2)}) %all-to-all-start.1) | async-done | bytes 1572896 | tf_op jit(solution)/shard_map/all_to_all | solution.py:303
  61.8 4.3 %all-to-all-start.2 = ((bf16[8,144,768]{2,1,0:T(8,128)(2,1)}), bf16[8,144,768]{2,1,0:T(8,128)(2,1)}, u32[]{:S(2)}, u32[]{:S(2)}) async-start(bf16[8,144,768]{2,1,0:T(8,128)(2,1)} %spectrum.5), calls=%async_computation.2 | async-start | bytes 3538944 | tf_op jit(solution)/shard_map/all_to_all | solution.py:303
  66.1 3.2 %collective-permute-start.3 = (bf16[256,768]{1,0:T(8,128)(2,1)S(1)}, bf16[256,768]{1,0:T(8,128)(2,1)S(1)}, u32[]{:S(2)}, u32[]{:S(2)}) collective-permute-start(bf16[256,768]{1,0:T(8,128)(2,1)S(1)} %get-tuple-element.61), channel_id=1, source_target_pairs={{0,1},{1,2},{3,0},{7,6},{6,5},{4,7},{8,9},{9,10},{11,8},{15,14},{1... | collective-permute-start | bytes 1179656 | tf_op jit(solution)/shard_map/ppermute | solution.py:217
  69.5 2.3 %collective-permute-start.5 = (bf16[256,768]{1,0:T(8,128)(2,1)}, bf16[256,768]{1,0:T(8,128)(2,1)}, u32[]{:S(2)}, u32[]{:S(2)}) collective-permute-start(bf16[256,768]{1,0:T(8,128)(2,1)} %get-tuple-element.60), channel_id=1, source_target_pairs={{0,2},{2,0},{3,1},{7,5},{5,7},{4,6},{8,10},{10,8},{11,9},{15,13},{... | collective-permute-start | bytes 1179656 | tf_op jit(solution)/shard_map/ppermute | solution.py:217
  71.8 10.0 %collective-permute-done.3 = bf16[256,768]{1,0:T(8,128)(2,1)S(1)} collective-permute-done((bf16[256,768]{1,0:T(8,128)(2,1)S(1)}, bf16[256,768]{1,0:T(8,128)(2,1)S(1)}, u32[]{:S(2)}, u32[]{:S(2)}) %collective-permute-start.3) | collective-permute-done | bytes 393248 | tf_op jit(solution)/shard_map/ppermute | solution.py:217
  81.8 2.9 %insert.4 = bf16[3,256,768]{2,1,0:T(8,128)(2,1)S(1)} custom-call(bf16[8,128,768]{2,1,0:T(8,128)(2,1)} %all-to-all-done.1.received, s32[1,1024]{1,0:T(1,128)S(1)} %reshape_reshape.3.codes), custom_call_target="tpu_custom_call" | custom-call | tf_op jit(solution)/shard_map/insert/pallas_call | solution.py:365
  85.9 11.1 %collective-permute-start.6 = (bf16[256,768]{1,0:T(8,128)(2,1)}, bf16[256,768]{1,0:T(8,128)(2,1)S(1)}, u32[]{:S(2)}, u32[]{:S(2)}) collective-permute-start(bf16[256,768]{1,0:T(8,128)(2,1)} %get-tuple-element.64), channel_id=1, source_target_pairs={{0,1},{1,2},{3,0},{7,6},{6,5},{4,7},{8,9},{9,10},{11,8},{15,14},{1... | collective-permute-start | bytes 1179656 | tf_op jit(solution)/shard_map/ppermute | solution.py:217
  99.0 6.5 %collective-permute-start.10 = (bf16[256,768]{1,0:T(8,128)(2,1)}, bf16[256,768]{1,0:T(8,128)(2,1)}, u32[]{:S(2)}, u32[]{:S(2)}) collective-permute-start(bf16[256,768]{1,0:T(8,128)(2,1)} %get-tuple-element.63), channel_id=1, source_target_pairs={{0,2},{2,0},{3,1},{7,5},{5,7},{4,6},{8,10},{10,8},{11,9},{15,13},{... | collective-permute-start | bytes 1179656 | tf_op jit(solution)/shard_map/ppermute | solution.py:217
  109.1 1.7 %fusion.2 = s32[256,384]{1,0:T(8,128)S(1)} fusion(s32[256]{0:T(256)S(1)} %get-tuple-element.50, s32[256,384]{1,0:T(8,128)S(1)} %convert_reduce_fusion, s32[768,384]{1,0:T(8,128)} %param.18), kind=kOutput, calls=%fused_computation.4 | convolution fusion | flops 151781376 | bytes 1967104 | tf_op jit(solution)/shard_map/dot_general | solution.py:323
  111.1 3.2 %insert.5 = bf16[3,256,768]{2,1,0:T(8,128)(2,1)S(1)} custom-call(bf16[8,144,768]{2,1,0:T(8,128)(2,1)} %all-to-all-done.2.received, s32[1,1152]{1,0:T(1,128)S(1)} %reshape.184.codes), custom_call_target="tpu_custom_call" | custom-call | tf_op jit(solution)/shard_map/insert/pallas_call | solution.py:365
  115.7 5.8 %collective-permute-done.10 = bf16[256,768]{1,0:T(8,128)(2,1)} collective-permute-done((bf16[256,768]{1,0:T(8,128)(2,1)}, bf16[256,768]{1,0:T(8,128)(2,1)}, u32[]{:S(2)}, u32[]{:S(2)}) %collective-permute-start.10) | collective-permute-done | bytes 393248 | tf_op jit(solution)/shard_map/ppermute | solution.py:217
  121.5 9.5 %collective-permute-start.13 = (bf16[256,768]{1,0:T(8,128)(2,1)S(1)}, bf16[256,768]{1,0:T(8,128)(2,1)S(1)}, u32[]{:S(2)}, u32[]{:S(2)}) collective-permute-start(bf16[256,768]{1,0:T(8,128)(2,1)S(1)} %get-tuple-element.58), channel_id=1, source_target_pairs={{0,2},{2,0},{3,1},{4,6},{6,4},{7,5},{8,10},{10,8},{11,9},{12,14},{... | collective-permute-start | bytes 1179656 | tf_op jit(solution)/shard_map/ppermute | solution.py:217
  131.0 2.1 %collective-permute-start.12 = (bf16[256,768]{1,0:T(8,128)(2,1)S(1)}, bf16[256,768]{1,0:T(8,128)(2,1)S(1)}, u32[]{:S(2)}, u32[]{:S(2)}) collective-permute-start(bf16[256,768]{1,0:T(8,128)(2,1)S(1)} %get-tuple-element.57), channel_id=1, source_target_pairs={{0,1},{1,2},{3,0},{4,5},{5,6},{7,4},{8,9},{9,10},{11,8},{12,13},{1... | collective-permute-start | bytes 1179656 | tf_op jit(solution)/shard_map/ppermute | solution.py:217
  134.4 1.4 fusion.10
  139.0 23.8 %collective-permute-done.13 = bf16[256,768]{1,0:T(8,128)(2,1)S(1)} collective-permute-done((bf16[256,768]{1,0:T(8,128)(2,1)S(1)}, bf16[256,768]{1,0:T(8,128)(2,1)S(1)}, u32[]{:S(2)}, u32[]{:S(2)}) %collective-permute-start.13) | collective-permute-done | bytes 393248 | tf_op jit(solution)/shard_map/ppermute | solution.py:217
  (84 shorter events, 22.4 us)
Async XLA Ops:
  7.4 28.5 %all-to-all-start = ((bf16[8,144,768]{2,1,0:T(8,128)(2,1)}), bf16[8,144,768]{2,1,0:T(8,128)(2,1)S(1)}, u32[]{:S(2)}, u32[]{:S(2)}) async-start(bf16[8,144,768]{2,1,0:T(8,128)(2,1)} %get-tuple-element.29), calls=%async_computation | async-start | bytes 3538944 | tf_op jit(solution)/shard_map/all_to_all | solution.py:305
  12.6 6.8 %copy-start.7 = (bf16[16,128]{1,0:T(8,128)(2,1)S(1)}, bf16[16,128]{1,0:T(8,128)(2,1)}, u32[]{:S(2)}) copy-start(bf16[16,128]{1,0:T(8,128)(2,1)} %get-tuple-element.31) | copy-start | bytes 12292
  19.4 5.0 %collective-permute-start.2 = (bf16[16,128]{1,0:T(8,128)(2,1)S(1)}, bf16[16,128]{1,0:T(8,128)(2,1)S(1)}, u32[]{:S(2)}, u32[]{:S(2)}) collective-permute-start(bf16[16,128]{1,0:T(8,128)(2,1)S(1)} %copy-done.7), channel_id=1, source_target_pairs={{0,3},{1,0},{2,1},{3,2},{4,7},{5,4},{6,5},{7,6},{8,11},{9,8},{10,9... | collective-permute-start | bytes 12296 | tf_op jit(solution)/shard_map/ppermute | solution.py:296
  23.1 4.5 %collective-permute-start.1 = (bf16[16,128]{1,0:T(8,128)(2,1)S(1)}, bf16[16,128]{1,0:T(8,128)(2,1)S(1)}, u32[]{:S(2)}, u32[]{:S(2)}) collective-permute-start(bf16[16,128]{1,0:T(8,128)(2,1)S(1)} %copy-done.7), channel_id=1, source_target_pairs={{0,2},{1,3},{2,0},{3,1},{4,6},{5,7},{6,4},{7,5},{8,10},{9,11},{10,... | collective-permute-start | bytes 12296 | tf_op jit(solution)/shard_map/ppermute | solution.py:296
  23.1 5.4 %collective-permute-start = (bf16[16,128]{1,0:T(8,128)(2,1)S(1)}, bf16[16,128]{1,0:T(8,128)(2,1)S(1)}, u32[]{:S(2)}, u32[]{:S(2)}) collective-permute-start(bf16[16,128]{1,0:T(8,128)(2,1)S(1)} %copy-done.7), channel_id=1, source_target_pairs={{0,1},{1,2},{2,3},{3,0},{4,5},{5,6},{6,7},{7,4},{8,9},{9,10},{10,1... | collective-permute-start | bytes 12296 | tf_op jit(solution)/shard_map/ppermute | solution.py:296
  36.3 4.6 %copy-start = (s32[768,384]{1,0:T(8,128)S(1)}, s32[768,384]{1,0:T(8,128)}, u32[]{:S(2)}) copy-start(s32[768,384]{1,0:T(8,128)} %param.18) | copy-start | bytes 3538948
  36.3 25.5 %all-to-all-start.1 = ((bf16[8,128,768]{2,1,0:T(8,128)(2,1)}), bf16[8,128,768]{2,1,0:T(8,128)(2,1)}, u32[]{:S(2)}, u32[]{:S(2)}) async-start(bf16[8,128,768]{2,1,0:T(8,128)(2,1)} %spectrum.4), calls=%async_computation.1 | async-start | bytes 3145728 | tf_op jit(solution)/shard_map/all_to_all | solution.py:303
  44.4 9.7 %collective-permute-start.4 = (bf16[256,768]{1,0:T(8,128)(2,1)S(1)}, bf16[256,768]{1,0:T(8,128)(2,1)S(1)}, u32[]{:S(2)}, u32[]{:S(2)}) collective-permute-start(bf16[256,768]{1,0:T(8,128)(2,1)S(1)} %get-tuple-element.62), channel_id=1, source_target_pairs={{1,0},{2,1},{3,2},{6,7},{5,6},{4,5},{9,8},{10,9},{11,10},{14,15},{... | collective-permute-start | bytes 1179656 | tf_op jit(solution)/shard_map/ppermute | solution.py:217
  61.8 45.6 %all-to-all-start.2 = ((bf16[8,144,768]{2,1,0:T(8,128)(2,1)}), bf16[8,144,768]{2,1,0:T(8,128)(2,1)}, u32[]{:S(2)}, u32[]{:S(2)}) async-start(bf16[8,144,768]{2,1,0:T(8,128)(2,1)} %spectrum.5), calls=%async_computation.2 | async-start | bytes 3538944 | tf_op jit(solution)/shard_map/all_to_all | solution.py:303
  66.1 15.6 %collective-permute-start.3 = (bf16[256,768]{1,0:T(8,128)(2,1)S(1)}, bf16[256,768]{1,0:T(8,128)(2,1)S(1)}, u32[]{:S(2)}, u32[]{:S(2)}) collective-permute-start(bf16[256,768]{1,0:T(8,128)(2,1)S(1)} %get-tuple-element.61), channel_id=1, source_target_pairs={{0,1},{1,2},{3,0},{7,6},{6,5},{4,7},{8,9},{9,10},{11,8},{15,14},{1... | collective-permute-start | bytes 1179656 | tf_op jit(solution)/shard_map/ppermute | solution.py:217
  69.5 29.5 %collective-permute-start.5 = (bf16[256,768]{1,0:T(8,128)(2,1)}, bf16[256,768]{1,0:T(8,128)(2,1)}, u32[]{:S(2)}, u32[]{:S(2)}) collective-permute-start(bf16[256,768]{1,0:T(8,128)(2,1)} %get-tuple-element.60), channel_id=1, source_target_pairs={{0,2},{2,0},{3,1},{7,5},{5,7},{4,6},{8,10},{10,8},{11,9},{15,13},{... | collective-permute-start | bytes 1179656 | tf_op jit(solution)/shard_map/ppermute | solution.py:217
  81.8 2.9 %copy-start.2 = (bf16[256,768]{1,0:T(8,128)(2,1)}, bf16[256,768]{1,0:T(8,128)(2,1)S(1)}, u32[]{:S(2)}) copy-start(bf16[256,768]{1,0:T(8,128)(2,1)S(1)} %collective-permute-done.3) | copy-start | bytes 1179652
  84.7 13.6 %copy-start.6 = (f32[16]{0:T(128)S(1)}, f32[16]{0:T(128)}, u32[]{:S(2)}) copy-start(f32[16]{0:T(128)} %refs_3_.5) | copy-start | bytes 196
  85.9 20.9 %collective-permute-start.6 = (bf16[256,768]{1,0:T(8,128)(2,1)}, bf16[256,768]{1,0:T(8,128)(2,1)S(1)}, u32[]{:S(2)}, u32[]{:S(2)}) collective-permute-start(bf16[256,768]{1,0:T(8,128)(2,1)} %get-tuple-element.64), channel_id=1, source_target_pairs={{0,1},{1,2},{3,0},{7,6},{6,5},{4,7},{8,9},{9,10},{11,8},{15,14},{1... | collective-permute-start | bytes 1179656 | tf_op jit(solution)/shard_map/ppermute | solution.py:217
  97.0 10.5 %collective-permute-start.7 = (bf16[256,768]{1,0:T(8,128)(2,1)}, bf16[256,768]{1,0:T(8,128)(2,1)}, u32[]{:S(2)}, u32[]{:S(2)}) collective-permute-start(bf16[256,768]{1,0:T(8,128)(2,1)} %get-tuple-element.65), channel_id=1, source_target_pairs={{1,0},{2,1},{3,2},{6,7},{5,6},{4,5},{9,8},{10,9},{11,10},{14,15},{... | collective-permute-start | bytes 1179656 | tf_op jit(solution)/shard_map/ppermute | solution.py:217
  99.0 22.5 %collective-permute-start.10 = (bf16[256,768]{1,0:T(8,128)(2,1)}, bf16[256,768]{1,0:T(8,128)(2,1)}, u32[]{:S(2)}, u32[]{:S(2)}) collective-permute-start(bf16[256,768]{1,0:T(8,128)(2,1)} %get-tuple-element.63), channel_id=1, source_target_pairs={{0,2},{2,0},{3,1},{7,5},{5,7},{4,6},{8,10},{10,8},{11,9},{15,13},{... | collective-permute-start | bytes 1179656 | tf_op jit(solution)/shard_map/ppermute | solution.py:217
  114.3 18.8 %copy-start.3 = (bf16[256,768]{1,0:T(8,128)(2,1)S(1)}, bf16[256,768]{1,0:T(8,128)(2,1)}, u32[]{:S(2)}) copy-start(bf16[256,768]{1,0:T(8,128)(2,1)} %copy-done.2) | copy-start | bytes 1179652
  114.4 22.9 %collective-permute-start.8 = (bf16[256,768]{1,0:T(8,128)(2,1)S(1)}, bf16[256,768]{1,0:T(8,128)(2,1)S(1)}, u32[]{:S(2)}, u32[]{:S(2)}) collective-permute-start(bf16[256,768]{1,0:T(8,128)(2,1)S(1)} %get-tuple-element.59), channel_id=1, source_target_pairs={{1,0},{2,1},{3,2},{5,4},{6,5},{7,6},{9,8},{10,9},{11,10},{13,12},{... | collective-permute-start | bytes 1179656 | tf_op jit(solution)/shard_map/ppermute | solution.py:217
  121.5 41.2 %collective-permute-start.13 = (bf16[256,768]{1,0:T(8,128)(2,1)S(1)}, bf16[256,768]{1,0:T(8,128)(2,1)S(1)}, u32[]{:S(2)}, u32[]{:S(2)}) collective-permute-start(bf16[256,768]{1,0:T(8,128)(2,1)S(1)} %get-tuple-element.58), channel_id=1, source_target_pairs={{0,2},{2,0},{3,1},{4,6},{6,4},{7,5},{8,10},{10,8},{11,9},{12,14},{... | collective-permute-start | bytes 1179656 | tf_op jit(solution)/shard_map/ppermute | solution.py:217
  131.0 3.4 %copy-start.5 = (bf16[256,768]{1,0:T(8,128)(2,1)S(1)}, bf16[256,768]{1,0:T(8,128)(2,1)}, u32[]{:S(2)}) copy-start(bf16[256,768]{1,0:T(8,128)(2,1)} %copy-done.4) | copy-start | bytes 1179652
  131.0 31.7 %collective-permute-start.12 = (bf16[256,768]{1,0:T(8,128)(2,1)S(1)}, bf16[256,768]{1,0:T(8,128)(2,1)S(1)}, u32[]{:S(2)}, u32[]{:S(2)}) collective-permute-start(bf16[256,768]{1,0:T(8,128)(2,1)S(1)} %get-tuple-element.57), channel_id=1, source_target_pairs={{0,1},{1,2},{3,0},{4,5},{5,6},{7,4},{8,9},{9,10},{11,8},{12,13},{1... | collective-permute-start | bytes 1179656 | tf_op jit(solution)/shard_map/ppermute | solution.py:217
  137.4 25.7 %collective-permute-start.9 = (bf16[256,768]{1,0:T(8,128)(2,1)S(1)}, bf16[256,768]{1,0:T(8,128)(2,1)S(1)}, u32[]{:S(2)}, u32[]{:S(2)}) collective-permute-start(bf16[256,768]{1,0:T(8,128)(2,1)S(1)} %convert_element_type.114), channel_id=1, source_target_pairs={{4,16},{12,24},{16,4},{24,12},{5,17},{13,25},{17,5},{25,13},{6,18}... | collective-permute-start | bytes 1179656 | tf_op jit(solution)/shard_map/ppermute | solution.py:400
  138.3 24.9 %collective-permute-start.11 = (bf16[256,768]{1,0:T(8,128)(2,1)S(1)}, bf16[256,768]{1,0:T(8,128)(2,1)S(1)}, u32[]{:S(2)}, u32[]{:S(2)}) collective-permute-start(bf16[256,768]{1,0:T(8,128)(2,1)S(1)} %convert_element_type.126), channel_id=1, source_target_pairs={{4,16},{12,24},{16,4},{24,12},{5,17},{13,25},{17,5},{25,13},{6,18}... | collective-permute-start | bytes 1179656 | tf_op jit(solution)/shard_map/ppermute | solution.py:400
  163.2 1.3 copy-start.1
  (1 other events, 0.7 us)

commit v13 on v9

--- a/solution.py
+++ b/solution.py
@@ -357,9 +357,7 @@
         if c == 0:
             codes_in, _ = lax.optimization_barrier((codes_in, weighted[1:]))
         if c > 0 and mirrored:
-            codes_in, arrived[c - 1][0], arrived[c - 1][2] = lax.optimization_barrier(
-                (codes_in, arrived[c - 1][0], arrived[c - 1][2])
-            )
+            codes_in, arrived[c - 1][2] = lax.optimization_barrier((codes_in, arrived[c - 1][2]))
         parts = pl.pallas_call(
             functools.partial(insert_kernel, bins, meta_at),
             out_shape=jax.ShapeDtypeStruct(

time: 155 us -> 157 us (1.013)
  starting transfers between devices: 45.6 us -> 54.7 us
  waiting for transfers between devices: 62 us -> 53.9 us
    ppermute x9, waiting for transfers between devices: 52.3 us -> 41.1 us  [slab_exchange(): arrived.append(lax.ppermute(block, ('batch', 'slab'), perm))]
    ppermute x9, starting transfers between devices: 30.8 us -> 39.9 us  [slab_exchange(): arrived.append(lax.ppermute(block, ('batch', 'slab'), perm))]
    all_to_all x3, waiting for transfers between devices: 9.7 us -> 12.9 us  [per_device(): received.append(lax.all_to_all(send, 'batch', 0, 0, tiled=True))]
  transfers between devices with their start and end apart: 13 -> 13, of which waited for: 9 -> 6; matrix products, arithmetic and copies ran while one was open for 10% -> 10% of each run, Pallas kernels for 13% -> 13%
where the time goes in v13:
time: 157 us; the launch traced here: 156 us
  starting transfers between devices  54.7 us (35%)
  waiting for transfers between devices  53.9 us (34%)
  Pallas kernels  27.5 us (18%)
  other arithmetic  12.4 us (8%)
  local copies, waits for them, and re-layouts  5.1 us (3%)
  matrix products  2.19 us (1%)
    ppermute x9, waiting for transfers between devices, slab_exchange(): arrived.append(lax.ppermute(block, ('batch', 'slab'), perm))  41.1 us
    ppermute x9, starting transfers between devices, slab_exchange(): arrived.append(lax.ppermute(block, ('batch', 'slab'), perm))  39.9 us
    pallas_call x3, Pallas kernels, per_device(): pl.pallas_call(functools.partial(spectrum_kernel, runs, with_meta), out_s...  20.2 us
    all_to_all x3, starting transfers between devices, per_device(): received.append(lax.all_to_all(send, 'batch', 0, 0, tiled=True))  14 us
    all_to_all x3, waiting for transfers between devices, per_device(): received.append(lax.all_to_all(send, 'batch', 0, 0, tiled=True))  12.9 us
    pallas_call x3, Pallas kernels, per_device(): pl.pallas_call(functools.partial(insert_kernel, bins, meta_at), out_shape...  7.31 us
    select_n x3, other arithmetic, choose(): chosen = jnp.where(index == d, parts[d], chosen)  4.67 us
    add x3, other arithmetic, per_device(): sums[c] = sums[c] + block[:each * planes].astype(jnp.float32)  4.4 us
  transfers between devices with their start and end apart: 13, of which 6 were waited for; matrix products, arithmetic and copies ran while one was open for 10% of the time, Pallas kernels for 13%

profile of v13, /device:TPU:0, one launch (start us, length us, event | category | flops | bytes accessed | tf_op | source)
XLA Modules:
  0.0 156.3 jit_solution(11765802532714258740)
XLA Ops:
  0.0 6.8 %spectrum.3 = bf16[8,144,768]{2,1,0:T(8,128)(2,1)} custom-call(s32[8]{0:T(128)} %classes.5, s32[2,8]{1,0:T(2,128)} %bitcast.90, s32[8]{0:T(128)} %defocus_class.5, f32[16]{0:T(128)} %defocus.5, s32[4,8]{1,0:T(4,128)} %bitcast.87, bf16[8,384,384]{2,1,0:T(8,128)(2,1)} %images_in.5, bf16[256,384]{1,0:T(8,128)(2,1)} %constant.169.clone.left_in, ...), custom_call_target="tpu_custom_call" | custom-call | tf_op jit(solution)/shard_map/spectrum/pallas_call | solution.py:277
  6.8 5.2 %all-to-all-start = ((bf16[8,144,768]{2,1,0:T(8,128)(2,1)}), bf16[8,144,768]{2,1,0:T(8,128)(2,1)S(1)}, u32[]{:S(2)}, u32[]{:S(2)}) async-start(bf16[8,144,768]{2,1,0:T(8,128)(2,1)} %spectrum.3), calls=%async_computation | async-start | bytes 3538944 | tf_op jit(solution)/shard_map/all_to_all | solution.py:305
  12.0 6.7 %spectrum.4 = bf16[8,128,768]{2,1,0:T(8,128)(2,1)} custom-call(s32[8]{0:T(128)} %classes.5, s32[2,8]{1,0:T(2,128)} %bitcast.91, s32[8]{0:T(128)} %defocus_class.5, f32[16]{0:T(128)} %defocus.5, s32[4,8]{1,0:T(4,128)} %bitcast.88, bf16[8,384,384]{2,1,0:T(8,128)(2,1)} %images_in.5, bf16[256,384]{1,0:T(8,128)(2,1)} %constant.170.clone.left_in, ...), custom_call_target="tpu_custom_call" | custom-call | tf_op jit(solution)/shard_map/spectrum/pallas_call | solution.py:277
  18.7 6.7 %spectrum.5 = bf16[8,128,768]{2,1,0:T(8,128)(2,1)} custom-call(s32[8]{0:T(128)} %classes.5, s32[2,8]{1,0:T(2,128)} %bitcast.92, s32[8]{0:T(128)} %defocus_class.5, f32[16]{0:T(128)} %defocus.5, s32[4,8]{1,0:T(4,128)} %bitcast.89, bf16[8,384,384]{2,1,0:T(8,128)(2,1)} %images_in.5, bf16[256,384]{1,0:T(8,128)(2,1)} %constant.171.clone.left_in, ...), custom_call_target="tpu_custom_call" | custom-call | tf_op jit(solution)/shard_map/spectrum/pallas_call | solution.py:277
  25.5 9.7 %all-to-all-done.received = bf16[8,144,768]{2,1,0:T(8,128)(2,1)S(1)} async-done(((bf16[8,144,768]{2,1,0:T(8,128)(2,1)}), bf16[8,144,768]{2,1,0:T(8,128)(2,1)S(1)}, u32[]{:S(2)}, u32[]{:S(2)}) %all-to-all-start) | async-done | bytes 1769504 | tf_op jit(solution)/shard_map/all_to_all | solution.py:305
  35.1 4.5 %all-to-all-start.1 = ((bf16[8,128,768]{2,1,0:T(8,128)(2,1)}), bf16[8,128,768]{2,1,0:T(8,128)(2,1)}, u32[]{:S(2)}, u32[]{:S(2)}) async-start(bf16[8,128,768]{2,1,0:T(8,128)(2,1)} %spectrum.4), calls=%async_computation.1 | async-start | bytes 3145728 | tf_op jit(solution)/shard_map/all_to_all | solution.py:305
  40.9 1.7 %insert.3 = bf16[3,272,768]{2,1,0:T(8,128)(2,1)S(1)} custom-call(bf16[8,144,768]{2,1,0:T(8,128)(2,1)S(1)} %all-to-all-done.received, s32[1,1152]{1,0:T(1,128)S(1)} %reshape.197.codes), custom_call_target="tpu_custom_call" | custom-call | tf_op jit(solution)/shard_map/insert/pallas_call | solution.py:361
  45.9 5.6 %collective-permute-start.1 = (bf16[272,768]{1,0:T(8,128)(2,1)}, bf16[272,768]{1,0:T(8,128)(2,1)S(1)}, u32[]{:S(2)}, u32[]{:S(2)}) collective-permute-start(bf16[272,768]{1,0:T(8,128)(2,1)} %get-tuple-element.27), channel_id=1, source_target_pairs={{0,2},{2,0},{3,1},{4,6},{6,4},{7,5},{8,10},{10,8},{11,9},{12,14},{... | collective-permute-start | bytes 1253384 | tf_op jit(solution)/shard_map/ppermute | solution.py:234
  51.5 1.9 %collective-permute-start = (bf16[272,768]{1,0:T(8,128)(2,1)}, bf16[272,768]{1,0:T(8,128)(2,1)}, u32[]{:S(2)}, u32[]{:S(2)}) collective-permute-start(bf16[272,768]{1,0:T(8,128)(2,1)} %get-tuple-element.25), channel_id=1, source_target_pairs={{0,1},{1,2},{3,0},{4,5},{5,6},{7,4},{8,9},{9,10},{11,8},{12,13},{1... | collective-permute-start | bytes 1253384 | tf_op jit(solution)/shard_map/ppermute | solution.py:234
  53.8 3.5 %collective-permute-done.2 = bf16[272,768]{1,0:T(8,128)(2,1)S(1)} collective-permute-done((bf16[272,768]{1,0:T(8,128)(2,1)S(1)}, bf16[272,768]{1,0:T(8,128)(2,1)S(1)}, u32[]{:S(2)}, u32[]{:S(2)}) %collective-permute-start.2) | collective-permute-done | bytes 417824 | tf_op jit(solution)/shard_map/ppermute | solution.py:234
  57.3 3.2 %all-to-all-done.1.received = bf16[8,128,768]{2,1,0:T(8,128)(2,1)} async-done(((bf16[8,128,768]{2,1,0:T(8,128)(2,1)}), bf16[8,128,768]{2,1,0:T(8,128)(2,1)}, u32[]{:S(2)}, u32[]{:S(2)}) %all-to-all-start.1) | async-done | bytes 1572896 | tf_op jit(solution)/shard_map/all_to_all | solution.py:305
  60.5 4.3 %all-to-all-start.2 = ((bf16[8,128,768]{2,1,0:T(8,128)(2,1)}), bf16[8,128,768]{2,1,0:T(8,128)(2,1)}, u32[]{:S(2)}, u32[]{:S(2)}) async-start(bf16[8,128,768]{2,1,0:T(8,128)(2,1)} %spectrum.5), calls=%async_computation.2 | async-start | bytes 3145728 | tf_op jit(solution)/shard_map/all_to_all | solution.py:305
  64.8 2.8 %insert.4 = bf16[3,256,768]{2,1,0:T(8,128)(2,1)S(1)} custom-call(bf16[8,128,768]{2,1,0:T(8,128)(2,1)} %all-to-all-done.1.received, s32[1,1024]{1,0:T(1,128)S(1)} %reshape_reshape.6.codes), custom_call_target="tpu_custom_call" | custom-call | tf_op jit(solution)/shard_map/insert/pallas_call | solution.py:361
  70.0 20.2 %collective-permute-start.5 = (bf16[256,768]{1,0:T(8,128)(2,1)}, bf16[256,768]{1,0:T(8,128)(2,1)}, u32[]{:S(2)}, u32[]{:S(2)}) collective-permute-start(bf16[256,768]{1,0:T(8,128)(2,1)} %get-tuple-element.38), channel_id=1, source_target_pairs={{0,2},{2,0},{3,1},{7,5},{5,7},{4,6},{8,10},{10,8},{11,9},{15,13},{... | collective-permute-start | bytes 1179656 | tf_op jit(solution)/shard_map/ppermute | solution.py:234
  90.2 1.9 %collective-permute-start.4 = (bf16[256,768]{1,0:T(8,128)(2,1)}, bf16[256,768]{1,0:T(8,128)(2,1)}, u32[]{:S(2)}, u32[]{:S(2)}) collective-permute-start(bf16[256,768]{1,0:T(8,128)(2,1)} %get-tuple-element.37), channel_id=1, source_target_pairs={{0,1},{1,2},{3,0},{7,6},{6,5},{4,7},{8,9},{9,10},{11,8},{15,14},{1... | collective-permute-start | bytes 1179656 | tf_op jit(solution)/shard_map/ppermute | solution.py:234
  93.4 2.8 %insert.5 = bf16[3,256,768]{2,1,0:T(8,128)(2,1)S(1)} custom-call(bf16[8,128,768]{2,1,0:T(8,128)(2,1)} %all-to-all-done.2.received, s32[1,1024]{1,0:T(1,128)S(1)} %reshape_reshape.7.codes), custom_call_target="tpu_custom_call" | custom-call | tf_op jit(solution)/shard_map/insert/pallas_call | solution.py:361
  97.6 2.5 %select_bitcast_fusion.4 = (bf16[256,768]{1,0:T(8,128)(2,1)}, bf16[256,768]{1,0:T(8,128)(2,1)}, bf16[256,768]{1,0:T(8,128)(2,1)}) fusion(pred[]{:T(512)S(6)} %eq.270, pred[]{:T(512)S(6)} %eq.269, bf16[3,256,768]{2,1,0:T(8,128)(2,1)} %copy-done, pred[]{:T(512)S(6)} %eq.272, pred[]{:T(512)S(6)} %eq.271, pred[]{:T(512)S(6)} %eq.282, pred[]{:T(512)S(6)} %eq.281), kind=kLoop, calls=%fused_computation.38 | loop fusion | flops 1179648 | bytes 2359302 | tf_op jit(solution)/shard_map/jit(_where)/select_n | solution.py:241
  100.2 14.7 %collective-permute-done.5 = bf16[256,768]{1,0:T(8,128)(2,1)} collective-permute-done((bf16[256,768]{1,0:T(8,128)(2,1)}, bf16[256,768]{1,0:T(8,128)(2,1)}, u32[]{:S(2)}, u32[]{:S(2)}) %collective-permute-start.5) | collective-permute-done | bytes 393248 | tf_op jit(solution)/shard_map/ppermute | solution.py:234
  116.2 4.6 %collective-permute-start.8 = (bf16[256,768]{1,0:T(8,128)(2,1)}, bf16[256,768]{1,0:T(8,128)(2,1)}, u32[]{:S(2)}, u32[]{:S(2)}) collective-permute-start(bf16[256,768]{1,0:T(8,128)(2,1)} %get-tuple-element.34), channel_id=1, source_target_pairs={{0,1},{1,2},{3,0},{4,5},{5,6},{7,4},{8,9},{9,10},{11,8},{12,13},{1... | collective-permute-start | bytes 1179656 | tf_op jit(solution)/shard_map/ppermute | solution.py:234
  120.8 1.9 %collective-permute-start.9 = (bf16[256,768]{1,0:T(8,128)(2,1)}, bf16[256,768]{1,0:T(8,128)(2,1)}, u32[]{:S(2)}, u32[]{:S(2)}) collective-permute-start(bf16[256,768]{1,0:T(8,128)(2,1)} %get-tuple-element.35), channel_id=1, source_target_pairs={{0,2},{2,0},{3,1},{4,6},{6,4},{7,5},{8,10},{10,8},{11,9},{12,14},{... | collective-permute-start | bytes 1179656 | tf_op jit(solution)/shard_map/ppermute | solution.py:234
  125.0 1.5 fusion.10
  129.1 7.1 %collective-permute-done.8 = bf16[256,768]{1,0:T(8,128)(2,1)} collective-permute-done((bf16[256,768]{1,0:T(8,128)(2,1)}, bf16[256,768]{1,0:T(8,128)(2,1)}, u32[]{:S(2)}, u32[]{:S(2)}) %collective-permute-start.8) | collective-permute-done | bytes 393248 | tf_op jit(solution)/shard_map/ppermute | solution.py:234
  136.2 15.7 %collective-permute-done.9 = bf16[256,768]{1,0:T(8,128)(2,1)} collective-permute-done((bf16[256,768]{1,0:T(8,128)(2,1)}, bf16[256,768]{1,0:T(8,128)(2,1)}, u32[]{:S(2)}, u32[]{:S(2)}) %collective-permute-start.9) | collective-permute-done | bytes 393248 | tf_op jit(solution)/shard_map/ppermute | solution.py:234
  151.9 1.5 fusion.8
  (83 shorter events, 18.7 us)
Async XLA Ops:
  6.8 28.3 %all-to-all-start = ((bf16[8,144,768]{2,1,0:T(8,128)(2,1)}), bf16[8,144,768]{2,1,0:T(8,128)(2,1)S(1)}, u32[]{:S(2)}, u32[]{:S(2)}) async-start(bf16[8,144,768]{2,1,0:T(8,128)(2,1)} %spectrum.3), calls=%async_computation | async-start | bytes 3538944 | tf_op jit(solution)/shard_map/all_to_all | solution.py:305
  25.4 14.5 %copy-start.2 = (s32[768,384]{1,0:T(8,128)S(1)}, s32[768,384]{1,0:T(8,128)}, u32[]{:S(2)}) copy-start(s32[768,384]{1,0:T(8,128)} %param.18) | copy-start | bytes 3538948
  35.1 25.4 %all-to-all-start.1 = ((bf16[8,128,768]{2,1,0:T(8,128)(2,1)}), bf16[8,128,768]{2,1,0:T(8,128)(2,1)}, u32[]{:S(2)}, u32[]{:S(2)}) async-start(bf16[8,128,768]{2,1,0:T(8,128)(2,1)} %spectrum.4), calls=%async_computation.1 | async-start | bytes 3145728 | tf_op jit(solution)/shard_map/all_to_all | solution.py:305
  42.6 2.3 %copy-start.6 = (f32[16]{0:T(128)S(1)}, f32[16]{0:T(128)}, u32[]{:S(2)}) copy-start(f32[16]{0:T(128)} %defocus.5) | copy-start | bytes 196
  43.6 13.6 %collective-permute-start.2 = (bf16[272,768]{1,0:T(8,128)(2,1)S(1)}, bf16[272,768]{1,0:T(8,128)(2,1)S(1)}, u32[]{:S(2)}, u32[]{:S(2)}) collective-permute-start(bf16[272,768]{1,0:T(8,128)(2,1)S(1)} %get-tuple-element.26), channel_id=1, source_target_pairs={{1,0},{2,1},{3,2},{5,4},{6,5},{7,6},{9,8},{10,9},{11,10},{13,12},{... | collective-permute-start | bytes 1253384 | tf_op jit(solution)/shard_map/ppermute | solution.py:234
  45.9 46.2 %collective-permute-start.1 = (bf16[272,768]{1,0:T(8,128)(2,1)}, bf16[272,768]{1,0:T(8,128)(2,1)S(1)}, u32[]{:S(2)}, u32[]{:S(2)}) collective-permute-start(bf16[272,768]{1,0:T(8,128)(2,1)} %get-tuple-element.27), channel_id=1, source_target_pairs={{0,2},{2,0},{3,1},{4,6},{6,4},{7,5},{8,10},{10,8},{11,9},{12,14},{... | collective-permute-start | bytes 1253384 | tf_op jit(solution)/shard_map/ppermute | solution.py:234
  51.5 40.7 %collective-permute-start = (bf16[272,768]{1,0:T(8,128)(2,1)}, bf16[272,768]{1,0:T(8,128)(2,1)}, u32[]{:S(2)}, u32[]{:S(2)}) collective-permute-start(bf16[272,768]{1,0:T(8,128)(2,1)} %get-tuple-element.25), channel_id=1, source_target_pairs={{0,1},{1,2},{3,0},{4,5},{5,6},{7,4},{8,9},{9,10},{11,8},{12,13},{1... | collective-permute-start | bytes 1253384 | tf_op jit(solution)/shard_map/ppermute | solution.py:234
  60.5 32.9 %all-to-all-start.2 = ((bf16[8,128,768]{2,1,0:T(8,128)(2,1)}), bf16[8,128,768]{2,1,0:T(8,128)(2,1)}, u32[]{:S(2)}, u32[]{:S(2)}) async-start(bf16[8,128,768]{2,1,0:T(8,128)(2,1)} %spectrum.5), calls=%async_computation.2 | async-start | bytes 3145728 | tf_op jit(solution)/shard_map/all_to_all | solution.py:305
  68.7 24.7 %collective-permute-start.3 = (bf16[256,768]{1,0:T(8,128)(2,1)}, bf16[256,768]{1,0:T(8,128)(2,1)}, u32[]{:S(2)}, u32[]{:S(2)}) collective-permute-start(bf16[256,768]{1,0:T(8,128)(2,1)} %get-tuple-element.39), channel_id=1, source_target_pairs={{1,0},{2,1},{3,2},{6,7},{5,6},{4,5},{9,8},{10,9},{11,10},{14,15},{... | collective-permute-start | bytes 1179656 | tf_op jit(solution)/shard_map/ppermute | solution.py:234
  70.0 44.9 %collective-permute-start.5 = (bf16[256,768]{1,0:T(8,128)(2,1)}, bf16[256,768]{1,0:T(8,128)(2,1)}, u32[]{:S(2)}, u32[]{:S(2)}) collective-permute-start(bf16[256,768]{1,0:T(8,128)(2,1)} %get-tuple-element.38), channel_id=1, source_target_pairs={{0,2},{2,0},{3,1},{7,5},{5,7},{4,6},{8,10},{10,8},{11,9},{15,13},{... | collective-permute-start | bytes 1179656 | tf_op jit(solution)/shard_map/ppermute | solution.py:234
  90.2 34.8 %collective-permute-start.4 = (bf16[256,768]{1,0:T(8,128)(2,1)}, bf16[256,768]{1,0:T(8,128)(2,1)}, u32[]{:S(2)}, u32[]{:S(2)}) collective-permute-start(bf16[256,768]{1,0:T(8,128)(2,1)} %get-tuple-element.37), channel_id=1, source_target_pairs={{0,1},{1,2},{3,0},{7,6},{6,5},{4,7},{8,9},{9,10},{11,8},{15,14},{1... | collective-permute-start | bytes 1179656 | tf_op jit(solution)/shard_map/ppermute | solution.py:234
  96.2 1.0 copy-start
  97.6 25.2 %copy-start.3 = (s32[768,384]{1,0:T(8,128)S(1)}, s32[768,384]{1,0:T(8,128)}, u32[]{:S(2)}) copy-start(s32[768,384]{1,0:T(8,128)} %param.18) | copy-start | bytes 3538948
  114.9 13.2 %collective-permute-start.6 = (bf16[256,768]{1,0:T(8,128)(2,1)}, bf16[256,768]{1,0:T(8,128)(2,1)}, u32[]{:S(2)}, u32[]{:S(2)}) collective-permute-start(bf16[256,768]{1,0:T(8,128)(2,1)} %get-tuple-element.36), channel_id=1, source_target_pairs={{1,0},{2,1},{3,2},{5,4},{6,5},{7,6},{9,8},{10,9},{11,10},{13,12},{... | collective-permute-start | bytes 1179656 | tf_op jit(solution)/shard_map/ppermute | solution.py:234
  116.2 20.0 %collective-permute-start.8 = (bf16[256,768]{1,0:T(8,128)(2,1)}, bf16[256,768]{1,0:T(8,128)(2,1)}, u32[]{:S(2)}, u32[]{:S(2)}) collective-permute-start(bf16[256,768]{1,0:T(8,128)(2,1)} %get-tuple-element.34), channel_id=1, source_target_pairs={{0,1},{1,2},{3,0},{4,5},{5,6},{7,4},{8,9},{9,10},{11,8},{12,13},{1... | collective-permute-start | bytes 1179656 | tf_op jit(solution)/shard_map/ppermute | solution.py:234
  120.8 31.1 %collective-permute-start.9 = (bf16[256,768]{1,0:T(8,128)(2,1)}, bf16[256,768]{1,0:T(8,128)(2,1)}, u32[]{:S(2)}, u32[]{:S(2)}) collective-permute-start(bf16[256,768]{1,0:T(8,128)(2,1)} %get-tuple-element.35), channel_id=1, source_target_pairs={{0,2},{2,0},{3,1},{4,6},{6,4},{7,5},{8,10},{10,8},{11,9},{12,14},{... | collective-permute-start | bytes 1179656 | tf_op jit(solution)/shard_map/ppermute | solution.py:234
  125.0 1.6 %copy-start.5 = (f32[48,16]{1,0:T(8,128)S(1)}, f32[48,16]{1,0:T(8,128)}, u32[]{:S(2)}) copy-start(f32[48,16]{1,0:T(8,128)} %copy.53) | copy-start | bytes 9220
  128.2 23.7 %copy-start.1 = (bf16[3,256,768]{2,1,0:T(8,128)(2,1)S(1)}, bf16[3,256,768]{2,1,0:T(8,128)(2,1)}, u32[]{:S(2)}) copy-start(bf16[3,256,768]{2,1,0:T(8,128)(2,1)} %copy-done) | copy-start | bytes 3538948
  128.2 25.3 %collective-permute-start.7 = (bf16[256,768]{1,0:T(8,128)(2,1)S(1)}, bf16[256,768]{1,0:T(8,128)(2,1)S(1)}, u32[]{:S(2)}, u32[]{:S(2)}) collective-permute-start(bf16[256,768]{1,0:T(8,128)(2,1)S(1)} %convert_element_type.130), channel_id=1, source_target_pairs={{4,16},{12,24},{16,4},{24,12},{5,17},{13,25},{17,5},{25,13},{6,18}... | collective-permute-start | bytes 1179656 | tf_op jit(solution)/shard_map/ppermute | solution.py:395
  153.5 1.3 copy-start.4

commit v14 on v13

--- a/solution.py
+++ b/solution.py
@@ -11,7 +11,7 @@
 
 TAU_PRIOR = 4.0
 PHASE_OFFSET = 0.1
-CHUNKS = ((2, False), (2, True), (2, False))
+CHUNKS = ((2, False), (2, False), (2, False))
 SHARES = 6
 META_BASE = 32
 META_ROWS = 16

time: 157 us -> 163 us (1.038)
  the two profiles are of different devices: /device:TPU:0 before, /device:TPU:21 now
where the time goes in v14:
time: 163 us; the launch traced here: 162 us
  starting transfers between devices  58 us (36%)
  waiting for transfers between devices  57.4 us (35%)
  Pallas kernels  27.5 us (17%)
  other arithmetic  11 us (7%)
  matrix products  4.2 us (3%)
  local copies, waits for them, and re-layouts  3.58 us (2%)
    ppermute x9, waiting for transfers between devices, slab_exchange(): arrived.append(lax.ppermute(block, ('batch', 'slab'), perm))  51.5 us
    all_to_all x3, starting transfers between devices, per_device(): received.append(lax.all_to_all(send, 'batch', 0, 0, tiled=True))  36 us
    ppermute x9, starting transfers between devices, slab_exchange(): arrived.append(lax.ppermute(block, ('batch', 'slab'), perm))  22 us
    pallas_call x3, Pallas kernels, per_device(): pl.pallas_call(functools.partial(spectrum_kernel, runs, with_meta), out_s...  20.2 us
    pallas_call x3, Pallas kernels, per_device(): pl.pallas_call(functools.partial(insert_kernel, bins, meta_at), out_shape...  7.28 us
    all_to_all x3, waiting for transfers between devices, per_device(): received.append(lax.all_to_all(send, 'batch', 0, 0, tiled=True))  5.92 us
    add x3, other arithmetic, per_device(): sums[c] = sums[c] + block[:each * planes].astype(jnp.float32)  4.49 us
    select_n x3, other arithmetic, choose(): chosen = jnp.where(index == d, parts[d], chosen)  3.43 us
  transfers between devices with their start and end apart: 12, of which 4 were waited for; matrix products, arithmetic and copies ran while one was open for 9% of the time, Pallas kernels for 13%

profile of v14, /device:TPU:21, one launch (start us, length us, event | category | flops | bytes accessed | tf_op | source)
XLA Modules:
  0.0 162.1 jit_solution(3065195113449710586)
XLA Ops:
  0.0 6.8 %spectrum.3 = bf16[8,144,768]{2,1,0:T(8,128)(2,1)} custom-call(s32[8]{0:T(128)} %classes.5, s32[2,8]{1,0:T(2,128)} %bitcast.90, s32[8]{0:T(128)} %defocus_class.5, f32[16]{0:T(128)} %defocus.5, s32[4,8]{1,0:T(4,128)} %bitcast.87, bf16[8,384,384]{2,1,0:T(8,128)(2,1)} %images_in.5, bf16[256,384]{1,0:T(8,128)(2,1)} %constant.163.clone.left_in, ...), custom_call_target="tpu_custom_call" | custom-call | tf_op jit(solution)/shard_map/spectrum/pallas_call | solution.py:277
  6.8 4.6 %all-to-all-start = ((bf16[8,144,768]{2,1,0:T(8,128)(2,1)}), bf16[8,144,768]{2,1,0:T(8,128)(2,1)S(1)}, u32[]{:S(2)}, u32[]{:S(2)}) async-start(bf16[8,144,768]{2,1,0:T(8,128)(2,1)} %spectrum.3), calls=%async_computation | async-start | bytes 3538944 | tf_op jit(solution)/shard_map/all_to_all | solution.py:305
  11.3 6.7 %spectrum.4 = bf16[8,128,768]{2,1,0:T(8,128)(2,1)} custom-call(s32[8]{0:T(128)} %classes.5, s32[2,8]{1,0:T(2,128)} %bitcast.91, s32[8]{0:T(128)} %defocus_class.5, f32[16]{0:T(128)} %defocus.5, s32[4,8]{1,0:T(4,128)} %bitcast.88, bf16[8,384,384]{2,1,0:T(8,128)(2,1)} %images_in.5, bf16[256,384]{1,0:T(8,128)(2,1)} %constant.164.clone.left_in, ...), custom_call_target="tpu_custom_call" | custom-call | tf_op jit(solution)/shard_map/spectrum/pallas_call | solution.py:277
  18.1 6.7 %spectrum.5 = bf16[8,128,768]{2,1,0:T(8,128)(2,1)} custom-call(s32[8]{0:T(128)} %classes.5, s32[2,8]{1,0:T(2,128)} %bitcast.92, s32[8]{0:T(128)} %defocus_class.5, f32[16]{0:T(128)} %defocus.5, s32[4,8]{1,0:T(4,128)} %bitcast.89, bf16[8,384,384]{2,1,0:T(8,128)(2,1)} %images_in.5, bf16[256,384]{1,0:T(8,128)(2,1)} %constant.165.clone.left_in, ...), custom_call_target="tpu_custom_call" | custom-call | tf_op jit(solution)/shard_map/spectrum/pallas_call | solution.py:277
  24.8 5.9 %all-to-all-done.received = bf16[8,144,768]{2,1,0:T(8,128)(2,1)S(1)} async-done(((bf16[8,144,768]{2,1,0:T(8,128)(2,1)}), bf16[8,144,768]{2,1,0:T(8,128)(2,1)S(1)}, u32[]{:S(2)}, u32[]{:S(2)}) %all-to-all-start) | async-done | bytes 1769504 | tf_op jit(solution)/shard_map/all_to_all | solution.py:305
  30.7 7.9 %all-to-all-start.1 = ((bf16[8,128,768]{2,1,0:T(8,128)(2,1)}), bf16[8,128,768]{2,1,0:T(8,128)(2,1)}, u32[]{:S(2)}, u32[]{:S(2)}) async-start(bf16[8,128,768]{2,1,0:T(8,128)(2,1)} %spectrum.4), calls=%async_computation.1 | async-start | bytes 3145728 | tf_op jit(solution)/shard_map/all_to_all | solution.py:305
  40.4 1.7 %insert.3 = bf16[3,272,768]{2,1,0:T(8,128)(2,1)S(1)} custom-call(bf16[8,144,768]{2,1,0:T(8,128)(2,1)S(1)} %all-to-all-done.received, s32[1,1152]{1,0:T(1,128)S(1)} %reshape.197.codes), custom_call_target="tpu_custom_call" | custom-call | tf_op jit(solution)/shard_map/insert/pallas_call | solution.py:361
  43.1 3.2 %collective-permute-start.2 = (bf16[272,768]{1,0:T(8,128)(2,1)S(1)}, bf16[272,768]{1,0:T(8,128)(2,1)S(1)}, u32[]{:S(2)}, u32[]{:S(2)}) collective-permute-start(bf16[272,768]{1,0:T(8,128)(2,1)S(1)} %get-tuple-element.22), channel_id=1, source_target_pairs={{1,0},{2,1},{3,2},{5,4},{6,5},{7,6},{9,8},{10,9},{11,10},{13,12},{... | collective-permute-start | bytes 1253384 | tf_op jit(solution)/shard_map/ppermute | solution.py:234
  48.5 3.1 %collective-permute-start = (bf16[272,768]{1,0:T(8,128)(2,1)}, bf16[272,768]{1,0:T(8,128)(2,1)}, u32[]{:S(2)}, u32[]{:S(2)}) collective-permute-start(bf16[272,768]{1,0:T(8,128)(2,1)} %get-tuple-element.21), channel_id=1, source_target_pairs={{0,1},{1,2},{3,0},{4,5},{5,6},{7,4},{8,9},{9,10},{11,8},{12,13},{1... | collective-permute-start | bytes 1253384 | tf_op jit(solution)/shard_map/ppermute | solution.py:234
  52.0 4.1 %collective-permute-done.2 = bf16[272,768]{1,0:T(8,128)(2,1)S(1)} collective-permute-done((bf16[272,768]{1,0:T(8,128)(2,1)S(1)}, bf16[272,768]{1,0:T(8,128)(2,1)S(1)}, u32[]{:S(2)}, u32[]{:S(2)}) %collective-permute-start.2) | collective-permute-done | bytes 417824 | tf_op jit(solution)/shard_map/ppermute | solution.py:234
  56.1 23.5 %all-to-all-start.2 = ((bf16[8,128,768]{2,1,0:T(8,128)(2,1)}), bf16[8,128,768]{2,1,0:T(8,128)(2,1)}, u32[]{:S(2)}, u32[]{:S(2)}) async-start(bf16[8,128,768]{2,1,0:T(8,128)(2,1)} %spectrum.5), calls=%async_computation.2 | async-start | bytes 3145728 | tf_op jit(solution)/shard_map/all_to_all | solution.py:305
  79.6 2.8 %insert.4 = bf16[3,256,768]{2,1,0:T(8,128)(2,1)S(1)} custom-call(bf16[8,128,768]{2,1,0:T(8,128)(2,1)} %all-to-all-done.1.received, s32[1,1024]{1,0:T(1,128)S(1)} %reshape_reshape.6.codes), custom_call_target="tpu_custom_call" | custom-call | tf_op jit(solution)/shard_map/insert/pallas_call | solution.py:361
  83.6 1.9 %collective-permute-start.3 = (bf16[256,768]{1,0:T(8,128)(2,1)}, bf16[256,768]{1,0:T(8,128)(2,1)}, u32[]{:S(2)}, u32[]{:S(2)}) collective-permute-start(bf16[256,768]{1,0:T(8,128)(2,1)} %get-tuple-element.32), channel_id=1, source_target_pairs={{1,0},{2,1},{3,2},{5,4},{6,5},{7,6},{9,8},{10,9},{11,10},{13,12},{... | collective-permute-start | bytes 1179656 | tf_op jit(solution)/shard_map/ppermute | solution.py:234
  86.8 4.0 %collective-permute-start.4 = (bf16[256,768]{1,0:T(8,128)(2,1)}, bf16[256,768]{1,0:T(8,128)(2,1)}, u32[]{:S(2)}, u32[]{:S(2)}) collective-permute-start(bf16[256,768]{1,0:T(8,128)(2,1)} %get-tuple-element.30), channel_id=1, source_target_pairs={{0,1},{1,2},{3,0},{4,5},{5,6},{7,4},{8,9},{9,10},{11,8},{12,13},{1... | collective-permute-start | bytes 1179656 | tf_op jit(solution)/shard_map/ppermute | solution.py:234
  92.0 29.3 %collective-permute-done.3 = bf16[256,768]{1,0:T(8,128)(2,1)} collective-permute-done((bf16[256,768]{1,0:T(8,128)(2,1)}, bf16[256,768]{1,0:T(8,128)(2,1)}, u32[]{:S(2)}, u32[]{:S(2)}) %collective-permute-start.3) | collective-permute-done | bytes 393248 | tf_op jit(solution)/shard_map/ppermute | solution.py:234
  121.3 2.8 %insert.5 = bf16[3,256,768]{2,1,0:T(8,128)(2,1)S(1)} custom-call(bf16[8,128,768]{2,1,0:T(8,128)(2,1)} %all-to-all-done.2.received, s32[1,1024]{1,0:T(1,128)S(1)} %reshape_reshape.7.codes), custom_call_target="tpu_custom_call" | custom-call | tf_op jit(solution)/shard_map/insert/pallas_call | solution.py:361
  125.9 1.9 %collective-permute-start.6 = (bf16[256,768]{1,0:T(8,128)(2,1)}, bf16[256,768]{1,0:T(8,128)(2,1)}, u32[]{:S(2)}, u32[]{:S(2)}) collective-permute-start(bf16[256,768]{1,0:T(8,128)(2,1)} %get-tuple-element.33), channel_id=1, source_target_pairs={{0,1},{1,2},{3,0},{4,5},{5,6},{7,4},{8,9},{9,10},{11,8},{12,13},{1... | collective-permute-start | bytes 1179656 | tf_op jit(solution)/shard_map/ppermute | solution.py:234
  127.9 1.3 collective-permute-start.7
  129.2 4.0 %collective-permute-start.8 = (bf16[256,768]{1,0:T(8,128)(2,1)}, bf16[256,768]{1,0:T(8,128)(2,1)}, u32[]{:S(2)}, u32[]{:S(2)}) collective-permute-start(bf16[256,768]{1,0:T(8,128)(2,1)} %get-tuple-element.34), channel_id=1, source_target_pairs={{1,0},{2,1},{3,2},{5,4},{6,5},{7,6},{9,8},{10,9},{11,10},{13,12},{... | collective-permute-start | bytes 1179656 | tf_op jit(solution)/shard_map/ppermute | solution.py:234
  133.4 1.7 %fusion.2 = s32[256,384]{1,0:T(8,128)S(1)} fusion(s32[256]{0:T(256)S(1)} %bitcast.93, s32[256,384]{1,0:T(8,128)S(1)} %convert_reduce_fusion, s32[768,384]{1,0:T(8,128)} %param.18), kind=kOutput, calls=%fused_computation.4 | convolution fusion | flops 151781376 | bytes 1967104 | tf_op jit(solution)/shard_map/dot_general | solution.py:320
  136.5 1.3 fusion.12
  139.1 1.6 %fusion.10 = f32[256,768]{1,0:T(8,128)S(1)} fusion(bf16[256,768]{1,0:T(8,128)(2,1)} %collective-permute-done.3, bf16[256,768]{1,0:T(8,128)(2,1)} %collective-permute-done.5, bf16[256,768]{1,0:T(8,128)(2,1)} %collective-permute-done.4, pred[]{:T(512)S(6)} %eq.118, pred[]{:T(512)S(6)} %eq.104, pred[]{:T(512)S(6)} %eq.103, bf16[3,256,768]{2,1,0:T(8,128)(2,1)S(1)} %insert.4), kind=kLoop, calls=%fused_computation.21 | loop fusion | flops 1966080 | bytes 3145731 | tf_op jit(solution)/shard_map/add | solution.py:388
  140.8 18.1 %collective-permute-done.8 = bf16[256,768]{1,0:T(8,128)(2,1)} collective-permute-done((bf16[256,768]{1,0:T(8,128)(2,1)}, bf16[256,768]{1,0:T(8,128)(2,1)}, u32[]{:S(2)}, u32[]{:S(2)}) %collective-permute-start.8) | collective-permute-done | bytes 393248 | tf_op jit(solution)/shard_map/ppermute | solution.py:234
  158.9 1.5 fusion.8
  (78 shorter events, 15.2 us)
Async XLA Ops:
  6.8 23.9 %all-to-all-start = ((bf16[8,144,768]{2,1,0:T(8,128)(2,1)}), bf16[8,144,768]{2,1,0:T(8,128)(2,1)S(1)}, u32[]{:S(2)}, u32[]{:S(2)}) async-start(bf16[8,144,768]{2,1,0:T(8,128)(2,1)} %spectrum.3), calls=%async_computation | async-start | bytes 3538944 | tf_op jit(solution)/shard_map/all_to_all | solution.py:305
  24.8 14.8 %copy-start.2 = (s32[768,384]{1,0:T(8,128)S(1)}, s32[768,384]{1,0:T(8,128)}, u32[]{:S(2)}) copy-start(s32[768,384]{1,0:T(8,128)} %param.18) | copy-start | bytes 3538948
  30.7 25.3 %all-to-all-start.1 = ((bf16[8,128,768]{2,1,0:T(8,128)(2,1)}), bf16[8,128,768]{2,1,0:T(8,128)(2,1)}, u32[]{:S(2)}, u32[]{:S(2)}) async-start(bf16[8,128,768]{2,1,0:T(8,128)(2,1)} %spectrum.4), calls=%async_computation.1 | async-start | bytes 3145728 | tf_op jit(solution)/shard_map/all_to_all | solution.py:305
  38.9 0.6 copy-start.4
  42.1 4.2 %copy-start.6 = (f32[16]{0:T(128)S(1)}, f32[16]{0:T(128)}, u32[]{:S(2)}) copy-start(f32[16]{0:T(128)} %defocus.5) | copy-start | bytes 196
  43.1 13.0 %collective-permute-start.2 = (bf16[272,768]{1,0:T(8,128)(2,1)S(1)}, bf16[272,768]{1,0:T(8,128)(2,1)S(1)}, u32[]{:S(2)}, u32[]{:S(2)}) collective-permute-start(bf16[272,768]{1,0:T(8,128)(2,1)S(1)} %get-tuple-element.22), channel_id=1, source_target_pairs={{1,0},{2,1},{3,2},{5,4},{6,5},{7,6},{9,8},{10,9},{11,10},{13,12},{... | collective-permute-start | bytes 1253384 | tf_op jit(solution)/shard_map/ppermute | solution.py:234
  47.2 43.5 %collective-permute-start.1 = (bf16[272,768]{1,0:T(8,128)(2,1)}, bf16[272,768]{1,0:T(8,128)(2,1)S(1)}, u32[]{:S(2)}, u32[]{:S(2)}) collective-permute-start(bf16[272,768]{1,0:T(8,128)(2,1)} %get-tuple-element.23), channel_id=1, source_target_pairs={{0,2},{2,0},{3,1},{4,6},{6,4},{7,5},{8,10},{10,8},{11,9},{12,14},{... | collective-permute-start | bytes 1253384 | tf_op jit(solution)/shard_map/ppermute | solution.py:234
  48.5 42.2 %collective-permute-start = (bf16[272,768]{1,0:T(8,128)(2,1)}, bf16[272,768]{1,0:T(8,128)(2,1)}, u32[]{:S(2)}, u32[]{:S(2)}) collective-permute-start(bf16[272,768]{1,0:T(8,128)(2,1)} %get-tuple-element.21), channel_id=1, source_target_pairs={{0,1},{1,2},{3,0},{4,5},{5,6},{7,4},{8,9},{9,10},{11,8},{12,13},{1... | collective-permute-start | bytes 1253384 | tf_op jit(solution)/shard_map/ppermute | solution.py:234
  56.1 65.2 %all-to-all-start.2 = ((bf16[8,128,768]{2,1,0:T(8,128)(2,1)}), bf16[8,128,768]{2,1,0:T(8,128)(2,1)}, u32[]{:S(2)}, u32[]{:S(2)}) async-start(bf16[8,128,768]{2,1,0:T(8,128)(2,1)} %spectrum.5), calls=%async_computation.2 | async-start | bytes 3145728 | tf_op jit(solution)/shard_map/all_to_all | solution.py:305
  83.6 37.8 %collective-permute-start.3 = (bf16[256,768]{1,0:T(8,128)(2,1)}, bf16[256,768]{1,0:T(8,128)(2,1)}, u32[]{:S(2)}, u32[]{:S(2)}) collective-permute-start(bf16[256,768]{1,0:T(8,128)(2,1)} %get-tuple-element.32), channel_id=1, source_target_pairs={{1,0},{2,1},{3,2},{5,4},{6,5},{7,6},{9,8},{10,9},{11,10},{13,12},{... | collective-permute-start | bytes 1179656 | tf_op jit(solution)/shard_map/ppermute | solution.py:234
  85.5 53.7 %collective-permute-start.5 = (bf16[256,768]{1,0:T(8,128)(2,1)}, bf16[256,768]{1,0:T(8,128)(2,1)}, u32[]{:S(2)}, u32[]{:S(2)}) collective-permute-start(bf16[256,768]{1,0:T(8,128)(2,1)} %get-tuple-element.31), channel_id=1, source_target_pairs={{0,2},{2,0},{3,1},{4,6},{6,4},{7,5},{8,10},{10,8},{11,9},{12,14},{... | collective-permute-start | bytes 1179656 | tf_op jit(solution)/shard_map/ppermute | solution.py:234
  86.8 52.4 %collective-permute-start.4 = (bf16[256,768]{1,0:T(8,128)(2,1)}, bf16[256,768]{1,0:T(8,128)(2,1)}, u32[]{:S(2)}, u32[]{:S(2)}) collective-permute-start(bf16[256,768]{1,0:T(8,128)(2,1)} %get-tuple-element.30), channel_id=1, source_target_pairs={{0,1},{1,2},{3,0},{4,5},{5,6},{7,4},{8,9},{9,10},{11,8},{12,13},{1... | collective-permute-start | bytes 1179656 | tf_op jit(solution)/shard_map/ppermute | solution.py:234
  124.1 1.4 copy-start
  124.1 1.6 %copy-start.5 = (s32[64,5]{0,1:T(8,128)S(1)}, s32[64,5]{0,1:T(8,128)}, u32[]{:S(2)}) copy-start(s32[64,5]{0,1:T(8,128)} %copy-done.4) | copy-start | bytes 3844
  125.9 14.9 %collective-permute-start.6 = (bf16[256,768]{1,0:T(8,128)(2,1)}, bf16[256,768]{1,0:T(8,128)(2,1)}, u32[]{:S(2)}, u32[]{:S(2)}) collective-permute-start(bf16[256,768]{1,0:T(8,128)(2,1)} %get-tuple-element.33), channel_id=1, source_target_pairs={{0,1},{1,2},{3,0},{4,5},{5,6},{7,4},{8,9},{9,10},{11,8},{12,13},{1... | collective-permute-start | bytes 1179656 | tf_op jit(solution)/shard_map/ppermute | solution.py:234
  127.9 12.9 %collective-permute-start.7 = (bf16[256,768]{1,0:T(8,128)(2,1)}, bf16[256,768]{1,0:T(8,128)(2,1)}, u32[]{:S(2)}, u32[]{:S(2)}) collective-permute-start(bf16[256,768]{1,0:T(8,128)(2,1)} %get-tuple-element.35), channel_id=1, source_target_pairs={{0,2},{2,0},{3,1},{4,6},{6,4},{7,5},{8,10},{10,8},{11,9},{12,14},{... | collective-permute-start | bytes 1179656 | tf_op jit(solution)/shard_map/ppermute | solution.py:234
  129.2 29.7 %collective-permute-start.8 = (bf16[256,768]{1,0:T(8,128)(2,1)}, bf16[256,768]{1,0:T(8,128)(2,1)}, u32[]{:S(2)}, u32[]{:S(2)}) collective-permute-start(bf16[256,768]{1,0:T(8,128)(2,1)} %get-tuple-element.34), channel_id=1, source_target_pairs={{1,0},{2,1},{3,2},{5,4},{6,5},{7,6},{9,8},{10,9},{11,10},{13,12},{... | collective-permute-start | bytes 1179656 | tf_op jit(solution)/shard_map/ppermute | solution.py:234
  139.1 19.8 %copy-start.1 = (bf16[3,256,768]{2,1,0:T(8,128)(2,1)S(1)}, bf16[3,256,768]{2,1,0:T(8,128)(2,1)}, u32[]{:S(2)}) copy-start(bf16[3,256,768]{2,1,0:T(8,128)(2,1)} %copy-done) | copy-start | bytes 3538948
  140.8 19.7 %copy-start.3 = (bf16[48,16,768]{2,1,0:T(8,128)(2,1)S(1)}, bf16[48,16,768]{2,1,0:T(8,128)(2,1)}, u32[]{:S(2)}) copy-start(bf16[48,16,768]{2,1,0:T(8,128)(2,1)} %param.19) | copy-start | bytes 3538948

commit v15 on v9

--- a/solution.py
+++ b/solution.py
@@ -11,7 +11,7 @@
 
 TAU_PRIOR = 4.0
 PHASE_OFFSET = 0.1
-CHUNKS = ((2, False), (2, True), (2, False))
+CHUNKS = ((2, False), (3, True), (1, False))
 SHARES = 6
 META_BASE = 32
 META_ROWS = 16
@@ -252,7 +252,10 @@
     mirrored = slab_count == 4 and batch_count % 2 == 0 and 2 * particles <= META_ROWS
     mirrored = mirrored and batch_count * LANES <= 4 * length
     half_batch = batch_count // 2
-    sizes = [rows * share // SHARES for share, _ in CHUNKS]
+    shares = [share for share, _ in CHUNKS]
+    if rows % (8 * SHARES):
+        shares = [SHARES // len(CHUNKS)] * len(CHUNKS)
+    sizes = [rows * share // SHARES for share in shares]
     starts = [sum(sizes[:c]) for c in range(len(CHUNKS))]
     roles = [slab_roles(batch_count, mirrored and swapped) for _, swapped in CHUNKS]
     freq = jnp.arange(length, dtype=jnp.int32)

time: 155 us -> 159 us (1.026)
  the two profiles are of different devices: /device:TPU:0 before, /device:TPU:11 now
where the time goes in v15:
time: 159 us; the launch traced here: 158 us
  waiting for transfers between devices  70.8 us (45%)
  starting transfers between devices  39.3 us (25%)
  Pallas kernels  28.3 us (18%)
  other arithmetic  11.3 us (7%)
  local copies, waits for them, and re-layouts  5.8 us (4%)
  matrix products  2.21 us (1%)
    ppermute x9, waiting for transfers between devices, slab_exchange(): arrived.append(lax.ppermute(block, ('batch', 'slab'), perm))  57.5 us
    ppermute x9, starting transfers between devices, slab_exchange(): arrived.append(lax.ppermute(block, ('batch', 'slab'), perm))  21.3 us
    pallas_call x3, Pallas kernels, per_device(): pl.pallas_call(functools.partial(spectrum_kernel, runs, with_meta), out_s...  20.4 us
    all_to_all x3, starting transfers between devices, per_device(): received.append(lax.all_to_all(send, 'batch', 0, 0, tiled=True))  16.1 us
    pallas_call x3, Pallas kernels, per_device(): pl.pallas_call(functools.partial(insert_kernel, bins, meta_at), out_shape...  7.88 us
    ppermute x1, waiting for transfers between devices, per_device(): handed = lax.ppermute(sums[c].astype(jnp.bfloat16), 'batch', over)  7.74 us
    all_to_all x3, waiting for transfers between devices, per_device(): received.append(lax.all_to_all(send, 'batch', 0, 0, tiled=True))  5.53 us
    select_n x3, other arithmetic, choose(): chosen = jnp.where(index == d, parts[d], chosen)  4.33 us
  transfers between devices with their start and end apart: 13, of which 8 were waited for; matrix products, arithmetic and copies ran while one was open for 9% of the time, Pallas kernels for 14%

profile of v15, /device:TPU:11, one launch (start us, length us, event | category | flops | bytes accessed | tf_op | source)
XLA Modules:
  0.0 158.4 jit_solution(3829430405090169122)
XLA Ops:
  0.0 6.8 %spectrum.3 = bf16[8,144,768]{2,1,0:T(8,128)(2,1)} custom-call(s32[8]{0:T(128)} %classes.5, s32[2,8]{1,0:T(2,128)} %bitcast.90, s32[8]{0:T(128)} %defocus_class.5, f32[16]{0:T(128)} %defocus.5, s32[4,8]{1,0:T(4,128)} %bitcast.87, bf16[8,384,384]{2,1,0:T(8,128)(2,1)} %images_in.5, bf16[256,384]{1,0:T(8,128)(2,1)} %constant.188.clone.left_in, ...), custom_call_target="tpu_custom_call" | custom-call | tf_op jit(solution)/shard_map/spectrum/pallas_call | solution.py:280
  6.8 4.6 %all-to-all-start = ((bf16[8,144,768]{2,1,0:T(8,128)(2,1)}), bf16[8,144,768]{2,1,0:T(8,128)(2,1)S(1)}, u32[]{:S(2)}, u32[]{:S(2)}) async-start(bf16[8,144,768]{2,1,0:T(8,128)(2,1)} %spectrum.3), calls=%async_computation | async-start | bytes 3538944 | tf_op jit(solution)/shard_map/all_to_all | solution.py:308
  12.9 5.3 %spectrum.5 = bf16[8,64,768]{2,1,0:T(8,128)(2,1)} custom-call(s32[8]{0:T(128)} %classes.5, s32[2,8]{1,0:T(2,128)} %bitcast.91, s32[8]{0:T(128)} %defocus_class.5, f32[16]{0:T(128)} %defocus.5, s32[4,8]{1,0:T(4,128)} %bitcast.88, bf16[8,384,384]{2,1,0:T(8,128)(2,1)} %images_in.5, bf16[128,384]{1,0:T(8,128)(2,1)} %constant.190.clone.left_in, ...), custom_call_target="tpu_custom_call" | custom-call | tf_op jit(solution)/shard_map/spectrum/pallas_call | solution.py:280
  18.2 8.4 %spectrum.4 = bf16[8,192,768]{2,1,0:T(8,128)(2,1)} custom-call(s32[8]{0:T(128)} %classes.5, s32[2,8]{1,0:T(2,128)} %bitcast.92, s32[8]{0:T(128)} %defocus_class.5, f32[16]{0:T(128)} %defocus.5, s32[4,8]{1,0:T(4,128)} %bitcast.89, bf16[8,384,384]{2,1,0:T(8,128)(2,1)} %images_in.5, bf16[384,384]{1,0:T(8,128)(2,1)} %constant.189.clone.left_in, ...), custom_call_target="tpu_custom_call" | custom-call | tf_op jit(solution)/shard_map/spectrum/pallas_call | solution.py:280
  27.4 5.5 %all-to-all-done.received = bf16[8,144,768]{2,1,0:T(8,128)(2,1)S(1)} async-done(((bf16[8,144,768]{2,1,0:T(8,128)(2,1)}), bf16[8,144,768]{2,1,0:T(8,128)(2,1)S(1)}, u32[]{:S(2)}, u32[]{:S(2)}) %all-to-all-start) | async-done | bytes 1769504 | tf_op jit(solution)/shard_map/all_to_all | solution.py:308
  33.0 5.9 %all-to-all-start.1 = ((bf16[8,192,768]{2,1,0:T(8,128)(2,1)}), bf16[8,192,768]{2,1,0:T(8,128)(2,1)}, u32[]{:S(2)}, u32[]{:S(2)}) async-start(bf16[8,192,768]{2,1,0:T(8,128)(2,1)} %spectrum.4), calls=%async_computation.1 | async-start | bytes 4718592 | tf_op jit(solution)/shard_map/all_to_all | solution.py:308
  42.4 3.2 %collective-permute-start = (bf16[272,768]{1,0:T(8,128)(2,1)S(1)}, bf16[272,768]{1,0:T(8,128)(2,1)S(1)}, u32[]{:S(2)}, u32[]{:S(2)}) collective-permute-start(bf16[272,768]{1,0:T(8,128)(2,1)S(1)} %get-tuple-element.33), channel_id=1, source_target_pairs={{0,1},{1,2},{3,0},{4,5},{5,6},{7,4},{8,9},{9,10},{11,8},{12,13},{1... | collective-permute-start | bytes 1253384 | tf_op jit(solution)/shard_map/ppermute | solution.py:234
  45.6 2.1 %collective-permute-start.1 = (bf16[272,768]{1,0:T(8,128)(2,1)S(1)}, bf16[272,768]{1,0:T(8,128)(2,1)S(1)}, u32[]{:S(2)}, u32[]{:S(2)}) collective-permute-start(bf16[272,768]{1,0:T(8,128)(2,1)S(1)} %get-tuple-element.34), channel_id=1, source_target_pairs={{1,0},{2,1},{3,2},{5,4},{6,5},{7,6},{9,8},{10,9},{11,10},{13,12},{... | collective-permute-start | bytes 1253384 | tf_op jit(solution)/shard_map/ppermute | solution.py:234
  49.5 5.7 %collective-permute-done = bf16[272,768]{1,0:T(8,128)(2,1)S(1)} collective-permute-done((bf16[272,768]{1,0:T(8,128)(2,1)S(1)}, bf16[272,768]{1,0:T(8,128)(2,1)S(1)}, u32[]{:S(2)}, u32[]{:S(2)}) %collective-permute-start) | collective-permute-done | bytes 417824 | tf_op jit(solution)/shard_map/ppermute | solution.py:234
  55.2 11.1 %collective-permute-done.1 = bf16[272,768]{1,0:T(8,128)(2,1)S(1)} collective-permute-done((bf16[272,768]{1,0:T(8,128)(2,1)S(1)}, bf16[272,768]{1,0:T(8,128)(2,1)S(1)}, u32[]{:S(2)}, u32[]{:S(2)}) %collective-permute-start.1) | collective-permute-done | bytes 417824 | tf_op jit(solution)/shard_map/ppermute | solution.py:234
  67.8 5.7 %all-to-all-start.2 = ((bf16[8,64,768]{2,1,0:T(8,128)(2,1)}), bf16[8,64,768]{2,1,0:T(8,128)(2,1)}, u32[]{:S(2)}, u32[]{:S(2)}) async-start(bf16[8,64,768]{2,1,0:T(8,128)(2,1)} %spectrum.5), calls=%async_computation.2 | async-start | bytes 1572864 | tf_op jit(solution)/shard_map/all_to_all | solution.py:308
  73.5 4.6 %insert.4 = bf16[3,384,768]{2,1,0:T(8,128)(2,1)S(1)} custom-call(bf16[8,192,768]{2,1,0:T(8,128)(2,1)} %all-to-all-done.1.received, s32[1,1536]{1,0:T(1,128)S(1)} %reshape_reshape.6.codes), custom_call_target="tpu_custom_call" | custom-call | tf_op jit(solution)/shard_map/insert/pallas_call | solution.py:366
  80.8 4.0 %collective-permute-start.4 = (bf16[384,768]{1,0:T(8,128)(2,1)}, bf16[384,768]{1,0:T(8,128)(2,1)}, u32[]{:S(2)}, u32[]{:S(2)}) collective-permute-start(bf16[384,768]{1,0:T(8,128)(2,1)} %get-tuple-element.31), channel_id=1, source_target_pairs={{1,0},{2,1},{3,2},{6,7},{5,6},{4,5},{9,8},{10,9},{11,10},{14,15},{... | collective-permute-start | bytes 1769480 | tf_op jit(solution)/shard_map/ppermute | solution.py:234
  85.0 2.3 %collective-permute-start.5 = (bf16[384,768]{1,0:T(8,128)(2,1)}, bf16[384,768]{1,0:T(8,128)(2,1)}, u32[]{:S(2)}, u32[]{:S(2)}) collective-permute-start(bf16[384,768]{1,0:T(8,128)(2,1)} %get-tuple-element.29), channel_id=1, source_target_pairs={{0,2},{2,0},{3,1},{7,5},{5,7},{4,6},{8,10},{10,8},{11,9},{15,13},{... | collective-permute-start | bytes 1769480 | tf_op jit(solution)/shard_map/ppermute | solution.py:234
  87.3 16.4 %collective-permute-done.3 = bf16[384,768]{1,0:T(8,128)(2,1)} collective-permute-done((bf16[384,768]{1,0:T(8,128)(2,1)}, bf16[384,768]{1,0:T(8,128)(2,1)}, u32[]{:S(2)}, u32[]{:S(2)}) %collective-permute-start.3) | collective-permute-done | bytes 589856 | tf_op jit(solution)/shard_map/ppermute | solution.py:234
  103.7 6.8 %collective-permute-done.4 = bf16[384,768]{1,0:T(8,128)(2,1)} collective-permute-done((bf16[384,768]{1,0:T(8,128)(2,1)}, bf16[384,768]{1,0:T(8,128)(2,1)}, u32[]{:S(2)}, u32[]{:S(2)}) %collective-permute-start.4) | collective-permute-done | bytes 589856 | tf_op jit(solution)/shard_map/ppermute | solution.py:234
  113.3 2.1 %select_bitcast_fusion.7 = (bf16[128,768]{1,0:T(8,128)(2,1)}, bf16[128,768]{1,0:T(8,128)(2,1)}, bf16[128,768]{1,0:T(8,128)(2,1)}) fusion(pred[]{:T(512)S(6)} %eq.280, pred[]{:T(512)S(6)} %eq.279, bf16[3,128,768]{2,1,0:T(8,128)(2,1)} %copy-done, pred[]{:T(512)S(6)} %eq.284, pred[]{:T(512)S(6)} %eq.283, pred[]{:T(512)S(6)} %eq.282, pred[]{:T(512)S(6)} %eq.281), kind=kLoop, calls=%fused_computation.47 | loop fusion | flops 589824 | bytes 1179654 | tf_op jit(solution)/shard_map/jit(_where)/select_n | solution.py:241
  115.4 6.8 %collective-permute-done.5 = bf16[384,768]{1,0:T(8,128)(2,1)} collective-permute-done((bf16[384,768]{1,0:T(8,128)(2,1)}, bf16[384,768]{1,0:T(8,128)(2,1)}, u32[]{:S(2)}, u32[]{:S(2)}) %collective-permute-start.5) | collective-permute-done | bytes 589856 | tf_op jit(solution)/shard_map/ppermute | solution.py:234
  123.2 2.4 %collective-permute-start.8 = (bf16[128,768]{1,0:T(8,128)(2,1)}, bf16[128,768]{1,0:T(8,128)(2,1)S(1)}, u32[]{:S(2)}, u32[]{:S(2)}) collective-permute-start(bf16[128,768]{1,0:T(8,128)(2,1)} %get-tuple-element.35), channel_id=1, source_target_pairs={{0,1},{1,2},{3,0},{4,5},{5,6},{7,4},{8,9},{9,10},{11,8},{12,13},{1... | collective-permute-start | bytes 589832 | tf_op jit(solution)/shard_map/ppermute | solution.py:234
  127.0 3.5 %collective-permute-start.6 = (bf16[128,768]{1,0:T(8,128)(2,1)}, bf16[128,768]{1,0:T(8,128)(2,1)S(1)}, u32[]{:S(2)}, u32[]{:S(2)}) collective-permute-start(bf16[128,768]{1,0:T(8,128)(2,1)} %get-tuple-element.37), channel_id=1, source_target_pairs={{1,0},{2,1},{3,2},{5,4},{6,5},{7,6},{9,8},{10,9},{11,10},{13,12},{... | collective-permute-start | bytes 589832 | tf_op jit(solution)/shard_map/ppermute | solution.py:234
  132.1 2.3 %fusion.5 = f32[384,768]{1,0:T(8,128)S(1)} fusion(bf16[384,768]{1,0:T(8,128)(2,1)} %collective-permute-done.4, bf16[384,768]{1,0:T(8,128)(2,1)} %collective-permute-done.5, bf16[384,768]{1,0:T(8,128)(2,1)} %collective-permute-done.3, pred[]{:T(512)S(6)} %eq.304, pred[]{:T(512)S(6)} %eq.303, pred[]{:T(512)S(6)} %eq.302, bf16[3,384,768]{2,1,0:T(8,128)(2,1)S(1)} %insert.4), kind=kLoop, calls=%fused_computation.10 | loop fusion | flops 2949120 | bytes 4718595 | tf_op jit(solution)/shard_map/add | solution.py:393
  134.8 10.8 %collective-permute-done.6 = bf16[128,768]{1,0:T(8,128)(2,1)S(1)} collective-permute-done((bf16[128,768]{1,0:T(8,128)(2,1)}, bf16[128,768]{1,0:T(8,128)(2,1)S(1)}, u32[]{:S(2)}, u32[]{:S(2)}) %collective-permute-start.6) | collective-permute-done | bytes 196640 | tf_op jit(solution)/shard_map/ppermute | solution.py:234
  145.6 1.9 %collective-permute-start.7 = (bf16[384,768]{1,0:T(8,128)(2,1)S(1)}, bf16[384,768]{1,0:T(8,128)(2,1)S(1)}, u32[]{:S(2)}, u32[]{:S(2)}) collective-permute-start(bf16[384,768]{1,0:T(8,128)(2,1)S(1)} %convert_element_type.130), channel_id=1, source_target_pairs={{4,16},{12,24},{16,4},{24,12},{5,17},{13,25},{17,5},{25,13},{6,18}... | collective-permute-start | bytes 1769480 | tf_op jit(solution)/shard_map/ppermute | solution.py:400
  149.1 7.7 %collective-permute-done.7 = bf16[384,768]{1,0:T(8,128)(2,1)S(1)} collective-permute-done((bf16[384,768]{1,0:T(8,128)(2,1)S(1)}, bf16[384,768]{1,0:T(8,128)(2,1)S(1)}, u32[]{:S(2)}, u32[]{:S(2)}) %collective-permute-start.7) | collective-permute-done | bytes 589856 | tf_op jit(solution)/shard_map/ppermute | solution.py:400
  (122 shorter events, 22.1 us)
Async XLA Ops:
  6.8 26.1 %all-to-all-start = ((bf16[8,144,768]{2,1,0:T(8,128)(2,1)}), bf16[8,144,768]{2,1,0:T(8,128)(2,1)S(1)}, u32[]{:S(2)}, u32[]{:S(2)}) async-start(bf16[8,144,768]{2,1,0:T(8,128)(2,1)} %spectrum.3), calls=%async_computation | async-start | bytes 3538944 | tf_op jit(solution)/shard_map/all_to_all | solution.py:308
  18.2 8.4 %copy-start.20 = (f32[16]{0:T(128)S(1)}, f32[16]{0:T(128)}, u32[]{:S(2)}) copy-start(f32[16]{0:T(128)} %defocus.5) | copy-start | bytes 196
  27.4 11.8 %copy-start.3 = (s32[768,384]{1,0:T(8,128)S(1)}, s32[768,384]{1,0:T(8,128)}, u32[]{:S(2)}) copy-start(s32[768,384]{1,0:T(8,128)} %param.18) | copy-start | bytes 3538948
  33.0 34.8 %all-to-all-start.1 = ((bf16[8,192,768]{2,1,0:T(8,128)(2,1)}), bf16[8,192,768]{2,1,0:T(8,128)(2,1)}, u32[]{:S(2)}, u32[]{:S(2)}) async-start(bf16[8,192,768]{2,1,0:T(8,128)(2,1)} %spectrum.4), calls=%async_computation.1 | async-start | bytes 4718592 | tf_op jit(solution)/shard_map/all_to_all | solution.py:308
  42.4 12.9 %collective-permute-start = (bf16[272,768]{1,0:T(8,128)(2,1)S(1)}, bf16[272,768]{1,0:T(8,128)(2,1)S(1)}, u32[]{:S(2)}, u32[]{:S(2)}) collective-permute-start(bf16[272,768]{1,0:T(8,128)(2,1)S(1)} %get-tuple-element.33), channel_id=1, source_target_pairs={{0,1},{1,2},{3,0},{4,5},{5,6},{7,4},{8,9},{9,10},{11,8},{12,13},{1... | collective-permute-start | bytes 1253384 | tf_op jit(solution)/shard_map/ppermute | solution.py:234
  45.6 20.7 %collective-permute-start.1 = (bf16[272,768]{1,0:T(8,128)(2,1)S(1)}, bf16[272,768]{1,0:T(8,128)(2,1)S(1)}, u32[]{:S(2)}, u32[]{:S(2)}) collective-permute-start(bf16[272,768]{1,0:T(8,128)(2,1)S(1)} %get-tuple-element.34), channel_id=1, source_target_pairs={{1,0},{2,1},{3,2},{5,4},{6,5},{7,6},{9,8},{10,9},{11,10},{13,12},{... | collective-permute-start | bytes 1253384 | tf_op jit(solution)/shard_map/ppermute | solution.py:234
  48.2 36.8 %collective-permute-start.2 = (bf16[272,768]{1,0:T(8,128)(2,1)}, bf16[272,768]{1,0:T(8,128)(2,1)S(1)}, u32[]{:S(2)}, u32[]{:S(2)}) collective-permute-start(bf16[272,768]{1,0:T(8,128)(2,1)} %get-tuple-element.32), channel_id=1, source_target_pairs={{0,2},{2,0},{3,1},{4,6},{6,4},{7,5},{8,10},{10,8},{11,9},{12,14},{... | collective-permute-start | bytes 1253384 | tf_op jit(solution)/shard_map/ppermute | solution.py:234
  55.2 12.5 %copy-start.6 = (bf16[272,768]{1,0:T(8,128)(2,1)}, bf16[272,768]{1,0:T(8,128)(2,1)S(1)}, u32[]{:S(2)}) copy-start(bf16[272,768]{1,0:T(8,128)(2,1)S(1)} %collective-permute-done) | copy-start | bytes 1253380
  67.8 42.7 %all-to-all-start.2 = ((bf16[8,64,768]{2,1,0:T(8,128)(2,1)}), bf16[8,64,768]{2,1,0:T(8,128)(2,1)}, u32[]{:S(2)}, u32[]{:S(2)}) async-start(bf16[8,64,768]{2,1,0:T(8,128)(2,1)} %spectrum.5), calls=%async_computation.2 | async-start | bytes 1572864 | tf_op jit(solution)/shard_map/all_to_all | solution.py:308
  79.5 24.2 %collective-permute-start.3 = (bf16[384,768]{1,0:T(8,128)(2,1)}, bf16[384,768]{1,0:T(8,128)(2,1)}, u32[]{:S(2)}, u32[]{:S(2)}) collective-permute-start(bf16[384,768]{1,0:T(8,128)(2,1)} %get-tuple-element.30), channel_id=1, source_target_pairs={{0,1},{1,2},{3,0},{7,6},{6,5},{4,7},{8,9},{9,10},{11,8},{15,14},{1... | collective-permute-start | bytes 1769480 | tf_op jit(solution)/shard_map/ppermute | solution.py:234
  80.8 29.7 %collective-permute-start.4 = (bf16[384,768]{1,0:T(8,128)(2,1)}, bf16[384,768]{1,0:T(8,128)(2,1)}, u32[]{:S(2)}, u32[]{:S(2)}) collective-permute-start(bf16[384,768]{1,0:T(8,128)(2,1)} %get-tuple-element.31), channel_id=1, source_target_pairs={{1,0},{2,1},{3,2},{6,7},{5,6},{4,5},{9,8},{10,9},{11,10},{14,15},{... | collective-permute-start | bytes 1769480 | tf_op jit(solution)/shard_map/ppermute | solution.py:234
  85.0 30.4 %copy-start.10 = (bf16[272,768]{1,0:T(8,128)(2,1)}, bf16[272,768]{1,0:T(8,128)(2,1)S(1)}, u32[]{:S(2)}) copy-start(bf16[272,768]{1,0:T(8,128)(2,1)S(1)} %collective-permute-done.2) | copy-start | bytes 1253380
  85.0 37.1 %collective-permute-start.5 = (bf16[384,768]{1,0:T(8,128)(2,1)}, bf16[384,768]{1,0:T(8,128)(2,1)}, u32[]{:S(2)}, u32[]{:S(2)}) collective-permute-start(bf16[384,768]{1,0:T(8,128)(2,1)} %get-tuple-element.29), channel_id=1, source_target_pairs={{0,2},{2,0},{3,1},{7,5},{5,7},{4,6},{8,10},{10,8},{11,9},{15,13},{... | collective-permute-start | bytes 1769480 | tf_op jit(solution)/shard_map/ppermute | solution.py:234
  113.1 9.2 %copy-start.4 = (s32[768,384]{1,0:T(8,128)S(1)}, s32[768,384]{1,0:T(8,128)}, u32[]{:S(2)}) copy-start(s32[768,384]{1,0:T(8,128)} %param.18) | copy-start | bytes 3538948
  122.4 8.1 %copy-start.15 = (f32[48,16]{1,0:T(8,128)S(1)}, f32[48,16]{1,0:T(8,128)}, u32[]{:S(2)}) copy-start(f32[48,16]{1,0:T(8,128)} %copy.52) | copy-start | bytes 9220
  122.4 8.1 %copy-start.16 = (f32[48,16]{1,0:T(8,128)S(1)}, f32[48,16]{1,0:T(8,128)}, u32[]{:S(2)}) copy-start(f32[48,16]{1,0:T(8,128)} %copy.53) | copy-start | bytes 9220
  122.8 8.0 %copy-start.13 = (f32[16,384]{1,0:T(8,128)S(1)}, f32[16,384]{1,0:T(8,128)}, u32[]{:S(2)}) copy-start(f32[16,384]{1,0:T(8,128)} %get-tuple-element.65) | copy-start | bytes 73732
  122.8 8.0 %copy-start.14 = (f32[16,384]{1,0:T(8,128)S(1)}, f32[16,384]{1,0:T(8,128)}, u32[]{:S(2)}) copy-start(f32[16,384]{1,0:T(8,128)} %get-tuple-element.66) | copy-start | bytes 73732
  123.2 24.6 %collective-permute-start.8 = (bf16[128,768]{1,0:T(8,128)(2,1)}, bf16[128,768]{1,0:T(8,128)(2,1)S(1)}, u32[]{:S(2)}, u32[]{:S(2)}) collective-permute-start(bf16[128,768]{1,0:T(8,128)(2,1)} %get-tuple-element.35), channel_id=1, source_target_pairs={{0,1},{1,2},{3,0},{4,5},{5,6},{7,4},{8,9},{9,10},{11,8},{12,13},{1... | collective-permute-start | bytes 589832 | tf_op jit(solution)/shard_map/ppermute | solution.py:234
  125.7 22.1 %collective-permute-start.9 = (bf16[128,768]{1,0:T(8,128)(2,1)S(1)}, bf16[128,768]{1,0:T(8,128)(2,1)S(1)}, u32[]{:S(2)}, u32[]{:S(2)}) collective-permute-start(bf16[128,768]{1,0:T(8,128)(2,1)S(1)} %copy-done.12), channel_id=1, source_target_pairs={{0,2},{2,0},{3,1},{4,6},{6,4},{7,5},{8,10},{10,8},{11,9},{12,14},{... | collective-permute-start | bytes 589832 | tf_op jit(solution)/shard_map/ppermute | solution.py:234
  127.0 18.6 %collective-permute-start.6 = (bf16[128,768]{1,0:T(8,128)(2,1)}, bf16[128,768]{1,0:T(8,128)(2,1)S(1)}, u32[]{:S(2)}, u32[]{:S(2)}) collective-permute-start(bf16[128,768]{1,0:T(8,128)(2,1)} %get-tuple-element.37), channel_id=1, source_target_pairs={{1,0},{2,1},{3,2},{5,4},{6,5},{7,6},{9,8},{10,9},{11,10},{13,12},{... | collective-permute-start | bytes 589832 | tf_op jit(solution)/shard_map/ppermute | solution.py:234
  134.8 12.8 %slice-start = ((f32[48,16,384]{2,1,0:T(8,128)}), f32[16,16,384]{2,1,0:T(8,128)S(1)}, s32[]{:S(2)}) async-start(f32[48,16,384]{2,1,0:T(8,128)} %copy-done.2), calls=%async_computation.3 | async-start | bytes 786432 | tf_op jit(solution)/shard_map/slice | solution.py:440
  134.8 12.8 %copy-start.5 = (bf16[48,16,768]{2,1,0:T(8,128)(2,1)S(1)}, bf16[48,16,768]{2,1,0:T(8,128)(2,1)}, u32[]{:S(2)}) copy-start(bf16[48,16,768]{2,1,0:T(8,128)(2,1)} %param.19) | copy-start | bytes 3538948
  145.6 11.2 %collective-permute-start.7 = (bf16[384,768]{1,0:T(8,128)(2,1)S(1)}, bf16[384,768]{1,0:T(8,128)(2,1)S(1)}, u32[]{:S(2)}, u32[]{:S(2)}) collective-permute-start(bf16[384,768]{1,0:T(8,128)(2,1)S(1)} %convert_element_type.130), channel_id=1, source_target_pairs={{4,16},{12,24},{16,4},{24,12},{5,17},{13,25},{17,5},{25,13},{6,18}... | collective-permute-start | bytes 1769480 | tf_op jit(solution)/shard_map/ppermute | solution.py:400
  (13 other events, 43.7 us)

commit v16 on v15

--- a/solution.py
+++ b/solution.py
@@ -389,16 +389,19 @@
     for c, each in enumerate(sizes):
         if not mirrored:
             break
-        for block in arrived[c]:
-            sums[c] = sums[c] + block[: each * planes].astype(jnp.float32)
         over = [(b, block) for b, block in enumerate(roles[c]) if b != block]
         if over:
             if c + 1 < len(sizes):
-                sums[c], arrived[c + 1][2] = lax.optimization_barrier(
-                    (sums[c], arrived[c + 1][2])
+                arrived[c][1], *arrived[-1] = lax.optimization_barrier(
+                    (arrived[c][1], *arrived[-1])
                 )
+            for block in arrived[c]:
+                sums[c] = sums[c] + block[: each * planes].astype(jnp.float32)
             handed = lax.ppermute(sums[c].astype(jnp.bfloat16), "batch", over)
             sums[c] = jnp.where(blocks[c] == batch, sums[c], handed.astype(jnp.float32))
+            continue
+        for block in arrived[c]:
+            sums[c] = sums[c] + block[: each * planes].astype(jnp.float32)
 
     meta_all = [meta_layer]
     if mirrored:

time: 159 us -> 163 us (1.025)
  the two profiles are of different devices: /device:TPU:11 before, /device:TPU:1 now
where the time goes in v16:
time: 163 us; the launch traced here: 162 us
  waiting for transfers between devices  58.9 us (36%)
  starting transfers between devices  53.8 us (33%)
  Pallas kernels  28.3 us (17%)
  other arithmetic  10.8 us (7%)
  local copies, waits for them, and re-layouts  7.49 us (5%)
  matrix products  2.2 us (1%)
    ppermute x9, waiting for transfers between devices, slab_exchange(): arrived.append(lax.ppermute(block, ('batch', 'slab'), perm))  47.5 us
    ppermute x9, starting transfers between devices, slab_exchange(): arrived.append(lax.ppermute(block, ('batch', 'slab'), perm))  34.4 us
    pallas_call x3, Pallas kernels, per_device(): pl.pallas_call(functools.partial(spectrum_kernel, runs, with_meta), out_s...  20.4 us
    all_to_all x3, starting transfers between devices, per_device(): received.append(lax.all_to_all(send, 'batch', 0, 0, tiled=True))  17.4 us
    pallas_call x3, Pallas kernels, per_device(): pl.pallas_call(functools.partial(insert_kernel, bins, meta_at), out_shape...  7.88 us
    ppermute x1, waiting for transfers between devices, per_device(): handed = lax.ppermute(sums[c].astype(jnp.bfloat16), 'batch', over)  7.75 us
    unnamed x50, local copies, waits for them, and re-layouts  4.43 us
    select_n x3, other arithmetic, choose(): chosen = jnp.where(index == d, parts[d], chosen)  4.35 us
  transfers between devices with their start and end apart: 13, of which 9 were waited for; matrix products, arithmetic and copies ran while one was open for 8% of the time, Pallas kernels for 13%

profile of v16, /device:TPU:1, one launch (start us, length us, event | category | flops | bytes accessed | tf_op | source)
XLA Modules:
  0.0 162.1 jit_solution(7197584352289135402)
XLA Ops:
  0.0 6.8 %spectrum.3 = bf16[8,144,768]{2,1,0:T(8,128)(2,1)} custom-call(s32[8]{0:T(128)} %classes.5, s32[2,8]{1,0:T(2,128)} %bitcast.91, s32[8]{0:T(128)} %defocus_class.5, f32[16]{0:T(128)} %defocus.5, s32[4,8]{1,0:T(4,128)} %bitcast.88, bf16[8,384,384]{2,1,0:T(8,128)(2,1)} %images_in.5, bf16[256,384]{1,0:T(8,128)(2,1)} %constant.188.clone.left_in, ...), custom_call_target="tpu_custom_call" | custom-call | tf_op jit(solution)/shard_map/spectrum/pallas_call | solution.py:280
  6.8 5.2 %all-to-all-start = ((bf16[8,144,768]{2,1,0:T(8,128)(2,1)}), bf16[8,144,768]{2,1,0:T(8,128)(2,1)S(1)}, u32[]{:S(2)}, u32[]{:S(2)}) async-start(bf16[8,144,768]{2,1,0:T(8,128)(2,1)} %spectrum.3), calls=%async_computation | async-start | bytes 3538944 | tf_op jit(solution)/shard_map/all_to_all | solution.py:308
  13.5 5.3 %spectrum.5 = bf16[8,64,768]{2,1,0:T(8,128)(2,1)} custom-call(s32[8]{0:T(128)} %classes.5, s32[2,8]{1,0:T(2,128)} %bitcast.92, s32[8]{0:T(128)} %defocus_class.5, f32[16]{0:T(128)} %defocus.5, s32[4,8]{1,0:T(4,128)} %bitcast.89, bf16[8,384,384]{2,1,0:T(8,128)(2,1)} %images_in.5, bf16[128,384]{1,0:T(8,128)(2,1)} %constant.190.clone.left_in, ...), custom_call_target="tpu_custom_call" | custom-call | tf_op jit(solution)/shard_map/spectrum/pallas_call | solution.py:280
  18.8 8.4 %spectrum.4 = bf16[8,192,768]{2,1,0:T(8,128)(2,1)} custom-call(s32[8]{0:T(128)} %classes.5, s32[2,8]{1,0:T(2,128)} %bitcast.93, s32[8]{0:T(128)} %defocus_class.5, f32[16]{0:T(128)} %defocus.5, s32[4,8]{1,0:T(4,128)} %bitcast.90, bf16[8,384,384]{2,1,0:T(8,128)(2,1)} %images_in.5, bf16[384,384]{1,0:T(8,128)(2,1)} %constant.189.clone.left_in, ...), custom_call_target="tpu_custom_call" | custom-call | tf_op jit(solution)/shard_map/spectrum/pallas_call | solution.py:280
  28.1 3.6 %all-to-all-done.received = bf16[8,144,768]{2,1,0:T(8,128)(2,1)S(1)} async-done(((bf16[8,144,768]{2,1,0:T(8,128)(2,1)}), bf16[8,144,768]{2,1,0:T(8,128)(2,1)S(1)}, u32[]{:S(2)}, u32[]{:S(2)}) %all-to-all-start) | async-done | bytes 1769504 | tf_op jit(solution)/shard_map/all_to_all | solution.py:308
  31.7 7.7 %all-to-all-start.1 = ((bf16[8,192,768]{2,1,0:T(8,128)(2,1)}), bf16[8,192,768]{2,1,0:T(8,128)(2,1)}, u32[]{:S(2)}, u32[]{:S(2)}) async-start(bf16[8,192,768]{2,1,0:T(8,128)(2,1)} %spectrum.4), calls=%async_computation.1 | async-start | bytes 4718592 | tf_op jit(solution)/shard_map/all_to_all | solution.py:308
  43.0 3.2 %collective-permute-start = (bf16[272,768]{1,0:T(8,128)(2,1)S(1)}, bf16[272,768]{1,0:T(8,128)(2,1)S(1)}, u32[]{:S(2)}, u32[]{:S(2)}) collective-permute-start(bf16[272,768]{1,0:T(8,128)(2,1)S(1)} %get-tuple-element.39), channel_id=1, source_target_pairs={{0,1},{1,2},{3,0},{4,5},{5,6},{7,4},{8,9},{9,10},{11,8},{12,13},{1... | collective-permute-start | bytes 1253384 | tf_op jit(solution)/shard_map/ppermute | solution.py:234
  48.1 5.0 %collective-permute-start.2 = (bf16[272,768]{1,0:T(8,128)(2,1)}, bf16[272,768]{1,0:T(8,128)(2,1)S(1)}, u32[]{:S(2)}, u32[]{:S(2)}) collective-permute-start(bf16[272,768]{1,0:T(8,128)(2,1)} %get-tuple-element.38), channel_id=1, source_target_pairs={{0,2},{2,0},{3,1},{4,6},{6,4},{7,5},{8,10},{10,8},{11,9},{12,14},{... | collective-permute-start | bytes 1253384 | tf_op jit(solution)/shard_map/ppermute | solution.py:234
  53.1 4.6 %collective-permute-done = bf16[272,768]{1,0:T(8,128)(2,1)S(1)} collective-permute-done((bf16[272,768]{1,0:T(8,128)(2,1)S(1)}, bf16[272,768]{1,0:T(8,128)(2,1)S(1)}, u32[]{:S(2)}, u32[]{:S(2)}) %collective-permute-start) | collective-permute-done | bytes 417824 | tf_op jit(solution)/shard_map/ppermute | solution.py:234
  57.6 9.7 %collective-permute-done.1 = bf16[272,768]{1,0:T(8,128)(2,1)S(1)} collective-permute-done((bf16[272,768]{1,0:T(8,128)(2,1)S(1)}, bf16[272,768]{1,0:T(8,128)(2,1)S(1)}, u32[]{:S(2)}, u32[]{:S(2)}) %collective-permute-start.1) | collective-permute-done | bytes 417824 | tf_op jit(solution)/shard_map/ppermute | solution.py:234
  68.8 4.5 %all-to-all-start.2 = ((bf16[8,64,768]{2,1,0:T(8,128)(2,1)}), bf16[8,64,768]{2,1,0:T(8,128)(2,1)}, u32[]{:S(2)}, u32[]{:S(2)}) async-start(bf16[8,64,768]{2,1,0:T(8,128)(2,1)} %spectrum.5), calls=%async_computation.2 | async-start | bytes 1572864 | tf_op jit(solution)/shard_map/all_to_all | solution.py:308
  73.3 4.6 %insert.4 = bf16[3,384,768]{2,1,0:T(8,128)(2,1)S(1)} custom-call(bf16[8,192,768]{2,1,0:T(8,128)(2,1)} %all-to-all-done.1.received, s32[1,1536]{1,0:T(1,128)S(1)} %reshape_reshape.6.codes), custom_call_target="tpu_custom_call" | custom-call | tf_op jit(solution)/shard_map/insert/pallas_call | solution.py:366
  79.4 5.8 %collective-permute-start.3 = (bf16[384,768]{1,0:T(8,128)(2,1)}, bf16[384,768]{1,0:T(8,128)(2,1)}, u32[]{:S(2)}, u32[]{:S(2)}) collective-permute-start(bf16[384,768]{1,0:T(8,128)(2,1)} %get-tuple-element.36), channel_id=1, source_target_pairs={{0,1},{1,2},{3,0},{7,6},{6,5},{4,7},{8,9},{9,10},{11,8},{15,14},{1... | collective-permute-start | bytes 1769480 | tf_op jit(solution)/shard_map/ppermute | solution.py:234
  85.2 2.1 %collective-permute-start.4 = (bf16[384,768]{1,0:T(8,128)(2,1)}, bf16[384,768]{1,0:T(8,128)(2,1)}, u32[]{:S(2)}, u32[]{:S(2)}) collective-permute-start(bf16[384,768]{1,0:T(8,128)(2,1)} %get-tuple-element.37), channel_id=1, source_target_pairs={{1,0},{2,1},{3,2},{6,7},{5,6},{4,5},{9,8},{10,9},{11,10},{14,15},{... | collective-permute-start | bytes 1769480 | tf_op jit(solution)/shard_map/ppermute | solution.py:234
  87.6 3.2 %collective-permute-start.5 = (bf16[384,768]{1,0:T(8,128)(2,1)}, bf16[384,768]{1,0:T(8,128)(2,1)}, u32[]{:S(2)}, u32[]{:S(2)}) collective-permute-start(bf16[384,768]{1,0:T(8,128)(2,1)} %get-tuple-element.35), channel_id=1, source_target_pairs={{0,2},{2,0},{3,1},{7,5},{5,7},{4,6},{8,10},{10,8},{11,9},{15,13},{... | collective-permute-start | bytes 1769480 | tf_op jit(solution)/shard_map/ppermute | solution.py:234
  90.7 7.0 %collective-permute-done.3 = bf16[384,768]{1,0:T(8,128)(2,1)} collective-permute-done((bf16[384,768]{1,0:T(8,128)(2,1)}, bf16[384,768]{1,0:T(8,128)(2,1)}, u32[]{:S(2)}, u32[]{:S(2)}) %collective-permute-start.3) | collective-permute-done | bytes 589856 | tf_op jit(solution)/shard_map/ppermute | solution.py:234
  97.7 12.2 %collective-permute-done.4 = bf16[384,768]{1,0:T(8,128)(2,1)} collective-permute-done((bf16[384,768]{1,0:T(8,128)(2,1)}, bf16[384,768]{1,0:T(8,128)(2,1)}, u32[]{:S(2)}, u32[]{:S(2)}) %collective-permute-start.4) | collective-permute-done | bytes 589856 | tf_op jit(solution)/shard_map/ppermute | solution.py:234
  112.8 2.1 %select_bitcast_fusion.6 = (bf16[128,768]{1,0:T(8,128)(2,1)}, bf16[128,768]{1,0:T(8,128)(2,1)}, bf16[128,768]{1,0:T(8,128)(2,1)}) fusion(pred[]{:T(512)S(6)} %eq.282, pred[]{:T(512)S(6)} %eq.281, bf16[3,128,768]{2,1,0:T(8,128)(2,1)} %copy-done, pred[]{:T(512)S(6)} %eq.280, pred[]{:T(512)S(6)} %eq.279, pred[]{:T(512)S(6)} %eq.284, pred[]{:T(512)S(6)} %eq.283), kind=kLoop, calls=%fused_computation.46 | loop fusion | flops 589824 | bytes 1179654 | tf_op jit(solution)/shard_map/jit(_where)/select_n | solution.py:241
  118.7 10.1 %collective-permute-start.6 = (bf16[128,768]{1,0:T(8,128)(2,1)}, bf16[128,768]{1,0:T(8,128)(2,1)S(1)}, u32[]{:S(2)}, u32[]{:S(2)}) collective-permute-start(bf16[128,768]{1,0:T(8,128)(2,1)} %get-tuple-element.42), channel_id=1, source_target_pairs={{0,1},{1,2},{3,0},{4,5},{5,6},{7,4},{8,9},{9,10},{11,8},{12,13},{1... | collective-permute-start | bytes 589832 | tf_op jit(solution)/shard_map/ppermute | solution.py:234
  128.7 2.5 %collective-permute-start.7 = (bf16[128,768]{1,0:T(8,128)(2,1)S(1)}, bf16[128,768]{1,0:T(8,128)(2,1)S(1)}, u32[]{:S(2)}, u32[]{:S(2)}) collective-permute-start(bf16[128,768]{1,0:T(8,128)(2,1)S(1)} %copy-done.12), channel_id=1, source_target_pairs={{0,2},{2,0},{3,1},{4,6},{6,4},{7,5},{8,10},{10,8},{11,9},{12,14},{... | collective-permute-start | bytes 589832 | tf_op jit(solution)/shard_map/ppermute | solution.py:234
  133.8 4.3 %collective-permute-done.6 = bf16[128,768]{1,0:T(8,128)(2,1)S(1)} collective-permute-done((bf16[128,768]{1,0:T(8,128)(2,1)}, bf16[128,768]{1,0:T(8,128)(2,1)S(1)}, u32[]{:S(2)}, u32[]{:S(2)}) %collective-permute-start.6) | collective-permute-done | bytes 196640 | tf_op jit(solution)/shard_map/ppermute | solution.py:234
  138.2 8.3 %collective-permute-done.7 = bf16[128,768]{1,0:T(8,128)(2,1)S(1)} collective-permute-done((bf16[128,768]{1,0:T(8,128)(2,1)S(1)}, bf16[128,768]{1,0:T(8,128)(2,1)S(1)}, u32[]{:S(2)}, u32[]{:S(2)}) %collective-permute-start.7) | collective-permute-done | bytes 196640 | tf_op jit(solution)/shard_map/ppermute | solution.py:234
  146.5 1.9 %fusion.80 = (bf16[384,768]{1,0:T(8,128)(2,1)S(1)}, f32[384,768]{1,0:T(8,128)S(1)}) fusion(bf16[384,768]{1,0:T(8,128)(2,1)} %collective-permute-done.4, bf16[384,768]{1,0:T(8,128)(2,1)} %collective-permute-done.5, bf16[384,768]{1,0:T(8,128)(2,1)} %collective-permute-done.3, bf16[3,384,768]{2,1,0:T(8,128)(2,1)S(1)} %insert.4, pred[]{:T(512)S(6)} %eq.304, ...), kind=kLoop, calls=%fused_computation.179 | loop fusion | flops 3244032 | bytes 5308419 | tf_op jit(solution)/shard_map/convert_element_type | solution.py:400
  151.9 7.8 %collective-permute-done.9 = bf16[384,768]{1,0:T(8,128)(2,1)S(1)} collective-permute-done((bf16[384,768]{1,0:T(8,128)(2,1)S(1)}, bf16[384,768]{1,0:T(8,128)(2,1)S(1)}, u32[]{:S(2)}, u32[]{:S(2)}) %collective-permute-start.9) | collective-permute-done | bytes 589856 | tf_op jit(solution)/shard_map/ppermute | solution.py:400
  (121 shorter events, 25.8 us)
Async XLA Ops:
  6.8 24.9 %all-to-all-start = ((bf16[8,144,768]{2,1,0:T(8,128)(2,1)}), bf16[8,144,768]{2,1,0:T(8,128)(2,1)S(1)}, u32[]{:S(2)}, u32[]{:S(2)}) async-start(bf16[8,144,768]{2,1,0:T(8,128)(2,1)} %spectrum.3), calls=%async_computation | async-start | bytes 3538944 | tf_op jit(solution)/shard_map/all_to_all | solution.py:308
  28.1 11.7 %copy-start.3 = (s32[768,384]{1,0:T(8,128)S(1)}, s32[768,384]{1,0:T(8,128)}, u32[]{:S(2)}) copy-start(s32[768,384]{1,0:T(8,128)} %param.18) | copy-start | bytes 3538948
  31.7 37.1 %all-to-all-start.1 = ((bf16[8,192,768]{2,1,0:T(8,128)(2,1)}), bf16[8,192,768]{2,1,0:T(8,128)(2,1)}, u32[]{:S(2)}, u32[]{:S(2)}) async-start(bf16[8,192,768]{2,1,0:T(8,128)(2,1)} %spectrum.4), calls=%async_computation.1 | async-start | bytes 4718592 | tf_op jit(solution)/shard_map/all_to_all | solution.py:308
  43.0 14.6 %collective-permute-start = (bf16[272,768]{1,0:T(8,128)(2,1)S(1)}, bf16[272,768]{1,0:T(8,128)(2,1)S(1)}, u32[]{:S(2)}, u32[]{:S(2)}) collective-permute-start(bf16[272,768]{1,0:T(8,128)(2,1)S(1)} %get-tuple-element.39), channel_id=1, source_target_pairs={{0,1},{1,2},{3,0},{4,5},{5,6},{7,4},{8,9},{9,10},{11,8},{12,13},{1... | collective-permute-start | bytes 1253384 | tf_op jit(solution)/shard_map/ppermute | solution.py:234
  46.2 21.1 %collective-permute-start.1 = (bf16[272,768]{1,0:T(8,128)(2,1)S(1)}, bf16[272,768]{1,0:T(8,128)(2,1)S(1)}, u32[]{:S(2)}, u32[]{:S(2)}) collective-permute-start(bf16[272,768]{1,0:T(8,128)(2,1)S(1)} %get-tuple-element.40), channel_id=1, source_target_pairs={{1,0},{2,1},{3,2},{5,4},{6,5},{7,6},{9,8},{10,9},{11,10},{13,12},{... | collective-permute-start | bytes 1253384 | tf_op jit(solution)/shard_map/ppermute | solution.py:234
  48.1 39.5 %collective-permute-start.2 = (bf16[272,768]{1,0:T(8,128)(2,1)}, bf16[272,768]{1,0:T(8,128)(2,1)S(1)}, u32[]{:S(2)}, u32[]{:S(2)}) collective-permute-start(bf16[272,768]{1,0:T(8,128)(2,1)} %get-tuple-element.38), channel_id=1, source_target_pairs={{0,2},{2,0},{3,1},{4,6},{6,4},{7,5},{8,10},{10,8},{11,9},{12,14},{... | collective-permute-start | bytes 1253384 | tf_op jit(solution)/shard_map/ppermute | solution.py:234
  57.6 11.2 %copy-start.6 = (bf16[272,768]{1,0:T(8,128)(2,1)}, bf16[272,768]{1,0:T(8,128)(2,1)S(1)}, u32[]{:S(2)}) copy-start(bf16[272,768]{1,0:T(8,128)(2,1)S(1)} %collective-permute-done) | copy-start | bytes 1253380
  68.8 41.1 %all-to-all-start.2 = ((bf16[8,64,768]{2,1,0:T(8,128)(2,1)}), bf16[8,64,768]{2,1,0:T(8,128)(2,1)}, u32[]{:S(2)}, u32[]{:S(2)}) async-start(bf16[8,64,768]{2,1,0:T(8,128)(2,1)} %spectrum.5), calls=%async_computation.2 | async-start | bytes 1572864 | tf_op jit(solution)/shard_map/all_to_all | solution.py:308
  77.9 9.6 %copy-start.17 = (s32[64,5]{0,1:T(8,128)S(1)}, s32[64,5]{0,1:T(8,128)}, u32[]{:S(2)}) copy-start(s32[64,5]{0,1:T(8,128)} %copy.59) | copy-start | bytes 3844
  79.4 18.4 %collective-permute-start.3 = (bf16[384,768]{1,0:T(8,128)(2,1)}, bf16[384,768]{1,0:T(8,128)(2,1)}, u32[]{:S(2)}, u32[]{:S(2)}) collective-permute-start(bf16[384,768]{1,0:T(8,128)(2,1)} %get-tuple-element.36), channel_id=1, source_target_pairs={{0,1},{1,2},{3,0},{7,6},{6,5},{4,7},{8,9},{9,10},{11,8},{15,14},{1... | collective-permute-start | bytes 1769480 | tf_op jit(solution)/shard_map/ppermute | solution.py:234
  85.2 24.7 %collective-permute-start.4 = (bf16[384,768]{1,0:T(8,128)(2,1)}, bf16[384,768]{1,0:T(8,128)(2,1)}, u32[]{:S(2)}, u32[]{:S(2)}) collective-permute-start(bf16[384,768]{1,0:T(8,128)(2,1)} %get-tuple-element.37), channel_id=1, source_target_pairs={{1,0},{2,1},{3,2},{6,7},{5,6},{4,5},{9,8},{10,9},{11,10},{14,15},{... | collective-permute-start | bytes 1769480 | tf_op jit(solution)/shard_map/ppermute | solution.py:234
  87.6 27.3 %copy-start.10 = (bf16[272,768]{1,0:T(8,128)(2,1)}, bf16[272,768]{1,0:T(8,128)(2,1)S(1)}, u32[]{:S(2)}) copy-start(bf16[272,768]{1,0:T(8,128)(2,1)S(1)} %collective-permute-done.2) | copy-start | bytes 1253380
  87.6 28.7 %collective-permute-start.5 = (bf16[384,768]{1,0:T(8,128)(2,1)}, bf16[384,768]{1,0:T(8,128)(2,1)}, u32[]{:S(2)}, u32[]{:S(2)}) collective-permute-start(bf16[384,768]{1,0:T(8,128)(2,1)} %get-tuple-element.35), channel_id=1, source_target_pairs={{0,2},{2,0},{3,1},{7,5},{5,7},{4,6},{8,10},{10,8},{11,9},{15,13},{... | collective-permute-start | bytes 1769480 | tf_op jit(solution)/shard_map/ppermute | solution.py:234
  116.5 12.2 %copy-start.12 = (bf16[128,768]{1,0:T(8,128)(2,1)S(1)}, bf16[128,768]{1,0:T(8,128)(2,1)}, u32[]{:S(2)}) copy-start(bf16[128,768]{1,0:T(8,128)(2,1)} %get-tuple-element.43) | copy-start | bytes 589828
  116.5 14.7 %copy-start.15 = (f32[48,16]{1,0:T(8,128)S(1)}, f32[48,16]{1,0:T(8,128)}, u32[]{:S(2)}) copy-start(f32[48,16]{1,0:T(8,128)} %copy.52) | copy-start | bytes 9220
  116.5 14.7 %copy-start.16 = (f32[48,16]{1,0:T(8,128)S(1)}, f32[48,16]{1,0:T(8,128)}, u32[]{:S(2)}) copy-start(f32[48,16]{1,0:T(8,128)} %copy.53) | copy-start | bytes 9220
  116.9 14.6 %copy-start.13 = (f32[16,384]{1,0:T(8,128)S(1)}, f32[16,384]{1,0:T(8,128)}, u32[]{:S(2)}) copy-start(f32[16,384]{1,0:T(8,128)} %get-tuple-element.71) | copy-start | bytes 73732
  117.0 14.6 %copy-start.14 = (f32[16,384]{1,0:T(8,128)S(1)}, f32[16,384]{1,0:T(8,128)}, u32[]{:S(2)}) copy-start(f32[16,384]{1,0:T(8,128)} %get-tuple-element.72) | copy-start | bytes 73732
  117.4 16.5 %collective-permute-start.8 = (bf16[128,768]{1,0:T(8,128)(2,1)}, bf16[128,768]{1,0:T(8,128)(2,1)S(1)}, u32[]{:S(2)}, u32[]{:S(2)}) collective-permute-start(bf16[128,768]{1,0:T(8,128)(2,1)} %get-tuple-element.41), channel_id=1, source_target_pairs={{1,0},{2,1},{3,2},{5,4},{6,5},{7,6},{9,8},{10,9},{11,10},{13,12},{... | collective-permute-start | bytes 589832 | tf_op jit(solution)/shard_map/ppermute | solution.py:234
  118.7 19.5 %collective-permute-start.6 = (bf16[128,768]{1,0:T(8,128)(2,1)}, bf16[128,768]{1,0:T(8,128)(2,1)S(1)}, u32[]{:S(2)}, u32[]{:S(2)}) collective-permute-start(bf16[128,768]{1,0:T(8,128)(2,1)} %get-tuple-element.42), channel_id=1, source_target_pairs={{0,1},{1,2},{3,0},{4,5},{5,6},{7,4},{8,9},{9,10},{11,8},{12,13},{1... | collective-permute-start | bytes 589832 | tf_op jit(solution)/shard_map/ppermute | solution.py:234
  128.7 17.8 %collective-permute-start.7 = (bf16[128,768]{1,0:T(8,128)(2,1)S(1)}, bf16[128,768]{1,0:T(8,128)(2,1)S(1)}, u32[]{:S(2)}, u32[]{:S(2)}) collective-permute-start(bf16[128,768]{1,0:T(8,128)(2,1)S(1)} %copy-done.12), channel_id=1, source_target_pairs={{0,2},{2,0},{3,1},{4,6},{6,4},{7,5},{8,10},{10,8},{11,9},{12,14},{... | collective-permute-start | bytes 589832 | tf_op jit(solution)/shard_map/ppermute | solution.py:234
  133.8 16.5 %copy-start.5 = (bf16[48,16,768]{2,1,0:T(8,128)(2,1)S(1)}, bf16[48,16,768]{2,1,0:T(8,128)(2,1)}, u32[]{:S(2)}) copy-start(bf16[48,16,768]{2,1,0:T(8,128)(2,1)} %param.19) | copy-start | bytes 3538948
  133.8 16.5 %slice-start = ((f32[48,16,384]{2,1,0:T(8,128)}), f32[16,16,384]{2,1,0:T(8,128)S(1)}, s32[]{:S(2)}) async-start(f32[48,16,384]{2,1,0:T(8,128)} %copy-done.2), calls=%async_computation.3 | async-start | bytes 786432 | tf_op jit(solution)/shard_map/slice | solution.py:443
  148.4 11.2 %collective-permute-start.9 = (bf16[384,768]{1,0:T(8,128)(2,1)S(1)}, bf16[384,768]{1,0:T(8,128)(2,1)S(1)}, u32[]{:S(2)}, u32[]{:S(2)}) collective-permute-start(bf16[384,768]{1,0:T(8,128)(2,1)S(1)} %get-tuple-element.33), channel_id=1, source_target_pairs={{4,16},{12,24},{16,4},{24,12},{5,17},{13,25},{17,5},{25,13},{6,18}... | collective-permute-start | bytes 1769480 | tf_op jit(solution)/shard_map/ppermute | solution.py:400
  (13 other events, 37.7 us)

commit v17 on v15

--- a/solution.py
+++ b/solution.py
@@ -11,7 +11,7 @@
 
 TAU_PRIOR = 4.0
 PHASE_OFFSET = 0.1
-CHUNKS = ((2, False), (3, True), (1, False))
+CHUNKS = ((1, False), (2, True), (3, False))
 SHARES = 6
 META_BASE = 32
 META_ROWS = 16

time: 159 us -> 173 us (1.088)
  the two profiles are of different devices: /device:TPU:11 before, /device:TPU:17 now
where the time goes in v17:
time: 173 us
  waiting for transfers between devices  74.5 us (43%)
  starting transfers between devices  49.3 us (28%)
  Pallas kernels  27 us (16%)
  other arithmetic  9.75 us (6%)
  local copies, waits for them, and re-layouts  6.34 us (4%)
  matrix products  5.15 us (3%)
    ppermute x9, waiting for transfers between devices, slab_exchange(): arrived.append(lax.ppermute(block, ('batch', 'slab'), perm))  55.6 us
    ppermute x9, starting transfers between devices, slab_exchange(): arrived.append(lax.ppermute(block, ('batch', 'slab'), perm))  23.7 us
    pallas_call x3, Pallas kernels, per_device(): pl.pallas_call(functools.partial(spectrum_kernel, runs, with_meta), out_s...  20.4 us
    all_to_all x3, starting transfers between devices, per_device(): received.append(lax.all_to_all(send, 'batch', 0, 0, tiled=True))  16.3 us
    all_to_all x3, waiting for transfers between devices, per_device(): received.append(lax.all_to_all(send, 'batch', 0, 0, tiled=True))  14.3 us
    ppermute x1, starting transfers between devices, per_device(): handed = lax.ppermute(sums[c].astype(jnp.bfloat16), 'batch', over)  9.2 us
    pallas_call x3, Pallas kernels, per_device(): pl.pallas_call(functools.partial(insert_kernel, bins, meta_at), out_shape...  6.6 us
    ppermute x1, waiting for transfers between devices, per_device(): handed = lax.ppermute(sums[c].astype(jnp.bfloat16), 'batch', over)  4.62 us
  transfers between devices with their start and end apart: 13, of which 6 were waited for; matrix products, arithmetic and copies ran while one was open for 10% of the time, Pallas kernels for 13%

profile of v17, /device:TPU:17, one launch (start us, length us, event | category | flops | bytes accessed | tf_op | source)
XLA Modules:
  0.0 172.6 jit_solution(13041607436604194643)
XLA Ops:
  0.0 5.3 %spectrum.3 = bf16[8,80,768]{2,1,0:T(8,128)(2,1)} custom-call(s32[8]{0:T(128)} %classes.5, s32[2,8]{1,0:T(2,128)} %bitcast.90, s32[8]{0:T(128)} %defocus_class.5, f32[16]{0:T(128)} %defocus.5, s32[4,8]{1,0:T(4,128)} %bitcast.87, bf16[8,384,384]{2,1,0:T(8,128)(2,1)} %images_in.5, bf16[128,384]{1,0:T(8,128)(2,1)} %constant.188.clone.left_in, ...), custom_call_target="tpu_custom_call" | custom-call | tf_op jit(solution)/shard_map/spectrum/pallas_call | solution.py:280
  5.3 4.4 %all-to-all-start = ((bf16[8,80,768]{2,1,0:T(8,128)(2,1)}), bf16[8,80,768]{2,1,0:T(8,128)(2,1)S(1)}, u32[]{:S(2)}, u32[]{:S(2)}) async-start(bf16[8,80,768]{2,1,0:T(8,128)(2,1)} %spectrum.3), calls=%async_computation | async-start | bytes 1966080 | tf_op jit(solution)/shard_map/all_to_all | solution.py:308
  11.3 6.7 %spectrum.4 = bf16[8,128,768]{2,1,0:T(8,128)(2,1)} custom-call(s32[8]{0:T(128)} %classes.5, s32[2,8]{1,0:T(2,128)} %bitcast.91, s32[8]{0:T(128)} %defocus_class.5, f32[16]{0:T(128)} %defocus.5, s32[4,8]{1,0:T(4,128)} %bitcast.88, bf16[8,384,384]{2,1,0:T(8,128)(2,1)} %images_in.5, bf16[256,384]{1,0:T(8,128)(2,1)} %constant.189.clone.left_in, ...), custom_call_target="tpu_custom_call" | custom-call | tf_op jit(solution)/shard_map/spectrum/pallas_call | solution.py:280
  17.9 8.4 %spectrum.5 = bf16[8,192,768]{2,1,0:T(8,128)(2,1)} custom-call(s32[8]{0:T(128)} %classes.5, s32[2,8]{1,0:T(2,128)} %bitcast.92, s32[8]{0:T(128)} %defocus_class.5, f32[16]{0:T(128)} %defocus.5, s32[4,8]{1,0:T(4,128)} %bitcast.89, bf16[8,384,384]{2,1,0:T(8,128)(2,1)} %images_in.5, bf16[384,384]{1,0:T(8,128)(2,1)} %constant.190.clone.left_in, ...), custom_call_target="tpu_custom_call" | custom-call | tf_op jit(solution)/shard_map/spectrum/pallas_call | solution.py:280
  27.2 4.2 %all-to-all-start.1 = ((bf16[8,128,768]{2,1,0:T(8,128)(2,1)}), bf16[8,128,768]{2,1,0:T(8,128)(2,1)S(1)}, u32[]{:S(2)}, u32[]{:S(2)}) async-start(bf16[8,128,768]{2,1,0:T(8,128)(2,1)} %spectrum.4), calls=%async_computation.1 | async-start | bytes 3145728 | tf_op jit(solution)/shard_map/all_to_all | solution.py:308
  31.8 1.5 fusion.6
  34.7 14.3 %all-to-all-done.1.received = bf16[8,128,768]{2,1,0:T(8,128)(2,1)S(1)} async-done(((bf16[8,128,768]{2,1,0:T(8,128)(2,1)}), bf16[8,128,768]{2,1,0:T(8,128)(2,1)S(1)}, u32[]{:S(2)}, u32[]{:S(2)}) %all-to-all-start.1) | async-done | bytes 1572896 | tf_op jit(solution)/shard_map/all_to_all | solution.py:308
  49.0 7.7 %all-to-all-start.2 = ((bf16[8,192,768]{2,1,0:T(8,128)(2,1)}), bf16[8,192,768]{2,1,0:T(8,128)(2,1)}, u32[]{:S(2)}, u32[]{:S(2)}) async-start(bf16[8,192,768]{2,1,0:T(8,128)(2,1)} %spectrum.5), calls=%async_computation.2 | async-start | bytes 4718592 | tf_op jit(solution)/shard_map/all_to_all | solution.py:308
  58.8 4.0 %collective-permute-start.1 = (bf16[144,768]{1,0:T(8,128)(2,1)S(1)}, bf16[144,768]{1,0:T(8,128)(2,1)S(1)}, u32[]{:S(2)}, u32[]{:S(2)}) collective-permute-start(bf16[144,768]{1,0:T(8,128)(2,1)S(1)} %get-tuple-element.37), channel_id=1, source_target_pairs={{1,0},{2,1},{3,2},{5,4},{6,5},{7,6},{9,8},{10,9},{11,10},{13,12},{... | collective-permute-start | bytes 663560 | tf_op jit(solution)/shard_map/ppermute | solution.py:234
  63.0 1.9 %collective-permute-start.2 = (bf16[144,768]{1,0:T(8,128)(2,1)}, bf16[144,768]{1,0:T(8,128)(2,1)S(1)}, u32[]{:S(2)}, u32[]{:S(2)}) collective-permute-start(bf16[144,768]{1,0:T(8,128)(2,1)} %get-tuple-element.35), channel_id=1, source_target_pairs={{0,2},{2,0},{3,1},{4,6},{6,4},{7,5},{8,10},{10,8},{11,9},{12,14},{... | collective-permute-start | bytes 663560 | tf_op jit(solution)/shard_map/ppermute | solution.py:234
  66.2 4.6 %collective-permute-done.1 = bf16[144,768]{1,0:T(8,128)(2,1)S(1)} collective-permute-done((bf16[144,768]{1,0:T(8,128)(2,1)S(1)}, bf16[144,768]{1,0:T(8,128)(2,1)S(1)}, u32[]{:S(2)}, u32[]{:S(2)}) %collective-permute-start.1) | collective-permute-done | bytes 221216 | tf_op jit(solution)/shard_map/ppermute | solution.py:234
  71.6 1.4 insert.4
  73.9 4.0 %collective-permute-start.3 = (bf16[256,768]{1,0:T(8,128)(2,1)S(1)}, bf16[256,768]{1,0:T(8,128)(2,1)}, u32[]{:S(2)}, u32[]{:S(2)}) collective-permute-start(bf16[256,768]{1,0:T(8,128)(2,1)S(1)} %get-tuple-element.33), channel_id=1, source_target_pairs={{0,1},{1,2},{3,0},{7,6},{6,5},{4,7},{8,9},{9,10},{11,8},{15,14},{1... | collective-permute-start | bytes 1179656 | tf_op jit(solution)/shard_map/ppermute | solution.py:234
  77.9 1.9 %collective-permute-start.4 = (bf16[256,768]{1,0:T(8,128)(2,1)S(1)}, bf16[256,768]{1,0:T(8,128)(2,1)}, u32[]{:S(2)}, u32[]{:S(2)}) collective-permute-start(bf16[256,768]{1,0:T(8,128)(2,1)S(1)} %get-tuple-element.34), channel_id=1, source_target_pairs={{1,0},{2,1},{3,2},{6,7},{5,6},{4,5},{9,8},{10,9},{11,10},{14,15},{... | collective-permute-start | bytes 1179656 | tf_op jit(solution)/shard_map/ppermute | solution.py:234
  81.2 18.0 %collective-permute-done.3 = bf16[256,768]{1,0:T(8,128)(2,1)} collective-permute-done((bf16[256,768]{1,0:T(8,128)(2,1)S(1)}, bf16[256,768]{1,0:T(8,128)(2,1)}, u32[]{:S(2)}, u32[]{:S(2)}) %collective-permute-start.3) | collective-permute-done | bytes 393248 | tf_op jit(solution)/shard_map/ppermute | solution.py:234
  99.2 4.6 %insert.5 = bf16[3,384,768]{2,1,0:T(8,128)(2,1)S(1)} custom-call(bf16[8,192,768]{2,1,0:T(8,128)(2,1)} %all-to-all-done.2.received, s32[1,1536]{1,0:T(1,128)S(1)} %reshape_reshape.7.codes), custom_call_target="tpu_custom_call" | custom-call | tf_op jit(solution)/shard_map/insert/pallas_call | solution.py:366
  107.3 1.6 copy.51
  110.2 6.1 %collective-permute-start.9 = (bf16[384,768]{1,0:T(8,128)(2,1)S(1)}, bf16[384,768]{1,0:T(8,128)(2,1)S(1)}, u32[]{:S(2)}, u32[]{:S(2)}) collective-permute-start(bf16[384,768]{1,0:T(8,128)(2,1)S(1)} %get-tuple-element.30), channel_id=1, source_target_pairs={{0,2},{2,0},{3,1},{4,6},{6,4},{7,5},{8,10},{10,8},{11,9},{12,14},{... | collective-permute-start | bytes 1769480 | tf_op jit(solution)/shard_map/ppermute | solution.py:234
  116.3 1.9 %collective-permute-start.6 = (bf16[384,768]{1,0:T(8,128)(2,1)}, bf16[384,768]{1,0:T(8,128)(2,1)S(1)}, u32[]{:S(2)}, u32[]{:S(2)}) collective-permute-start(bf16[384,768]{1,0:T(8,128)(2,1)} %get-tuple-element.31), channel_id=1, source_target_pairs={{1,0},{2,1},{3,2},{5,4},{6,5},{7,6},{9,8},{10,9},{11,10},{13,12},{... | collective-permute-start | bytes 1769480 | tf_op jit(solution)/shard_map/ppermute | solution.py:234
  119.5 2.0 %fusion.1 = f32[48,16,384]{2,1,0:T(8,128)S(1)} fusion(f32[48,16]{1,0:T(8,128)S(1)} %get-tuple-element.40, f32[48,16,16]{2,1,0:T(8,128)S(1)} %get-tuple-element.39, f32[48,16,16]{2,1,0:T(8,128)S(1)} %get-tuple-element.38, f32[16,384]{1,0:T(8,128)} %get-tuple-element.66, f32[16,384]{1,0:T(8,128)} %get-tuple-element.65), kind=kOutput, calls=%fused_computation.2 | convolution fusion | flops 114167808 | bytes 1330176 | tf_op jit(solution)/shard_map/kzd,dx->kzx/dot_general | solution.py:432
  123.3 1.5 fusion.9
  124.9 31.5 %collective-permute-done.6 = bf16[384,768]{1,0:T(8,128)(2,1)S(1)} collective-permute-done((bf16[384,768]{1,0:T(8,128)(2,1)}, bf16[384,768]{1,0:T(8,128)(2,1)S(1)}, u32[]{:S(2)}, u32[]{:S(2)}) %collective-permute-start.6) | collective-permute-done | bytes 589856 | tf_op jit(solution)/shard_map/ppermute | solution.py:234
  156.5 9.2 %collective-permute-start.7 = (bf16[256,768]{1,0:T(8,128)(2,1)S(1)}, bf16[256,768]{1,0:T(8,128)(2,1)S(1)}, u32[]{:S(2)}, u32[]{:S(2)}) collective-permute-start(bf16[256,768]{1,0:T(8,128)(2,1)S(1)} %convert_element_type.130), channel_id=1, source_target_pairs={{4,16},{12,24},{16,4},{24,12},{5,17},{13,25},{17,5},{25,13},{6,18}... | collective-permute-start | bytes 1179656 | tf_op jit(solution)/shard_map/ppermute | solution.py:400
  166.5 4.6 %collective-permute-done.7 = bf16[256,768]{1,0:T(8,128)(2,1)S(1)} collective-permute-done((bf16[256,768]{1,0:T(8,128)(2,1)S(1)}, bf16[256,768]{1,0:T(8,128)(2,1)S(1)}, u32[]{:S(2)}, u32[]{:S(2)}) %collective-permute-start.7) | collective-permute-done | bytes 393248 | tf_op jit(solution)/shard_map/ppermute | solution.py:400
  (105 shorter events, 20.4 us)
Async XLA Ops:
  5.3 4.4 %copy-start.11 = (f32[16]{0:T(128)S(1)}, f32[16]{0:T(128)}, u32[]{:S(2)}) copy-start(f32[16]{0:T(128)} %defocus.5) | copy-start | bytes 196
  5.3 21.9 %all-to-all-start = ((bf16[8,80,768]{2,1,0:T(8,128)(2,1)}), bf16[8,80,768]{2,1,0:T(8,128)(2,1)S(1)}, u32[]{:S(2)}, u32[]{:S(2)}) async-start(bf16[8,80,768]{2,1,0:T(8,128)(2,1)} %spectrum.3), calls=%async_computation | async-start | bytes 1966080 | tf_op jit(solution)/shard_map/all_to_all | solution.py:308
  17.9 8.5 %copy-start.12 = (f32[16]{0:T(128)S(1)}, f32[16]{0:T(128)}, u32[]{:S(2)}) copy-start(f32[16]{0:T(128)} %defocus.5) | copy-start | bytes 196
  27.2 21.8 %all-to-all-start.1 = ((bf16[8,128,768]{2,1,0:T(8,128)(2,1)}), bf16[8,128,768]{2,1,0:T(8,128)(2,1)S(1)}, u32[]{:S(2)}, u32[]{:S(2)}) async-start(bf16[8,128,768]{2,1,0:T(8,128)(2,1)} %spectrum.4), calls=%async_computation.1 | async-start | bytes 3145728 | tf_op jit(solution)/shard_map/all_to_all | solution.py:308
  34.7 22.0 %copy-start = (bf16[3,144,768]{2,1,0:T(8,128)(2,1)}, bf16[3,144,768]{2,1,0:T(8,128)(2,1)S(1)}, u32[]{:S(2)}) copy-start(bf16[3,144,768]{2,1,0:T(8,128)(2,1)S(1)} %insert.3) | copy-start | bytes 1990660
  49.0 50.2 %all-to-all-start.2 = ((bf16[8,192,768]{2,1,0:T(8,128)(2,1)}), bf16[8,192,768]{2,1,0:T(8,128)(2,1)}, u32[]{:S(2)}, u32[]{:S(2)}) async-start(bf16[8,192,768]{2,1,0:T(8,128)(2,1)} %spectrum.5), calls=%async_computation.2 | async-start | bytes 4718592 | tf_op jit(solution)/shard_map/all_to_all | solution.py:308
  57.5 8.8 %collective-permute-start = (bf16[144,768]{1,0:T(8,128)(2,1)S(1)}, bf16[144,768]{1,0:T(8,128)(2,1)S(1)}, u32[]{:S(2)}, u32[]{:S(2)}) collective-permute-start(bf16[144,768]{1,0:T(8,128)(2,1)S(1)} %get-tuple-element.36), channel_id=1, source_target_pairs={{0,1},{1,2},{3,0},{4,5},{5,6},{7,4},{8,9},{9,10},{11,8},{12,13},{1... | collective-permute-start | bytes 663560 | tf_op jit(solution)/shard_map/ppermute | solution.py:234
  58.8 12.1 %collective-permute-start.1 = (bf16[144,768]{1,0:T(8,128)(2,1)S(1)}, bf16[144,768]{1,0:T(8,128)(2,1)S(1)}, u32[]{:S(2)}, u32[]{:S(2)}) collective-permute-start(bf16[144,768]{1,0:T(8,128)(2,1)S(1)} %get-tuple-element.37), channel_id=1, source_target_pairs={{1,0},{2,1},{3,2},{5,4},{6,5},{7,6},{9,8},{10,9},{11,10},{13,12},{... | collective-permute-start | bytes 663560 | tf_op jit(solution)/shard_map/ppermute | solution.py:234
  63.0 16.9 %collective-permute-start.2 = (bf16[144,768]{1,0:T(8,128)(2,1)}, bf16[144,768]{1,0:T(8,128)(2,1)S(1)}, u32[]{:S(2)}, u32[]{:S(2)}) collective-permute-start(bf16[144,768]{1,0:T(8,128)(2,1)} %get-tuple-element.35), channel_id=1, source_target_pairs={{0,2},{2,0},{3,1},{4,6},{6,4},{7,5},{8,10},{10,8},{11,9},{12,14},{... | collective-permute-start | bytes 663560 | tf_op jit(solution)/shard_map/ppermute | solution.py:234
  66.2 4.7 %copy-start.5 = (bf16[144,768]{1,0:T(8,128)(2,1)}, bf16[144,768]{1,0:T(8,128)(2,1)S(1)}, u32[]{:S(2)}) copy-start(bf16[144,768]{1,0:T(8,128)(2,1)S(1)} %collective-permute-done) | copy-start | bytes 663556
  73.9 25.3 %collective-permute-start.3 = (bf16[256,768]{1,0:T(8,128)(2,1)S(1)}, bf16[256,768]{1,0:T(8,128)(2,1)}, u32[]{:S(2)}, u32[]{:S(2)}) collective-permute-start(bf16[256,768]{1,0:T(8,128)(2,1)S(1)} %get-tuple-element.33), channel_id=1, source_target_pairs={{0,1},{1,2},{3,0},{7,6},{6,5},{4,7},{8,9},{9,10},{11,8},{15,14},{1... | collective-permute-start | bytes 1179656 | tf_op jit(solution)/shard_map/ppermute | solution.py:234
  77.9 21.3 %collective-permute-start.4 = (bf16[256,768]{1,0:T(8,128)(2,1)S(1)}, bf16[256,768]{1,0:T(8,128)(2,1)}, u32[]{:S(2)}, u32[]{:S(2)}) collective-permute-start(bf16[256,768]{1,0:T(8,128)(2,1)S(1)} %get-tuple-element.34), channel_id=1, source_target_pairs={{1,0},{2,1},{3,2},{6,7},{5,6},{4,5},{9,8},{10,9},{11,10},{14,15},{... | collective-permute-start | bytes 1179656 | tf_op jit(solution)/shard_map/ppermute | solution.py:234
  79.9 23.9 %copy-start.9 = (bf16[144,768]{1,0:T(8,128)(2,1)}, bf16[144,768]{1,0:T(8,128)(2,1)S(1)}, u32[]{:S(2)}) copy-start(bf16[144,768]{1,0:T(8,128)(2,1)S(1)} %collective-permute-done.2) | copy-start | bytes 663556
  79.9 42.7 %collective-permute-start.5 = (bf16[256,768]{1,0:T(8,128)(2,1)}, bf16[256,768]{1,0:T(8,128)(2,1)}, u32[]{:S(2)}, u32[]{:S(2)}) collective-permute-start(bf16[256,768]{1,0:T(8,128)(2,1)} %get-tuple-element.32), channel_id=1, source_target_pairs={{0,2},{2,0},{3,1},{7,5},{5,7},{4,6},{8,10},{10,8},{11,9},{15,13},{... | collective-permute-start | bytes 1179656 | tf_op jit(solution)/shard_map/ppermute | solution.py:234
  108.9 56.8 %collective-permute-start.8 = (bf16[384,768]{1,0:T(8,128)(2,1)}, bf16[384,768]{1,0:T(8,128)(2,1)S(1)}, u32[]{:S(2)}, u32[]{:S(2)}) collective-permute-start(bf16[384,768]{1,0:T(8,128)(2,1)} %get-tuple-element.29), channel_id=1, source_target_pairs={{0,1},{1,2},{3,0},{4,5},{5,6},{7,4},{8,9},{9,10},{11,8},{12,13},{1... | collective-permute-start | bytes 1769480 | tf_op jit(solution)/shard_map/ppermute | solution.py:234
  110.2 55.5 %collective-permute-start.9 = (bf16[384,768]{1,0:T(8,128)(2,1)S(1)}, bf16[384,768]{1,0:T(8,128)(2,1)S(1)}, u32[]{:S(2)}, u32[]{:S(2)}) collective-permute-start(bf16[384,768]{1,0:T(8,128)(2,1)S(1)} %get-tuple-element.30), channel_id=1, source_target_pairs={{0,2},{2,0},{3,1},{4,6},{6,4},{7,5},{8,10},{10,8},{11,9},{12,14},{... | collective-permute-start | bytes 1769480 | tf_op jit(solution)/shard_map/ppermute | solution.py:234
  116.3 40.1 %collective-permute-start.6 = (bf16[384,768]{1,0:T(8,128)(2,1)}, bf16[384,768]{1,0:T(8,128)(2,1)S(1)}, u32[]{:S(2)}, u32[]{:S(2)}) collective-permute-start(bf16[384,768]{1,0:T(8,128)(2,1)} %get-tuple-element.31), channel_id=1, source_target_pairs={{1,0},{2,1},{3,2},{5,4},{6,5},{7,6},{9,8},{10,9},{11,10},{13,12},{... | collective-permute-start | bytes 1769480 | tf_op jit(solution)/shard_map/ppermute | solution.py:234
  119.4 2.1 %copy-start.1 = (bf16[3,144,768]{2,1,0:T(8,128)(2,1)S(1)}, bf16[3,144,768]{2,1,0:T(8,128)(2,1)}, u32[]{:S(2)}) copy-start(bf16[3,144,768]{2,1,0:T(8,128)(2,1)} %copy-done) | copy-start | bytes 1990660
  119.4 2.1 %copy-start.6 = (bf16[144,768]{1,0:T(8,128)(2,1)S(1)}, bf16[144,768]{1,0:T(8,128)(2,1)}, u32[]{:S(2)}) copy-start(bf16[144,768]{1,0:T(8,128)(2,1)} %copy-done.5) | copy-start | bytes 663556
  119.4 2.1 %copy-start.8 = (bf16[144,768]{1,0:T(8,128)(2,1)S(1)}, bf16[144,768]{1,0:T(8,128)(2,1)}, u32[]{:S(2)}) copy-start(bf16[144,768]{1,0:T(8,128)(2,1)} %copy-done.7) | copy-start | bytes 663556
  119.5 2.1 %copy-start.10 = (bf16[144,768]{1,0:T(8,128)(2,1)S(1)}, bf16[144,768]{1,0:T(8,128)(2,1)}, u32[]{:S(2)}) copy-start(bf16[144,768]{1,0:T(8,128)(2,1)} %copy-done.9) | copy-start | bytes 663556
  156.5 9.8 %slice-start.1 = ((f32[48,16,384]{2,1,0:T(8,128)}), f32[24,16,384]{2,1,0:T(8,128)S(1)}, s32[]{:S(2)}) async-start(f32[48,16,384]{2,1,0:T(8,128)} %copy-done.2), calls=%async_computation.4 | async-start | bytes 1179648 | tf_op jit(solution)/shard_map/slice | solution.py:440
  156.5 14.7 %collective-permute-start.7 = (bf16[256,768]{1,0:T(8,128)(2,1)S(1)}, bf16[256,768]{1,0:T(8,128)(2,1)S(1)}, u32[]{:S(2)}, u32[]{:S(2)}) collective-permute-start(bf16[256,768]{1,0:T(8,128)(2,1)S(1)} %convert_element_type.130), channel_id=1, source_target_pairs={{4,16},{12,24},{16,4},{24,12},{5,17},{13,25},{17,5},{25,13},{6,18}... | collective-permute-start | bytes 1179656 | tf_op jit(solution)/shard_map/ppermute | solution.py:400
  166.5 4.7 %slice-start = ((f32[48,16,384]{2,1,0:T(8,128)}), f32[16,16,384]{2,1,0:T(8,128)S(1)}, s32[]{:S(2)}) async-start(f32[48,16,384]{2,1,0:T(8,128)} %copy-done.2), calls=%async_computation.3 | async-start | bytes 786432 | tf_op jit(solution)/shard_map/slice | solution.py:440
  (4 other events, 4.9 us)

commit v18 on v9

--- a/solution.py
+++ b/solution.py
@@ -88,7 +88,7 @@
     loads = [pltpu.make_async_copy(left_in, left, load_sems.at[0])]
     for p in range(particles):
         loads.append(pltpu.make_async_copy(images_in.at[p], images.at[p], load_sems.at[1 + p]))
-    loads.append(pltpu.make_async_copy(right_in, right, load_sems.at[1 + particles]))
+    loads.append(pltpu.make_async_copy(right_in, right.at[:length], load_sems.at[1 + particles]))
     for load in loads:
         load.start()
 
@@ -143,6 +143,8 @@
         joined[p * rows : (p + 1) * rows, :length] = section[:rows]
         joined[p * rows : (p + 1) * rows, length:] = section[rows:]
     loads[1 + particles].wait()
+    right[length:, :length] = -right[:length, length:]
+    right[length:, length:] = right[:length, :length]
     sends = []
     for first in range(0, particles, 2):
         spectrum = jnp.dot(
@@ -260,7 +262,7 @@
     fields = slab_count + 1
 
     cosine, minus_sine, table_right = dft_tables(length)
-    table_right = jnp.asarray(table_right.astype(jnp.bfloat16))
+    table_right = jnp.asarray(table_right[:length].astype(jnp.bfloat16))
     received = []
     weighted = []
     for c, each in enumerate(sizes):

time: 155 us -> 155 us (level)
  no operation moved by 1% of the time
where the time goes in v18:
time: 155 us; the launch traced here: 154 us
  waiting for transfers between devices  62 us (40%)
  starting transfers between devices  45.6 us (29%)
  Pallas kernels  27.5 us (18%)
  other arithmetic  11 us (7%)
  local copies, waits for them, and re-layouts  4.2 us (3%)
  matrix products  3.47 us (2%)
    ppermute x9, waiting for transfers between devices, slab_exchange(): arrived.append(lax.ppermute(block, ('batch', 'slab'), perm))  52.3 us
    ppermute x9, starting transfers between devices, slab_exchange(): arrived.append(lax.ppermute(block, ('batch', 'slab'), perm))  30.8 us
    pallas_call x3, Pallas kernels, per_device(): pl.pallas_call(functools.partial(spectrum_kernel, runs, with_meta), out_s...  20.1 us
    all_to_all x3, starting transfers between devices, per_device(): received.append(lax.all_to_all(send, 'batch', 0, 0, tiled=True))  13.9 us
    all_to_all x3, waiting for transfers between devices, per_device(): received.append(lax.all_to_all(send, 'batch', 0, 0, tiled=True))  9.69 us
    pallas_call x3, Pallas kernels, per_device(): pl.pallas_call(functools.partial(insert_kernel, bins, meta_at), out_shape...  7.31 us
    add x3, other arithmetic, per_device(): sums[c] = sums[c] + block[:each * planes].astype(jnp.float32)  4.4 us
    select_n x3, other arithmetic, choose(): chosen = jnp.where(index == d, parts[d], chosen)  3.28 us
  transfers between devices with their start and end apart: 13, of which 9 were waited for; matrix products, arithmetic and copies ran while one was open for 10% of the time, Pallas kernels for 13%

profile of v18, /device:TPU:0, one launch (start us, length us, event | category | flops | bytes accessed | tf_op | source)
XLA Modules:
  0.0 154.1 jit_solution(16507222143487140180)
XLA Ops:
  0.0 6.8 %spectrum.3 = bf16[8,144,768]{2,1,0:T(8,128)(2,1)} custom-call(s32[8]{0:T(128)} %classes.5, s32[2,8]{1,0:T(2,128)} %bitcast.90, s32[8]{0:T(128)} %defocus_class.5, f32[16]{0:T(128)} %defocus.5, s32[4,8]{1,0:T(4,128)} %bitcast.87, bf16[8,384,384]{2,1,0:T(8,128)(2,1)} %images_in.5, bf16[256,384]{1,0:T(8,128)(2,1)} %constant.169.clone.left_in, ...), custom_call_target="tpu_custom_call" | custom-call | tf_op jit(solution)/shard_map/spectrum/pallas_call | solution.py:279
  6.8 5.2 %all-to-all-start = ((bf16[8,144,768]{2,1,0:T(8,128)(2,1)}), bf16[8,144,768]{2,1,0:T(8,128)(2,1)S(1)}, u32[]{:S(2)}, u32[]{:S(2)}) async-start(bf16[8,144,768]{2,1,0:T(8,128)(2,1)} %spectrum.3), calls=%async_computation | async-start | bytes 3538944 | tf_op jit(solution)/shard_map/all_to_all | solution.py:307
  12.0 6.7 %spectrum.4 = bf16[8,128,768]{2,1,0:T(8,128)(2,1)} custom-call(s32[8]{0:T(128)} %classes.5, s32[2,8]{1,0:T(2,128)} %bitcast.91, s32[8]{0:T(128)} %defocus_class.5, f32[16]{0:T(128)} %defocus.5, s32[4,8]{1,0:T(4,128)} %bitcast.88, bf16[8,384,384]{2,1,0:T(8,128)(2,1)} %images_in.5, bf16[256,384]{1,0:T(8,128)(2,1)} %constant.170.clone.left_in, ...), custom_call_target="tpu_custom_call" | custom-call | tf_op jit(solution)/shard_map/spectrum/pallas_call | solution.py:279
  18.6 6.7 %spectrum.5 = bf16[8,128,768]{2,1,0:T(8,128)(2,1)} custom-call(s32[8]{0:T(128)} %classes.5, s32[2,8]{1,0:T(2,128)} %bitcast.92, s32[8]{0:T(128)} %defocus_class.5, f32[16]{0:T(128)} %defocus.5, s32[4,8]{1,0:T(4,128)} %bitcast.89, bf16[8,384,384]{2,1,0:T(8,128)(2,1)} %images_in.5, bf16[256,384]{1,0:T(8,128)(2,1)} %constant.171.clone.left_in, ...), custom_call_target="tpu_custom_call" | custom-call | tf_op jit(solution)/shard_map/spectrum/pallas_call | solution.py:279
  25.4 9.7 %all-to-all-done.received = bf16[8,144,768]{2,1,0:T(8,128)(2,1)S(1)} async-done(((bf16[8,144,768]{2,1,0:T(8,128)(2,1)}), bf16[8,144,768]{2,1,0:T(8,128)(2,1)S(1)}, u32[]{:S(2)}, u32[]{:S(2)}) %all-to-all-start) | async-done | bytes 1769504 | tf_op jit(solution)/shard_map/all_to_all | solution.py:307
  35.1 4.5 %all-to-all-start.1 = ((bf16[8,128,768]{2,1,0:T(8,128)(2,1)}), bf16[8,128,768]{2,1,0:T(8,128)(2,1)}, u32[]{:S(2)}, u32[]{:S(2)}) async-start(bf16[8,128,768]{2,1,0:T(8,128)(2,1)} %spectrum.4), calls=%async_computation.1 | async-start | bytes 3145728 | tf_op jit(solution)/shard_map/all_to_all | solution.py:307
  40.9 1.7 %insert.3 = bf16[3,272,768]{2,1,0:T(8,128)(2,1)S(1)} custom-call(bf16[8,144,768]{2,1,0:T(8,128)(2,1)S(1)} %all-to-all-done.received, s32[1,1152]{1,0:T(1,128)S(1)} %reshape.197.codes), custom_call_target="tpu_custom_call" | custom-call | tf_op jit(solution)/shard_map/insert/pallas_call | solution.py:365
  43.5 3.5 %collective-permute-start = (bf16[272,768]{1,0:T(8,128)(2,1)S(1)}, bf16[272,768]{1,0:T(8,128)(2,1)S(1)}, u32[]{:S(2)}, u32[]{:S(2)}) collective-permute-start(bf16[272,768]{1,0:T(8,128)(2,1)S(1)} %get-tuple-element.30), channel_id=1, source_target_pairs={{0,1},{1,2},{3,0},{4,5},{5,6},{7,4},{8,9},{9,10},{11,8},{12,13},{1... | collective-permute-start | bytes 1253384 | tf_op jit(solution)/shard_map/ppermute | solution.py:236
  49.2 5.6 %collective-permute-start.2 = (bf16[272,768]{1,0:T(8,128)(2,1)}, bf16[272,768]{1,0:T(8,128)(2,1)}, u32[]{:S(2)}, u32[]{:S(2)}) collective-permute-start(bf16[272,768]{1,0:T(8,128)(2,1)} %get-tuple-element.29), channel_id=1, source_target_pairs={{0,2},{2,0},{3,1},{4,6},{6,4},{7,5},{8,10},{10,8},{11,9},{12,14},{... | collective-permute-start | bytes 1253384 | tf_op jit(solution)/shard_map/ppermute | solution.py:236
  55.1 4.5 %collective-permute-done = bf16[272,768]{1,0:T(8,128)(2,1)S(1)} collective-permute-done((bf16[272,768]{1,0:T(8,128)(2,1)S(1)}, bf16[272,768]{1,0:T(8,128)(2,1)S(1)}, u32[]{:S(2)}, u32[]{:S(2)}) %collective-permute-start) | collective-permute-done | bytes 417824 | tf_op jit(solution)/shard_map/ppermute | solution.py:236
  59.7 8.2 %collective-permute-done.1 = bf16[272,768]{1,0:T(8,128)(2,1)S(1)} collective-permute-done((bf16[272,768]{1,0:T(8,128)(2,1)S(1)}, bf16[272,768]{1,0:T(8,128)(2,1)S(1)}, u32[]{:S(2)}, u32[]{:S(2)}) %collective-permute-start.1) | collective-permute-done | bytes 417824 | tf_op jit(solution)/shard_map/ppermute | solution.py:236
  67.8 4.3 %all-to-all-start.2 = ((bf16[8,128,768]{2,1,0:T(8,128)(2,1)}), bf16[8,128,768]{2,1,0:T(8,128)(2,1)}, u32[]{:S(2)}, u32[]{:S(2)}) async-start(bf16[8,128,768]{2,1,0:T(8,128)(2,1)} %spectrum.5), calls=%async_computation.2 | async-start | bytes 3145728 | tf_op jit(solution)/shard_map/all_to_all | solution.py:307
  72.1 2.8 %insert.4 = bf16[3,256,768]{2,1,0:T(8,128)(2,1)S(1)} custom-call(bf16[8,128,768]{2,1,0:T(8,128)(2,1)} %all-to-all-done.1.received, s32[1,1024]{1,0:T(1,128)S(1)} %reshape_reshape.6.codes), custom_call_target="tpu_custom_call" | custom-call | tf_op jit(solution)/shard_map/insert/pallas_call | solution.py:365
  76.1 4.1 %collective-permute-start.3 = (bf16[256,768]{1,0:T(8,128)(2,1)}, bf16[256,768]{1,0:T(8,128)(2,1)}, u32[]{:S(2)}, u32[]{:S(2)}) collective-permute-start(bf16[256,768]{1,0:T(8,128)(2,1)} %get-tuple-element.42), channel_id=1, source_target_pairs={{0,1},{1,2},{3,0},{7,6},{6,5},{4,7},{8,9},{9,10},{11,8},{15,14},{1... | collective-permute-start | bytes 1179656 | tf_op jit(solution)/shard_map/ppermute | solution.py:236
  81.5 5.5 %collective-permute-start.5 = (bf16[256,768]{1,0:T(8,128)(2,1)}, bf16[256,768]{1,0:T(8,128)(2,1)}, u32[]{:S(2)}, u32[]{:S(2)}) collective-permute-start(bf16[256,768]{1,0:T(8,128)(2,1)} %get-tuple-element.41), channel_id=1, source_target_pairs={{0,2},{2,0},{3,1},{7,5},{5,7},{4,6},{8,10},{10,8},{11,9},{15,13},{... | collective-permute-start | bytes 1179656 | tf_op jit(solution)/shard_map/ppermute | solution.py:236
  89.1 2.7 %collective-permute-done.3 = bf16[256,768]{1,0:T(8,128)(2,1)} collective-permute-done((bf16[256,768]{1,0:T(8,128)(2,1)}, bf16[256,768]{1,0:T(8,128)(2,1)}, u32[]{:S(2)}, u32[]{:S(2)}) %collective-permute-start.3) | collective-permute-done | bytes 393248 | tf_op jit(solution)/shard_map/ppermute | solution.py:236
  91.8 2.5 %collective-permute-done.4 = bf16[256,768]{1,0:T(8,128)(2,1)} collective-permute-done((bf16[256,768]{1,0:T(8,128)(2,1)}, bf16[256,768]{1,0:T(8,128)(2,1)}, u32[]{:S(2)}, u32[]{:S(2)}) %collective-permute-start.4) | collective-permute-done | bytes 393248 | tf_op jit(solution)/shard_map/ppermute | solution.py:236
  94.3 2.8 %insert.5 = bf16[3,256,768]{2,1,0:T(8,128)(2,1)S(1)} custom-call(bf16[8,128,768]{2,1,0:T(8,128)(2,1)} %all-to-all-done.2.received, s32[1,1024]{1,0:T(1,128)S(1)} %reshape_reshape.7.codes), custom_call_target="tpu_custom_call" | custom-call | tf_op jit(solution)/shard_map/insert/pallas_call | solution.py:365
  100.9 10.3 %collective-permute-done.5 = bf16[256,768]{1,0:T(8,128)(2,1)} collective-permute-done((bf16[256,768]{1,0:T(8,128)(2,1)}, bf16[256,768]{1,0:T(8,128)(2,1)}, u32[]{:S(2)}, u32[]{:S(2)}) %collective-permute-start.5) | collective-permute-done | bytes 393248 | tf_op jit(solution)/shard_map/ppermute | solution.py:236
  111.2 5.5 %collective-permute-start.8 = (bf16[256,768]{1,0:T(8,128)(2,1)}, bf16[256,768]{1,0:T(8,128)(2,1)}, u32[]{:S(2)}, u32[]{:S(2)}) collective-permute-start(bf16[256,768]{1,0:T(8,128)(2,1)} %get-tuple-element.38), channel_id=1, source_target_pairs={{0,1},{1,2},{3,0},{4,5},{5,6},{7,4},{8,9},{9,10},{11,8},{12,13},{1... | collective-permute-start | bytes 1179656 | tf_op jit(solution)/shard_map/ppermute | solution.py:236
  116.7 2.7 %collective-permute-start.9 = (bf16[256,768]{1,0:T(8,128)(2,1)}, bf16[256,768]{1,0:T(8,128)(2,1)}, u32[]{:S(2)}, u32[]{:S(2)}) collective-permute-start(bf16[256,768]{1,0:T(8,128)(2,1)} %get-tuple-element.39), channel_id=1, source_target_pairs={{0,2},{2,0},{3,1},{4,6},{6,4},{7,5},{8,10},{10,8},{11,9},{12,14},{... | collective-permute-start | bytes 1179656 | tf_op jit(solution)/shard_map/ppermute | solution.py:236
  119.6 1.7 %fusion.2 = s32[256,384]{1,0:T(8,128)S(1)} fusion(s32[256]{0:T(256)S(1)} %bitcast.93, s32[256,384]{1,0:T(8,128)S(1)} %convert_reduce_fusion, s32[768,384]{1,0:T(8,128)} %param.18), kind=kOutput, calls=%fused_computation.4 | convolution fusion | flops 151781376 | bytes 1967104 | tf_op jit(solution)/shard_map/dot_general | solution.py:322
  127.1 5.7 %collective-permute-done.8 = bf16[256,768]{1,0:T(8,128)(2,1)} collective-permute-done((bf16[256,768]{1,0:T(8,128)(2,1)}, bf16[256,768]{1,0:T(8,128)(2,1)}, u32[]{:S(2)}, u32[]{:S(2)}) %collective-permute-start.8) | collective-permute-done | bytes 393248 | tf_op jit(solution)/shard_map/ppermute | solution.py:236
  132.8 16.8 %collective-permute-done.9 = bf16[256,768]{1,0:T(8,128)(2,1)} collective-permute-done((bf16[256,768]{1,0:T(8,128)(2,1)}, bf16[256,768]{1,0:T(8,128)(2,1)}, u32[]{:S(2)}, u32[]{:S(2)}) %collective-permute-start.9) | collective-permute-done | bytes 393248 | tf_op jit(solution)/shard_map/ppermute | solution.py:236
  (81 shorter events, 23.2 us)
Async XLA Ops:
  6.8 28.3 %all-to-all-start = ((bf16[8,144,768]{2,1,0:T(8,128)(2,1)}), bf16[8,144,768]{2,1,0:T(8,128)(2,1)S(1)}, u32[]{:S(2)}, u32[]{:S(2)}) async-start(bf16[8,144,768]{2,1,0:T(8,128)(2,1)} %spectrum.3), calls=%async_computation | async-start | bytes 3538944 | tf_op jit(solution)/shard_map/all_to_all | solution.py:307
  25.4 14.6 %copy-start.2 = (s32[768,384]{1,0:T(8,128)S(1)}, s32[768,384]{1,0:T(8,128)}, u32[]{:S(2)}) copy-start(s32[768,384]{1,0:T(8,128)} %param.18) | copy-start | bytes 3538948
  35.1 32.7 %all-to-all-start.1 = ((bf16[8,128,768]{2,1,0:T(8,128)(2,1)}), bf16[8,128,768]{2,1,0:T(8,128)(2,1)}, u32[]{:S(2)}, u32[]{:S(2)}) async-start(bf16[8,128,768]{2,1,0:T(8,128)(2,1)} %spectrum.4), calls=%async_computation.1 | async-start | bytes 3145728 | tf_op jit(solution)/shard_map/all_to_all | solution.py:307
  42.6 5.7 %copy-start.5 = (f32[16]{0:T(128)S(1)}, f32[16]{0:T(128)}, u32[]{:S(2)}) copy-start(f32[16]{0:T(128)} %defocus.5) | copy-start | bytes 196
  43.5 16.2 %collective-permute-start = (bf16[272,768]{1,0:T(8,128)(2,1)S(1)}, bf16[272,768]{1,0:T(8,128)(2,1)S(1)}, u32[]{:S(2)}, u32[]{:S(2)}) collective-permute-start(bf16[272,768]{1,0:T(8,128)(2,1)S(1)} %get-tuple-element.30), channel_id=1, source_target_pairs={{0,1},{1,2},{3,0},{4,5},{5,6},{7,4},{8,9},{9,10},{11,8},{12,13},{1... | collective-permute-start | bytes 1253384 | tf_op jit(solution)/shard_map/ppermute | solution.py:236
  46.9 20.9 %collective-permute-start.1 = (bf16[272,768]{1,0:T(8,128)(2,1)S(1)}, bf16[272,768]{1,0:T(8,128)(2,1)S(1)}, u32[]{:S(2)}, u32[]{:S(2)}) collective-permute-start(bf16[272,768]{1,0:T(8,128)(2,1)S(1)} %get-tuple-element.31), channel_id=1, source_target_pairs={{1,0},{2,1},{3,2},{5,4},{6,5},{7,6},{9,8},{10,9},{11,10},{13,12},{... | collective-permute-start | bytes 1253384 | tf_op jit(solution)/shard_map/ppermute | solution.py:236
  49.2 39.4 %collective-permute-start.2 = (bf16[272,768]{1,0:T(8,128)(2,1)}, bf16[272,768]{1,0:T(8,128)(2,1)}, u32[]{:S(2)}, u32[]{:S(2)}) collective-permute-start(bf16[272,768]{1,0:T(8,128)(2,1)} %get-tuple-element.29), channel_id=1, source_target_pairs={{0,2},{2,0},{3,1},{4,6},{6,4},{7,5},{8,10},{10,8},{11,9},{12,14},{... | collective-permute-start | bytes 1253384 | tf_op jit(solution)/shard_map/ppermute | solution.py:236
  67.8 26.4 %all-to-all-start.2 = ((bf16[8,128,768]{2,1,0:T(8,128)(2,1)}), bf16[8,128,768]{2,1,0:T(8,128)(2,1)}, u32[]{:S(2)}, u32[]{:S(2)}) async-start(bf16[8,128,768]{2,1,0:T(8,128)(2,1)} %spectrum.5), calls=%async_computation.2 | async-start | bytes 3145728 | tf_op jit(solution)/shard_map/all_to_all | solution.py:307
  76.1 15.7 %collective-permute-start.3 = (bf16[256,768]{1,0:T(8,128)(2,1)}, bf16[256,768]{1,0:T(8,128)(2,1)}, u32[]{:S(2)}, u32[]{:S(2)}) collective-permute-start(bf16[256,768]{1,0:T(8,128)(2,1)} %get-tuple-element.42), channel_id=1, source_target_pairs={{0,1},{1,2},{3,0},{7,6},{6,5},{4,7},{8,9},{9,10},{11,8},{15,14},{1... | collective-permute-start | bytes 1179656 | tf_op jit(solution)/shard_map/ppermute | solution.py:236
  80.2 14.1 %collective-permute-start.4 = (bf16[256,768]{1,0:T(8,128)(2,1)}, bf16[256,768]{1,0:T(8,128)(2,1)}, u32[]{:S(2)}, u32[]{:S(2)}) collective-permute-start(bf16[256,768]{1,0:T(8,128)(2,1)} %get-tuple-element.43), channel_id=1, source_target_pairs={{1,0},{2,1},{3,2},{6,7},{5,6},{4,5},{9,8},{10,9},{11,10},{14,15},{... | collective-permute-start | bytes 1179656 | tf_op jit(solution)/shard_map/ppermute | solution.py:236
  81.5 29.7 %collective-permute-start.5 = (bf16[256,768]{1,0:T(8,128)(2,1)}, bf16[256,768]{1,0:T(8,128)(2,1)}, u32[]{:S(2)}, u32[]{:S(2)}) collective-permute-start(bf16[256,768]{1,0:T(8,128)(2,1)} %get-tuple-element.41), channel_id=1, source_target_pairs={{0,2},{2,0},{3,1},{7,5},{5,7},{4,6},{8,10},{10,8},{11,9},{15,13},{... | collective-permute-start | bytes 1179656 | tf_op jit(solution)/shard_map/ppermute | solution.py:236
  97.1 1.4 copy-start
  98.5 27.7 %collective-permute-start.6 = (bf16[256,768]{1,0:T(8,128)(2,1)}, bf16[256,768]{1,0:T(8,128)(2,1)}, u32[]{:S(2)}, u32[]{:S(2)}) collective-permute-start(bf16[256,768]{1,0:T(8,128)(2,1)} %get-tuple-element.40), channel_id=1, source_target_pairs={{1,0},{2,1},{3,2},{5,4},{6,5},{7,6},{9,8},{10,9},{11,10},{13,12},{... | collective-permute-start | bytes 1179656 | tf_op jit(solution)/shard_map/ppermute | solution.py:236
  111.2 21.7 %collective-permute-start.8 = (bf16[256,768]{1,0:T(8,128)(2,1)}, bf16[256,768]{1,0:T(8,128)(2,1)}, u32[]{:S(2)}, u32[]{:S(2)}) collective-permute-start(bf16[256,768]{1,0:T(8,128)(2,1)} %get-tuple-element.38), channel_id=1, source_target_pairs={{0,1},{1,2},{3,0},{4,5},{5,6},{7,4},{8,9},{9,10},{11,8},{12,13},{1... | collective-permute-start | bytes 1179656 | tf_op jit(solution)/shard_map/ppermute | solution.py:236
  116.7 33.0 %collective-permute-start.9 = (bf16[256,768]{1,0:T(8,128)(2,1)}, bf16[256,768]{1,0:T(8,128)(2,1)}, u32[]{:S(2)}, u32[]{:S(2)}) collective-permute-start(bf16[256,768]{1,0:T(8,128)(2,1)} %get-tuple-element.39), channel_id=1, source_target_pairs={{0,2},{2,0},{3,1},{4,6},{6,4},{7,5},{8,10},{10,8},{11,9},{12,14},{... | collective-permute-start | bytes 1179656 | tf_op jit(solution)/shard_map/ppermute | solution.py:236
  123.0 1.6 %copy-start.4 = (f32[48,16]{1,0:T(8,128)S(1)}, f32[48,16]{1,0:T(8,128)}, u32[]{:S(2)}) copy-start(f32[48,16]{1,0:T(8,128)} %copy.53) | copy-start | bytes 9220
  126.2 23.5 %copy-start.1 = (bf16[3,256,768]{2,1,0:T(8,128)(2,1)S(1)}, bf16[3,256,768]{2,1,0:T(8,128)(2,1)}, u32[]{:S(2)}) copy-start(bf16[3,256,768]{2,1,0:T(8,128)(2,1)} %copy-done) | copy-start | bytes 3538948
  126.2 25.0 %collective-permute-start.7 = (bf16[256,768]{1,0:T(8,128)(2,1)S(1)}, bf16[256,768]{1,0:T(8,128)(2,1)S(1)}, u32[]{:S(2)}, u32[]{:S(2)}) collective-permute-start(bf16[256,768]{1,0:T(8,128)(2,1)S(1)} %convert_element_type.130), channel_id=1, source_target_pairs={{4,16},{12,24},{16,4},{24,12},{5,17},{13,25},{17,5},{25,13},{6,18}... | collective-permute-start | bytes 1179656 | tf_op jit(solution)/shard_map/ppermute | solution.py:399
  151.2 1.3 copy-start.3
